TPU v7x, 32 devices: a whole 2x2x4 slice. The times are simulated.
32 devices in a mesh: dp: 16 (over z, y, x), blk: 2 (over core).
Axes of the slice: x: 2, y: 2, z: 4, core: 2. Of those that a mesh axis runs over, the one named last changes fastest.
Arguments:
- gene_ids: int32 [16, 1024], P('dp', 'blk'), may hold values from 0 to 2303, as said below
- values: float32 [16, 1024], P('dp', 'blk'), may hold values from -6 to 6
- knowledge: bfloat16 [16, 1024, 768], P('dp', 'blk'), may hold values from -6 to 6
- lengths: int32 [16], P('dp'), may hold values from 513 to 1024, as said below
- groups: int32 [16], P('dp'), may hold values from 0 to 63
- gene_table: bfloat16 [2304, 768], replicated, may hold values from -6 to 6
- group_table: bfloat16 [64, 768], replicated, may hold values from -4 to 4
- w_know: bfloat16 [768, 768], replicated, may hold values from -0.21875 to 0.21875
- w_value: float32 [768], replicated, may hold values from -5 to 5
- norm1_gain: float32 [768], replicated, may hold values from 0.5 to 1.5
- norm1_bias: float32 [768], replicated, may hold values from -2 to 2
- w_qkv: bfloat16 [768, 2304], replicated, may hold values from -0.21875 to 0.21875
- bias_q: float32 [768], replicated, may hold values from -2 to 2
- bias_v: float32 [768], replicated, may hold values from -2 to 2
- w_out: bfloat16 [768, 768], replicated, may hold values from -1.75 to 1.75
- bias_out: float32 [768], replicated, may hold values from -2 to 2
- norm2_gain: float32 [768], replicated, may hold values from 0.5 to 1.5
- norm2_bias: float32 [768], replicated, may hold values from -2 to 2
- w_up: bfloat16 [768, 3072], replicated, may hold values from -0.21875 to 0.21875
- bias_up: float32 [3072], replicated, may hold values from -2 to 2
- w_down: bfloat16 [3072, 768], replicated, may hold values from -0.109375 to 0.109375
- bias_down: float32 [768], replicated, may hold values from -2 to 2
- cotangent: bfloat16 [16, 1024, 768], P('dp', 'blk'), may hold values from -6 to 6
Outputs:
- block_output: bfloat16 [16, 1024, 768], P('dp', 'blk')
- gene_table_grad: float32 [2304, 768], P(('dp', 'blk'))
- group_table_grad: float32 [64, 768], P(None, 'dp')
- w_know_grad: float32 [768, 768], P('dp')
- w_value_grad: float32 [768], P('dp')
- norm1_gain_grad: float32 [768], P('dp')
- norm1_bias_grad: float32 [768], P('dp')
- w_qkv_grad: float32 [768, 2304], P('dp')
- bias_q_grad: float32 [768], P('dp')
- bias_v_grad: float32 [768], P('dp')
- w_out_grad: float32 [768, 768], P('dp')
- bias_out_grad: float32 [768], P('dp')
- norm2_gain_grad: float32 [768], P('dp')
- norm2_bias_grad: float32 [768], P('dp')
- w_up_grad: float32 [768, 3072], P('dp')
- bias_up_grad: float32 [3072], P('dp')
- w_down_grad: float32 [3072, 768], P('dp')
- bias_down_grad: float32 [768], P('dp')
Inputs may be any that keep to these rules, and one draw needn't show every extreme that they name: lengths[c] is the number of live genes of cell c, which come first; some cell is full. `gene_ids`: take each run of 512 positions of a cell (one device's) and vocabulary blocks of 72 consecutive genes (block = gene // 72): at most 32 positions of a run name genes of one block, and in every run some block is named by exactly 32 positions.
All inputs are finite; a program needn't handle non-finite values.
Results may differ from a plain program's by a relative error of at most 0.015.
Values may be sent and summed in bfloat16 or wider, within the bound.
No kernel may reach another device: no remote copies, remote signals or barrier semaphores. Data moves between devices by JAX's collectives and lax.ppermute only.
A program may use at most 256 MiB of HBM per device.

v0:
```python
import jax
import jax.numpy as jnp
from jax import lax
from jax.sharding import PartitionSpec as P

HEADS = 12
HEAD_DIM = 64
VOC_DEV = 72


EPSILON = 1e-05


def as_sent(value):
    return jax.tree.map(lambda a: a.astype(jnp.bfloat16) if a.dtype == jnp.float32 else a, value)


def layer_norm(values_in, gain_vec, offset):
    center = values_in - jnp.mean(values_in, -1, keepdims=True)
    spread = jnp.mean(center * center, -1, keepdims=True)
    return center * lax.rsqrt(spread + EPSILON) * gain_vec + offset


def contract_rows(left, right):
    return lax.dot_general(
        left, right, (((0,), (0,)), ((), ())), preferred_element_type=jnp.float32
    )


def contract_cols(left, right):
    return lax.dot_general(
        left, right, (((1,), (1,)), ((), ())), preferred_element_type=jnp.float32
    )


def row_sums(array):
    return jnp.sum(array.astype(jnp.float32), 0)


def onehot_rows(grad_rows, slot_ids, count):
    targets = jnp.arange(count, dtype=jnp.int32)
    picker = (slot_ids[:, None] == targets[None, :]).astype(jnp.float32)
    return lax.dot_general(
        picker,
        grad_rows,
        (((0,), (0,)), ((), ())),
        precision=lax.Precision.HIGHEST,
        preferred_element_type=jnp.float32,
    )


def body(
    gene_ids,
    values,
    knowledge,
    lengths,
    groups,
    gene_table,
    group_table,
    w_know,
    w_value,
    norm1_gain,
    norm1_bias,
    w_qkv,
    bias_q,
    bias_v,
    w_out,
    bias_out,
    norm2_gain,
    norm2_bias,
    w_up,
    bias_up,
    w_down,
    bias_down,
    cotangent,
):
    model_width = w_out.shape[0]
    local_rows = gene_ids.shape[1]
    blocks = lax.axis_size("blk")
    block_index = lax.axis_index("blk")
    cell_len = local_rows * blocks
    token_ids = gene_ids[0]
    expression = values[0]
    prior = knowledge[0]
    length = lengths[0]
    positions = block_index * local_rows + jnp.arange(local_rows)
    live_rows = (positions < length).astype(jnp.float32)[:, None]
    group_hot = (jnp.arange(group_table.shape[0]) == groups[0]).astype(jnp.float32)
    group_row = group_table[groups[0]].astype(jnp.float32)
    embedded = (
        gene_table[token_ids].astype(jnp.float32)
        + group_row[None, :]
        + expression[:, None] * w_value[None, :]
        + jnp.dot(prior, w_know, preferred_element_type=jnp.float32)
    )
    normed, norm1_back = jax.vjp(layer_norm, embedded, norm1_gain, norm1_bias)
    normed_low = normed.astype(jnp.bfloat16)
    projected = jnp.dot(normed_low, w_qkv, preferred_element_type=jnp.float32)
    queries = (projected[:, :model_width] + bias_q).astype(jnp.bfloat16)
    key_rows = projected[:, model_width : 2 * model_width].astype(jnp.bfloat16)
    value_rows = (projected[:, 2 * model_width :] + bias_v).astype(jnp.bfloat16)
    key_all, value_all = (
        lax.all_gather(key_rows, "blk", axis=0, tiled=True),
        lax.all_gather(value_rows, "blk", axis=0, tiled=True),
    )
    key_heads = key_all.reshape(cell_len, HEADS, HEAD_DIM)
    value_heads = value_all.reshape(cell_len, HEADS, HEAD_DIM)
    key_live = jnp.arange(cell_len) < length
    score_scale = HEAD_DIM ** (-0.5)
    block_rows = 512
    count_blocks = local_rows // block_rows
    query_blocks = queries.reshape(count_blocks, block_rows, HEADS, HEAD_DIM)

    def block_scores(query_block):
        scores = (
            jnp.einsum("qhd,khd->hqk", query_block, key_heads, preferred_element_type=jnp.float32)
            * score_scale
        )
        return jnp.where(key_live[None, None, :], scores, -jnp.inf)

    def attend(query_block):
        scores = block_scores(query_block)
        row_max = jnp.max(scores, -1, keepdims=True)
        shifted = jnp.exp(scores - row_max)
        row_total = jnp.sum(shifted, -1, keepdims=True)
        attn_probs = (shifted / row_total).astype(jnp.bfloat16)
        out_block = jnp.einsum(
            "hqk,khd->qhd", attn_probs, value_heads, preferred_element_type=jnp.float32
        )
        return (out_block, row_max + jnp.log(row_total))

    attended, log_totals = lax.map(attend, query_blocks)
    attended = attended.reshape(local_rows, model_width).astype(jnp.bfloat16)
    residual = embedded + (jnp.dot(attended, w_out, preferred_element_type=jnp.float32) + bias_out)
    normed_two, norm2_back = jax.vjp(layer_norm, residual, norm2_gain, norm2_bias)
    normed_two_low = normed_two.astype(jnp.bfloat16)
    hidden = jnp.dot(normed_two_low, w_up, preferred_element_type=jnp.float32) + bias_up
    activated, gelu_back = jax.vjp(
        lambda inner_in: jax.nn.gelu(inner_in, approximate=False), hidden
    )
    activated_low = activated.astype(jnp.bfloat16)
    final_rows = residual + (
        jnp.dot(activated_low, w_down, preferred_element_type=jnp.float32) + bias_down
    )
    block_output = (live_rows * final_rows).astype(jnp.bfloat16)
    grad_final = cotangent[0].astype(jnp.float32) * live_rows
    grad_ffn = grad_final.astype(jnp.bfloat16)
    w_down_grad = contract_rows(activated_low, grad_ffn)
    bias_down_grad = row_sums(grad_ffn)
    grad_act = contract_cols(grad_ffn, w_down)
    grad_hidden = gelu_back(grad_act)[0].astype(jnp.bfloat16)
    w_up_grad = contract_rows(normed_two_low, grad_hidden)
    bias_up_grad = row_sums(grad_hidden)
    grad_normed_two = contract_cols(grad_hidden, w_up)
    grad_resid_norm, norm2_gain_grad, norm2_bias_grad = norm2_back(grad_normed_two)
    grad_residual = grad_final + grad_resid_norm
    grad_branch = grad_residual.astype(jnp.bfloat16)
    w_out_grad = contract_rows(attended, grad_branch)
    bias_out_grad = row_sums(grad_branch)
    grad_attended = contract_cols(grad_branch, w_out).astype(jnp.bfloat16)
    grad_blocks = grad_attended.reshape(count_blocks, block_rows, HEADS, HEAD_DIM)

    def attend_back(carry, inputs):
        key_grad, value_grad = carry
        query_block, grad_block, log_total = inputs
        scores = block_scores(query_block)
        probs_wide = jnp.exp(scores - log_total)
        probs_low = probs_wide.astype(jnp.bfloat16)
        value_grad = value_grad + jnp.einsum(
            "hqk,qhd->khd", probs_low, grad_block, preferred_element_type=jnp.float32
        )
        grad_probs = jnp.einsum(
            "qhd,khd->hqk", grad_block, value_heads, preferred_element_type=jnp.float32
        )
        row_inner = jnp.sum(probs_wide * grad_probs, -1, keepdims=True)
        grad_scores = (probs_wide * (grad_probs - row_inner)).astype(jnp.bfloat16)
        query_grad = (
            jnp.einsum("hqk,khd->qhd", grad_scores, key_heads, preferred_element_type=jnp.float32)
            * score_scale
        )
        key_grad = (
            key_grad
            + jnp.einsum(
                "hqk,qhd->khd", grad_scores, query_block, preferred_element_type=jnp.float32
            )
            * score_scale
        )
        return ((key_grad, value_grad), query_grad)

    empty_heads = jnp.zeros((cell_len, HEADS, HEAD_DIM), jnp.float32)
    (key_part, value_part), query_grads = lax.scan(
        attend_back, (empty_heads, empty_heads), (query_blocks, grad_blocks, log_totals)
    )
    key_grad, value_grad = (
        lax.psum_scatter(
            key_part.reshape(cell_len, model_width).astype(jnp.bfloat16),
            "blk",
            scatter_dimension=0,
            tiled=True,
        ).astype(jnp.float32),
        lax.psum_scatter(
            value_part.reshape(cell_len, model_width).astype(jnp.bfloat16),
            "blk",
            scatter_dimension=0,
            tiled=True,
        ).astype(jnp.float32),
    )
    query_low = query_grads.reshape(local_rows, model_width).astype(jnp.bfloat16)
    value_low = value_grad.astype(jnp.bfloat16)
    grad_qkv = jnp.concatenate([query_low, key_grad.astype(jnp.bfloat16), value_low], axis=1)
    w_qkv_grad = contract_rows(normed_low, grad_qkv)
    bias_q_grad = row_sums(query_low)
    bias_v_grad = row_sums(value_low)
    grad_normed = contract_cols(grad_qkv, w_qkv)
    grad_embed_norm, norm1_gain_grad, norm1_bias_grad = norm1_back(grad_normed)
    grad_embedded = grad_residual + grad_embed_norm
    w_know_grad = contract_rows(prior, grad_embedded.astype(jnp.bfloat16))
    w_value_grad = jnp.sum(expression[:, None] * grad_embedded, 0)
    group_grad = group_hot[:, None] * jnp.sum(grad_embedded, 0)[None, :]
    shares = (
        lax.psum_scatter(group_grad, "dp", scatter_dimension=1, tiled=True),
        lax.psum_scatter(w_know_grad, "dp", scatter_dimension=0, tiled=True),
        lax.psum_scatter(w_value_grad, "dp", scatter_dimension=0, tiled=True),
        lax.psum_scatter(norm1_gain_grad, "dp", scatter_dimension=0, tiled=True),
        lax.psum_scatter(norm1_bias_grad, "dp", scatter_dimension=0, tiled=True),
        lax.psum_scatter(w_qkv_grad, "dp", scatter_dimension=0, tiled=True),
        lax.psum_scatter(bias_q_grad, "dp", scatter_dimension=0, tiled=True),
        lax.psum_scatter(bias_v_grad, "dp", scatter_dimension=0, tiled=True),
        lax.psum_scatter(w_out_grad, "dp", scatter_dimension=0, tiled=True),
        lax.psum_scatter(bias_out_grad, "dp", scatter_dimension=0, tiled=True),
        lax.psum_scatter(norm2_gain_grad, "dp", scatter_dimension=0, tiled=True),
        lax.psum_scatter(norm2_bias_grad, "dp", scatter_dimension=0, tiled=True),
        lax.psum_scatter(w_up_grad, "dp", scatter_dimension=0, tiled=True),
        lax.psum_scatter(bias_up_grad, "dp", scatter_dimension=0, tiled=True),
        lax.psum_scatter(w_down_grad, "dp", scatter_dimension=0, tiled=True),
        lax.psum_scatter(bias_down_grad, "dp", scatter_dimension=0, tiled=True),
    )
    summed = jax.tree.map(
        lambda part: part.astype(jnp.float32), lax.psum(as_sent(tuple(shares)), "blk")
    )
    gene_grad = lax.psum_scatter(
        onehot_rows(grad_embedded, token_ids, lax.axis_size(("dp", "blk")) * VOC_DEV),
        ("dp", "blk"),
        scatter_dimension=0,
        tiled=True,
    )
    return (block_output.reshape(1, local_rows, model_width), gene_grad) + tuple(summed)


def solution(mesh):
    in_specs = (
        P("dp", "blk"),
        P("dp", "blk"),
        P("dp", "blk", None),
        P("dp"),
        P("dp"),
        P(),
        P(),
        P(),
        P(),
        P(),
        P(),
        P(),
        P(),
        P(),
        P(),
        P(),
        P(),
        P(),
        P(),
        P(),
        P(),
        P(),
        P("dp", "blk", None),
    )
    out_specs = (
        P("dp", "blk", None),
        P(("dp", "blk"), None),
        P(None, "dp"),
        P("dp", None),
        P("dp"),
        P("dp"),
        P("dp"),
        P("dp", None),
        P("dp"),
        P("dp"),
        P("dp", None),
        P("dp"),
        P("dp"),
        P("dp"),
        P("dp", None),
        P("dp"),
        P("dp", None),
        P("dp"),
    )
    return jax.shard_map(body, mesh=mesh, in_specs=in_specs, out_specs=out_specs, check_vma=False)
```

profile of v0, /device:TPU:0, one launch (start us, length us, event | category | flops | bytes accessed | tf_op | source)
XLA Modules:
  0.0 1245.6 jit_solution(10177652255455617880)
XLA Ops:
  9.7 5.5 gather_fusion
  15.3 2.6 fusion.52
  19.0 2.1 fusion.45
  21.2 2.1 copy-done.10
  24.4 3.3 fusion.18
  28.6 2.3 copy.56
  30.9 6.1 all-gather.5.cloned.1.call-done
  37.0 2.6 copy.57
  39.6 14.2 %fusion.6 = (f32[12,512]{1,0:T(8,128)S(1)}, f32[12,512,1024]{2,1,0:T(8,128)}) fusion(pred[1024]{0:T(1024)(128)(4,1)S(1)} %iota_compare_fusion.2, bf16[512,12,64]{0,2,1:T(8,128)(2,1)} %bitcast.87, bf16[1024,12,64]{0,2,1:T(8,128)(2,1)} %bitcast.85), kind=kOutput, calls=%fused_computation.12 | convolution fusion | flops 824174592 | bytes 27550720 | tf_op jit(solution)/shard_map/while/body/eval_jaxpr/qhd,khd->hqk/dot_general | solution.py:116
  53.9 11.2 fusion
  66.3 2.6 copy.55
  68.9 12.0 fusion.22
  82.3 20.7 %multiply_convert_fusion.1 = (bf16[512,3072]{1,0:T(8,128)(2,1)}, f32[512,3072]{1,0:T(8,128)}, f32[512,3072]{1,0:T(8,128)}) fusion(f32[3072]{0:T(1024)S(1)} %copy-done.41, bf16[768,3072]{1,0:T(8,128)(2,1)} %param.41, f32[512,768]{1,0:T(8,128)S(1)} %get-tuple-element.174, f32[768]{0:T(1024)S(1)} %copy-done.45, f32[768]{0:T(1024)S(1)} %copy-done.37, ...), kind=kOutput, calls=%fused_computation.17 | convolution fusion | flops 2521694208 | bytes 22042624 | tf_op jit(solution)/shard_map/dot_general | solution.py:137
  103.0 9.2 convert_reduce_fusion
  112.2 3.5 multiply_reduce_fusion.1
  121.1 2.3 copy.58
  123.4 12.9 %fusion.15 = bf16[12,64,1024]{2,1,0:T(8,128)(2,1)} fusion(bf16[512,12,64]{0,2,1:T(8,128)(2,1)} %bitcast.92, f32[12,512]{1,0:T(8,128)} %log_add_fusion, f32[12,512,1024]{2,1,0:T(8,128)} %get-tuple-element.172, pred[1024]{0:T(1024)(128)(4,1)S(1)} %iota_compare_fusion.2), kind=kOutput, calls=%fused_computation.39 | convolution fusion | flops 831258624 | bytes 27550720 | tf_op jit(solution)/shard_map/while/body/eval_jaxpr/hqk,qhd->khd/dot_general | solution.py:169
  136.4 18.4 %multiply_reduce_fusion = (f32[12,512]{1,0:T(8,128)}, f32[12,512,1024]{2,1,0:T(8,128)}) fusion(f32[12,512]{1,0:T(8,128)} %log_add_fusion, f32[12,512,1024]{2,1,0:T(8,128)} %get-tuple-element.172, pred[1024]{0:T(1024)(128)(4,1)S(1)} %iota_compare_fusion.2, bf16[512,12,64]{0,2,1:T(8,128)(2,1)} %bitcast.93, bf16[1024,12,64]{0,2,1:T(8,128)(2,1)} %bitcast.91), kind=kOutput, calls=%fused_computation.2 | convolution fusion | flops 836757504 | bytes 52741120 | tf_op jit(solution)/shard_map/while/body/eval_jaxpr/qhd,khd->hqk/dot_general | solution.py:172
  154.8 17.0 %multiply_convert_fusion = bf16[12,512,1024]{2,1,0:T(8,128)(2,1)S(1)} fusion(f32[12,512,1024]{2,1,0:T(8,128)} %get-tuple-element.178, f32[12,512]{1,0:T(8,128)} %get-tuple-element.177, f32[12,512]{1,0:T(8,128)} %log_add_fusion, f32[12,512,1024]{2,1,0:T(8,128)} %get-tuple-element.172, pred[1024]{0:T(1024)(128)(4,1)S(1)} %iota_compare_fusion.2), kind=kLoop, calls=%fused_computation.1 | loop fusion | flops 37748736 | bytes 62964736 | tf_op jit(solution)/shard_map/while/body/eval_jaxpr/convert_element_type | solution.py:176
  171.8 4.1 multiply_convert_fusion.2
  176.9 3.6 fusion.54
  180.7 10.4 convert_reduce_fusion.4
  191.2 5.3 multiply_reduce_fusion.2
  200.4 2.2 convolution_bitcast_fusion
  202.6 3.2 copy.60
  205.9 7.3 fusion.24
  213.9 8.9 fusion.46
  222.9 8.5 fusion.39
  233.1 88.7 %reduce-scatter.22.cloned.1.call-done = f32[48,768]{1,0:T(8,128)} async-done(((f32[768,768]{1,0:T(8,128)}), f32[48,768]{1,0:T(8,128)}) %reduce-scatter.22.cloned.1.call-update) | async-done | bytes 147472 | tf_op jit(solution)/shard_map/reduce_scatter | solution.py:229
  323.3 131.7 %reduce-scatter.28.cloned.1.call-done = f32[48,768]{1,0:T(8,128)} async-done(((f32[768,768]{1,0:T(8,128)}), f32[48,768]{1,0:T(8,128)}) %reduce-scatter.28.cloned.1.call-update) | async-done | bytes 147472
  454.9 1.7 copy.61
  456.6 154.0 %reduce-scatter.20.cloned.1.call-done = f32[48,2304]{1,0:T(8,128)} async-done(((f32[768,2304]{1,0:T(8,128)}), f32[48,2304]{1,0:T(8,128)}) %reduce-scatter.20.cloned.1.call-update) | async-done | bytes 442384 | tf_op jit(solution)/shard_map/reduce_scatter | solution.py:226
  610.7 1.7 convert_element_type.268
  612.4 173.6 %reduce-scatter.24.cloned.1.call-done = f32[48,3072]{1,0:T(8,128)} async-done(((f32[768,3072]{1,0:T(8,128)}), f32[48,3072]{1,0:T(8,128)}) %reduce-scatter.24.cloned.1.call-update) | async-done | bytes 589840 | tf_op jit(solution)/shard_map/reduce_scatter | solution.py:233
  786.1 1.8 convert_element_type.285
  787.9 174.7 %reduce-scatter.26.cloned.1.call-done = f32[192,768]{1,0:T(8,128)} async-done(((f32[3072,768]{1,0:T(8,128)}), f32[192,768]{1,0:T(8,128)}) %reduce-scatter.26.cloned.1.call-update) | async-done | bytes 589840 | tf_op jit(solution)/shard_map/reduce_scatter | solution.py:235
  962.6 1.8 convert_element_type.290
  964.5 10.0 fusion.13
  977.1 7.3 fusion.23
  984.6 76.1 %all-reduce.10 = (bf16[768]{0:T(1024)(128)(2,1)}, bf16[768]{0:T(1024)(128)(2,1)}, bf16[768]{0:T(1024)(128)(2,1)}, bf16[768]{0:T(1024)(128)(2,1)}, bf16[768]{0:T(...) all-reduce(f32[768]{0:T(1024)} %get-tuple-element.129, ...), channel_id=7, replica_groups=mesh['dp'=16,'blk'=2] {'dp'}, use_global_device_ids=true, to_apply=%region_20.21.clone | all-reduce | flops 9984 | bytes 59904
  1072.7 15.3 %reduce-scatter.18.cloned.1.call-done = f32[64,48]{0,1:T(8,128)} async-done(((f32[64,768]{0,1:T(8,128)}), f32[64,48]{0,1:T(8,128)}) %reduce-scatter.18.cloned.1.call-update) | async-done | bytes 12304 | tf_op jit(solution)/shard_map/reduce_scatter | solution.py:221
  1088.8 4.7 all-reduce.11
  1106.4 4.6 all-reduce.15.cloned.1.call-done
  1111.0 1.7 copy.59
  1114.3 1.7 convert_element_type.269
  1116.0 1.8 convert_element_type.286
  1117.8 1.8 convert_element_type.291
  1119.7 118.9 %reduce-scatter.16.cloned.1.call-done = f32[72,768]{1,0:T(8,128)} async-done(((f32[2304,768]{1,0:T(8,128)}), f32[72,768]{1,0:T(8,128)}) %reduce-scatter.16.cloned.1.call-update) | async-done | bytes 221200 | tf_op jit(solution)/shard_map/reduce_scatter | solution.py:241
  (179 shorter events, 49.9 us)
Async XLA Ops:
  7.2 11.8 copy-start
  7.2 29.8 %all-gather.5.cloned.1.call-start = ((), (), s32[]{:S(2)}) async-start(), calls=%async_computation.10 | async-start | bytes 2359296 | tf_op jit(solution)/shard_map/all_gather | solution.py:103
  9.7 5.6 copy-start.38
  9.7 5.6 copy-start.42
  15.2 3.8 copy-start.35
  15.2 3.8 copy-start.44
  17.9 3.3 copy-start.6
  17.9 3.3 copy-start.19
  19.0 2.2 copy-start.30
  19.0 5.4 copy-start.33
  19.0 5.4 copy-start.34
  21.2 2.1 copy-start.10
  24.4 42.0 %all-gather.3.cloned.1.call-start = ((), (), s32[]{:S(2)}) async-start(), calls=%async_computation.9 | async-start | bytes 2359296 | tf_op jit(solution)/shard_map/all_gather | solution.py:104
  27.7 163.4 %reduce-scatter.14.cloned.1.call-start = ((), (), s32[]{:S(2)}) async-start(), calls=%async_computation.12 | async-start | bytes 2359296 | tf_op jit(solution)/shard_map/reduce_scatter | solution.py:201
  53.9 11.2 copy-start.17
  68.9 12.0 copy-start.7
  68.9 12.0 copy-start.40
  68.9 12.0 copy-start.43
  80.9 22.1 %copy-start.16 = (bf16[12,64,512]{2,1,0:T(8,128)(2,1)}, bf16[12,64,512]{2,1,0:T(8,128)(2,1)S(1)}, u32[]{:S(2)}) copy-start(bf16[12,64,512]{2,1,0:T(8,128)(2,1)S(1)} %fusion.22) | copy-start | bytes 2359300
  81.0 31.2 %slice-start = ((s8[4718592]{0:T(1024)(128)(4,1)}), s8[4194304]{0:T(1024)(128)(4,1)S(1)}, s32[]{:S(2)}) async-start(s8[4718592]{0:T(1024)(128)(4,1)} %bitcast.103), calls=%async_computation.21 | async-start | bytes 8388608
  81.9 33.8 %copy-start.5 = (f32[512,768]{1,0:T(8,128)}, f32[512,768]{1,0:T(8,128)S(1)}, u32[]{:S(2)}) copy-start(f32[512,768]{1,0:T(8,128)S(1)} %get-tuple-element.174) | copy-start | bytes 4718596
  81.9 33.8 %copy-start.21 = (f32[512]{0:T(512)}, f32[512]{0:T(512)S(1)}, u32[]{:S(2)}) copy-start(f32[512]{0:T(512)S(1)} %broadcast_multiply_fusion.1) | copy-start | bytes 6148
  82.3 33.4 %copy-start.32 = (f32[512]{0:T(512)}, f32[512]{0:T(512)S(1)}, u32[]{:S(2)}) copy-start(f32[512]{0:T(512)S(1)} %fusion.32) | copy-start | bytes 6148
  82.3 20.7 %copy-start.11 = (bf16[1,512,768]{2,1,0:T(8,128)(2,1)S(1)}, bf16[1,512,768]{2,1,0:T(8,128)(2,1)}, u32[]{:S(2)}) copy-start(bf16[1,512,768]{2,1,0:T(8,128)(2,1)} %param.45) | copy-start | bytes 2359300
  82.3 29.9 %slice-start.1 = ((s8[4718592]{0:T(1024)(128)(4,1)}), s8[524288]{0:T(1024)(128)(4,1)S(1)}, s32[]{:S(2)}) async-start(s8[4718592]{0:T(1024)(128)(4,1)} %bitcast.103), calls=%async_computation.22 | async-start | bytes 1048576
  112.2 3.5 copy-start.47
  116.4 2.1 copy-start.23
  136.4 54.8 %reduce-scatter.12.cloned.1.call-start = ((), (), s32[]{:S(2)}) async-start(), calls=%async_computation.11 | async-start | bytes 2359296 | tf_op jit(solution)/shard_map/reduce_scatter | solution.py:195
  154.8 17.0 %copy-start.4 = (bf16[512,768]{0,1:T(8,128)(2,1)S(1)}, bf16[512,768]{0,1:T(8,128)(2,1)}, u32[]{:S(2)}) copy-start(bf16[512,768]{0,1:T(8,128)(2,1)} %copy.56) | copy-start | bytes 2359300
  171.8 5.0 copy-start.1
  176.9 144.9 %reduce-scatter.22.cloned.1.call-start = ((), (), s32[]{:S(2)}) async-start(), calls=%async_computation.16 | async-start | bytes 2506752 | tf_op jit(solution)/shard_map/reduce_scatter | solution.py:229
  180.5 10.7 copy-start.20
  180.5 274.4 %reduce-scatter.28.cloned.1.call-start = ((), (), s32[]{:S(2)}) async-start(), calls=%async_computation.19 | async-start | bytes 2506752
  191.2 5.3 copy-start.26
  191.2 5.3 copy-start.8
  191.2 5.3 copy-start.31
  191.2 5.3 copy-start.36
  196.5 1.6 copy-start.39
  197.2 3.2 copy-start.14
  205.8 404.8 %reduce-scatter.20.cloned.1.call-start = ((), (), s32[]{:S(2)}) async-start(), calls=%async_computation.15 | async-start | bytes 7520256 | tf_op jit(solution)/shard_map/reduce_scatter | solution.py:226
  213.2 572.8 %reduce-scatter.24.cloned.1.call-start = ((), (), s32[]{:S(2)}) async-start(), calls=%async_computation.17 | async-start | bytes 10027008 | tf_op jit(solution)/shard_map/reduce_scatter | solution.py:233
  222.8 739.8 %reduce-scatter.26.cloned.1.call-start = ((), (), s32[]{:S(2)}) async-start(), calls=%async_computation.18 | async-start | bytes 10027008 | tf_op jit(solution)/shard_map/reduce_scatter | solution.py:235
  231.4 856.6 %reduce-scatter.18.cloned.1.call-start = ((), (), s32[]{:S(2)}) async-start(), calls=%async_computation.14 | async-start | bytes 417792 | tf_op jit(solution)/shard_map/reduce_scatter | solution.py:221
  233.0 878.0 %all-reduce.15.cloned.1.call-start = ((), (), s32[]{:S(2)}) async-start(), calls=%async_computation.20 | async-start | bytes 2162688 | tf_op jit(solution)/shard_map/psum | solution.py:239
  964.4 274.1 %reduce-scatter.16.cloned.1.call-start = ((), (), s32[]{:S(2)}) async-start(), calls=%async_computation.13 | async-start | bytes 7299072 | tf_op jit(solution)/shard_map/reduce_scatter | solution.py:241
  977.1 7.3 copy-start.15
  977.1 7.5 copy-start.27
  977.1 7.5 copy-start.28
  (14 other events, 15.2 us)
Sparse Core Ops, SparseCore 0:
  24.5 12.4 all-gather.4
  38.6 10.9 all-gather.2
  136.5 10.2 reduce-scatter.13
  177.0 10.2 reduce-scatter.11
  192.0 129.6 reduce-scatter.21
  327.2 127.6 reduce-scatter.27
  460.3 150.3 reduce-scatter.19
  616.3 169.6 reduce-scatter.23
  792.7 169.8 reduce-scatter.25
  967.7 120.3 reduce-scatter.17
  1092.1 18.9 all-reduce.14
  1118.1 120.3 reduce-scatter.15
where the time goes:
time: 1250 us
  waiting for transfers between devices  868 us (69%)
  matrix products  166 us (13%)
  blocking collectives  80.8 us (6%)
  other arithmetic  66.4 us (5%)
  local copies, waits for them, and re-layouts  45.9 us (4%)
  between operations  17.8 us (1%)
    reduce_scatter x1, waiting for transfers between devices, body(): lax.psum_scatter(w_down_grad, 'dp', scatter_dimension=0, tiled=True)  175 us
    reduce_scatter x1, waiting for transfers between devices, body(): lax.psum_scatter(w_up_grad, 'dp', scatter_dimension=0, tiled=True)  174 us
    reduce_scatter x1, waiting for transfers between devices, body(): lax.psum_scatter(w_qkv_grad, 'dp', scatter_dimension=0, tiled=True)  154 us
    unnamed x13, waiting for transfers between devices  132 us
    reduce_scatter x1, waiting for transfers between devices, body(): lax.psum_scatter(onehot_rows(grad_embedded, token_ids, lax.axis_size(('dp...  119 us
    reduce_scatter x1, waiting for transfers between devices, body(): lax.psum_scatter(w_out_grad, 'dp', scatter_dimension=0, tiled=True)  88.7 us
    unnamed x1, blocking collectives  76.1 us
    dot_general x5, matrix products, contract_rows(): lax.dot_general(left, right, (((0,), (0,)), ((), ())), preferred_element_...  30.5 us
  transfers between devices with their start and end apart: 12, of which 9 were waited for; matrix products, arithmetic and copies ran while one was open for 15% of the time, Pallas kernels for 0%

commit v1 on v0

v1 whole, which is shorter than its diff:
```python
import jax
import jax.numpy as jnp
from jax import lax
from jax.experimental import pallas as pl
from jax.experimental.pallas import tpu as pltpu
from jax.sharding import PartitionSpec as P

HEAD_DIM = 64
VOC_DEV = 72
EPSILON = 1e-05
LOW = jnp.bfloat16
WIDE = jnp.float32
GRANT = 52 << 20


def dot(left, right, left_dim=1, right_dim=0):
    return lax.dot_general(
        left, right, (((left_dim,), (right_dim,)), ((), ())), preferred_element_type=WIDE
    )


def column_sums(array):
    return jnp.sum(array, 0, keepdims=True)


def row_means(array):
    return jnp.mean(array, -1, keepdims=True)


def normalize(array):
    center = array - row_means(array)
    scale = lax.rsqrt(row_means(center * center) + EPSILON)
    return center * scale, scale


def norm_back(grad, unit, scale, gain):
    inner = grad * gain
    return scale * (inner - row_means(inner) - unit * row_means(inner * unit))


def half_of(index, half):
    return pl.ds(pl.multiple_of(index * half, 128), half)


def whole(shape):
    return pl.BlockSpec(shape, lambda *_: (0,) * len(shape))


def params():
    return pltpu.CompilerParams(vmem_limit_bytes=GRANT)


def shaped(shape, dtype):
    return jax.ShapeDtypeStruct(shape, dtype)


def embed_kernel(
    ids_ref,
    expression_ref,
    prior_ref,
    table_ref,
    group_ref,
    w_know_ref,
    w_value_ref,
    gain_ref,
    offset_ref,
    w_key_ref,
    w_val_ref,
    bias_val_ref,
    embedded_ref,
    normed_ref,
    kv_ref,
):
    rows, width = prior_ref.shape
    embedded = dot(prior_ref[...], w_know_ref[...])
    if table_ref.shape[0] == rows:
        gathered = table_ref[...].astype(WIDE)
    else:
        ids = jnp.broadcast_to(ids_ref[...], (8, rows)).T[:, :1]
        slots = lax.broadcasted_iota(jnp.int32, (rows, table_ref.shape[0]), 1)
        picker = jnp.where(slots == ids, 1.0, 0.0).astype(LOW)
        gathered = dot(picker, table_ref[...])
    expression = jnp.broadcast_to(expression_ref[...], (8, rows)).T[:, :1]
    embedded = gathered + group_ref[...] + expression * w_value_ref[...] + embedded
    embedded_ref[...] = embedded
    unit, _ = normalize(embedded)
    normed = (unit * gain_ref[...] + offset_ref[...]).astype(LOW)
    normed_ref[...] = normed
    kv_ref[:, :width] = dot(normed, w_key_ref[...]).astype(LOW)
    kv_ref[:, width:] = (dot(normed, w_val_ref[...]) + bias_val_ref[...]).astype(LOW)


def embed(
    ids, expression, prior, table, group_row, w_know, w_value, gain, offset, w_qkv, bias_v
):
    rows, width = prior.shape
    columns = lambda index: pl.BlockSpec((width, width), lambda _: (0, index))
    return pl.pallas_call(
        embed_kernel,
        grid=(1,),
        in_specs=[
            whole((1, rows)),
            whole((1, rows)),
            whole((rows, width)),
            whole(table.shape),
            whole((1, width)),
            whole((width, width)),
            whole((1, width)),
            whole((1, width)),
            whole((1, width)),
            columns(1),
            columns(2),
            whole((1, width)),
        ],
        out_specs=[whole((rows, width)), whole((rows, width)), whole((rows, 2 * width))],
        out_shape=[
            shaped((rows, width), WIDE),
            shaped((rows, width), LOW),
            shaped((rows, 2 * width), LOW),
        ],
        compiler_params=params(),
        name="embed",
    )(ids, expression, prior, table, group_row, w_know, w_value, gain, offset, w_qkv, w_qkv, bias_v)


def query_kernel(normed_ref, w_query_ref, bias_ref, out_ref):
    out_ref[...] = (dot(normed_ref[...], w_query_ref[...]) + bias_ref[...]).astype(LOW)


def project_queries(normed, w_qkv, bias_q):
    rows, width = normed.shape
    return pl.pallas_call(
        query_kernel,
        grid=(1,),
        in_specs=[whole((rows, width)), whole((width, width)), whole((1, width))],
        out_specs=whole((rows, width)),
        out_shape=shaped((rows, width), LOW),
        compiler_params=params(),
        cost_estimate=pl.CostEstimate(
            flops=2 * rows * width * width, bytes_accessed=4 * rows * width, transcendentals=0
        ),
        name="queries",
    )(normed, w_qkv, bias_q)


def attend_kernel(live_ref, q_ref, ko_ref, vo_ref, kr_ref, vr_ref, out_ref, p_ref, c_ref):
    rows = q_ref.shape[0]
    lane = lax.broadcasted_iota(jnp.int32, (rows, 128), 1)
    place = lax.broadcasted_iota(jnp.int32, (rows, 128), 0)
    queries = q_ref[...] * LOW(HEAD_DIM**-0.5)
    halves = []
    for index, k_ref in enumerate((ko_ref, kr_ref)):
        dead = jnp.where(place < live_ref[index], 0.0, -1e30).astype(LOW)
        halves.append((k_ref[...], dead))
    values = [vo_ref[...].T, vr_ref[...].T]
    outs = []
    for head in range(2):
        inside = (lane < HEAD_DIM) if head == 0 else (lane >= HEAD_DIM)
        spare = HEAD_DIM * (1 - head)
        asked = jnp.where(inside, queries, jnp.where(lane == spare, 1.0, 0.0).astype(LOW))
        scores = [dot(jnp.where(lane == spare, dead, keys), asked, 1, 1) for keys, dead in halves]
        top = jnp.maximum(*[jnp.max(part, 0, keepdims=True) for part in scores])
        mass, mixed = 0.0, 0.0
        for index in range(2):
            probs = jnp.exp(scores[index] - top)
            mass = mass + column_sums(probs)
            low = probs.astype(LOW)
            p_ref[head, index * rows : (index + 1) * rows, :] = low
            mixed = mixed + dot(values[index][head * HEAD_DIM : (head + 1) * HEAD_DIM], low)
        inverse = 1.0 / mass
        c_ref[0, head : head + 1, :] = inverse
        outs.append(mixed * inverse)
    out_ref[...] = jnp.concatenate(outs, 0).T.astype(LOW)


def attend(live, queries, kv_own, kv_other):
    rows, width = queries.shape
    pairs = width // 128
    block = lambda shift: pl.BlockSpec((rows, 128), lambda j, _: (0, shift + j))
    return pl.pallas_call(
        attend_kernel,
        grid_spec=pltpu.PrefetchScalarGridSpec(
            num_scalar_prefetch=1,
            grid=(pairs,),
            in_specs=[block(0), block(0), block(pairs), block(0), block(pairs)],
            out_specs=[
                block(0),
                pl.BlockSpec((2, 2 * rows, rows), lambda j, _: (j, 0, 0)),
                pl.BlockSpec((1, 2, rows), lambda j, _: (j, 0, 0)),
            ],
        ),
        out_shape=[
            shaped((rows, width), LOW),
            shaped((2 * pairs, 2 * rows, rows), LOW),
            shaped((pairs, 2, rows), WIDE),
        ],
        compiler_params=params(),
        cost_estimate=pl.CostEstimate(
            flops=16 * rows * rows * width,
            bytes_accessed=8 * rows * rows * pairs,
            transcendentals=4 * rows * rows * pairs,
        ),
        name="attend",
    )(live, queries, kv_own, kv_own, kv_other, kv_other)


def attend_back_kernel(
    q_ref,
    ko_ref,
    vo_ref,
    kr_ref,
    vr_ref,
    a_ref,
    g_ref,
    p_ref,
    c_ref,
    after_ref,
    dq_ref,
    dkvo_ref,
    dkvr_ref,
):
    rows = q_ref.shape[0]
    lane = lax.broadcasted_iota(jnp.int32, (rows, 128), 1)
    mixed = a_ref[...].astype(WIDE).T
    grad = g_ref[...].astype(WIDE).T
    grad = jnp.concatenate(
        [grad[:HEAD_DIM] * c_ref[0, :1, :], grad[HEAD_DIM:] * c_ref[0, 1:, :]], 0
    )
    inner = grad * mixed
    inner = [column_sums(inner[:HEAD_DIM]), column_sums(inner[HEAD_DIM:])]
    first = lax.broadcasted_iota(jnp.int32, (128, rows), 0) < HEAD_DIM
    low = grad.astype(LOW)
    masked = [
        jnp.where(first, low, jnp.zeros_like(low)),
        jnp.where(first, jnp.zeros_like(low), low),
    ]
    grad_rows = grad.T.astype(LOW)
    queries = q_ref[...]
    parts = [0.0, 0.0]
    for index, (k_ref, v_ref, out_ref) in enumerate(
        ((ko_ref, vo_ref, dkvo_ref), (kr_ref, vr_ref, dkvr_ref))
    ):
        keys = k_ref[...].T
        values = v_ref[...]
        key_grads, val_grads = [], []
        for head in range(2):
            probs = p_ref[head, index * rows : (index + 1) * rows, :]
            wide = dot(values, masked[head]) - inner[head]
            score = (probs.astype(WIDE) * wide).astype(LOW)
            val_grads.append(dot(probs, grad_rows))
            key_grads.append(dot(score, queries))
            parts[head] = parts[head] + dot(keys[head * HEAD_DIM : (head + 1) * HEAD_DIM], score)
        chosen = lane < HEAD_DIM
        out_ref[0] = (jnp.where(chosen, *key_grads) * HEAD_DIM**-0.5).astype(LOW)
        out_ref[1] = jnp.where(chosen, *val_grads).astype(LOW)
    dq_ref[...] = (jnp.concatenate(parts, 0).T * HEAD_DIM**-0.5).astype(LOW)


def attend_back(queries, kv_own, kv_other, attended, grad, probs, inverse, start, count, after):
    rows, width = queries.shape
    pairs = width // 128
    block = lambda shift: pl.BlockSpec((rows, 128), lambda j: (0, shift + j))
    near, far = block(start), block(pairs + start)
    both = pl.BlockSpec((2, rows, 128), lambda j: (0, 0, j))
    return pl.pallas_call(
        attend_back_kernel,
        grid=(count,),
        in_specs=[
            near,
            near,
            far,
            near,
            far,
            near,
            near,
            pl.BlockSpec((2, 2 * rows, rows), lambda j: (start + j, 0, 0)),
            pl.BlockSpec((1, 2, rows), lambda j: (start + j, 0, 0)),
            pl.BlockSpec(memory_space=pl.ANY),
        ],
        out_specs=[block(0), both, both],
        out_shape=[
            shaped((rows, 128 * count), LOW),
            shaped((2, rows, 128 * count), LOW),
            shaped((2, rows, 128 * count), LOW),
        ],
        compiler_params=params(),
        cost_estimate=pl.CostEstimate(
            flops=32 * rows * rows * 128 * count * 2,
            bytes_accessed=8 * rows * rows * count,
            transcendentals=0,
        ),
        name="attend_back",
    )(queries, kv_own, kv_own, kv_other, kv_other, attended, grad, probs, inverse, after)


def ffn_kernel(
    place_ref,
    attended_ref,
    embedded_ref,
    cotangent_ref,
    w_out_ref,
    bias_out_ref,
    gain_ref,
    offset_ref,
    w_up_ref,
    bias_up_ref,
    w_down_ref,
    bias_down_ref,
    output_ref,
    g_residual_ref,
    g_attended_ref,
    up_send_ref,
    up_keep_ref,
    down_send_ref,
    down_keep_ref,
    vectors_ref,
    bias_up_grad_ref,
    residual_ref,
    normed_ref,
    turned_ref,
    total_ref,
    g_normed_ref,
    g_out_ref,
):
    step, steps = pl.program_id(0), pl.num_programs(0)
    rows, width = attended_ref.shape
    tile = w_up_ref.shape[1]
    mine = place_ref[0]
    own, other = half_of(mine, width // 2), half_of(1 - mine, width // 2)
    alive = lax.broadcasted_iota(jnp.int32, (rows, 1), 0) < place_ref[1]

    @pl.when(step == 0)
    def _():
        residual = embedded_ref[...] + (dot(attended_ref[...], w_out_ref[...]) + bias_out_ref[...])
        residual_ref[...] = residual
        unit, _ = normalize(residual)
        normed = unit * gain_ref[...] + offset_ref[...]
        normed_ref[...] = normed.astype(LOW)
        turned_ref[...] = normed.T.astype(LOW)
        g_out_ref[...] = jnp.where(alive, cotangent_ref[...].astype(WIDE), 0.0).astype(LOW)
        total_ref[...] = jnp.zeros_like(total_ref)
        g_normed_ref[...] = jnp.zeros_like(g_normed_ref)

    g_out = g_out_ref[...]
    hidden = dot(normed_ref[...], w_up_ref[...]) + bias_up_ref[...]
    g_act = dot(g_out, w_down_ref[...], 1, 1)
    share = 0.5 * (1.0 + lax.erf(hidden * 0.5**0.5))
    density = jnp.exp(-0.5 * hidden * hidden) * 0.3989422804014327
    activated = (hidden * share).astype(LOW)
    g_wide = g_act * (share + hidden * density)
    g_hidden = g_wide.astype(LOW)
    total_ref[...] += dot(activated, w_down_ref[...])
    g_normed_ref[...] += dot(g_hidden, w_up_ref[...], 1, 1)
    down_send_ref[...] = dot(activated, g_out_ref[:, other], 0, 0).astype(LOW)
    down_keep_ref[...] = dot(activated, g_out_ref[:, own], 0, 0).astype(LOW)
    up = dot(turned_ref[...], g_hidden).astype(LOW)
    bias_up_grad_ref[...] = column_sums(g_hidden.astype(WIDE))
    columns = pl.ds(pl.multiple_of(lax.rem(step, steps // 2) * tile, 128), tile)

    @pl.when(step < steps // 2)
    def _():
        up_send_ref[:, columns] = up

    @pl.when(step >= steps // 2)
    def _():
        up_keep_ref[:, columns] = up

    @pl.when(step == steps - 1)
    def _():
        residual = residual_ref[...]
        final = residual + (total_ref[...] + bias_down_ref[...])
        output_ref[...] = jnp.where(alive, final, 0.0).astype(LOW)
        unit, scale = normalize(residual)
        g_final = g_out_ref[...].astype(WIDE)
        g_normed = g_normed_ref[...]
        g_residual = g_final + norm_back(g_normed, unit, scale, gain_ref[...])
        g_residual_ref[...] = g_residual
        g_branch = g_residual.astype(LOW)
        g_attended_ref[...] = dot(g_branch, w_out_ref[...], 1, 1).astype(LOW)
        vectors_ref[...] = jnp.concatenate(
            [
                column_sums(g_branch.astype(WIDE)),
                column_sums(g_normed * unit),
                column_sums(g_normed),
                column_sums(g_final),
            ],
            0,
        )
        normed_ref[...] = g_branch
        attended = attended_ref[...].astype(WIDE).T.astype(LOW)
        half = width // 2
        last = up_send_ref.shape[1] - half
        up_send_ref[:, last:] = dot(attended, normed_ref[:, other]).astype(LOW)
        up_keep_ref[:, last:] = dot(attended, normed_ref[:, own]).astype(LOW)


def feed_forward(
    place,
    attended,
    embedded,
    cotangent,
    w_out,
    bias_out,
    gain,
    offset,
    w_up,
    bias_up,
    w_down,
    bias_down,
):
    rows, width = attended.shape
    units = w_up.shape[1]
    tile = 768
    steps = units // tile
    turn = lambda j, place: lax.rem(j + (1 - place[0]) * (steps // 2), steps)
    down_tile = pl.BlockSpec((tile, width // 2), lambda j, place: (turn(j, place), 0))
    merged = units // 2 + width // 2
    return pl.pallas_call(
        ffn_kernel,
        grid_spec=pltpu.PrefetchScalarGridSpec(
            num_scalar_prefetch=1,
            grid=(steps,),
            in_specs=[
                whole((rows, width)),
                whole((rows, width)),
                whole((rows, width)),
                whole((width, width)),
                whole((1, width)),
                whole((1, width)),
                whole((1, width)),
                pl.BlockSpec((width, tile), lambda j, place: (0, turn(j, place))),
                pl.BlockSpec((1, tile), lambda j, place: (0, turn(j, place))),
                pl.BlockSpec((tile, width), lambda j, place: (turn(j, place), 0)),
                whole((1, width)),
            ],
            out_specs=[
                whole((rows, width)),
                whole((rows, width)),
                whole((rows, width)),
                whole((width, merged)),
                whole((width, merged)),
                down_tile,
                down_tile,
                whole((4, width)),
                pl.BlockSpec((1, tile), lambda j, place: (0, turn(j, place))),
            ],
            scratch_shapes=[
                pltpu.VMEM((rows, width), WIDE),
                pltpu.VMEM((rows, width), LOW),
                pltpu.VMEM((width, rows), LOW),
                pltpu.VMEM((rows, width), WIDE),
                pltpu.VMEM((rows, width), WIDE),
                pltpu.VMEM((rows, width), LOW),
            ],
        ),
        out_shape=[
            shaped((rows, width), LOW),
            shaped((rows, width), WIDE),
            shaped((rows, width), LOW),
            shaped((width, merged), LOW),
            shaped((width, merged), LOW),
            shaped((units, width // 2), LOW),
            shaped((units, width // 2), LOW),
            shaped((4, width), WIDE),
            shaped((1, units), WIDE),
        ],
        compiler_params=params(),
        cost_estimate=pl.CostEstimate(
            flops=12 * rows * width * units + 6 * rows * width * width,
            bytes_accessed=8 * width * units,
            transcendentals=2 * rows * units,
        ),
        name="feed_forward",
    )(
        place,
        attended,
        embedded,
        cotangent,
        w_out,
        bias_out,
        gain,
        offset,
        w_up,
        bias_up,
        w_down,
        bias_down,
    )


def project_back(place_ref, normed_turned, dq_ref, own_ref, got_ref, weights, joined_ref, send_ref, keep_ref, bias_ref):
    group = dq_ref.shape[1]
    half = 3 * group // 2
    mine = place_ref[0]
    joined_ref[:, :group] = dq_ref[...]
    for index in range(2):
        total = own_ref[index].astype(WIDE) + got_ref[index].astype(WIDE)
        joined_ref[:, (1 + index) * group : (2 + index) * group] = total.astype(LOW)
    send_ref[:, :half] = dot(normed_turned, joined_ref[:, half_of(1 - mine, half)]).astype(LOW)
    keep_ref[:, :half] = dot(normed_turned, joined_ref[:, half_of(mine, half)]).astype(LOW)
    bias_ref[0:1] = column_sums(joined_ref[:, :group].astype(WIDE))
    bias_ref[1:2] = column_sums(joined_ref[:, 2 * group :].astype(WIDE))
    back = 0.0
    for index, weight_ref in enumerate(weights):
        part = joined_ref[:, index * group : (index + 1) * group]
        back = back + dot(part, weight_ref[...], 1, 1)
    return back


def first_back_kernel(
    place_ref,
    normed_ref,
    dq_ref,
    own_ref,
    got_ref,
    wq_ref,
    wk_ref,
    wv_ref,
    send_ref,
    keep_ref,
    bias_ref,
    part_ref,
    turned_ref,
    joined_ref,
):
    @pl.when(pl.program_id(0) == 0)
    def _():
        turned_ref[...] = normed_ref[...].astype(WIDE).T.astype(LOW)
        part_ref[...] = jnp.zeros_like(part_ref)

    part_ref[...] += project_back(
        place_ref,
        turned_ref[...],
        dq_ref,
        own_ref,
        got_ref,
        (wq_ref, wk_ref, wv_ref),
        joined_ref,
        send_ref,
        keep_ref,
        bias_ref,
    )


def last_back_kernel(
    place_ref,
    normed_ref,
    dq_ref,
    own_ref,
    got_ref,
    wq_ref,
    wk_ref,
    wv_ref,
    part_ref,
    embedded_ref,
    g_residual_ref,
    gain_ref,
    prior_ref,
    expression_ref,
    bias_first_ref,
    vectors_ref,
    bias_up_ref,
    send_ref,
    keep_ref,
    g_low_ref,
    rows_ref,
    turned_ref,
    joined_ref,
    bias_ref,
):
    rows, width = normed_ref.shape
    half = width // 2
    mine = place_ref[0]
    turned_ref[...] = normed_ref[...].astype(WIDE).T.astype(LOW)
    back = part_ref[...] + project_back(
        place_ref,
        turned_ref[...],
        dq_ref,
        own_ref,
        got_ref,
        (wq_ref, wk_ref, wv_ref),
        joined_ref,
        send_ref,
        keep_ref,
        bias_ref,
    )
    unit, scale = normalize(embedded_ref[...])
    g_embedded = g_residual_ref[...] + norm_back(back, unit, scale, gain_ref[...])
    g_low_ref[...] = g_embedded.astype(LOW)
    prior = prior_ref[...].astype(WIDE).T.astype(LOW)
    send_ref[:, half:] = dot(prior, g_low_ref[:, half_of(1 - mine, half)]).astype(LOW)
    keep_ref[:, half:] = dot(prior, g_low_ref[:, half_of(mine, half)]).astype(LOW)
    expression = jnp.broadcast_to(expression_ref[...], (8, rows)).T[:, :1]
    total = column_sums(g_embedded)
    groups = rows_ref.shape[0] - 16
    hot = lax.broadcasted_iota(jnp.int32, (groups, width), 0) == place_ref[1]
    rows_ref[:groups] = jnp.where(hot, total, 0.0)
    rows_ref[groups:] = jnp.concatenate(
        [
            column_sums(expression * g_embedded),
            column_sums(back * unit),
            column_sums(back),
            jnp.concatenate([bias_first_ref[0, 0:1], bias_first_ref[1, 0:1], bias_ref[0:1]], 1),
            jnp.concatenate([bias_first_ref[0, 1:2], bias_first_ref[1, 1:2], bias_ref[1:2]], 1),
            vectors_ref[...],
            bias_up_ref[...],
            jnp.zeros((3, width), WIDE),
        ],
        0,
    )


def back_specs(rows, width, group, first):
    third = width // group
    weight = lambda part: pl.BlockSpec((width, group), lambda j, _: (0, part * third + first + j))
    both = pl.BlockSpec((2, rows, group), lambda j, _: (0, 0, j))
    return [
        whole((rows, width)),
        pl.BlockSpec((rows, group), lambda j, _: (0, j)),
        both,
        both,
        weight(0),
        weight(1),
        weight(2),
    ]


def first_back(place, normed, dq, own, got, w_qkv, group):
    rows, width = normed.shape
    count = dq.shape[1] // group
    half = 3 * group // 2
    tile = pl.BlockSpec((width, half), lambda j, _: (0, j))
    return pl.pallas_call(
        first_back_kernel,
        grid_spec=pltpu.PrefetchScalarGridSpec(
            num_scalar_prefetch=1,
            grid=(count,),
            in_specs=back_specs(rows, width, group, 0),
            out_specs=[
                tile,
                tile,
                pl.BlockSpec((None, 2, group), lambda j, _: (j, 0, 0)),
                whole((rows, width)),
            ],
            scratch_shapes=[
                pltpu.VMEM((width, rows), LOW),
                pltpu.VMEM((rows, 3 * group), LOW),
            ],
        ),
        out_shape=[
            shaped((width, count * half), LOW),
            shaped((width, count * half), LOW),
            shaped((count, 2, group), WIDE),
            shaped((rows, width), WIDE),
        ],
        compiler_params=params(),
        cost_estimate=pl.CostEstimate(
            flops=12 * rows * width * group * count,
            bytes_accessed=16 * width * width,
            transcendentals=0,
        ),
        name="first_back",
    )(place, normed, dq, own, got, w_qkv, w_qkv, w_qkv)


def last_back(
    place,
    normed,
    dq,
    own,
    got,
    w_qkv,
    group,
    part,
    embedded,
    g_residual,
    gain,
    prior,
    expression,
    bias_first,
    vectors,
    bias_up,
    groups,
):
    rows, width = normed.shape
    half = width // 2
    first = width // group - 1
    return pl.pallas_call(
        last_back_kernel,
        grid_spec=pltpu.PrefetchScalarGridSpec(
            num_scalar_prefetch=1,
            grid=(1,),
            in_specs=back_specs(rows, width, group, first)
            + [
                whole((rows, width)),
                whole((rows, width)),
                whole((rows, width)),
                whole((1, width)),
                whole((rows, width)),
                whole((1, rows)),
                whole(bias_first.shape),
                whole((4, width)),
                whole((4, width)),
            ],
            out_specs=[
                whole((width, width)),
                whole((width, width)),
                whole((rows, width)),
                whole((groups + 16, width)),
            ],
            scratch_shapes=[
                pltpu.VMEM((width, rows), LOW),
                pltpu.VMEM((rows, 3 * group), LOW),
                pltpu.VMEM((2, group), WIDE),
            ],
        ),
        out_shape=[
            shaped((width, width), LOW),
            shaped((width, width), LOW),
            shaped((rows, width), LOW),
            shaped((groups + 16, width), WIDE),
        ],
        compiler_params=params(),
        name="last_back",
    )(
        place,
        normed,
        dq,
        own,
        got,
        w_qkv,
        w_qkv,
        w_qkv,
        part,
        embedded,
        g_residual,
        gain,
        prior,
        expression,
        bias_first,
        vectors,
        bias_up,
    )


def gene_kernel(slots_ref, ids_ref, grad_ref, out_ref):
    slots = slots_ref[...]
    rows = grad_ref.shape[0]
    picker = jnp.where(slots == jnp.broadcast_to(ids_ref[...], (slots.shape[0], rows)), 1.0, 0.0)
    out_ref[...] = dot(picker.astype(LOW), grad_ref[...]).astype(LOW)


def gene_rows(slots, ids, grad):
    count = slots.shape[0]
    rows, width = grad.shape
    tile = min(count, 1152)
    return pl.pallas_call(
        gene_kernel,
        grid=(count // tile,),
        in_specs=[
            pl.BlockSpec((tile, 1), lambda j: (j, 0)),
            whole((1, rows)),
            whole((rows, width)),
        ],
        out_specs=pl.BlockSpec((tile, width), lambda j: (j, 0)),
        out_shape=shaped((count, width), LOW),
        compiler_params=params(),
        cost_estimate=pl.CostEstimate(
            flops=2 * rows * width * count, bytes_accessed=2 * width * count, transcendentals=0
        ),
        name="gene_rows",
    )(slots, ids, grad)


def swap_cores(array):
    return lax.ppermute(array, "blk", [(0, 1), (1, 0)])


def bits_apart(array, mask):
    count = lax.axis_size("dp")
    return lax.ppermute(array, "dp", [(i, i ^ mask) for i in range(count)])


def pick(array, position, index):
    return lax.dynamic_index_in_dim(array, index, position, keepdims=False)


def total(terms):
    wide = terms[0].astype(WIDE)
    for term in terms[1:]:
        wide = wide + term.astype(WIDE)
    return wide


class Share:
    def __init__(self, terms, turn, wire=LOW):
        count = lax.axis_size("dp")
        bits = count.bit_length() - 1
        self.me = lax.axis_index("dp")
        self.wire = wire
        self.terms = [term.reshape((2,) * bits + term.shape[1:]) for term in terms]
        self.left = list(range(bits - 1, -1, -1))
        order = list(range(bits - 2))
        self.order = order[1::-1] + order[2:] if turn else order

    def halve(self):
        bit = self.order.pop(0)
        mine = (self.me >> bit) & 1
        position = self.left.index(bit)
        sent = total([pick(term, position, 1 - mine) for term in self.terms]).astype(self.wire)
        got = bits_apart(sent, 1 << bit)
        self.terms = [pick(term, position, mine) for term in self.terms] + [got]
        self.left.remove(bit)
        return sent

    def finish(self):
        while self.order:
            self.halve()
        low, high = self.left[1], self.left[0]
        mine_low, mine_high = (self.me >> low) & 1, (self.me >> high) & 1
        arrived = []
        for step in (1, 2, 3):
            to_low, to_high = mine_low ^ (step & 1), mine_high ^ (step >> 1)
            sent = total([pick(pick(term, 0, to_high), 0, to_low) for term in self.terms])
            mask = ((step & 1) << low) | ((step >> 1) << high)
            arrived.append(bits_apart(sent.astype(self.wire), mask))
        own = [pick(pick(term, 0, mine_high), 0, mine_low) for term in self.terms]
        return total(own + arrived)


def both_halves(own, block_index):
    other = swap_cores(own)
    return (
        jnp.where(block_index == 0, own, other),
        jnp.where(block_index == 0, other, own),
    )


def body(
    gene_ids,
    values,
    knowledge,
    lengths,
    groups,
    gene_table,
    group_table,
    w_know,
    w_value,
    norm1_gain,
    norm1_bias,
    w_qkv,
    bias_q,
    bias_v,
    w_out,
    bias_out,
    norm2_gain,
    norm2_bias,
    w_up,
    bias_up,
    w_down,
    bias_down,
    cotangent,
):
    width = w_out.shape[0]
    units = w_up.shape[1]
    rows = gene_ids.shape[1]
    count = lax.axis_size("dp")
    mine = lax.axis_index("blk")
    length, group = lengths[0], groups[0]
    prior = knowledge[0]
    row = lambda vector: vector.reshape(1, -1)
    live_own = length - mine * rows
    live_other = length - (1 - mine) * rows
    group_row = group_table[group].astype(WIDE)[None]
    if gene_table.shape[0] > 8 * rows:
        table = gene_table[gene_ids[0]]
    else:
        table = gene_table
    embedded, normed, kv_own = embed(
        gene_ids,
        values,
        prior,
        table,
        group_row,
        w_know,
        row(w_value),
        row(norm1_gain),
        row(norm1_bias),
        w_qkv,
        row(bias_v),
    )
    kv_other = swap_cores(kv_own)
    queries = project_queries(normed, w_qkv, row(bias_q))
    attended, probs, inverse = attend(
        jnp.stack([live_own, live_other]).astype(jnp.int32), queries, kv_own, kv_other
    )
    (
        block_output,
        g_residual,
        g_attended,
        up_send,
        up_keep,
        down_send,
        down_keep,
        vectors,
        bias_up_grad,
    ) = feed_forward(
        jnp.stack([mine, live_own]).astype(jnp.int32),
        attended,
        embedded,
        cotangent[0],
        w_out,
        row(bias_out),
        row(norm2_gain),
        row(norm2_bias),
        w_up,
        row(bias_up),
        w_down,
        row(bias_down),
    )

    owners = lambda array: array.reshape(count, -1, array.shape[-1])
    down = Share([owners(down_keep), owners(swap_cores(down_send))], 0)
    up = Share([owners(up_keep), owners(swap_cores(up_send))], 1)
    dq1, own1, other1 = attend_back(
        queries, kv_own, kv_other, attended, g_attended, probs, inverse, 0, 4, g_attended
    )
    got1 = swap_cores(other1)
    down.halve()
    after = up.halve()
    dq2, own2, other2 = attend_back(
        queries, kv_own, kv_other, attended, g_attended, probs, inverse, 4, 2, after
    )
    got2 = swap_cores(other2)
    place = jnp.stack([mine, group]).astype(jnp.int32)
    qkv_send, qkv_keep, bias_first, part = first_back(
        place, normed, dq1, own1, got1, w_qkv, 256
    )
    tail_send, tail_keep, g_low, sums = last_back(
        place,
        normed,
        dq2,
        own2,
        got2,
        w_qkv,
        256,
        part,
        embedded,
        g_residual,
        row(norm1_gain),
        prior,
        values,
        bias_first,
        vectors,
        bias_up_grad.reshape(count, 4, -1).swapaxes(0, 1).reshape(4, width),
        group_table.shape[0],
    )
    slot = jnp.arange(count * VOC_DEV, dtype=jnp.int32)[:, None]
    slot = slot + slot // VOC_DEV * VOC_DEV
    gene_send = gene_rows(slot + (1 - mine) * VOC_DEV, gene_ids, g_low)
    gene_got = swap_cores(gene_send)
    gene_keep = gene_rows(slot + mine * VOC_DEV, gene_ids, g_low)
    qkv = Share([owners(qkv_keep), owners(swap_cores(qkv_send))], 0)
    tail = Share([owners(tail_keep), owners(swap_cores(tail_send))], 1)
    half = width // 2
    gene_terms = [owners(gene_keep), owners(gene_got)]
    gene_left = Share([term[..., :half] for term in gene_terms], 0)
    gene_right = Share([term[..., half:] for term in gene_terms], 1)

    sums = sums.reshape(-1, count, width // count).swapaxes(0, 1).reshape(count, 2, -1)
    small = Share([pick(sums, 1, mine), swap_cores(pick(sums, 1, 1 - mine))], 0, WIDE)

    down_halves = both_halves(down.finish(), mine)
    up_halves = both_halves(up.finish(), mine)
    qkv_halves = both_halves(qkv.finish(), mine)
    gene_grad = jnp.concatenate([gene_left.finish(), gene_right.finish()], 1)
    tail_halves = both_halves(tail.finish(), mine)
    small = jnp.concatenate(both_halves(small.finish(), mine)).reshape(-1, width // count)
    join = lambda pieces: jnp.concatenate(pieces, 1)
    q_parts, k_parts, v_parts = [], [], []
    cut = 384
    for index in range(3):
        if index < 2:
            low, high = [side[:, index * cut : (index + 1) * cut] for side in qkv_halves]
        else:
            low, high = [side[:, :cut] for side in tail_halves]
        q_parts.append(low[:, :256])
        k_parts += [low[:, 256:], high[:, :128]]
        v_parts.append(high[:, 128:])
    extra = small[group_table.shape[0] :]
    return (
        block_output[None],
        gene_grad,
        small[: group_table.shape[0]],
        join([side[:, cut:] for side in tail_halves]),
        extra[0],
        extra[1],
        extra[2],
        join(q_parts + k_parts + v_parts),
        extra[3],
        extra[4],
        join([side[:, units // 2 :] for side in up_halves]),
        extra[5],
        extra[6],
        extra[7],
        join([side[:, : units // 2] for side in up_halves]),
        extra[9:13].reshape(-1),
        join(down_halves),
        extra[8],
    )


def solution(mesh):
    in_specs = (
        P("dp", "blk"),
        P("dp", "blk"),
        P("dp", "blk", None),
        P("dp"),
        P("dp"),
        P(),
        P(),
        P(),
        P(),
        P(),
        P(),
        P(),
        P(),
        P(),
        P(),
        P(),
        P(),
        P(),
        P(),
        P(),
        P(),
        P(),
        P("dp", "blk", None),
    )
    out_specs = (
        P("dp", "blk", None),
        P(("dp", "blk"), None),
        P(None, "dp"),
        P("dp", None),
        P("dp"),
        P("dp"),
        P("dp"),
        P("dp", None),
        P("dp"),
        P("dp"),
        P("dp", None),
        P("dp"),
        P("dp"),
        P("dp"),
        P("dp", None),
        P("dp"),
        P("dp", None),
        P("dp"),
    )
    return jax.shard_map(body, mesh=mesh, in_specs=in_specs, out_specs=out_specs, check_vma=False)
```

time: 1250 us -> 296 us (0.24)
  waiting for transfers between devices: 868 us -> 77.5 us
  matrix products: 166 us -> 0 us
  Pallas kernels: 0 us -> 99.7 us
  blocking collectives: 80.8 us -> 0 us
  starting transfers between devices: 1.05 us -> 53.9 us
  other arithmetic: 66.4 us -> 34.1 us
  local copies, waits for them, and re-layouts: 45.9 us -> 23.2 us
  between operations: 17.8 us -> 2.87 us
    reduce_scatter x8 -> x0, waiting for transfers between devices: 725 us -> none  [the longest x1 175 us: body(): lax.psum_scatter(w_down_grad, 'dp', scatter_dimension=0, tiled=True)]
    dot_general x21 -> x0, matrix products: 166 us -> none  [the longest x5 30.5 us: contract_rows(): lax.dot_general(left, right, (((0,), (0,)), ((), ())), preferred_element_...]
    unnamed x13 -> x0, waiting for transfers between devices: 132 us -> none
    pallas_call x0 -> x10, Pallas kernels: none -> 99.7 us  [the longest x1 28.7 us: feed_forward(): pl.pallas_call(ffn_kernel, grid_spec=pltpu.PrefetchScalarGridSpec(num_sca...]
    ppermute x0 -> x49, waiting for transfers between devices: none -> 77.5 us  [the longest x35 70.3 us: bits_apart(): return lax.ppermute(array, 'dp', [(i, i ^ mask) for i in range(count)])]
    unnamed x1 -> x0, blocking collectives: 76.1 us -> none
    ppermute x0 -> x49, starting transfers between devices: none -> 53.9 us  [the longest x35 50.9 us: bits_apart(): return lax.ppermute(array, 'dp', [(i, i ^ mask) for i in range(count)])]
    convert_element_type x24 -> x19, other arithmetic: 47.8 us -> 22.1 us  [the longest x12 15.4 us: halve(): total([pick(term, position, 1 - mine) for term in self.terms])]
  transfers between devices with their start and end apart: 12 -> 49, of which waited for: 9 -> 20; matrix products, arithmetic and copies ran while one was open for 15% -> 17% of each run, Pallas kernels for 0% -> 10%
where the time goes in v1:
time: 296 us; the launch traced here: 291 us
  Pallas kernels  99.7 us (34%)
  waiting for transfers between devices  77.5 us (26%)
  starting transfers between devices  53.9 us (18%)
  other arithmetic  34.1 us (12%)
  local copies, waits for them, and re-layouts  23.2 us (8%)
    ppermute x35, waiting for transfers between devices, bits_apart(): return lax.ppermute(array, 'dp', [(i, i ^ mask) for i in range(count)])  70.3 us
    ppermute x35, starting transfers between devices, bits_apart(): return lax.ppermute(array, 'dp', [(i, i ^ mask) for i in range(count)])  50.9 us
    pallas_call x1, Pallas kernels, feed_forward(): pl.pallas_call(ffn_kernel, grid_spec=pltpu.PrefetchScalarGridSpec(num_sca...  28.7 us
    pallas_call x2, Pallas kernels, attend_back(): pl.pallas_call(attend_back_kernel, grid=(count,), in_specs=[near, near, f...  20 us
    pallas_call x1, Pallas kernels, attend(): pl.pallas_call(attend_kernel, grid_spec=pltpu.PrefetchScalarGridSpec(num_...  17.7 us
    convert_element_type x12, other arithmetic, halve(): total([pick(term, position, 1 - mine) for term in self.terms])  15.4 us
    unnamed x60, local copies, waits for them, and re-layouts  14.3 us
    pallas_call x1, Pallas kernels, embed(): pl.pallas_call(embed_kernel, grid=(1,), in_specs=[whole((1, rows)), whole...  10.4 us
  transfers between devices with their start and end apart: 49, of which 20 were waited for; matrix products, arithmetic and copies ran while one was open for 17% of the time, Pallas kernels for 10%

profile of v1, /device:TPU:0, one launch (start us, length us, event | category | flops | bytes accessed | tf_op | source)
XLA Modules:
  0.0 291.2 jit_solution(13494512841090293948)
XLA Ops:
  7.3 10.4 %embed.1 = (f32[512,768]{1,0:T(8,128)}, bf16[512,768]{1,0:T(8,128)(2,1)S(1)}, bf16[512,1536]{1,0:T(8,128)(2,1)}) custom-call(s32[1,512]{1,0:T(1,128)S(1)} %copy-done.7, f32[1,512]{1,0:T(1,128)S(1)} %copy-done.5, bf16[512,768]{1,0:T(8,128)(2,1)S(1)} %bitcast.291, bf16[2304,768]{1,0:T(8,128)(2,1)} %table_ref.1, f32[1,768]{1,0:T(1,128)S(1)} %fusion.69.group_ref, ...), custom_call_target="tpu_custom_call" | custom-call | tf_op jit(solution)/shard_map/embed/pallas_call | solution.py:98
  18.9 2.1 queries.1.q_ref
  21.5 17.7 %attend.1 = (bf16[512,768]{1,0:T(8,128)(2,1)S(1)}, bf16[12,1024,512]{2,1,0:T(8,128)(2,1)}, f32[6,2,512]{2,1,0:T(2,128)S(1)}) custom-call(s32[2]{0:T(128)S(1)} %get-tuple-element.150.live_ref, bf16[512,768]{1,0:T(8,128)(2,1)S(1)} %queries.1.q_ref, bf16[512,1536]{1,0:T(8,128)(2,1)} %get-tuple-element.48.ko_ref.vo_ref, ...), custom_call_target="tpu_custom_call" | custom-call | flops 3221225472 | bytes 12582912 | tf_op jit(solution)/shard_map/attend/pallas_call | solution.py:180
  39.2 28.7 %feed_forward.1 = (bf16[512,768]{1,0:T(8,128)(2,1)}, f32[512,768]{1,0:T(8,128)}, bf16[512,768]{1,0:T(8,128)(2,1)S(1)}, bf16[768,1920]{1,0:T(8,128)(2,1)}, bf16[7...) custom-call(s32[2]{0:T(128)S(1)} %get-tuple-element.149.place_ref, ...), custom_call_target="tpu_custom_call" | custom-call | flops 16307453952 | bytes 18874368 | tf_op jit(solution)/shard_map/feed_forward/pallas_call | solution.py:418
  68.9 12.6 %attend_back.3 = (bf16[512,512]{1,0:T(8,128)(2,1)S(1)}, bf16[2,512,512]{2,1,0:T(8,128)(2,1)}, bf16[2,512,512]{2,1,0:T(8,128)(2,1)}) custom-call(bf16[512,768]{1,0:T(8,128)(2,1)S(1)} %queries.1.q_ref, bf16[512,1536]{1,0:T(8,128)(2,1)} %get-tuple-element.48.ko_ref.vo_ref, bf16[512,1536]{1,0:T(8,128)(2,1)} %get-tuple-element.48.ko_ref.vo_ref, ...), custom_call_target="tpu_custom_call" | custom-call | flops 8589934592 | bytes 8388608 | tf_op jit(solution)/shard_map/attend_back/pallas_call | solution.py:265
  82.1 2.4 collective-permute-done.3.got_ref
  85.5 7.4 %first_back.1 = (bf16[768,768]{1,0:T(8,128)(2,1)}, bf16[768,768]{1,0:T(8,128)(2,1)}, f32[2,2,256]{2,1,0:T(2,128)S(1)}, f32[512,768]{1,0:T(8,128)}) custom-call(s32[2]{0:T(128)S(1)} %pad_add_fusion.2.place_ref, bf16[512,768]{1,0:T(8,128)(2,1)S(1)} %get-tuple-element.47.normed_ref, bf16[512,512]{1,0:T(8,128)(2,1)S(1)} %get-tuple-element.60.dq_ref, ...), custom_call_target="tpu_custom_call" | custom-call | flops 2415919104 | bytes 9437184 | tf_op jit(solution)/shard_map/first_back/pallas_call | solution.py:632
  93.5 2.7 collective-permute-done.29
  97.6 2.9 %collective-permute-start.30 = (bf16[2,2,2,48,768]{4,3,2,1,0:T(8,128)(2,1)S(1)}, bf16[2,2,2,48,768]{4,3,2,1,0:T(8,128)(2,1)S(1)}, u32[]{:S(2)}, u32[]{:S(2)}) collective-permute-start(bf16[2,2,2,48,768]{4,3,2,1,0:T(8,128)(2,1)S(1)} %fusion.6), channel_id=1, source_target_pairs={{0,2},{2,0},{4,6},{6,4},{8,10},{10,8},{12,14},{14,12},{16,18},{18,... | collective-permute-start | bytes 1769480 | tf_op jit(solution)/shard_map/ppermute | solution.py:780
  100.5 13.7 %collective-permute-done.30 = bf16[2,2,2,48,768]{4,3,2,1,0:T(8,128)(2,1)S(1)} collective-permute-done((bf16[2,2,2,48,768]{4,3,2,1,0:T(8,128)(2,1)S(1)}, bf16[2,2,2,48,768]{4,3,2,1,0:T(8,128)(2,1)S(1)}, u32[]{:S(2)}, u32[]{:S(2)}) %collective-permute-start.30) | collective-permute-done | bytes 589856 | tf_op jit(solution)/shard_map/ppermute | solution.py:780
  115.3 1.8 collective-permute-start.31
  118.8 5.2 %collective-permute-done.31 = bf16[2,2,48,768]{3,2,1,0:T(8,128)(2,1)} collective-permute-done((bf16[2,2,48,768]{3,2,1,0:T(8,128)(2,1)S(1)}, bf16[2,2,48,768]{3,2,1,0:T(8,128)(2,1)}, u32[]{:S(2)}, u32[]{:S(2)}) %collective-permute-start.31) | collective-permute-done | bytes 294944 | tf_op jit(solution)/shard_map/ppermute | solution.py:780
  126.7 2.7 collective-permute-start.33
  129.7 3.3 %fusion.after_ref = bf16[2,2,2,48,1920]{4,3,2,1,0:T(8,128)(2,1)} fusion(bf16[2,2,2,2,48,1920]{5,4,3,2,1,0:T(8,128)(2,1)} %bitcast.10, s32[]{:T(128)S(6)} %select_n.435, bf16[2,2,2,2,48,1920]{5,4,3,2,1,0:T(8,128)(2,1)} %bitcast.309), kind=kLoop, calls=%fused_computation.2 | loop fusion | flops 2949120 | bytes 4423684 | tf_op jit(solution)/shard_map/convert_element_type | solution.py:809
  133.5 2.0 collective-permute-done.34
  136.6 7.4 %attend_back.2 = (bf16[512,256]{1,0:T(8,128)(2,1)S(1)}, bf16[2,512,256]{2,1,0:T(8,128)(2,1)S(1)}, bf16[2,512,256]{2,1,0:T(8,128)(2,1)S(1)}) custom-call(bf16[512,768]{1,0:T(8,128)(2,1)} %copy-done.1, bf16[512,1536]{1,0:T(8,128)(2,1)} %get-tuple-element.48.ko_ref.vo_ref, bf16[512,1536]{1,0:T(8,128)(2,1)} %get-tuple-element.48.ko_ref.vo_ref, ...), custom_call_target="tpu_custom_call" | custom-call | flops 4294967296 | bytes 4194304 | tf_op jit(solution)/shard_map/attend_back/pallas_call | solution.py:265
  144.4 2.6 fusion.2
  148.4 1.6 collective-permute-start.36
  151.4 8.7 %last_back.1 = (bf16[768,768]{1,0:T(8,128)(2,1)}, bf16[768,768]{1,0:T(8,128)(2,1)}, bf16[512,768]{1,0:T(8,128)(2,1)}, f32[80,768]{1,0:T(8,128)S(1)}) custom-call(s32[2]{0:T(128)S(1)} %pad_add_fusion.2.place_ref, bf16[512,768]{1,0:T(8,128)(2,1)} %copy-done, bf16[512,256]{1,0:T(8,128)(2,1)S(1)} %get-tuple-element.57.dq_ref, ...), custom_call_target="tpu_custom_call" | custom-call | tf_op jit(solution)/shard_map/last_back/pallas_call | solution.py:687
  162.9 2.3 gene_rows.3
  166.1 10.5 %collective-permute-done.16 = f32[2,2,2,1920]{3,2,1,0:T(2,128)S(1)} collective-permute-done((f32[2,2,2,1920]{3,2,1,0:T(2,128)S(1)}, f32[2,2,2,1920]{3,2,1,0:T(2,128)S(1)}, u32[]{:S(2)}, u32[]{:S(2)}) %collective-permute-start.16) | collective-permute-done | bytes 61472 | tf_op jit(solution)/shard_map/ppermute | solution.py:780
  176.6 1.6 collective-permute-start.17
  178.2 2.4 gene_rows.2
  180.8 2.5 collective-permute-done.17
  183.6 1.6 collective-permute-start.19
  185.2 2.7 collective-permute-start.20
  187.9 2.5 fusion.3
  190.4 1.7 collective-permute-start.44
  192.5 1.6 collective-permute-done.21
  198.9 7.5 %collective-permute-done.44 = bf16[2,2,192,384]{3,2,1,0:T(8,128)(2,1)} collective-permute-done((bf16[2,2,192,384]{3,2,1,0:T(8,128)(2,1)}, bf16[2,2,192,384]{3,2,1,0:T(8,128)(2,1)}, u32[]{:S(2)}, u32[]{:S(2)}) %collective-permute-start.44) | collective-permute-done | bytes 589856 | tf_op jit(solution)/shard_map/ppermute | solution.py:780
  206.5 1.7 fusion.24
  208.3 1.7 collective-permute-start.46
  210.0 2.7 collective-permute-start.47
  212.7 1.8 fusion.1
  216.1 6.2 %collective-permute-done.46 = bf16[192,384]{1,0:T(8,128)(2,1)S(1)} collective-permute-done((bf16[192,384]{1,0:T(8,128)(2,1)S(1)}, bf16[192,384]{1,0:T(8,128)(2,1)S(1)}, u32[]{:S(2)}, u32[]{:S(2)}) %collective-permute-start.46) | collective-permute-done | bytes 147488 | tf_op jit(solution)/shard_map/ppermute | solution.py:780
  225.4 1.7 collective-permute-start.23
  228.0 4.8 %collective-permute-done.37 = bf16[2,2,48,1920]{3,2,1,0:T(8,128)(2,1)S(1)} collective-permute-done((bf16[2,2,48,1920]{3,2,1,0:T(8,128)(2,1)S(1)}, bf16[2,2,48,1920]{3,2,1,0:T(8,128)(2,1)S(1)}, u32[]{:S(2)}, u32[]{:S(2)}) %collective-permute-start.37) | collective-permute-done | bytes 737312 | tf_op jit(solution)/shard_map/ppermute | solution.py:780
  232.8 1.8 fusion.18
  236.2 2.8 collective-permute-start.40
  239.1 2.2 collective-permute-done.23
  243.3 1.7 collective-permute-start.5
  245.2 7.1 %collective-permute-done.24 = bf16[2,2,48,768]{3,2,1,0:T(8,128)(2,1)S(1)} collective-permute-done((bf16[2,2,48,768]{3,2,1,0:T(8,128)(2,1)S(1)}, bf16[2,2,48,768]{3,2,1,0:T(8,128)(2,1)S(1)}, u32[]{:S(2)}, u32[]{:S(2)}) %collective-permute-start.24) | collective-permute-done | bytes 294944 | tf_op jit(solution)/shard_map/ppermute | solution.py:780
  252.3 1.6 collective-permute-start.10
  255.0 2.6 collective-permute-start.25
  257.6 2.4 collective-permute-start.27
  261.4 2.5 collective-permute-done.26
  281.6 2.5 collective-permute-start.13
  286.2 3.2 %collective-permute-done.13 = bf16[72,384]{1,0:T(8,128)(2,1)S(1)} collective-permute-done((bf16[72,384]{1,0:T(8,128)(2,1)S(1)}, bf16[72,384]{1,0:T(8,128)(2,1)S(1)}, u32[]{:S(2)}, u32[]{:S(2)}) %collective-permute-start.13) | collective-permute-done | bytes 55328 | tf_op jit(solution)/shard_map/ppermute | solution.py:780
  (204 shorter events, 64.4 us)
Async XLA Ops:
  17.7 3.8 %collective-permute-start = (bf16[512,1536]{1,0:T(8,128)(2,1)}, bf16[512,1536]{1,0:T(8,128)(2,1)}, u32[]{:S(2)}, u32[]{:S(2)}) collective-permute-start(bf16[512,1536]{1,0:T(8,128)(2,1)} %get-tuple-element.48.ko_ref.vo_ref), channel_id=1, source_target_pairs={{0,1},{1,0},{2,3},{3,2},{4,5},{5,4},{6,7},{7,6},{8,9},{9,8},{10,11... | collective-permute-start | bytes 4718600 | tf_op jit(solution)/shard_map/ppermute | solution.py:775
  81.5 3.0 %collective-permute-start.3 = (bf16[2,512,512]{2,1,0:T(8,128)(2,1)}, bf16[2,512,512]{2,1,0:T(8,128)(2,1)S(1)}, u32[]{:S(2)}, u32[]{:S(2)}) collective-permute-start(bf16[2,512,512]{2,1,0:T(8,128)(2,1)} %get-tuple-element.62), channel_id=1, source_target_pairs={{0,1},{1,0},{2,3},{3,2},{4,5},{5,4},{6,7},{7,6},{8,9},{9,8},{10,11... | collective-permute-start | bytes 3145736 | tf_op jit(solution)/shard_map/ppermute | solution.py:775
  81.9 47.8 %collective-permute-start.1 = (bf16[768,1920]{1,0:T(8,128)(2,1)}, bf16[768,1920]{1,0:T(8,128)(2,1)}, u32[]{:S(2)}, u32[]{:S(2)}) collective-permute-start(bf16[768,1920]{1,0:T(8,128)(2,1)} %get-tuple-element.56), channel_id=1, source_target_pairs={{0,1},{1,0},{2,3},{3,2},{4,5},{5,4},{6,7},{7,6},{8,9},{9,8},{10,11... | collective-permute-start | bytes 8847368 | tf_op jit(solution)/shard_map/ppermute | solution.py:775
  92.9 3.3 %collective-permute-start.29 = (bf16[768,768]{1,0:T(8,128)(2,1)}, bf16[768,768]{1,0:T(8,128)(2,1)}, u32[]{:S(2)}, u32[]{:S(2)}) collective-permute-start(bf16[768,768]{1,0:T(8,128)(2,1)} %get-tuple-element.73), channel_id=1, source_target_pairs={{0,1},{1,0},{2,3},{3,2},{4,5},{5,4},{6,7},{7,6},{8,9},{9,8},{10,11... | collective-permute-start | bytes 3538952 | tf_op jit(solution)/shard_map/ppermute | solution.py:775
  93.4 51.0 %collective-permute-start.42 = (bf16[3072,384]{1,0:T(8,128)(2,1)}, bf16[3072,384]{1,0:T(8,128)(2,1)}, u32[]{:S(2)}, u32[]{:S(2)}) collective-permute-start(bf16[3072,384]{1,0:T(8,128)(2,1)} %get-tuple-element.75), channel_id=1, source_target_pairs={{0,1},{1,0},{2,3},{3,2},{4,5},{5,4},{6,7},{7,6},{8,9},{9,8},{10,11... | collective-permute-start | bytes 7077896 | tf_op jit(solution)/shard_map/ppermute | solution.py:775
  97.6 16.6 %collective-permute-start.30 = (bf16[2,2,2,48,768]{4,3,2,1,0:T(8,128)(2,1)S(1)}, bf16[2,2,2,48,768]{4,3,2,1,0:T(8,128)(2,1)S(1)}, u32[]{:S(2)}, u32[]{:S(2)}) collective-permute-start(bf16[2,2,2,48,768]{4,3,2,1,0:T(8,128)(2,1)S(1)} %fusion.6), channel_id=1, source_target_pairs={{0,2},{2,0},{4,6},{6,4},{8,10},{10,8},{12,14},{14,12},{16,18},{18,... | collective-permute-start | bytes 1769480 | tf_op jit(solution)/shard_map/ppermute | solution.py:780
  115.3 8.7 %collective-permute-start.31 = (bf16[2,2,48,768]{3,2,1,0:T(8,128)(2,1)S(1)}, bf16[2,2,48,768]{3,2,1,0:T(8,128)(2,1)}, u32[]{:S(2)}, u32[]{:S(2)}) collective-permute-start(bf16[2,2,48,768]{3,2,1,0:T(8,128)(2,1)S(1)} %fusion.9), channel_id=1, source_target_pairs={{0,4},{2,6},{4,0},{6,2},{8,12},{10,14},{12,8},{14,10},{16,20},{18,... | collective-permute-start | bytes 884744 | tf_op jit(solution)/shard_map/ppermute | solution.py:780
  125.2 7.7 %collective-permute-start.32 = (bf16[48,768]{1,0:T(8,128)(2,1)S(1)}, bf16[48,768]{1,0:T(8,128)(2,1)S(1)}, u32[]{:S(2)}, u32[]{:S(2)}) collective-permute-start(bf16[48,768]{1,0:T(8,128)(2,1)S(1)} %get-tuple-element.112), channel_id=1, source_target_pairs={{0,8},{2,10},{4,12},{6,14},{8,0},{10,2},{12,4},{14,6},{16,24},{18,... | collective-permute-start | bytes 221192 | tf_op jit(solution)/shard_map/ppermute | solution.py:780
  126.7 6.8 %collective-permute-start.33 = (bf16[48,768]{1,0:T(8,128)(2,1)S(1)}, bf16[48,768]{1,0:T(8,128)(2,1)S(1)}, u32[]{:S(2)}, u32[]{:S(2)}) collective-permute-start(bf16[48,768]{1,0:T(8,128)(2,1)S(1)} %get-tuple-element.114), channel_id=1, source_target_pairs={{0,16},{2,18},{4,20},{6,22},{8,24},{10,26},{12,28},{14,30},{16,0},... | collective-permute-start | bytes 221192 | tf_op jit(solution)/shard_map/ppermute | solution.py:780
  129.4 6.2 %collective-permute-start.34 = (bf16[48,768]{1,0:T(8,128)(2,1)S(1)}, bf16[48,768]{1,0:T(8,128)(2,1)S(1)}, u32[]{:S(2)}, u32[]{:S(2)}) collective-permute-start(bf16[48,768]{1,0:T(8,128)(2,1)S(1)} %get-tuple-element.113), channel_id=1, source_target_pairs={{0,24},{2,26},{4,28},{6,30},{8,16},{10,18},{12,20},{14,22},{16,8},... | collective-permute-start | bytes 221192 | tf_op jit(solution)/shard_map/ppermute | solution.py:780
  136.5 13.5 %collective-permute-start.35 = (f32[48,768]{1,0:T(8,128)S(1)}, f32[48,768]{1,0:T(8,128)S(1)}, u32[]{:S(2)}, u32[]{:S(2)}) collective-permute-start(f32[48,768]{1,0:T(8,128)S(1)} %fusion.33), channel_id=1, source_target_pairs={{0,1},{1,0},{2,3},{3,2},{4,5},{5,4},{6,7},{7,6},{8,9},{9,8},{10,11... | collective-permute-start | bytes 442376 | tf_op jit(solution)/shard_map/ppermute | solution.py:775
  144.0 7.4 %collective-permute-start.2 = (bf16[2,512,256]{2,1,0:T(8,128)(2,1)S(1)}, bf16[2,512,256]{2,1,0:T(8,128)(2,1)S(1)}, u32[]{:S(2)}, u32[]{:S(2)}) collective-permute-start(bf16[2,512,256]{2,1,0:T(8,128)(2,1)S(1)} %get-tuple-element.59), channel_id=1, source_target_pairs={{0,1},{1,0},{2,3},{3,2},{4,5},{5,4},{6,7},{7,6},{8,9},{9,8},{10,11... | collective-permute-start | bytes 1572872 | tf_op jit(solution)/shard_map/ppermute | solution.py:775
  147.0 38.2 %collective-permute-start.43 = (bf16[2,2,2,192,384]{4,3,2,1,0:T(8,128)(2,1)}, bf16[2,2,2,192,384]{4,3,2,1,0:T(8,128)(2,1)}, u32[]{:S(2)}, u32[]{:S(2)}) collective-permute-start(bf16[2,2,2,192,384]{4,3,2,1,0:T(8,128)(2,1)} %fusion.2), channel_id=1, source_target_pairs={{0,2},{2,0},{4,6},{6,4},{8,10},{10,8},{12,14},{14,12},{16,18},{18,... | collective-permute-start | bytes 3538952 | tf_op jit(solution)/shard_map/ppermute | solution.py:780
  148.4 61.5 %collective-permute-start.36 = (bf16[2,2,2,48,1920]{4,3,2,1,0:T(8,128)(2,1)}, bf16[2,2,2,48,1920]{4,3,2,1,0:T(8,128)(2,1)}, u32[]{:S(2)}, u32[]{:S(2)}) collective-permute-start(bf16[2,2,2,48,1920]{4,3,2,1,0:T(8,128)(2,1)} %fusion.after_ref), channel_id=1, source_target_pairs={{0,4},{2,6},{4,0},{6,2},{8,12},{10,14},{12,8},{14,10},{16,20},{18,... | collective-permute-start | bytes 4423688 | tf_op jit(solution)/shard_map/ppermute | solution.py:780
  161.6 3.6 %collective-permute-start.15 = (f32[16,1920]{1,0:T(8,128)S(1)}, f32[16,1920]{1,0:T(8,128)S(1)}, u32[]{:S(2)}, u32[]{:S(2)}) collective-permute-start(f32[16,1920]{1,0:T(8,128)S(1)} %bitcast.329), channel_id=1, source_target_pairs={{0,1},{1,0},{2,3},{3,2},{4,5},{5,4},{6,7},{7,6},{8,9},{9,8},{10,11... | collective-permute-start | bytes 368648 | tf_op jit(solution)/shard_map/ppermute | solution.py:775
  162.3 61.9 %collective-permute-start.22 = (bf16[768,768]{1,0:T(8,128)(2,1)}, bf16[768,768]{1,0:T(8,128)(2,1)}, u32[]{:S(2)}, u32[]{:S(2)}) collective-permute-start(bf16[768,768]{1,0:T(8,128)(2,1)} %get-tuple-element.71), channel_id=1, source_target_pairs={{0,1},{1,0},{2,3},{3,2},{4,5},{5,4},{6,7},{7,6},{8,9},{9,8},{10,11... | collective-permute-start | bytes 3538952 | tf_op jit(solution)/shard_map/ppermute | solution.py:775
  165.5 11.1 %collective-permute-start.16 = (f32[2,2,2,1920]{3,2,1,0:T(2,128)S(1)}, f32[2,2,2,1920]{3,2,1,0:T(2,128)S(1)}, u32[]{:S(2)}, u32[]{:S(2)}) collective-permute-start(f32[2,2,2,1920]{3,2,1,0:T(2,128)S(1)} %bitcast.330), channel_id=1, source_target_pairs={{0,2},{2,0},{4,6},{6,4},{8,10},{10,8},{12,14},{14,12},{16,18},{18,... | collective-permute-start | bytes 184328 | tf_op jit(solution)/shard_map/ppermute | solution.py:780
  176.6 6.7 %collective-permute-start.17 = (f32[2,2,1920]{2,1,0:T(2,128)S(1)}, f32[2,2,1920]{2,1,0:T(2,128)S(1)}, u32[]{:S(2)}, u32[]{:S(2)}) collective-permute-start(f32[2,2,1920]{2,1,0:T(2,128)S(1)} %bitcast_add_fusion), channel_id=1, source_target_pairs={{0,4},{2,6},{4,0},{6,2},{8,12},{10,14},{12,8},{14,10},{16,20},{18,... | collective-permute-start | bytes 92168 | tf_op jit(solution)/shard_map/ppermute | solution.py:780
  183.5 6.9 %collective-permute-start.18 = (f32[1920]{0:T(1024)S(1)}, f32[1920]{0:T(1024)S(1)}, u32[]{:S(2)}, u32[]{:S(2)}) collective-permute-start(f32[1920]{0:T(1024)S(1)} %add_add_fusion.3), channel_id=1, source_target_pairs={{0,8},{2,10},{4,12},{6,14},{8,0},{10,2},{12,4},{14,6},{16,24},{18,... | collective-permute-start | bytes 23048 | tf_op jit(solution)/shard_map/ppermute | solution.py:780
  183.6 6.8 %collective-permute-start.19 = (f32[1920]{0:T(1024)S(1)}, f32[1920]{0:T(1024)S(1)}, u32[]{:S(2)}, u32[]{:S(2)}) collective-permute-start(f32[1920]{0:T(1024)S(1)} %add_add_fusion.2), channel_id=1, source_target_pairs={{0,16},{2,18},{4,20},{6,22},{8,24},{10,26},{12,28},{14,30},{16,0},... | collective-permute-start | bytes 23048 | tf_op jit(solution)/shard_map/ppermute | solution.py:780
  185.2 6.9 %collective-permute-start.20 = (f32[1920]{0:T(1024)S(1)}, f32[1920]{0:T(1024)S(1)}, u32[]{:S(2)}, u32[]{:S(2)}) collective-permute-start(f32[1920]{0:T(1024)S(1)} %add_add_fusion), channel_id=1, source_target_pairs={{0,24},{2,26},{4,28},{6,30},{8,16},{10,18},{12,20},{14,22},{16,8},... | collective-permute-start | bytes 23048 | tf_op jit(solution)/shard_map/ppermute | solution.py:780
  190.4 52.6 %collective-permute-start.4 = (bf16[1152,768]{1,0:T(8,128)(2,1)}, bf16[1152,768]{1,0:T(8,128)(2,1)S(1)}, u32[]{:S(2)}, u32[]{:S(2)}) collective-permute-start(bf16[1152,768]{1,0:T(8,128)(2,1)} %gene_rows.3), channel_id=1, source_target_pairs={{0,1},{1,0},{2,3},{3,2},{4,5},{5,4},{6,7},{7,6},{8,9},{9,8},{10,11... | collective-permute-start | bytes 5308424 | tf_op jit(solution)/shard_map/ppermute | solution.py:775
  190.4 16.1 %collective-permute-start.44 = (bf16[2,2,192,384]{3,2,1,0:T(8,128)(2,1)}, bf16[2,2,192,384]{3,2,1,0:T(8,128)(2,1)}, u32[]{:S(2)}, u32[]{:S(2)}) collective-permute-start(bf16[2,2,192,384]{3,2,1,0:T(8,128)(2,1)} %fusion.3), channel_id=1, source_target_pairs={{0,4},{2,6},{4,0},{6,2},{8,12},{10,14},{12,8},{14,10},{16,20},{18,... | collective-permute-start | bytes 1769480 | tf_op jit(solution)/shard_map/ppermute | solution.py:780
  208.2 7.3 %collective-permute-start.45 = (bf16[192,384]{1,0:T(8,128)(2,1)S(1)}, bf16[192,384]{1,0:T(8,128)(2,1)S(1)}, u32[]{:S(2)}, u32[]{:S(2)}) collective-permute-start(bf16[192,384]{1,0:T(8,128)(2,1)S(1)} %get-tuple-element.109), channel_id=1, source_target_pairs={{0,8},{2,10},{4,12},{6,14},{8,0},{10,2},{12,4},{14,6},{16,24},{18,... | collective-permute-start | bytes 442376 | tf_op jit(solution)/shard_map/ppermute | solution.py:780
  208.3 14.0 %collective-permute-start.46 = (bf16[192,384]{1,0:T(8,128)(2,1)S(1)}, bf16[192,384]{1,0:T(8,128)(2,1)S(1)}, u32[]{:S(2)}, u32[]{:S(2)}) collective-permute-start(bf16[192,384]{1,0:T(8,128)(2,1)S(1)} %get-tuple-element.111), channel_id=1, source_target_pairs={{0,16},{2,18},{4,20},{6,22},{8,24},{10,26},{12,28},{14,30},{16,0},... | collective-permute-start | bytes 442376 | tf_op jit(solution)/shard_map/ppermute | solution.py:780
  210.0 12.3 %collective-permute-start.47 = (bf16[192,384]{1,0:T(8,128)(2,1)S(1)}, bf16[192,384]{1,0:T(8,128)(2,1)S(1)}, u32[]{:S(2)}, u32[]{:S(2)}) collective-permute-start(bf16[192,384]{1,0:T(8,128)(2,1)S(1)} %get-tuple-element.110), channel_id=1, source_target_pairs={{0,24},{2,26},{4,28},{6,30},{8,16},{10,18},{12,20},{14,22},{16,8},... | collective-permute-start | bytes 442376 | tf_op jit(solution)/shard_map/ppermute | solution.py:780
  215.5 17.4 %collective-permute-start.37 = (bf16[2,2,48,1920]{3,2,1,0:T(8,128)(2,1)S(1)}, bf16[2,2,48,1920]{3,2,1,0:T(8,128)(2,1)S(1)}, u32[]{:S(2)}, u32[]{:S(2)}) collective-permute-start(bf16[2,2,48,1920]{3,2,1,0:T(8,128)(2,1)S(1)} %fusion.1), channel_id=1, source_target_pairs={{0,2},{2,0},{4,6},{6,4},{8,10},{10,8},{12,14},{14,12},{16,18},{18,... | collective-permute-start | bytes 2211848 | tf_op jit(solution)/shard_map/ppermute | solution.py:780
  223.5 3.6 %collective-permute-start.48 = (f32[192,384]{1,0:T(8,128)S(1)}, f32[192,384]{1,0:T(8,128)S(1)}, u32[]{:S(2)}, u32[]{:S(2)}) collective-permute-start(f32[192,384]{1,0:T(8,128)S(1)} %fusion.27), channel_id=1, source_target_pairs={{0,1},{1,0},{2,3},{3,2},{4,5},{5,4},{6,7},{7,6},{8,9},{9,8},{10,11... | collective-permute-start | bytes 884744 | tf_op jit(solution)/shard_map/ppermute | solution.py:775
  225.4 15.8 %collective-permute-start.23 = (bf16[2,2,2,48,768]{4,3,2,1,0:T(8,128)(2,1)S(1)}, bf16[2,2,2,48,768]{4,3,2,1,0:T(8,128)(2,1)S(1)}, u32[]{:S(2)}, u32[]{:S(2)}) collective-permute-start(bf16[2,2,2,48,768]{4,3,2,1,0:T(8,128)(2,1)S(1)} %fusion.5), channel_id=1, source_target_pairs={{0,4},{2,6},{4,0},{6,2},{8,12},{10,14},{12,8},{14,10},{16,20},{18,... | collective-permute-start | bytes 1769480 | tf_op jit(solution)/shard_map/ppermute | solution.py:780
  234.6 20.4 %collective-permute-start.38 = (bf16[48,1920]{1,0:T(8,128)(2,1)S(1)}, bf16[48,1920]{1,0:T(8,128)(2,1)S(1)}, u32[]{:S(2)}, u32[]{:S(2)}) collective-permute-start(bf16[48,1920]{1,0:T(8,128)(2,1)S(1)} %get-tuple-element.106), channel_id=1, source_target_pairs={{0,8},{2,10},{4,12},{6,14},{8,0},{10,2},{12,4},{14,6},{16,24},{18,... | collective-permute-start | bytes 552968 | tf_op jit(solution)/shard_map/ppermute | solution.py:780
  234.7 22.9 %collective-permute-start.39 = (bf16[48,1920]{1,0:T(8,128)(2,1)S(1)}, bf16[48,1920]{1,0:T(8,128)(2,1)S(1)}, u32[]{:S(2)}, u32[]{:S(2)}) collective-permute-start(bf16[48,1920]{1,0:T(8,128)(2,1)S(1)} %get-tuple-element.108), channel_id=1, source_target_pairs={{0,16},{2,18},{4,20},{6,22},{8,24},{10,26},{12,28},{14,30},{16,0},... | collective-permute-start | bytes 552968 | tf_op jit(solution)/shard_map/ppermute | solution.py:780
  236.2 21.4 %collective-permute-start.40 = (bf16[48,1920]{1,0:T(8,128)(2,1)S(1)}, bf16[48,1920]{1,0:T(8,128)(2,1)S(1)}, u32[]{:S(2)}, u32[]{:S(2)}) collective-permute-start(bf16[48,1920]{1,0:T(8,128)(2,1)S(1)} %get-tuple-element.107), channel_id=1, source_target_pairs={{0,24},{2,26},{4,28},{6,30},{8,16},{10,18},{12,20},{14,22},{16,8},... | collective-permute-start | bytes 552968 | tf_op jit(solution)/shard_map/ppermute | solution.py:780
  242.3 10.0 %collective-permute-start.24 = (bf16[2,2,48,768]{3,2,1,0:T(8,128)(2,1)S(1)}, bf16[2,2,48,768]{3,2,1,0:T(8,128)(2,1)S(1)}, u32[]{:S(2)}, u32[]{:S(2)}) collective-permute-start(bf16[2,2,48,768]{3,2,1,0:T(8,128)(2,1)S(1)} %fusion.10), channel_id=1, source_target_pairs={{0,2},{2,0},{4,6},{6,4},{8,10},{10,8},{12,14},{14,12},{16,18},{18,... | collective-permute-start | bytes 884744 | tf_op jit(solution)/shard_map/ppermute | solution.py:780
  243.3 21.7 %collective-permute-start.5 = (bf16[2,2,2,72,384]{4,3,2,1,0:T(8,128)(2,1)S(1)}, bf16[2,2,2,72,384]{4,3,2,1,0:T(8,128)(2,1)S(1)}, u32[]{:S(2)}, u32[]{:S(2)}) collective-permute-start(bf16[2,2,2,72,384]{4,3,2,1,0:T(8,128)(2,1)S(1)} %fusion.12), channel_id=1, source_target_pairs={{0,2},{2,0},{4,6},{6,4},{8,10},{10,8},{12,14},{14,12},{16,18},{18,... | collective-permute-start | bytes 1327112 | tf_op jit(solution)/shard_map/ppermute | solution.py:780
  252.3 13.3 %collective-permute-start.10 = (bf16[2,2,2,72,384]{4,3,2,1,0:T(8,128)(2,1)S(1)}, bf16[2,2,2,72,384]{4,3,2,1,0:T(8,128)(2,1)S(1)}, u32[]{:S(2)}, u32[]{:S(2)}) collective-permute-start(bf16[2,2,2,72,384]{4,3,2,1,0:T(8,128)(2,1)S(1)} %fusion.13), channel_id=1, source_target_pairs={{0,4},{2,6},{4,0},{6,2},{8,12},{10,14},{12,8},{14,10},{16,20},{18,... | collective-permute-start | bytes 1327112 | tf_op jit(solution)/shard_map/ppermute | solution.py:780
  255.0 6.3 %collective-permute-start.25 = (bf16[48,768]{1,0:T(8,128)(2,1)S(1)}, bf16[48,768]{1,0:T(8,128)(2,1)S(1)}, u32[]{:S(2)}, u32[]{:S(2)}) collective-permute-start(bf16[48,768]{1,0:T(8,128)(2,1)S(1)} %get-tuple-element.115), channel_id=1, source_target_pairs={{0,8},{2,10},{4,12},{6,14},{8,0},{10,2},{12,4},{14,6},{16,24},{18,... | collective-permute-start | bytes 221192 | tf_op jit(solution)/shard_map/ppermute | solution.py:780
  257.6 6.4 %collective-permute-start.26 = (bf16[48,768]{1,0:T(8,128)(2,1)S(1)}, bf16[48,768]{1,0:T(8,128)(2,1)S(1)}, u32[]{:S(2)}, u32[]{:S(2)}) collective-permute-start(bf16[48,768]{1,0:T(8,128)(2,1)S(1)} %get-tuple-element.117), channel_id=1, source_target_pairs={{0,16},{2,18},{4,20},{6,22},{8,24},{10,26},{12,28},{14,30},{16,0},... | collective-permute-start | bytes 221192 | tf_op jit(solution)/shard_map/ppermute | solution.py:780
  257.6 6.3 %collective-permute-start.27 = (bf16[48,768]{1,0:T(8,128)(2,1)S(1)}, bf16[48,768]{1,0:T(8,128)(2,1)S(1)}, u32[]{:S(2)}, u32[]{:S(2)}) collective-permute-start(bf16[48,768]{1,0:T(8,128)(2,1)S(1)} %get-tuple-element.116), channel_id=1, source_target_pairs={{0,24},{2,26},{4,28},{6,30},{8,16},{10,18},{12,20},{14,22},{16,8},... | collective-permute-start | bytes 221192 | tf_op jit(solution)/shard_map/ppermute | solution.py:780
  261.3 5.1 %collective-permute-start.41 = (f32[48,1920]{1,0:T(8,128)S(1)}, f32[48,1920]{1,0:T(8,128)S(1)}, u32[]{:S(2)}, u32[]{:S(2)}) collective-permute-start(f32[48,1920]{1,0:T(8,128)S(1)} %fusion.21), channel_id=1, source_target_pairs={{0,1},{1,0},{2,3},{3,2},{4,5},{5,4},{6,7},{7,6},{8,9},{9,8},{10,11... | collective-permute-start | bytes 1105928 | tf_op jit(solution)/shard_map/ppermute | solution.py:775
  264.9 3.1 %collective-permute-start.28 = (f32[48,768]{1,0:T(8,128)S(1)}, f32[48,768]{1,0:T(8,128)S(1)}, u32[]{:S(2)}, u32[]{:S(2)}) collective-permute-start(f32[48,768]{1,0:T(8,128)S(1)} %fusion.39), channel_id=1, source_target_pairs={{0,1},{1,0},{2,3},{3,2},{4,5},{5,4},{6,7},{7,6},{8,9},{9,8},{10,11... | collective-permute-start | bytes 442376 | tf_op jit(solution)/shard_map/ppermute | solution.py:775
  265.1 11.3 %collective-permute-start.6 = (bf16[2,2,72,384]{3,2,1,0:T(8,128)(2,1)S(1)}, bf16[2,2,72,384]{3,2,1,0:T(8,128)(2,1)S(1)}, u32[]{:S(2)}, u32[]{:S(2)}) collective-permute-start(bf16[2,2,72,384]{3,2,1,0:T(8,128)(2,1)S(1)} %fusion.15), channel_id=1, source_target_pairs={{0,4},{2,6},{4,0},{6,2},{8,12},{10,14},{12,8},{14,10},{16,20},{18,... | collective-permute-start | bytes 663560 | tf_op jit(solution)/shard_map/ppermute | solution.py:780
  265.7 15.3 %collective-permute-start.11 = (bf16[2,2,72,384]{3,2,1,0:T(8,128)(2,1)S(1)}, bf16[2,2,72,384]{3,2,1,0:T(8,128)(2,1)S(1)}, u32[]{:S(2)}, u32[]{:S(2)}) collective-permute-start(bf16[2,2,72,384]{3,2,1,0:T(8,128)(2,1)S(1)} %fusion.14), channel_id=1, source_target_pairs={{0,2},{2,0},{4,6},{6,4},{8,10},{10,8},{12,14},{14,12},{16,18},{18,... | collective-permute-start | bytes 663560 | tf_op jit(solution)/shard_map/ppermute | solution.py:780
  276.5 7.5 %collective-permute-start.7 = (bf16[72,384]{1,0:T(8,128)(2,1)S(1)}, bf16[72,384]{1,0:T(8,128)(2,1)S(1)}, u32[]{:S(2)}, u32[]{:S(2)}) collective-permute-start(bf16[72,384]{1,0:T(8,128)(2,1)S(1)} %get-tuple-element.118), channel_id=1, source_target_pairs={{0,8},{2,10},{4,12},{6,14},{8,0},{10,2},{12,4},{14,6},{16,24},{18,... | collective-permute-start | bytes 165896 | tf_op jit(solution)/shard_map/ppermute | solution.py:780
  277.9 7.6 %collective-permute-start.8 = (bf16[72,384]{1,0:T(8,128)(2,1)S(1)}, bf16[72,384]{1,0:T(8,128)(2,1)S(1)}, u32[]{:S(2)}, u32[]{:S(2)}) collective-permute-start(bf16[72,384]{1,0:T(8,128)(2,1)S(1)} %get-tuple-element.120), channel_id=1, source_target_pairs={{0,16},{2,18},{4,20},{6,22},{8,24},{10,26},{12,28},{14,30},{16,0},... | collective-permute-start | bytes 165896 | tf_op jit(solution)/shard_map/ppermute | solution.py:780
  279.5 6.6 %collective-permute-start.9 = (bf16[72,384]{1,0:T(8,128)(2,1)S(1)}, bf16[72,384]{1,0:T(8,128)(2,1)S(1)}, u32[]{:S(2)}, u32[]{:S(2)}) collective-permute-start(bf16[72,384]{1,0:T(8,128)(2,1)S(1)} %get-tuple-element.119), channel_id=1, source_target_pairs={{0,24},{2,26},{4,28},{6,30},{8,16},{10,18},{12,20},{14,22},{16,8},... | collective-permute-start | bytes 165896 | tf_op jit(solution)/shard_map/ppermute | solution.py:780
  281.1 5.1 %collective-permute-start.12 = (bf16[72,384]{1,0:T(8,128)(2,1)S(1)}, bf16[72,384]{1,0:T(8,128)(2,1)S(1)}, u32[]{:S(2)}, u32[]{:S(2)}) collective-permute-start(bf16[72,384]{1,0:T(8,128)(2,1)S(1)} %get-tuple-element.121), channel_id=1, source_target_pairs={{0,8},{2,10},{4,12},{6,14},{8,0},{10,2},{12,4},{14,6},{16,24},{18,... | collective-permute-start | bytes 165896 | tf_op jit(solution)/shard_map/ppermute | solution.py:780
  281.6 7.8 %collective-permute-start.13 = (bf16[72,384]{1,0:T(8,128)(2,1)S(1)}, bf16[72,384]{1,0:T(8,128)(2,1)S(1)}, u32[]{:S(2)}, u32[]{:S(2)}) collective-permute-start(bf16[72,384]{1,0:T(8,128)(2,1)S(1)} %get-tuple-element.123), channel_id=1, source_target_pairs={{0,16},{2,18},{4,20},{6,22},{8,24},{10,26},{12,28},{14,30},{16,0},... | collective-permute-start | bytes 165896 | tf_op jit(solution)/shard_map/ppermute | solution.py:780
  284.1 6.1 %collective-permute-start.14 = (bf16[72,384]{1,0:T(8,128)(2,1)S(1)}, bf16[72,384]{1,0:T(8,128)(2,1)S(1)}, u32[]{:S(2)}, u32[]{:S(2)}) collective-permute-start(bf16[72,384]{1,0:T(8,128)(2,1)S(1)} %get-tuple-element.122), channel_id=1, source_target_pairs={{0,24},{2,26},{4,28},{6,30},{8,16},{10,18},{12,20},{14,22},{16,8},... | collective-permute-start | bytes 165896 | tf_op jit(solution)/shard_map/ppermute | solution.py:780
  (24 other events, 307.1 us)

commit v2 on v1

--- a/solution.py
+++ b/solution.py
@@ -1,3 +1,5 @@
+import functools
+
 import jax
 import jax.numpy as jnp
 from jax import lax
@@ -13,6 +15,9 @@
 GRANT = 52 << 20
 
 
+LONG = pl.CostEstimate(flops=10**12, bytes_accessed=1, transcendentals=0)
+
+
 def dot(left, right, left_dim=1, right_dim=0):
     return lax.dot_general(
         left, right, (((left_dim,), (right_dim,)), ((), ())), preferred_element_type=WIDE
@@ -46,8 +51,8 @@
     return pl.BlockSpec(shape, lambda *_: (0,) * len(shape))
 
 
-def params():
-    return pltpu.CompilerParams(vmem_limit_bytes=GRANT)
+def params(grant=GRANT):
+    return pltpu.CompilerParams(vmem_limit_bytes=grant)
 
 
 def shaped(shape, dtype):
@@ -55,6 +60,7 @@
 
 
 def embed_kernel(
+    place_ref,
     ids_ref,
     expression_ref,
     prior_ref,
@@ -81,50 +87,69 @@
         picker = jnp.where(slots == ids, 1.0, 0.0).astype(LOW)
         gathered = dot(picker, table_ref[...])
     expression = jnp.broadcast_to(expression_ref[...], (8, rows)).T[:, :1]
-    embedded = gathered + group_ref[...] + expression * w_value_ref[...] + embedded
+    groups = lax.broadcasted_iota(jnp.int32, (8, group_ref.shape[0]), 1)
+    group_row = dot(jnp.where(groups == place_ref[3], 1.0, 0.0).astype(LOW), group_ref[...])[:1]
+    embedded = gathered + group_row + expression * w_value_ref[...][None] + embedded
     embedded_ref[...] = embedded
     unit, _ = normalize(embedded)
-    normed = (unit * gain_ref[...] + offset_ref[...]).astype(LOW)
+    normed = (unit * gain_ref[...][None] + offset_ref[...][None]).astype(LOW)
     normed_ref[...] = normed
     kv_ref[:, :width] = dot(normed, w_key_ref[...]).astype(LOW)
-    kv_ref[:, width:] = (dot(normed, w_val_ref[...]) + bias_val_ref[...]).astype(LOW)
+    kv_ref[:, width:] = (dot(normed, w_val_ref[...]) + bias_val_ref[...][None]).astype(LOW)
 
 
 def embed(
-    ids, expression, prior, table, group_row, w_know, w_value, gain, offset, w_qkv, bias_v
+    place, ids, expression, prior, table, group_table, w_know, w_value, gain, offset, w_qkv, bias_v
 ):
     rows, width = prior.shape
-    columns = lambda index: pl.BlockSpec((width, width), lambda _: (0, index))
+    columns = lambda index: pl.BlockSpec((width, width), lambda *_: (0, index))
     return pl.pallas_call(
         embed_kernel,
-        grid=(1,),
-        in_specs=[
-            whole((1, rows)),
-            whole((1, rows)),
-            whole((rows, width)),
-            whole(table.shape),
-            whole((1, width)),
-            whole((width, width)),
-            whole((1, width)),
-            whole((1, width)),
-            whole((1, width)),
-            columns(1),
-            columns(2),
-            whole((1, width)),
-        ],
-        out_specs=[whole((rows, width)), whole((rows, width)), whole((rows, 2 * width))],
+        grid_spec=pltpu.PrefetchScalarGridSpec(
+            num_scalar_prefetch=1,
+            grid=(1,),
+            in_specs=[
+                whole((1, rows)),
+                whole((1, rows)),
+                whole((rows, width)),
+                whole(table.shape),
+                whole(group_table.shape),
+                whole((width, width)),
+                whole((width,)),
+                whole((width,)),
+                whole((width,)),
+                columns(1),
+                columns(2),
+                whole((width,)),
+            ],
+            out_specs=[whole((rows, width)), whole((rows, width)), whole((rows, 2 * width))],
+        ),
         out_shape=[
             shaped((rows, width), WIDE),
             shaped((rows, width), LOW),
             shaped((rows, 2 * width), LOW),
         ],
-        compiler_params=params(),
+        compiler_params=params(60 << 20),
         name="embed",
-    )(ids, expression, prior, table, group_row, w_know, w_value, gain, offset, w_qkv, w_qkv, bias_v)
+    )(
+        place,
+        ids,
+        expression,
+        prior,
+        table,
+        group_table,
+        w_know,
+        w_value,
+        gain,
+        offset,
+        w_qkv,
+        w_qkv,
+        bias_v,
+    )
 
 
 def query_kernel(normed_ref, w_query_ref, bias_ref, out_ref):
-    out_ref[...] = (dot(normed_ref[...], w_query_ref[...]) + bias_ref[...]).astype(LOW)
+    out_ref[...] = (dot(normed_ref[...], w_query_ref[...]) + bias_ref[...][None]).astype(LOW)
 
 
 def project_queries(normed, w_qkv, bias_q):
@@ -132,7 +157,7 @@
     return pl.pallas_call(
         query_kernel,
         grid=(1,),
-        in_specs=[whole((rows, width)), whole((width, width)), whole((1, width))],
+        in_specs=[whole((rows, width)), whole((width, width)), whole((width,))],
         out_specs=whole((rows, width)),
         out_shape=shaped((rows, width), LOW),
         compiler_params=params(),
@@ -143,14 +168,14 @@
     )(normed, w_qkv, bias_q)
 
 
-def attend_kernel(live_ref, q_ref, ko_ref, vo_ref, kr_ref, vr_ref, out_ref, p_ref, c_ref):
+def attend_kernel(place_ref, q_ref, ko_ref, vo_ref, kr_ref, vr_ref, out_ref, p_ref, c_ref):
     rows = q_ref.shape[0]
     lane = lax.broadcasted_iota(jnp.int32, (rows, 128), 1)
     place = lax.broadcasted_iota(jnp.int32, (rows, 128), 0)
     queries = q_ref[...] * LOW(HEAD_DIM**-0.5)
     halves = []
     for index, k_ref in enumerate((ko_ref, kr_ref)):
-        dead = jnp.where(place < live_ref[index], 0.0, -1e30).astype(LOW)
+        dead = jnp.where(place < place_ref[1 + index], 0.0, -1e30).astype(LOW)
         halves.append((k_ref[...], dead))
     values = [vo_ref[...].T, vr_ref[...].T]
     outs = []
@@ -173,7 +198,7 @@
     out_ref[...] = jnp.concatenate(outs, 0).T.astype(LOW)
 
 
-def attend(live, queries, kv_own, kv_other):
+def attend(place, queries, kv_own, kv_other):
     rows, width = queries.shape
     pairs = width // 128
     block = lambda shift: pl.BlockSpec((rows, 128), lambda j, _: (0, shift + j))
@@ -201,7 +226,7 @@
             transcendentals=4 * rows * rows * pairs,
         ),
         name="attend",
-    )(live, queries, kv_own, kv_own, kv_other, kv_other)
+    )(place, queries, kv_own, kv_own, kv_other, kv_other)
 
 
 def attend_back_kernel(
@@ -214,11 +239,9 @@
     g_ref,
     p_ref,
     c_ref,
-    after_ref,
-    dq_ref,
-    dkvo_ref,
-    dkvr_ref,
+    *rest,
 ):
+    dq_ref, dkvo_ref, dkvr_ref = rest[-3:]
     rows = q_ref.shape[0]
     lane = lax.broadcasted_iota(jnp.int32, (rows, 128), 1)
     mixed = a_ref[...].astype(WIDE).T
@@ -275,8 +298,8 @@
             near,
             pl.BlockSpec((2, 2 * rows, rows), lambda j: (start + j, 0, 0)),
             pl.BlockSpec((1, 2, rows), lambda j: (start + j, 0, 0)),
-            pl.BlockSpec(memory_space=pl.ANY),
-        ],
+        ]
+        + [pl.BlockSpec(memory_space=pl.ANY)] * len(after),
         out_specs=[block(0), both, both],
         out_shape=[
             shaped((rows, 128 * count), LOW),
@@ -284,13 +307,9 @@
             shaped((2, rows, 128 * count), LOW),
         ],
         compiler_params=params(),
-        cost_estimate=pl.CostEstimate(
-            flops=32 * rows * rows * 128 * count * 2,
-            bytes_accessed=8 * rows * rows * count,
-            transcendentals=0,
-        ),
+        cost_estimate=LONG,
         name="attend_back",
-    )(queries, kv_own, kv_own, kv_other, kv_other, attended, grad, probs, inverse, after)
+    )(queries, kv_own, kv_own, kv_other, kv_other, attended, grad, probs, inverse, *after)
 
 
 def ffn_kernel(
@@ -313,6 +332,8 @@
     up_keep_ref,
     down_send_ref,
     down_keep_ref,
+    out_send_ref,
+    out_keep_ref,
     vectors_ref,
     bias_up_grad_ref,
     residual_ref,
@@ -331,10 +352,10 @@
 
     @pl.when(step == 0)
     def _():
-        residual = embedded_ref[...] + (dot(attended_ref[...], w_out_ref[...]) + bias_out_ref[...])
+        residual = embedded_ref[...] + (dot(attended_ref[...], w_out_ref[...]) + bias_out_ref[...][None])
         residual_ref[...] = residual
         unit, _ = normalize(residual)
-        normed = unit * gain_ref[...] + offset_ref[...]
+        normed = unit * gain_ref[...][None] + offset_ref[...][None]
         normed_ref[...] = normed.astype(LOW)
         turned_ref[...] = normed.T.astype(LOW)
         g_out_ref[...] = jnp.where(alive, cotangent_ref[...].astype(WIDE), 0.0).astype(LOW)
@@ -368,12 +389,12 @@
     @pl.when(step == steps - 1)
     def _():
         residual = residual_ref[...]
-        final = residual + (total_ref[...] + bias_down_ref[...])
+        final = residual + (total_ref[...] + bias_down_ref[...][None])
         output_ref[...] = jnp.where(alive, final, 0.0).astype(LOW)
         unit, scale = normalize(residual)
         g_final = g_out_ref[...].astype(WIDE)
         g_normed = g_normed_ref[...]
-        g_residual = g_final + norm_back(g_normed, unit, scale, gain_ref[...])
+        g_residual = g_final + norm_back(g_normed, unit, scale, gain_ref[...][None])
         g_residual_ref[...] = g_residual
         g_branch = g_residual.astype(LOW)
         g_attended_ref[...] = dot(g_branch, w_out_ref[...], 1, 1).astype(LOW)
@@ -388,10 +409,8 @@
         )
         normed_ref[...] = g_branch
         attended = attended_ref[...].astype(WIDE).T.astype(LOW)
-        half = width // 2
-        last = up_send_ref.shape[1] - half
-        up_send_ref[:, last:] = dot(attended, normed_ref[:, other]).astype(LOW)
-        up_keep_ref[:, last:] = dot(attended, normed_ref[:, own]).astype(LOW)
+        out_send_ref[...] = dot(attended, normed_ref[:, other]).astype(LOW)
+        out_keep_ref[...] = dot(attended, normed_ref[:, own]).astype(LOW)
 
 
 def feed_forward(
@@ -414,7 +433,6 @@
     steps = units // tile
     turn = lambda j, place: lax.rem(j + (1 - place[0]) * (steps // 2), steps)
     down_tile = pl.BlockSpec((tile, width // 2), lambda j, place: (turn(j, place), 0))
-    merged = units // 2 + width // 2
     return pl.pallas_call(
         ffn_kernel,
         grid_spec=pltpu.PrefetchScalarGridSpec(
@@ -425,22 +443,24 @@
                 whole((rows, width)),
                 whole((rows, width)),
                 whole((width, width)),
-                whole((1, width)),
-                whole((1, width)),
-                whole((1, width)),
+                whole((width,)),
+                whole((width,)),
+                whole((width,)),
                 pl.BlockSpec((width, tile), lambda j, place: (0, turn(j, place))),
                 pl.BlockSpec((1, tile), lambda j, place: (0, turn(j, place))),
                 pl.BlockSpec((tile, width), lambda j, place: (turn(j, place), 0)),
-                whole((1, width)),
+                whole((width,)),
             ],
             out_specs=[
                 whole((rows, width)),
                 whole((rows, width)),
                 whole((rows, width)),
-                whole((width, merged)),
-                whole((width, merged)),
+                whole((width, units // 2)),
+                whole((width, units // 2)),
                 down_tile,
                 down_tile,
+                whole((width, width // 2)),
+                whole((width, width // 2)),
                 whole((4, width)),
                 pl.BlockSpec((1, tile), lambda j, place: (0, turn(j, place))),
             ],
@@ -457,10 +477,12 @@
             shaped((rows, width), LOW),
             shaped((rows, width), WIDE),
             shaped((rows, width), LOW),
-            shaped((width, merged), LOW),
-            shaped((width, merged), LOW),
+            shaped((width, units // 2), LOW),
+            shaped((width, units // 2), LOW),
             shaped((units, width // 2), LOW),
             shaped((units, width // 2), LOW),
+            shaped((width, width // 2), LOW),
+            shaped((width, width // 2), LOW),
             shaped((4, width), WIDE),
             shaped((1, units), WIDE),
         ],
@@ -515,6 +537,7 @@
     wq_ref,
     wk_ref,
     wv_ref,
+    after_ref,
     send_ref,
     keep_ref,
     bias_ref,
@@ -542,6 +565,7 @@
 
 
 def last_back_kernel(
+    groups,
     place_ref,
     normed_ref,
     dq_ref,
@@ -562,10 +586,13 @@
     send_ref,
     keep_ref,
     g_low_ref,
-    rows_ref,
+    small_send_ref,
+    small_keep_ref,
     turned_ref,
     joined_ref,
     bias_ref,
+    rows_ref,
+    owned_ref,
 ):
     rows, width = normed_ref.shape
     half = width // 2
@@ -584,17 +611,16 @@
         bias_ref,
     )
     unit, scale = normalize(embedded_ref[...])
-    g_embedded = g_residual_ref[...] + norm_back(back, unit, scale, gain_ref[...])
+    g_embedded = g_residual_ref[...] + norm_back(back, unit, scale, gain_ref[...][None])
     g_low_ref[...] = g_embedded.astype(LOW)
     prior = prior_ref[...].astype(WIDE).T.astype(LOW)
     send_ref[:, half:] = dot(prior, g_low_ref[:, half_of(1 - mine, half)]).astype(LOW)
     keep_ref[:, half:] = dot(prior, g_low_ref[:, half_of(mine, half)]).astype(LOW)
     expression = jnp.broadcast_to(expression_ref[...], (8, rows)).T[:, :1]
     total = column_sums(g_embedded)
-    groups = rows_ref.shape[0] - 16
-    hot = lax.broadcasted_iota(jnp.int32, (groups, width), 0) == place_ref[1]
+    hot = lax.broadcasted_iota(jnp.int32, (groups, width), 0) == place_ref[3]
     rows_ref[:groups] = jnp.where(hot, total, 0.0)
-    rows_ref[groups:] = jnp.concatenate(
+    rows_ref[groups : groups + 16] = jnp.concatenate(
         [
             column_sums(expression * g_embedded),
             column_sums(back * unit),
@@ -602,11 +628,27 @@
             jnp.concatenate([bias_first_ref[0, 0:1], bias_first_ref[1, 0:1], bias_ref[0:1]], 1),
             jnp.concatenate([bias_first_ref[0, 1:2], bias_first_ref[1, 1:2], bias_ref[1:2]], 1),
             vectors_ref[...],
-            bias_up_ref[...],
-            jnp.zeros((3, width), WIDE),
+            jnp.zeros((7, width), WIDE),
         ],
         0,
     )
+    count = owned_ref.shape[0]
+    share = width // count
+    owned_ref[...] = jnp.zeros_like(owned_ref)
+    for owner in range(count):
+        columns = slice(owner * share, (owner + 1) * share)
+        for start in range(0, groups + 16, 32):
+            size = min(32, groups + 16 - start)
+            lanes = slice(start * 4, start * 4 + share)
+            owned_ref[owner, :size, lanes] = rows_ref[start : start + size, columns]
+        at, lanes = groups % 32 + 9, slice(groups // 32 * 128, groups // 32 * 128 + share)
+        for part in range(4):
+            first = (owner * 4 + part) * share
+            owned_ref[owner, at + part : at + part + 1, lanes] = bias_up_ref[
+                :, first : first + share
+            ]
+    small_send_ref[...] = owned_ref[:, pl.ds(pl.multiple_of((1 - mine) * 16, 16), 16), :].astype(LOW)
+    small_keep_ref[...] = owned_ref[:, pl.ds(pl.multiple_of(mine * 16, 16), 16), :].astype(LOW)
 
 
 def back_specs(rows, width, group, first):
@@ -624,7 +666,7 @@
     ]
 
 
-def first_back(place, normed, dq, own, got, w_qkv, group):
+def first_back(place, normed, dq, own, got, w_qkv, group, after):
     rows, width = normed.shape
     count = dq.shape[1] // group
     half = 3 * group // 2
@@ -634,7 +676,7 @@
         grid_spec=pltpu.PrefetchScalarGridSpec(
             num_scalar_prefetch=1,
             grid=(count,),
-            in_specs=back_specs(rows, width, group, 0),
+            in_specs=back_specs(rows, width, group, 0) + [pl.BlockSpec(memory_space=pl.ANY)],
             out_specs=[
                 tile,
                 tile,
@@ -653,13 +695,9 @@
             shaped((rows, width), WIDE),
         ],
         compiler_params=params(),
-        cost_estimate=pl.CostEstimate(
-            flops=12 * rows * width * group * count,
-            bytes_accessed=16 * width * width,
-            transcendentals=0,
-        ),
+        cost_estimate=LONG,
         name="first_back",
-    )(place, normed, dq, own, got, w_qkv, w_qkv, w_qkv)
+    )(place, normed, dq, own, got, w_qkv, w_qkv, w_qkv, after)
 
 
 def last_back(
@@ -680,12 +718,13 @@
     vectors,
     bias_up,
     groups,
+    count,
 ):
     rows, width = normed.shape
     half = width // 2
     first = width // group - 1
     return pl.pallas_call(
-        last_back_kernel,
+        functools.partial(last_back_kernel, groups),
         grid_spec=pltpu.PrefetchScalarGridSpec(
             num_scalar_prefetch=1,
             grid=(1,),
@@ -694,32 +733,37 @@
                 whole((rows, width)),
                 whole((rows, width)),
                 whole((rows, width)),
-                whole((1, width)),
+                whole((width,)),
                 whole((rows, width)),
                 whole((1, rows)),
                 whole(bias_first.shape),
                 whole((4, width)),
-                whole((4, width)),
+                whole(bias_up.shape),
             ],
             out_specs=[
                 whole((width, width)),
                 whole((width, width)),
                 whole((rows, width)),
-                whole((groups + 16, width)),
+                whole((count, 16, 384)),
+                whole((count, 16, 384)),
             ],
             scratch_shapes=[
                 pltpu.VMEM((width, rows), LOW),
                 pltpu.VMEM((rows, 3 * group), LOW),
                 pltpu.VMEM((2, group), WIDE),
+                pltpu.VMEM((groups + 16, width), WIDE),
+                pltpu.VMEM((count, 32, 384), WIDE),
             ],
         ),
         out_shape=[
             shaped((width, width), LOW),
             shaped((width, width), LOW),
             shaped((rows, width), LOW),
-            shaped((groups + 16, width), WIDE),
+            shaped((count, 16, 384), LOW),
+            shaped((count, 16, 384), LOW),
         ],
         compiler_params=params(),
+        cost_estimate=LONG,
         name="last_back",
     )(
         place,
@@ -742,14 +786,14 @@
     )
 
 
-def gene_kernel(slots_ref, ids_ref, grad_ref, out_ref):
+def gene_kernel(slots_ref, ids_ref, grad_ref, after_ref, out_ref):
     slots = slots_ref[...]
     rows = grad_ref.shape[0]
     picker = jnp.where(slots == jnp.broadcast_to(ids_ref[...], (slots.shape[0], rows)), 1.0, 0.0)
     out_ref[...] = dot(picker.astype(LOW), grad_ref[...]).astype(LOW)
 
 
-def gene_rows(slots, ids, grad):
+def gene_rows(slots, ids, grad, after):
     count = slots.shape[0]
     rows, width = grad.shape
     tile = min(count, 1152)
@@ -760,15 +804,14 @@
             pl.BlockSpec((tile, 1), lambda j: (j, 0)),
             whole((1, rows)),
             whole((rows, width)),
+            pl.BlockSpec(memory_space=pl.ANY),
         ],
         out_specs=pl.BlockSpec((tile, width), lambda j: (j, 0)),
         out_shape=shaped((count, width), LOW),
         compiler_params=params(),
-        cost_estimate=pl.CostEstimate(
-            flops=2 * rows * width * count, bytes_accessed=2 * width * count, transcendentals=0
-        ),
+        cost_estimate=LONG,
         name="gene_rows",
-    )(slots, ids, grad)
+    )(slots, ids, grad, after)
 
 
 def swap_cores(array):
@@ -784,55 +827,191 @@
     return lax.dynamic_index_in_dim(array, index, position, keepdims=False)
 
 
-def total(terms):
-    wide = terms[0].astype(WIDE)
-    for term in terms[1:]:
-        wide = wide + term.astype(WIDE)
-    return wide
+LANES = 384
+
+
+def up16(rows):
+    return -(-rows // 16) * 16
 
 
 class Share:
-    def __init__(self, terms, turn, wire=LOW):
-        count = lax.axis_size("dp")
-        bits = count.bit_length() - 1
-        self.me = lax.axis_index("dp")
-        self.wire = wire
-        self.terms = [term.reshape((2,) * bits + term.shape[1:]) for term in terms]
-        self.left = list(range(bits - 1, -1, -1))
-        order = list(range(bits - 2))
-        self.order = order[1::-1] + order[2:] if turn else order
-
-    def halve(self):
-        bit = self.order.pop(0)
-        mine = (self.me >> bit) & 1
-        position = self.left.index(bit)
-        sent = total([pick(term, position, 1 - mine) for term in self.terms]).astype(self.wire)
-        got = bits_apart(sent, 1 << bit)
-        self.terms = [pick(term, position, mine) for term in self.terms] + [got]
-        self.left.remove(bit)
-        return sent
-
-    def finish(self):
-        while self.order:
-            self.halve()
-        low, high = self.left[1], self.left[0]
-        mine_low, mine_high = (self.me >> low) & 1, (self.me >> high) & 1
-        arrived = []
-        for step in (1, 2, 3):
-            to_low, to_high = mine_low ^ (step & 1), mine_high ^ (step >> 1)
-            sent = total([pick(pick(term, 0, to_high), 0, to_low) for term in self.terms])
-            mask = ((step & 1) << low) | ((step >> 1) << high)
-            arrived.append(bits_apart(sent.astype(self.wire), mask))
-        own = [pick(pick(term, 0, mine_high), 0, mine_low) for term in self.terms]
-        return total(own + arrived)
-
-
-def both_halves(own, block_index):
-    other = swap_cores(own)
-    return (
-        jnp.where(block_index == 0, own, other),
-        jnp.where(block_index == 0, other, own),
-    )
+    QUAD = "quad"
+
+    def __init__(self, segments, route):
+        self.bits = lax.axis_size("dp").bit_length() - 1
+        self.route = list(route)
+        self.rows = [arrays[0].shape[1] for arrays, _ in segments]
+        self.settle()
+        dims = tuple(range(self.bits - 1, -1, -1))
+        self.sources = [
+            (array.reshape((2,) * self.bits + array.shape[1:]), dims, block, [(index, 0)])
+            for index, (arrays, block) in enumerate(segments)
+            for array in arrays
+        ]
+        self.fixed = ()
+
+    def join(self, other):
+        shift = len(self.rows)
+        self.rows = self.rows + other.rows
+        self.sources += [
+            (array, dims, block, [(index + shift, start) for index, start in parts])
+            for array, dims, block, parts in other.sources
+        ]
+        self.settle()
+        return self
+
+    def settle(self):
+        self.places, place = [], 0
+        for rows in self.rows:
+            self.places.append(place)
+            place += up16(rows)
+        self.height = self.places[-1] + self.rows[-1]
+
+    def targets(self):
+        step = self.route[0] if self.route else None
+        if step is None:
+            return [{}]
+        if step == self.QUAD:
+            low, high = self.bits - 2, self.bits - 1
+            return [{low: way & 1, high: way >> 1} for way in (1, 2, 3)]
+        return [{step: 1}]
+
+    def left(self, target):
+        return [bit for bit in range(self.bits - 1, -1, -1) if bit not in self.fixed + tuple(target)]
+
+    def receive(self, targets, sent):
+        if self.route:
+            self.route.pop(0)
+        for target, array in zip(targets, sent):
+            mask = sum(flip << bit for bit, flip in target.items())
+            dims = tuple(self.left(target))
+            parts = list(enumerate(self.places))
+            self.sources.append((bits_apart(array, mask), dims, 0, parts))
+        self.fixed += tuple(targets[0])
+
+
+def combine(place, shares, after, last=None):
+    operands, specs, plan, out_specs, out_shape = [], [], [], [], []
+    steps = []
+    for share in shares:
+        targets = share.targets()
+        steps.append(targets)
+        for target in targets:
+            left = share.left(target) if last is None else []
+            used = []
+            for array, dims, block, parts in share.sources:
+                shape, where = [], []
+                for bit in dims:
+                    free = bit in left
+                    shape.append(2 if free else None)
+                    where.append(None if free else (bit, target.get(bit, 0)))
+
+                def index(_, place, where=tuple(where), block=block):
+                    lead = tuple(
+                        0 if at is None else (1 - place[4 + at[0]] if at[1] else place[4 + at[0]])
+                        for at in where
+                    )
+                    return lead + (0, block)
+
+                specs.append(pl.BlockSpec(tuple(shape) + (array.shape[-2], LANES), index))
+                used.append((len(operands), parts))
+                operands.append(array)
+            plan.append((share.rows, share.places, used))
+            if last is None:
+                shape = (2,) * len(left) + (share.height, LANES)
+                out_specs.append(whole(shape))
+                out_shape.append(shaped(shape, LOW))
+    if last is not None:
+        for shape, _ in last:
+            out_specs.append(whole(shape))
+            out_shape.append(shaped(shape, WIDE))
+    count = len(operands)
+
+    def kernel(*refs):
+        sources, outs = refs[1 : 1 + count], refs[1 + count + len(after) :]
+
+        def summed(item, segment):
+            rows, _, used = plan[item]
+            total = None
+            for operand, parts in used:
+                for index, start in parts:
+                    if index == segment:
+                        part = sources[operand][..., start : start + rows[segment], :].astype(WIDE)
+                        total = part if total is None else total + part
+            return total
+
+        if last is None:
+            for item, out in enumerate(outs):
+                for segment, start in enumerate(plan[item][1]):
+                    out[..., start : start + plan[item][0][segment], :] = summed(
+                        item, segment
+                    ).astype(LOW)
+        else:
+            for (_, pieces), out in zip(last, outs):
+                for item, segment, row, column in pieces:
+                    value = summed(item, segment)
+                    out[row : row + value.shape[0], column : column + LANES] = value
+
+    outs = pl.pallas_call(
+        kernel,
+        grid_spec=pltpu.PrefetchScalarGridSpec(
+            num_scalar_prefetch=1,
+            grid=(1,),
+            in_specs=specs + [pl.BlockSpec(memory_space=pl.ANY)] * len(after),
+            out_specs=out_specs,
+        ),
+        out_shape=out_shape,
+        compiler_params=params(),
+        cost_estimate=LONG,
+        name="combine",
+    )(place, *operands, *after)
+    if last is not None:
+        return outs
+    taken = 0
+    for share, targets in zip(shares, steps):
+        share.receive(targets, outs[taken : taken + len(targets)])
+        taken += len(targets)
+    return outs
+
+
+def assemble(place, own, other, shapes, pieces, small_row=None):
+    def kernel(place_ref, own_ref, other_ref, *outs):
+        first = place_ref[0] == 0
+
+        def of_core(core, rows, columns):
+            return jnp.where(first == (core == 0), own_ref[rows, columns], other_ref[rows, columns])
+
+        for core, row, rows, column, columns, target, out_column in pieces:
+            value = of_core(core, slice(row, row + rows), slice(column, column + columns))
+            outs[target][:, out_column : out_column + columns] = value
+        if small_row is None:
+            return
+        group_ref, vector_refs, long_ref = outs[2], outs[3:-1], outs[-1]
+        groups, share = group_ref.shape
+        rows = slice(small_row, small_row + 16)
+        for start in range(0, groups, 16):
+            lanes = slice(start // 32 * 128, start // 32 * 128 + share)
+            group_ref[start : start + 16] = of_core(start // 16 % 2, rows, lanes)
+        rest = of_core(0, rows, slice(groups // 32 * 128, groups // 32 * 128 + 128))
+        for index, ref in enumerate(vector_refs):
+            ref[...] = rest[index, :share]
+        long_ref[...] = jnp.concatenate(
+            [rest[9 + part : 10 + part, :share] for part in range(4)], 1
+        )[0]
+
+    return pl.pallas_call(
+        kernel,
+        grid_spec=pltpu.PrefetchScalarGridSpec(
+            num_scalar_prefetch=1,
+            grid=(1,),
+            in_specs=[whole(own.shape), whole(own.shape)],
+            out_specs=[whole(shape) for shape in shapes],
+        ),
+        out_shape=[shaped(shape, WIDE) for shape in shapes],
+        compiler_params=params(),
+        cost_estimate=LONG,
+        name="assemble",
+    )(place, own, other)
 
 
 def body(
@@ -868,31 +1047,33 @@
     length, group = lengths[0], groups[0]
     prior = knowledge[0]
     row = lambda vector: vector.reshape(1, -1)
-    live_own = length - mine * rows
-    live_other = length - (1 - mine) * rows
-    group_row = group_table[group].astype(WIDE)[None]
+    me = lax.axis_index("dp")
+    bits = count.bit_length() - 1
+    place = jnp.stack(
+        [mine, length - mine * rows, length - (1 - mine) * rows, group]
+        + [(me >> bit) & 1 for bit in range(bits)]
+    ).astype(jnp.int32)
     if gene_table.shape[0] > 8 * rows:
         table = gene_table[gene_ids[0]]
     else:
         table = gene_table
     embedded, normed, kv_own = embed(
+        place,
         gene_ids,
         values,
         prior,
         table,
-        group_row,
+        group_table,
         w_know,
-        row(w_value),
-        row(norm1_gain),
-        row(norm1_bias),
+        w_value,
+        norm1_gain,
+        norm1_bias,
         w_qkv,
-        row(bias_v),
+        bias_v,
     )
     kv_other = swap_cores(kv_own)
-    queries = project_queries(normed, w_qkv, row(bias_q))
-    attended, probs, inverse = attend(
-        jnp.stack([live_own, live_other]).astype(jnp.int32), queries, kv_own, kv_other
-    )
+    queries = project_queries(normed, w_qkv, bias_q)
+    attended, probs, inverse = attend(place, queries, kv_own, kv_other)
     (
         block_output,
         g_residual,
@@ -901,41 +1082,50 @@
         up_keep,
         down_send,
         down_keep,
+        out_send,
+        out_keep,
         vectors,
         bias_up_grad,
     ) = feed_forward(
-        jnp.stack([mine, live_own]).astype(jnp.int32),
+        place,
         attended,
         embedded,
         cotangent[0],
         w_out,
-        row(bias_out),
-        row(norm2_gain),
-        row(norm2_bias),
+        bias_out,
+        norm2_gain,
+        norm2_bias,
         w_up,
         row(bias_up),
         w_down,
-        row(bias_down),
+        bias_down,
     )
 
     owners = lambda array: array.reshape(count, -1, array.shape[-1])
-    down = Share([owners(down_keep), owners(swap_cores(down_send))], 0)
-    up = Share([owners(up_keep), owners(swap_cores(up_send))], 1)
+    low_bits = list(range(bits - 2))
+    turned = low_bits[1::-1] + low_bits[2:]
+    quad = [Share.QUAD]
+    up_terms = [owners(up_keep), owners(swap_cores(up_send))]
+    blocks = units // 2 // LANES
+    out_terms = [owners(out_keep), owners(swap_cores(out_send))]
+    down_terms = [owners(down_keep), owners(swap_cores(down_send))]
+    early = [
+        Share([(down_terms, 0), (out_terms, 0)], low_bits + quad),
+        Share([(up_terms, block) for block in range(blocks)], turned + quad),
+    ]
     dq1, own1, other1 = attend_back(
-        queries, kv_own, kv_other, attended, g_attended, probs, inverse, 0, 4, g_attended
+        queries, kv_own, kv_other, attended, g_attended, probs, inverse, 0, 4, []
     )
     got1 = swap_cores(other1)
-    down.halve()
-    after = up.halve()
+    sent = combine(place, early, [dq1])
     dq2, own2, other2 = attend_back(
-        queries, kv_own, kv_other, attended, g_attended, probs, inverse, 4, 2, after
+        queries, kv_own, kv_other, attended, g_attended, probs, inverse, 4, 2, sent
     )
     got2 = swap_cores(other2)
-    place = jnp.stack([mine, group]).astype(jnp.int32)
     qkv_send, qkv_keep, bias_first, part = first_back(
-        place, normed, dq1, own1, got1, w_qkv, 256
-    )
-    tail_send, tail_keep, g_low, sums = last_back(
+        place, normed, dq1, own1, got1, w_qkv, 256, dq2
+    )
+    tail_send, tail_keep, g_low, small_send, small_keep = last_back(
         place,
         normed,
         dq2,
@@ -946,65 +1136,104 @@
         part,
         embedded,
         g_residual,
-        row(norm1_gain),
+        norm1_gain,
         prior,
         values,
         bias_first,
         vectors,
-        bias_up_grad.reshape(count, 4, -1).swapaxes(0, 1).reshape(4, width),
+        bias_up_grad,
         group_table.shape[0],
+        count,
     )
     slot = jnp.arange(count * VOC_DEV, dtype=jnp.int32)[:, None]
     slot = slot + slot // VOC_DEV * VOC_DEV
-    gene_send = gene_rows(slot + (1 - mine) * VOC_DEV, gene_ids, g_low)
+    qkv = [owners(qkv_keep), owners(swap_cores(qkv_send))]
+    gene_send = gene_rows(slot + (1 - mine) * VOC_DEV, gene_ids, g_low, qkv[1])
     gene_got = swap_cores(gene_send)
-    gene_keep = gene_rows(slot + mine * VOC_DEV, gene_ids, g_low)
-    qkv = Share([owners(qkv_keep), owners(swap_cores(qkv_send))], 0)
-    tail = Share([owners(tail_keep), owners(swap_cores(tail_send))], 1)
-    half = width // 2
-    gene_terms = [owners(gene_keep), owners(gene_got)]
-    gene_left = Share([term[..., :half] for term in gene_terms], 0)
-    gene_right = Share([term[..., half:] for term in gene_terms], 1)
-
-    sums = sums.reshape(-1, count, width // count).swapaxes(0, 1).reshape(count, 2, -1)
-    small = Share([pick(sums, 1, mine), swap_cores(pick(sums, 1, 1 - mine))], 0, WIDE)
-
-    down_halves = both_halves(down.finish(), mine)
-    up_halves = both_halves(up.finish(), mine)
-    qkv_halves = both_halves(qkv.finish(), mine)
-    gene_grad = jnp.concatenate([gene_left.finish(), gene_right.finish()], 1)
-    tail_halves = both_halves(tail.finish(), mine)
-    small = jnp.concatenate(both_halves(small.finish(), mine)).reshape(-1, width // count)
-    join = lambda pieces: jnp.concatenate(pieces, 1)
-    q_parts, k_parts, v_parts = [], [], []
-    cut = 384
-    for index in range(3):
-        if index < 2:
-            low, high = [side[:, index * cut : (index + 1) * cut] for side in qkv_halves]
-        else:
-            low, high = [side[:, :cut] for side in tail_halves]
-        q_parts.append(low[:, :256])
-        k_parts += [low[:, 256:], high[:, :128]]
-        v_parts.append(high[:, 128:])
-    extra = small[group_table.shape[0] :]
+    gene_keep = gene_rows(slot + mine * VOC_DEV, gene_ids, g_low, gene_send)
+    share = width // count
+    small = [small_keep, swap_cores(small_send)]
+    tail = [owners(tail_keep), owners(swap_cores(tail_send))]
+    gene = [owners(gene_keep), owners(gene_got)]
+    late = [
+        Share([(qkv, 0), (qkv, 1), (gene, 0)], low_bits + quad),
+        Share([(tail, 0), (tail, 1), (small, 0), (gene, 1)], turned + quad),
+    ]
+    token = [gene_keep]
+    for _ in low_bits[1:]:
+        token = combine(place, early, token)
+    early = [early[0].join(early[1])]
+    token = combine(place, late, token)
+    token = combine(place, early, token)
+    for _ in low_bits[1:]:
+        token = combine(place, late, token)
+    late = [late[0].join(late[1])]
+    step = up16(share)
+    high = units // count
+    layout = [(0, 0, 0, 0), (0, 1, high + blocks * step, 0)]
+    layout += [(0, 2 + block, high + block * step, 0) for block in range(blocks)]
+    (own,) = combine(place, early, token, [((high + (blocks + 1) * step, LANES), layout)])
+    other = swap_cores(own)
+    combine(place, late, [own])
+    pieces = []
+    for core in range(2):
+        pieces.append((core, 0, high, 0, LANES, 0, core * LANES))
+        for block in range(blocks):
+            place_in = (core * blocks + block) * LANES
+            pieces.append((core, high + block * step, share, 0, LANES, 1, place_in))
+        pieces.append((core, high + blocks * step, share, 0, LANES, 2, core * LANES))
+    w_down_share, w_up_share, w_out_share = assemble(
+        place, own, other, [(high, width), (share, units), (share, width)], pieces
+    )
+    layout = [(0, 0, 0, 0), (0, 1, step, 0)]
+    layout += [(0, 3 + index, (2 + index) * step, 0) for index in range(3)]
+    own, gene_grad = combine(
+        place,
+        late,
+        [w_down_share],
+        [
+            ((4 * step + 16, LANES), layout),
+            ((VOC_DEV, width), [(0, 2, 0, 0), (0, 6, 0, LANES)]),
+        ],
+    )
+    other = swap_cores(own)
+    pieces = []
+    for block in range(3):
+        at = block * step
+        pieces.append((0, at, share, 0, 256, 0, block * 256))
+        pieces.append((0, at, share, 256, 128, 0, width + block * 256))
+        pieces.append((1, at, share, 0, 128, 0, width + block * 256 + 128))
+        pieces.append((1, at, share, 128, 256, 0, 2 * width + block * 256))
+    for core in range(2):
+        pieces.append((core, 3 * step, share, 0, LANES, 1, core * LANES))
+    w_qkv_share, w_know_share, group_share, *extra, bias_up_share = assemble(
+        place,
+        own,
+        other,
+        [(share, 3 * width), (share, width), (group_table.shape[0], share)]
+        + [(share,)] * 9
+        + [(units // count,)],
+        pieces,
+        4 * step,
+    )
     return (
         block_output[None],
         gene_grad,
-        small[: group_table.shape[0]],
-        join([side[:, cut:] for side in tail_halves]),
+        group_share,
+        w_know_share,
         extra[0],
         extra[1],
         extra[2],
-        join(q_parts + k_parts + v_parts),
+        w_qkv_share,
         extra[3],
         extra[4],
-        join([side[:, units // 2 :] for side in up_halves]),
+        w_out_share,
         extra[5],
         extra[6],
         extra[7],
-        join([side[:, : units // 2] for side in up_halves]),
-        extra[9:13].reshape(-1),
-        join(down_halves),
+        w_up_share,
+        bias_up_share,
+        w_down_share,
         extra[8],
     )
 

time: 296 us -> 222 us (0.75); the launches traced: 291 us -> 221 us
  Pallas kernels: 99.7 us -> 136 us
  other arithmetic: 34.1 us -> 0.28 us
  starting transfers between devices: 53.9 us -> 22.8 us
  waiting for transfers between devices: 77.5 us -> 51.8 us
  local copies, waits for them, and re-layouts: 23.2 us -> 7.7 us
    pallas_call x2 -> x12, Pallas kernels: 19.1 us -> 55.3 us  [the longest x8 30.9 us: combine(): pl.pallas_call(kernel, grid_spec=pltpu.PrefetchScalarGridSpec(num_scalar_...]
    ppermute x35 -> x14, starting transfers between devices: 50.9 us -> 20.1 us  [bits_apart(): return lax.ppermute(array, 'dp', [(i, i ^ mask) for i in range(count)])]
    convert_element_type x19 -> x0, other arithmetic: 22.1 us -> none  [the longest x12 15.4 us: halve(): total([pick(term, position, 1 - mine) for term in self.terms])]
    ppermute x35 -> x14, waiting for transfers between devices: 70.3 us -> 50.2 us  [bits_apart(): return lax.ppermute(array, 'dp', [(i, i ^ mask) for i in range(count)])]
    unnamed x60 -> x45, local copies, waits for them, and re-layouts: 14.3 us -> 7.09 us
    ppermute x14 -> x12, waiting for transfers between devices: 7.21 us -> 1.64 us  [swap_cores(): return lax.ppermute(array, 'blk', [(0, 1), (1, 0)])]
    concatenate x6 -> x0, other arithmetic: 5.12 us -> none  [the longest x4 3.05 us: body(): join = lambda pieces: jnp.concatenate(pieces, 1)]
    add x16 -> x2, other arithmetic: 5.22 us -> 0.28 us  [the longest x1 0.14 us: body(): gene_keep = gene_rows(slot + mine * VOC_DEV, gene_ids, g_low, gene_send)]
  transfers between devices with their start and end apart: 49 -> 26, of which waited for: 20 -> 11; matrix products, arithmetic and copies ran while one was open for 17% -> 0% of each run, Pallas kernels for 10% -> 34%
where the time goes in v2:
time: 222 us; the launch traced here: 221 us
  Pallas kernels  136 us (61%)
  waiting for transfers between devices  51.8 us (23%)
  starting transfers between devices  22.8 us (10%)
  local copies, waits for them, and re-layouts  7.7 us (3%)
    ppermute x14, waiting for transfers between devices, bits_apart(): return lax.ppermute(array, 'dp', [(i, i ^ mask) for i in range(count)])  50.2 us
    pallas_call x8, Pallas kernels, combine(): pl.pallas_call(kernel, grid_spec=pltpu.PrefetchScalarGridSpec(num_scalar_...  30.9 us
    pallas_call x1, Pallas kernels, feed_forward(): pl.pallas_call(ffn_kernel, grid_spec=pltpu.PrefetchScalarGridSpec(num_sca...  28.8 us
    pallas_call x2, Pallas kernels, attend_back(): pl.pallas_call(attend_back_kernel, grid=(count,), in_specs=[near, near, f...  20.3 us
    ppermute x14, starting transfers between devices, bits_apart(): return lax.ppermute(array, 'dp', [(i, i ^ mask) for i in range(count)])  20.1 us
    pallas_call x1, Pallas kernels, attend(): pl.pallas_call(attend_kernel, grid_spec=pltpu.PrefetchScalarGridSpec(num_...  17.3 us
    pallas_call x1, Pallas kernels, embed(): pl.pallas_call(embed_kernel, grid_spec=pltpu.PrefetchScalarGridSpec(num_s...  11.2 us
    pallas_call x1, Pallas kernels, last_back(): pl.pallas_call(functools.partial(last_back_kernel, groups), grid_spec=plt...  9.03 us
  transfers between devices with their start and end apart: 26, of which 11 were waited for; matrix products, arithmetic and copies ran while one was open for 0% of the time, Pallas kernels for 34%

profile of v2, /device:TPU:0, one launch (start us, length us, event | category | flops | bytes accessed | tf_op | source)
XLA Modules:
  0.0 220.7 jit_solution(5782730228763981656)
XLA Ops:
  2.0 0.6 stack.31.place_ref.refs_0_
  2.6 11.2 %embed.1 = (f32[512,768]{1,0:T(8,128)}, bf16[512,768]{1,0:T(8,128)(2,1)}, bf16[512,1536]{1,0:T(8,128)(2,1)}) custom-call(s32[8]{0:T(128)} %stack.31.place_ref.refs_0_, s32[1,512]{1,0:T(1,128)} %ids_ref.5, f32[1,512]{1,0:T(1,128)} %expression_ref.3, bf16[512,768]{1,0:T(8,128)(2,1)} %bitcast.42, bf16[2304,768]{1,0:T(8,128)(2,1)} %table_ref.1, ...), custom_call_target="tpu_custom_call" | custom-call | tf_op jit(solution)/shard_map/embed/pallas_call | solution.py:106
  14.2 1.1 copy-done
  15.3 2.1 queries.1.q_ref
  17.8 1.2 copy-done.21
  19.0 17.3 %attend.1 = (bf16[512,768]{1,0:T(8,128)(2,1)S(1)}, bf16[12,1024,512]{2,1,0:T(8,128)(2,1)}, f32[6,2,512]{2,1,0:T(2,128)S(1)}) custom-call(s32[8]{0:T(128)S(1)} %copy-done.7, bf16[512,768]{1,0:T(8,128)(2,1)S(1)} %queries.1.q_ref, bf16[512,1536]{1,0:T(8,128)(2,1)} %get-tuple-element.83.ko_ref.vo_ref, bf16[512,1536]{1,0:T(8,128)(2,1)} %get-tuple-element.83.ko_ref.vo_ref, ...), custom_call_target="tpu_custom_call" | custom-call | flops 3221225472 | bytes 12582912 | tf_op jit(solution)/shard_map/attend/pallas_call | solution.py:205
  36.2 0.9 copy-done.16
  37.1 28.8 %feed_forward.1 = (bf16[512,768]{1,0:T(8,128)(2,1)}, f32[512,768]{1,0:T(8,128)}, bf16[512,768]{1,0:T(8,128)(2,1)S(1)}, bf16[768,1536]{1,0:T(8,128)(2,1)}, bf16[7...) custom-call(s32[8]{0:T(128)S(1)} %copy-done.7, ...), custom_call_target="tpu_custom_call" | custom-call | flops 16307453952 | bytes 18874368 | tf_op jit(solution)/shard_map/feed_forward/pallas_call | solution.py:436
  65.9 0.9 copy-done.17
  67.4 12.7 %attend_back.2 = (bf16[512,512]{1,0:T(8,128)(2,1)S(1)}, bf16[2,512,512]{2,1,0:T(8,128)(2,1)}, bf16[2,512,512]{2,1,0:T(8,128)(2,1)}) custom-call(bf16[512,768]{1,0:T(8,128)(2,1)S(1)} %queries.1.q_ref, bf16[512,1536]{1,0:T(8,128)(2,1)} %get-tuple-element.83.ko_ref.vo_ref, bf16[512,1536]{1,0:T(8,128)(2,1)} %get-tuple-element.83.ko_ref.vo_ref, ...), custom_call_target="tpu_custom_call" | custom-call | flops 999999995904 | bytes 1 | tf_op jit(solution)/shard_map/attend_back/pallas_call | solution.py:288
  80.6 4.8 %combine.8 = (bf16[2,2,2,240,384]{4,3,2,1,0:T(8,128)(2,1)}, bf16[2,2,2,192,384]{4,3,2,1,0:T(8,128)(2,1)}) custom-call(s32[8]{0:T(128)S(1)} %copy-done.7, bf16[2,2,2,2,192,384]{5,4,3,2,1,0:T(8,128)(2,1)} %bitcast.69, bf16[2,2,2,2,192,384]{5,4,3,2,1,0:T(8,128)(2,1)} %bitcast.13.refs_2_.refs_18_.refs_34_, bf16[2,2,2,2,48,384]{5,4,3,2,1,0:T(8,128)(2,1)S(1)} %bitcast.30, ...), custom_call_target="tpu_custom_call" | custom-call | flops 999999995904 | bytes 1 | tf_op jit(solution)/shard_map/combine/pallas_call | solution.py:955
  85.4 2.6 %collective-permute-start.10 = (bf16[2,2,2,240,384]{4,3,2,1,0:T(8,128)(2,1)}, bf16[2,2,2,240,384]{4,3,2,1,0:T(8,128)(2,1)}, u32[]{:S(2)}, u32[]{:S(2)}) collective-permute-start(bf16[2,2,2,240,384]{4,3,2,1,0:T(8,128)(2,1)} %get-tuple-element.99.rest_0_), channel_id=1, source_target_pairs={{0,2},{2,0},{4,6},{6,4},{8,10},{10,8},{12,14},{14,12},{16,18},{18,... | collective-permute-start | bytes 4423688 | tf_op jit(solution)/shard_map/ppermute | solution.py:823
  88.0 1.5 collective-permute-start.11
  89.5 7.7 %attend_back.3 = (bf16[512,256]{1,0:T(8,128)(2,1)S(1)}, bf16[2,512,256]{2,1,0:T(8,128)(2,1)S(1)}, bf16[2,512,256]{2,1,0:T(8,128)(2,1)}) custom-call(bf16[512,768]{1,0:T(8,128)(2,1)} %copy-done.2, bf16[512,1536]{1,0:T(8,128)(2,1)} %get-tuple-element.83.ko_ref.vo_ref, bf16[512,1536]{1,0:T(8,128)(2,1)} %get-tuple-element.83.ko_ref.vo_ref, ...), custom_call_target="tpu_custom_call" | custom-call | flops 999999995904 | bytes 1 | tf_op jit(solution)/shard_map/attend_back/pallas_call | solution.py:288
  97.2 7.4 %first_back.1 = (bf16[768,768]{1,0:T(8,128)(2,1)}, bf16[768,768]{1,0:T(8,128)(2,1)}, f32[2,2,256]{2,1,0:T(2,128)S(1)}, f32[512,768]{1,0:T(8,128)}) custom-call(s32[8]{0:T(128)S(1)} %copy-done.7, bf16[512,768]{1,0:T(8,128)(2,1)S(1)} %copy-done.1, bf16[512,512]{1,0:T(8,128)(2,1)S(1)} %copy-done.20, bf16[2,512,512]{2,1,0:T(8,128)(2,1)} %get-tuple-element.91.own_ref, ...), custom_call_target="tpu_custom_call" | custom-call | flops 999999995904 | bytes 1 | tf_op jit(solution)/shard_map/first_back/pallas_call | solution.py:674
  105.2 9.0 %last_back.1 = (bf16[768,768]{1,0:T(8,128)(2,1)}, bf16[768,768]{1,0:T(8,128)(2,1)}, bf16[512,768]{1,0:T(8,128)(2,1)}, bf16[16,16,384]{2,1,0:T(8,128)(2,1)}, bf16[16,16,384]{2,1,0:T(8,128)(2,1)S(1)}) custom-call(s32[8]{0:T(128)S(1)} %copy-done.7, bf16[512,768]{1,0:T(8,128)(2,1)} %get-tuple-element.82.normed_ref, ...), custom_call_target="tpu_custom_call" | custom-call | flops 999999995904 | bytes 1 | tf_op jit(solution)/shard_map/last_back/pallas_call | solution.py:726
  114.8 1.1 copy-done.18
  115.9 2.4 %gene_rows.2.after_ref = bf16[1152,768]{1,0:T(8,128)(2,1)} custom-call(s32[1152,1]{1,0:T(8,128)S(1)} %broadcast_add_fusion.slots_ref, s32[1,512]{1,0:T(1,128)S(1)} %copy-done.6, bf16[512,768]{1,0:T(8,128)(2,1)S(1)} %copy-done.18, bf16[16,48,768]{2,1,0:T(8,128)(2,1)} %bitcast.20.after_ref), custom_call_target="tpu_custom_call" | custom-call | flops 999999995904 | bytes 1 | tf_op jit(solution)/shard_map/gene_rows/pallas_call | solution.py:800
  118.3 2.3 %gene_rows.3.refs_15_ = bf16[1152,768]{1,0:T(8,128)(2,1)} custom-call(s32[1152,1]{1,0:T(8,128)S(1)} %broadcast_add_fusion.1.slots_ref, s32[1,512]{1,0:T(1,128)S(1)} %copy-done.6, bf16[512,768]{1,0:T(8,128)(2,1)S(1)} %copy-done.18, bf16[1152,768]{1,0:T(8,128)(2,1)} %gene_rows.2.after_ref), custom_call_target="tpu_custom_call" | custom-call | flops 999999995904 | bytes 1 | tf_op jit(solution)/shard_map/gene_rows/pallas_call | solution.py:800
  121.2 4.0 %combine.9 = (bf16[2,2,240,384]{3,2,1,0:T(8,128)(2,1)}, bf16[2,2,192,384]{3,2,1,0:T(8,128)(2,1)}) custom-call(s32[8]{0:T(128)S(1)} %copy-done.7, bf16[2,2,2,2,192,384]{5,4,3,2,1,0:T(8,128)(2,1)} %bitcast.70, bf16[2,2,2,2,192,384]{5,4,3,2,1,0:T(8,128)(2,1)} %bitcast.13.refs_2_.refs_18_.refs_34_, bf16[2,2,2,2,48,384]{5,4,3,2,1,0:T(8,128)(2,1)S(1)} %bitcast.31, ...), custom_call_target="tpu_custom_call" | custom-call | flops 999999995904 | bytes 1 | tf_op jit(solution)/shard_map/combine/pallas_call | solution.py:955
  125.2 1.8 collective-permute-start.14
  126.9 1.5 collective-permute-start.15
  128.4 1.1 copy-done.8
  129.6 4.4 %combine.10 = (bf16[2,2,2,168,384]{4,3,2,1,0:T(8,128)(2,1)}, bf16[2,2,2,184,384]{4,3,2,1,0:T(8,128)(2,1)}) custom-call(s32[8]{0:T(128)S(1)} %copy-done.7, bf16[2,2,2,2,48,768]{5,4,3,2,1,0:T(8,128)(2,1)} %bitcast.87, bf16[2,2,2,2,48,768]{5,4,3,2,1,0:T(8,128)(2,1)} %bitcast.19.refs_2_.refs_4_.refs_20_.refs_22_.refs_38_.refs_40_, ...), custom_call_target="tpu_custom_call" | custom-call | flops 999999995904 | bytes 1 | tf_op jit(solution)/shard_map/combine/pallas_call | solution.py:955
  134.7 8.8 %collective-permute-done.15.refs_16_.refs_32_.refs_48_ = bf16[2,2,192,384]{3,2,1,0:T(8,128)(2,1)} collective-permute-done((bf16[2,2,192,384]{3,2,1,0:T(8,128)(2,1)}, bf16[2,2,192,384]{3,2,1,0:T(8,128)(2,1)}, u32[]{:S(2)}, u32[]{:S(2)}) %collective-permute-start.15) | collective-permute-done | bytes 589856 | tf_op jit(solution)/shard_map/ppermute | solution.py:823
  143.5 1.3 collective-permute-done.14.refs_6_.refs_22_.refs_38_
  144.8 4.0 %combine.11 = (bf16[432,384]{1,0:T(8,128)(2,1)}, bf16[432,384]{1,0:T(8,128)(2,1)}, bf16[432,384]{1,0:T(8,128)(2,1)}) custom-call(s32[8]{0:T(128)S(1)} %copy-done.7, bf16[2,2,2,2,192,384]{5,4,3,2,1,0:T(8,128)(2,1)} %bitcast.71, bf16[2,2,2,2,192,384]{5,4,3,2,1,0:T(8,128)(2,1)} %bitcast.13.refs_2_.refs_18_.refs_34_, ...), custom_call_target="tpu_custom_call" | custom-call | flops 999999995904 | bytes 1 | tf_op jit(solution)/shard_map/combine/pallas_call | solution.py:955
  148.9 1.9 collective-permute-start.18
  150.8 2.6 %collective-permute-start.19 = (bf16[432,384]{1,0:T(8,128)(2,1)}, bf16[432,384]{1,0:T(8,128)(2,1)}, u32[]{:S(2)}, u32[]{:S(2)}) collective-permute-start(bf16[432,384]{1,0:T(8,128)(2,1)} %get-tuple-element.121.refs_18_), channel_id=1, source_target_pairs={{0,16},{2,18},{4,20},{6,22},{8,24},{10,26},{12,28},{14,30},{16,0},... | collective-permute-start | bytes 995336 | tf_op jit(solution)/shard_map/ppermute | solution.py:823
  153.4 10.6 %collective-permute-done.12.refs_7_.refs_25_.refs_43_ = bf16[2,2,2,168,384]{4,3,2,1,0:T(8,128)(2,1)} collective-permute-done((bf16[2,2,2,168,384]{4,3,2,1,0:T(8,128)(2,1)}, bf16[2,2,2,168,384]{4,3,2,1,0:T(8,128)(2,1)}, u32[]{:S(2)}, u32[]{:S(2)}) %collective-permute-start.12) | collective-permute-done | bytes 1032224 | tf_op jit(solution)/shard_map/ppermute | solution.py:823
  164.0 4.0 %collective-permute-done.13.refs_16_.refs_17_.refs_35_.refs_53_ = bf16[2,2,2,184,384]{4,3,2,1,0:T(8,128)(2,1)} collective-permute-done((bf16[2,2,2,184,384]{4,3,2,1,0:T(8,128)(2,1)}, bf16[2,2,2,184,384]{4,3,2,1,0:T(8,128)(2,1)}, u32[]{:S(2)}, u32[]{:S(2)}) %collective-permute-start.13) | collective-permute-done | bytes 1130528 | tf_op jit(solution)/shard_map/ppermute | solution.py:823
  168.0 3.8 %combine.12 = (bf16[2,2,168,384]{3,2,1,0:T(8,128)(2,1)}, bf16[2,2,184,384]{3,2,1,0:T(8,128)(2,1)}) custom-call(s32[8]{0:T(128)S(1)} %copy-done.7, bf16[2,2,2,2,48,768]{5,4,3,2,1,0:T(8,128)(2,1)} %bitcast.89, bf16[2,2,2,2,48,768]{5,4,3,2,1,0:T(8,128)(2,1)} %bitcast.19.refs_2_.refs_4_.refs_20_.refs_22_.refs_38_.refs_40_, ...), custom_call_target="tpu_custom_call" | custom-call | flops 999999995904 | bytes 1 | tf_op jit(solution)/shard_map/combine/pallas_call | solution.py:955
  171.8 1.5 collective-permute-start.16
  173.3 1.5 collective-permute-start.17
  174.8 1.9 collective-permute-done.19.refs_18_
  176.8 3.4 %combine.13.refs_55_.own_ref = f32[432,384]{1,0:T(8,128)} custom-call(s32[8]{0:T(128)S(1)} %copy-done.7, bf16[2,2,2,2,192,384]{5,4,3,2,1,0:T(8,128)(2,1)} %bitcast.74, bf16[2,2,2,2,192,384]{5,4,3,2,1,0:T(8,128)(2,1)} %bitcast.13.refs_2_.refs_18_.refs_34_, bf16[2,2,2,2,48,384]{5,4,3,2,1,0:T(8,128)(2,1)} %bitcast.35, ...), custom_call_target="tpu_custom_call" | custom-call | flops 999999995904 | bytes 1 | tf_op jit(solution)/shard_map/combine/pallas_call | solution.py:955
  180.2 4.7 %collective-permute-done.16.refs_8_.refs_26_.refs_44_ = bf16[2,2,168,384]{3,2,1,0:T(8,128)(2,1)} collective-permute-done((bf16[2,2,168,384]{3,2,1,0:T(8,128)(2,1)}, bf16[2,2,168,384]{3,2,1,0:T(8,128)(2,1)}, u32[]{:S(2)}, u32[]{:S(2)}) %collective-permute-start.16) | collective-permute-done | bytes 516128 | tf_op jit(solution)/shard_map/ppermute | solution.py:823
  184.9 2.0 collective-permute-done.17.refs_18_.refs_36_.refs_54_
  186.9 3.7 %combine.14 = (bf16[360,384]{1,0:T(8,128)(2,1)}, bf16[360,384]{1,0:T(8,128)(2,1)}, bf16[360,384]{1,0:T(8,128)(2,1)}) custom-call(s32[8]{0:T(128)S(1)} %copy-done.7, bf16[2,2,2,2,48,768]{5,4,3,2,1,0:T(8,128)(2,1)} %bitcast.91, bf16[2,2,2,2,48,768]{5,4,3,2,1,0:T(8,128)(2,1)} %bitcast.19.refs_2_.refs_4_.refs_20_.refs_22_.refs_38_.refs_40_, ...), custom_call_target="tpu_custom_call" | custom-call | flops 999999995904 | bytes 1 | tf_op jit(solution)/shard_map/combine/pallas_call | solution.py:955
  190.5 1.6 collective-permute-start.21
  192.2 2.6 %collective-permute-start.22 = (bf16[360,384]{1,0:T(8,128)(2,1)}, bf16[360,384]{1,0:T(8,128)(2,1)}, u32[]{:S(2)}, u32[]{:S(2)}) collective-permute-start(bf16[360,384]{1,0:T(8,128)(2,1)} %get-tuple-element.126), channel_id=1, source_target_pairs={{0,16},{2,18},{4,20},{6,22},{8,24},{10,26},{12,28},{14,30},{16,0},... | collective-permute-start | bytes 829448 | tf_op jit(solution)/shard_map/ppermute | solution.py:823
  195.0 2.8 %assemble.2 = (f32[192,768]{1,0:T(8,128)}, f32[48,3072]{1,0:T(8,128)}, f32[48,768]{1,0:T(8,128)}) custom-call(s32[8]{0:T(128)S(1)} %copy-done.7, f32[432,384]{1,0:T(8,128)S(1)} %copy-done.9, f32[432,384]{1,0:T(8,128)} %collective-permute-done.24.other_ref), custom_call_target="tpu_custom_call" | custom-call | flops 999999995904 | bytes 1 | tf_op jit(solution)/shard_map/assemble/pallas_call | solution.py:1002
  197.8 3.1 %collective-permute-done.21.refs_19_ = bf16[360,384]{1,0:T(8,128)(2,1)} collective-permute-done((bf16[360,384]{1,0:T(8,128)(2,1)}, bf16[360,384]{1,0:T(8,128)(2,1)}, u32[]{:S(2)}, u32[]{:S(2)}) %collective-permute-start.21) | collective-permute-done | bytes 276512 | tf_op jit(solution)/shard_map/ppermute | solution.py:823
  201.0 13.1 %collective-permute-done.22.refs_20_ = bf16[360,384]{1,0:T(8,128)(2,1)} collective-permute-done((bf16[360,384]{1,0:T(8,128)(2,1)}, bf16[360,384]{1,0:T(8,128)(2,1)}, u32[]{:S(2)}, u32[]{:S(2)}) %collective-permute-start.22) | collective-permute-done | bytes 276512 | tf_op jit(solution)/shard_map/ppermute | solution.py:823
  214.1 2.9 %combine.15 = (f32[208,384]{1,0:T(8,128)S(1)}, f32[72,768]{1,0:T(8,128)}) custom-call(s32[8]{0:T(128)S(1)} %copy-done.7, bf16[2,2,2,2,48,768]{5,4,3,2,1,0:T(8,128)(2,1)} %bitcast.97, bf16[2,2,2,2,48,768]{5,4,3,2,1,0:T(8,128)(2,1)} %bitcast.19.refs_2_.refs_4_.refs_20_.refs_22_.refs_38_.refs_40_, bf16[2,2,2,2,48,768]{5,4,3,2,1,0:T(8,128)(2,1)} %bitcast.98, ...), custom_call_target="tpu_custom_call" | custom-call | flops 999999995904 | bytes 1 | tf_op jit(solution)/shard_map/combine/pallas_call | solution.py:955
  217.0 1.6 collective-permute-done.25.other_ref
  218.6 1.4 assemble.3
  220.0 0.7 copy.41
  (72 shorter events, 4.6 us)
Async XLA Ops:
  2.6 11.6 %copy-start.4 = (f32[768]{0:T(1024)S(1)}, f32[768]{0:T(1024)}, u32[]{:S(2)}) copy-start(f32[768]{0:T(1024)} %bias_ref.1) | copy-start | bytes 9220
  13.7 4.0 %collective-permute-start = (bf16[512,1536]{1,0:T(8,128)(2,1)}, bf16[512,1536]{1,0:T(8,128)(2,1)S(1)}, u32[]{:S(2)}, u32[]{:S(2)}) collective-permute-start(bf16[512,1536]{1,0:T(8,128)(2,1)} %get-tuple-element.83.ko_ref.vo_ref), channel_id=1, source_target_pairs={{0,1},{1,0},{2,3},{3,2},{4,5},{5,4},{6,7},{7,6},{8,9},{9,8},{10,11... | collective-permute-start | bytes 4718600 | tf_op jit(solution)/shard_map/ppermute | solution.py:818
  14.2 1.1 copy-start
  15.3 3.7 %copy-start.7 = (s32[8]{0:T(128)S(1)}, s32[8]{0:T(128)}, u32[]{:S(2)}) copy-start(s32[8]{0:T(128)} %stack.31.place_ref.refs_0_) | copy-start | bytes 100
  17.4 50.0 %copy-start.2 = (bf16[512,768]{1,0:T(8,128)(2,1)}, bf16[512,768]{1,0:T(8,128)(2,1)S(1)}, u32[]{:S(2)}) copy-start(bf16[512,768]{1,0:T(8,128)(2,1)S(1)} %queries.1.q_ref) | copy-start | bytes 2359300
  17.7 19.4 %copy-start.10 = (f32[3072]{0:T(1024)S(1)}, f32[3072]{0:T(1024)}, u32[]{:S(2)}) copy-start(f32[3072]{0:T(1024)} %param.42) | copy-start | bytes 36868
  17.7 19.4 %copy-start.11 = (f32[768]{0:T(1024)S(1)}, f32[768]{0:T(1024)}, u32[]{:S(2)}) copy-start(f32[768]{0:T(1024)} %bias_out_ref.1) | copy-start | bytes 9220
  17.7 19.4 %copy-start.12 = (f32[768]{0:T(1024)S(1)}, f32[768]{0:T(1024)}, u32[]{:S(2)}) copy-start(f32[768]{0:T(1024)} %gain_ref.4) | copy-start | bytes 9220
  17.7 19.4 %copy-start.13 = (f32[768]{0:T(1024)S(1)}, f32[768]{0:T(1024)}, u32[]{:S(2)}) copy-start(f32[768]{0:T(1024)} %offset_ref.3) | copy-start | bytes 9220
  17.7 19.4 %copy-start.14 = (f32[768]{0:T(1024)S(1)}, f32[768]{0:T(1024)}, u32[]{:S(2)}) copy-start(f32[768]{0:T(1024)} %bias_down_ref.1) | copy-start | bytes 9220
  17.8 1.2 copy-start.21
  36.2 0.9 copy-start.16
  65.9 0.9 copy-start.17
  66.8 78.0 %copy-start.15 = (bf16[768,384]{1,0:T(8,128)(2,1)}, bf16[768,384]{1,0:T(8,128)(2,1)S(1)}, u32[]{:S(2)}) copy-start(bf16[768,384]{1,0:T(8,128)(2,1)S(1)} %get-tuple-element.95) | copy-start | bytes 1769476
  66.8 13.8 %collective-permute-start.2 = (bf16[3072,384]{1,0:T(8,128)(2,1)}, bf16[3072,384]{1,0:T(8,128)(2,1)}, u32[]{:S(2)}, u32[]{:S(2)}) collective-permute-start(bf16[3072,384]{1,0:T(8,128)(2,1)} %get-tuple-element.94), channel_id=1, source_target_pairs={{0,1},{1,0},{2,3},{3,2},{4,5},{5,4},{6,7},{7,6},{8,9},{9,8},{10,11... | collective-permute-start | bytes 7077896 | tf_op jit(solution)/shard_map/ppermute | solution.py:818
  66.9 13.7 %collective-permute-start.3 = (bf16[768,384]{1,0:T(8,128)(2,1)}, bf16[768,384]{1,0:T(8,128)(2,1)}, u32[]{:S(2)}, u32[]{:S(2)}) collective-permute-start(bf16[768,384]{1,0:T(8,128)(2,1)} %get-tuple-element.96), channel_id=1, source_target_pairs={{0,1},{1,0},{2,3},{3,2},{4,5},{5,4},{6,7},{7,6},{8,9},{9,8},{10,11... | collective-permute-start | bytes 1769480 | tf_op jit(solution)/shard_map/ppermute | solution.py:818
  67.3 13.3 %collective-permute-start.4 = (bf16[768,1536]{1,0:T(8,128)(2,1)}, bf16[768,1536]{1,0:T(8,128)(2,1)}, u32[]{:S(2)}, u32[]{:S(2)}) collective-permute-start(bf16[768,1536]{1,0:T(8,128)(2,1)} %get-tuple-element.98), channel_id=1, source_target_pairs={{0,1},{1,0},{2,3},{3,2},{4,5},{5,4},{6,7},{7,6},{8,9},{9,8},{10,11... | collective-permute-start | bytes 7077896 | tf_op jit(solution)/shard_map/ppermute | solution.py:818
  80.1 5.3 %copy-start.19 = (bf16[512,512]{1,0:T(8,128)(2,1)}, bf16[512,512]{1,0:T(8,128)(2,1)S(1)}, u32[]{:S(2)}) copy-start(bf16[512,512]{1,0:T(8,128)(2,1)S(1)} %get-tuple-element.90.refs_13_.dq_ref) | copy-start | bytes 1572868
  80.1 17.1 %collective-permute-start.1 = (bf16[2,512,512]{2,1,0:T(8,128)(2,1)}, bf16[2,512,512]{2,1,0:T(8,128)(2,1)}, u32[]{:S(2)}, u32[]{:S(2)}) collective-permute-start(bf16[2,512,512]{2,1,0:T(8,128)(2,1)} %get-tuple-element.92), channel_id=1, source_target_pairs={{0,1},{1,0},{2,3},{3,2},{4,5},{5,4},{6,7},{7,6},{8,9},{9,8},{10,11... | collective-permute-start | bytes 3145736 | tf_op jit(solution)/shard_map/ppermute | solution.py:818
  85.4 35.8 %collective-permute-start.10 = (bf16[2,2,2,240,384]{4,3,2,1,0:T(8,128)(2,1)}, bf16[2,2,2,240,384]{4,3,2,1,0:T(8,128)(2,1)}, u32[]{:S(2)}, u32[]{:S(2)}) collective-permute-start(bf16[2,2,2,240,384]{4,3,2,1,0:T(8,128)(2,1)} %get-tuple-element.99.rest_0_), channel_id=1, source_target_pairs={{0,2},{2,0},{4,6},{6,4},{8,10},{10,8},{12,14},{14,12},{16,18},{18,... | collective-permute-start | bytes 4423688 | tf_op jit(solution)/shard_map/ppermute | solution.py:823
  88.0 32.7 %collective-permute-start.11 = (bf16[2,2,2,192,384]{4,3,2,1,0:T(8,128)(2,1)}, bf16[2,2,2,192,384]{4,3,2,1,0:T(8,128)(2,1)}, u32[]{:S(2)}, u32[]{:S(2)}) collective-permute-start(bf16[2,2,2,192,384]{4,3,2,1,0:T(8,128)(2,1)} %get-tuple-element.100.rest_1_), channel_id=1, source_target_pairs={{0,4},{2,6},{4,0},{6,2},{8,12},{10,14},{12,8},{14,10},{16,20},{18,... | collective-permute-start | bytes 3538952 | tf_op jit(solution)/shard_map/ppermute | solution.py:823
  89.5 7.7 %copy-start.1 = (bf16[512,768]{1,0:T(8,128)(2,1)S(1)}, bf16[512,768]{1,0:T(8,128)(2,1)}, u32[]{:S(2)}) copy-start(bf16[512,768]{1,0:T(8,128)(2,1)} %get-tuple-element.82.normed_ref) | copy-start | bytes 2359300
  89.5 7.7 %copy-start.20 = (bf16[512,512]{1,0:T(8,128)(2,1)S(1)}, bf16[512,512]{1,0:T(8,128)(2,1)}, u32[]{:S(2)}) copy-start(bf16[512,512]{1,0:T(8,128)(2,1)} %copy-done.19) | copy-start | bytes 1572868
  97.2 8.1 %collective-permute-start.6 = (bf16[2,512,256]{2,1,0:T(8,128)(2,1)}, bf16[2,512,256]{2,1,0:T(8,128)(2,1)}, u32[]{:S(2)}, u32[]{:S(2)}) collective-permute-start(bf16[2,512,256]{2,1,0:T(8,128)(2,1)} %get-tuple-element.105), channel_id=1, source_target_pairs={{0,1},{1,0},{2,3},{3,2},{4,5},{5,4},{6,7},{7,6},{8,9},{9,8},{10,11... | collective-permute-start | bytes 1572872 | tf_op jit(solution)/shard_map/ppermute | solution.py:818
  97.2 8.0 %copy-start.3 = (f32[768]{0:T(1024)S(1)}, f32[768]{0:T(1024)}, u32[]{:S(2)}) copy-start(f32[768]{0:T(1024)} %gain_ref.5) | copy-start | bytes 9220
  97.2 8.0 %copy-start.5 = (f32[1,512]{1,0:T(1,128)S(1)}, f32[1,512]{1,0:T(1,128)}, u32[]{:S(2)}) copy-start(f32[1,512]{1,0:T(1,128)} %expression_ref.3) | copy-start | bytes 6148
  104.6 10.1 %collective-permute-start.5 = (bf16[768,768]{1,0:T(8,128)(2,1)}, bf16[768,768]{1,0:T(8,128)(2,1)}, u32[]{:S(2)}, u32[]{:S(2)}) collective-permute-start(bf16[768,768]{1,0:T(8,128)(2,1)} %get-tuple-element.103), channel_id=1, source_target_pairs={{0,1},{1,0},{2,3},{3,2},{4,5},{5,4},{6,7},{7,6},{8,9},{9,8},{10,11... | collective-permute-start | bytes 3538952 | tf_op jit(solution)/shard_map/ppermute | solution.py:818
  105.2 9.6 %copy-start.6 = (s32[1,512]{1,0:T(1,128)S(1)}, s32[1,512]{1,0:T(1,128)}, u32[]{:S(2)}) copy-start(s32[1,512]{1,0:T(1,128)} %ids_ref.5) | copy-start | bytes 6148
  114.3 14.2 %collective-permute-start.8 = (bf16[768,768]{1,0:T(8,128)(2,1)}, bf16[768,768]{1,0:T(8,128)(2,1)}, u32[]{:S(2)}, u32[]{:S(2)}) collective-permute-start(bf16[768,768]{1,0:T(8,128)(2,1)} %get-tuple-element.113), channel_id=1, source_target_pairs={{0,1},{1,0},{2,3},{3,2},{4,5},{5,4},{6,7},{7,6},{8,9},{9,8},{10,11... | collective-permute-start | bytes 3538952 | tf_op jit(solution)/shard_map/ppermute | solution.py:818
  114.3 14.1 %collective-permute-start.9 = (bf16[16,16,384]{2,1,0:T(8,128)(2,1)}, bf16[16,16,384]{2,1,0:T(8,128)(2,1)}, u32[]{:S(2)}, u32[]{:S(2)}) collective-permute-start(bf16[16,16,384]{2,1,0:T(8,128)(2,1)} %get-tuple-element.115), channel_id=1, source_target_pairs={{0,1},{1,0},{2,3},{3,2},{4,5},{5,4},{6,7},{7,6},{8,9},{9,8},{10,11... | collective-permute-start | bytes 589832 | tf_op jit(solution)/shard_map/ppermute | solution.py:818
  114.8 1.1 copy-start.18
  118.3 10.2 %collective-permute-start.7 = (bf16[1152,768]{1,0:T(8,128)(2,1)}, bf16[1152,768]{1,0:T(8,128)(2,1)}, u32[]{:S(2)}, u32[]{:S(2)}) collective-permute-start(bf16[1152,768]{1,0:T(8,128)(2,1)} %gene_rows.2.after_ref), channel_id=1, source_target_pairs={{0,1},{1,0},{2,3},{3,2},{4,5},{5,4},{6,7},{7,6},{8,9},{9,8},{10,11... | collective-permute-start | bytes 5308424 | tf_op jit(solution)/shard_map/ppermute | solution.py:818
  125.2 19.7 %collective-permute-start.14 = (bf16[2,2,240,384]{3,2,1,0:T(8,128)(2,1)}, bf16[2,2,240,384]{3,2,1,0:T(8,128)(2,1)}, u32[]{:S(2)}, u32[]{:S(2)}) collective-permute-start(bf16[2,2,240,384]{3,2,1,0:T(8,128)(2,1)} %get-tuple-element.116.refs_15_), channel_id=1, source_target_pairs={{0,4},{2,6},{4,0},{6,2},{8,12},{10,14},{12,8},{14,10},{16,20},{18,... | collective-permute-start | bytes 2211848 | tf_op jit(solution)/shard_map/ppermute | solution.py:823
  126.9 16.6 %collective-permute-start.15 = (bf16[2,2,192,384]{3,2,1,0:T(8,128)(2,1)}, bf16[2,2,192,384]{3,2,1,0:T(8,128)(2,1)}, u32[]{:S(2)}, u32[]{:S(2)}) collective-permute-start(bf16[2,2,192,384]{3,2,1,0:T(8,128)(2,1)} %get-tuple-element.117.refs_16_), channel_id=1, source_target_pairs={{0,2},{2,0},{4,6},{6,4},{8,10},{10,8},{12,14},{14,12},{16,18},{18,... | collective-permute-start | bytes 1769480 | tf_op jit(solution)/shard_map/ppermute | solution.py:823
  128.4 1.1 copy-start.8
  133.9 30.1 %collective-permute-start.12 = (bf16[2,2,2,168,384]{4,3,2,1,0:T(8,128)(2,1)}, bf16[2,2,2,168,384]{4,3,2,1,0:T(8,128)(2,1)}, u32[]{:S(2)}, u32[]{:S(2)}) collective-permute-start(bf16[2,2,2,168,384]{4,3,2,1,0:T(8,128)(2,1)} %get-tuple-element.118.refs_49_), channel_id=1, source_target_pairs={{0,2},{2,0},{4,6},{6,4},{8,10},{10,8},{12,14},{14,12},{16,18},{18,... | collective-permute-start | bytes 3096584 | tf_op jit(solution)/shard_map/ppermute | solution.py:823
  134.5 33.6 %collective-permute-start.13 = (bf16[2,2,2,184,384]{4,3,2,1,0:T(8,128)(2,1)}, bf16[2,2,2,184,384]{4,3,2,1,0:T(8,128)(2,1)}, u32[]{:S(2)}, u32[]{:S(2)}) collective-permute-start(bf16[2,2,2,184,384]{4,3,2,1,0:T(8,128)(2,1)} %get-tuple-element.119.refs_50_), channel_id=1, source_target_pairs={{0,4},{2,6},{4,0},{6,2},{8,12},{10,14},{12,8},{14,10},{16,20},{18,... | collective-permute-start | bytes 3391496 | tf_op jit(solution)/shard_map/ppermute | solution.py:823
  148.9 26.0 %collective-permute-start.18 = (bf16[432,384]{1,0:T(8,128)(2,1)}, bf16[432,384]{1,0:T(8,128)(2,1)}, u32[]{:S(2)}, u32[]{:S(2)}) collective-permute-start(bf16[432,384]{1,0:T(8,128)(2,1)} %get-tuple-element.120.refs_17_), channel_id=1, source_target_pairs={{0,8},{2,10},{4,12},{6,14},{8,0},{10,2},{12,4},{14,6},{16,24},{18,... | collective-permute-start | bytes 995336 | tf_op jit(solution)/shard_map/ppermute | solution.py:823
  150.8 25.9 %collective-permute-start.19 = (bf16[432,384]{1,0:T(8,128)(2,1)}, bf16[432,384]{1,0:T(8,128)(2,1)}, u32[]{:S(2)}, u32[]{:S(2)}) collective-permute-start(bf16[432,384]{1,0:T(8,128)(2,1)} %get-tuple-element.121.refs_18_), channel_id=1, source_target_pairs={{0,16},{2,18},{4,20},{6,22},{8,24},{10,26},{12,28},{14,30},{16,0},... | collective-permute-start | bytes 995336 | tf_op jit(solution)/shard_map/ppermute | solution.py:823
  153.4 23.4 %collective-permute-start.20 = (bf16[432,384]{1,0:T(8,128)(2,1)}, bf16[432,384]{1,0:T(8,128)(2,1)}, u32[]{:S(2)}, u32[]{:S(2)}) collective-permute-start(bf16[432,384]{1,0:T(8,128)(2,1)} %get-tuple-element.122.refs_19_), channel_id=1, source_target_pairs={{0,24},{2,26},{4,28},{6,30},{8,16},{10,18},{12,20},{14,22},{16,8},... | collective-permute-start | bytes 995336 | tf_op jit(solution)/shard_map/ppermute | solution.py:823
  171.8 13.1 %collective-permute-start.16 = (bf16[2,2,168,384]{3,2,1,0:T(8,128)(2,1)}, bf16[2,2,168,384]{3,2,1,0:T(8,128)(2,1)}, u32[]{:S(2)}, u32[]{:S(2)}) collective-permute-start(bf16[2,2,168,384]{3,2,1,0:T(8,128)(2,1)} %get-tuple-element.123.refs_20_), channel_id=1, source_target_pairs={{0,4},{2,6},{4,0},{6,2},{8,12},{10,14},{12,8},{14,10},{16,20},{18,... | collective-permute-start | bytes 1548296 | tf_op jit(solution)/shard_map/ppermute | solution.py:823
  173.3 13.5 %collective-permute-start.17 = (bf16[2,2,184,384]{3,2,1,0:T(8,128)(2,1)}, bf16[2,2,184,384]{3,2,1,0:T(8,128)(2,1)}, u32[]{:S(2)}, u32[]{:S(2)}) collective-permute-start(bf16[2,2,184,384]{3,2,1,0:T(8,128)(2,1)} %get-tuple-element.124.refs_21_), channel_id=1, source_target_pairs={{0,2},{2,0},{4,6},{6,4},{8,10},{10,8},{12,14},{14,12},{16,18},{18,... | collective-permute-start | bytes 1695752 | tf_op jit(solution)/shard_map/ppermute | solution.py:823
  180.2 14.8 %collective-permute-start.24 = (f32[432,384]{1,0:T(8,128)}, f32[432,384]{1,0:T(8,128)}, u32[]{:S(2)}, u32[]{:S(2)}) collective-permute-start(f32[432,384]{1,0:T(8,128)} %combine.13.refs_55_.own_ref), channel_id=1, source_target_pairs={{0,1},{1,0},{2,3},{3,2},{4,5},{5,4},{6,7},{7,6},{8,9},{9,8},{10,11... | collective-permute-start | bytes 1990664 | tf_op jit(solution)/shard_map/ppermute | solution.py:818
  186.9 8.1 %copy-start.9 = (f32[432,384]{1,0:T(8,128)S(1)}, f32[432,384]{1,0:T(8,128)}, u32[]{:S(2)}) copy-start(f32[432,384]{1,0:T(8,128)} %combine.13.refs_55_.own_ref) | copy-start | bytes 1990660
  190.5 10.4 %collective-permute-start.21 = (bf16[360,384]{1,0:T(8,128)(2,1)}, bf16[360,384]{1,0:T(8,128)(2,1)}, u32[]{:S(2)}, u32[]{:S(2)}) collective-permute-start(bf16[360,384]{1,0:T(8,128)(2,1)} %get-tuple-element.125), channel_id=1, source_target_pairs={{0,8},{2,10},{4,12},{6,14},{8,0},{10,2},{12,4},{14,6},{16,24},{18,... | collective-permute-start | bytes 829448 | tf_op jit(solution)/shard_map/ppermute | solution.py:823
  192.2 21.9 %collective-permute-start.22 = (bf16[360,384]{1,0:T(8,128)(2,1)}, bf16[360,384]{1,0:T(8,128)(2,1)}, u32[]{:S(2)}, u32[]{:S(2)}) collective-permute-start(bf16[360,384]{1,0:T(8,128)(2,1)} %get-tuple-element.126), channel_id=1, source_target_pairs={{0,16},{2,18},{4,20},{6,22},{8,24},{10,26},{12,28},{14,30},{16,0},... | collective-permute-start | bytes 829448 | tf_op jit(solution)/shard_map/ppermute | solution.py:823
  194.8 19.3 %collective-permute-start.23 = (bf16[360,384]{1,0:T(8,128)(2,1)}, bf16[360,384]{1,0:T(8,128)(2,1)}, u32[]{:S(2)}, u32[]{:S(2)}) collective-permute-start(bf16[360,384]{1,0:T(8,128)(2,1)} %get-tuple-element.127), channel_id=1, source_target_pairs={{0,24},{2,26},{4,28},{6,30},{8,16},{10,18},{12,20},{14,22},{16,8},... | collective-permute-start | bytes 829448 | tf_op jit(solution)/shard_map/ppermute | solution.py:823
  217.0 1.6 collective-permute-start.25

commit v3 on v2

--- a/solution.py
+++ b/solution.py
@@ -10,9 +10,10 @@
 HEAD_DIM = 64
 VOC_DEV = 72
 EPSILON = 1e-05
+LANES = 384
 LOW = jnp.bfloat16
 WIDE = jnp.float32
-GRANT = 52 << 20
+GRANT = 44 << 20
 
 
 LONG = pl.CostEstimate(flops=10**12, bytes_accessed=1, transcendentals=0)
@@ -49,6 +50,14 @@
 
 def whole(shape):
     return pl.BlockSpec(shape, lambda *_: (0,) * len(shape))
+
+
+def up16(rows):
+    return -(-rows // 16) * 16
+
+
+def unread(arrays):
+    return [pl.BlockSpec(memory_space=pl.ANY)] * len(arrays)
 
 
 def params(grant=GRANT):
@@ -178,23 +187,27 @@
         dead = jnp.where(place < place_ref[1 + index], 0.0, -1e30).astype(LOW)
         halves.append((k_ref[...], dead))
     values = [vo_ref[...].T, vr_ref[...].T]
-    outs = []
+    ones = jnp.ones((16, rows), LOW)
+    scored, outs = [], []
     for head in range(2):
         inside = (lane < HEAD_DIM) if head == 0 else (lane >= HEAD_DIM)
         spare = HEAD_DIM * (1 - head)
         asked = jnp.where(inside, queries, jnp.where(lane == spare, 1.0, 0.0).astype(LOW))
-        scores = [dot(jnp.where(lane == spare, dead, keys), asked, 1, 1) for keys, dead in halves]
+        scored.append(
+            [dot(jnp.where(lane == spare, dead, keys), asked, 1, 1) for keys, dead in halves]
+        )
+    for head in range(2):
+        scores = scored[head]
         top = jnp.maximum(*[jnp.max(part, 0, keepdims=True) for part in scores])
-        mass, mixed = 0.0, 0.0
+        mixed = 0.0
         for index in range(2):
-            probs = jnp.exp(scores[index] - top)
-            mass = mass + column_sums(probs)
-            low = probs.astype(LOW)
+            low = jnp.exp(scores[index] - top).astype(LOW)
             p_ref[head, index * rows : (index + 1) * rows, :] = low
-            mixed = mixed + dot(values[index][head * HEAD_DIM : (head + 1) * HEAD_DIM], low)
-        inverse = 1.0 / mass
+            own = values[index][head * HEAD_DIM : (head + 1) * HEAD_DIM]
+            mixed = mixed + dot(jnp.concatenate([own, ones], 0), low)
+        inverse = 1.0 / mixed[HEAD_DIM : HEAD_DIM + 1]
         c_ref[0, head : head + 1, :] = inverse
-        outs.append(mixed * inverse)
+        outs.append(mixed[:HEAD_DIM] * inverse)
     out_ref[...] = jnp.concatenate(outs, 0).T.astype(LOW)
 
 
@@ -299,7 +312,7 @@
             pl.BlockSpec((2, 2 * rows, rows), lambda j: (start + j, 0, 0)),
             pl.BlockSpec((1, 2, rows), lambda j: (start + j, 0, 0)),
         ]
-        + [pl.BlockSpec(memory_space=pl.ANY)] * len(after),
+        + unread(after),
         out_specs=[block(0), both, both],
         out_shape=[
             shaped((rows, 128 * count), LOW),
@@ -326,91 +339,67 @@
     w_down_ref,
     bias_down_ref,
     output_ref,
-    g_residual_ref,
-    g_attended_ref,
+    residual_ref,
+    g_normed_ref,
     up_send_ref,
     up_keep_ref,
     down_send_ref,
     down_keep_ref,
-    out_send_ref,
-    out_keep_ref,
-    vectors_ref,
     bias_up_grad_ref,
-    residual_ref,
     normed_ref,
     turned_ref,
     total_ref,
-    g_normed_ref,
     g_out_ref,
+    g_halves_ref,
 ):
     step, steps = pl.program_id(0), pl.num_programs(0)
     rows, width = attended_ref.shape
-    tile = w_up_ref.shape[1]
+    half = width // 2
     mine = place_ref[0]
-    own, other = half_of(mine, width // 2), half_of(1 - mine, width // 2)
     alive = lax.broadcasted_iota(jnp.int32, (rows, 1), 0) < place_ref[1]
 
     @pl.when(step == 0)
     def _():
-        residual = embedded_ref[...] + (dot(attended_ref[...], w_out_ref[...]) + bias_out_ref[...][None])
+        residual = embedded_ref[...] + (
+            dot(attended_ref[...], w_out_ref[...]) + bias_out_ref[...][None]
+        )
         residual_ref[...] = residual
         unit, _ = normalize(residual)
         normed = unit * gain_ref[...][None] + offset_ref[...][None]
         normed_ref[...] = normed.astype(LOW)
         turned_ref[...] = normed.T.astype(LOW)
         g_out_ref[...] = jnp.where(alive, cotangent_ref[...].astype(WIDE), 0.0).astype(LOW)
+        g_halves_ref[:, :half] = g_out_ref[:, half_of(1 - mine, half)]
+        g_halves_ref[:, half:] = g_out_ref[:, half_of(mine, half)]
         total_ref[...] = jnp.zeros_like(total_ref)
         g_normed_ref[...] = jnp.zeros_like(g_normed_ref)
 
-    g_out = g_out_ref[...]
     hidden = dot(normed_ref[...], w_up_ref[...]) + bias_up_ref[...]
-    g_act = dot(g_out, w_down_ref[...], 1, 1)
+    g_act = dot(g_out_ref[...], w_down_ref[...], 1, 1)
     share = 0.5 * (1.0 + lax.erf(hidden * 0.5**0.5))
     density = jnp.exp(-0.5 * hidden * hidden) * 0.3989422804014327
     activated = (hidden * share).astype(LOW)
-    g_wide = g_act * (share + hidden * density)
-    g_hidden = g_wide.astype(LOW)
+    g_hidden = (g_act * (share + hidden * density)).astype(LOW)
     total_ref[...] += dot(activated, w_down_ref[...])
     g_normed_ref[...] += dot(g_hidden, w_up_ref[...], 1, 1)
-    down_send_ref[...] = dot(activated, g_out_ref[:, other], 0, 0).astype(LOW)
-    down_keep_ref[...] = dot(activated, g_out_ref[:, own], 0, 0).astype(LOW)
+    down = dot(activated, g_halves_ref[...], 0, 0).astype(LOW)
+    down_send_ref[...] = down[:, :half]
+    down_keep_ref[...] = down[:, half:]
     up = dot(turned_ref[...], g_hidden).astype(LOW)
     bias_up_grad_ref[...] = column_sums(g_hidden.astype(WIDE))
-    columns = pl.ds(pl.multiple_of(lax.rem(step, steps // 2) * tile, 128), tile)
 
     @pl.when(step < steps // 2)
     def _():
-        up_send_ref[:, columns] = up
+        up_send_ref[...] = up
 
     @pl.when(step >= steps // 2)
     def _():
-        up_keep_ref[:, columns] = up
+        up_keep_ref[...] = up
 
     @pl.when(step == steps - 1)
     def _():
-        residual = residual_ref[...]
-        final = residual + (total_ref[...] + bias_down_ref[...][None])
+        final = residual_ref[...] + (total_ref[...] + bias_down_ref[...][None])
         output_ref[...] = jnp.where(alive, final, 0.0).astype(LOW)
-        unit, scale = normalize(residual)
-        g_final = g_out_ref[...].astype(WIDE)
-        g_normed = g_normed_ref[...]
-        g_residual = g_final + norm_back(g_normed, unit, scale, gain_ref[...][None])
-        g_residual_ref[...] = g_residual
-        g_branch = g_residual.astype(LOW)
-        g_attended_ref[...] = dot(g_branch, w_out_ref[...], 1, 1).astype(LOW)
-        vectors_ref[...] = jnp.concatenate(
-            [
-                column_sums(g_branch.astype(WIDE)),
-                column_sums(g_normed * unit),
-                column_sums(g_normed),
-                column_sums(g_final),
-            ],
-            0,
-        )
-        normed_ref[...] = g_branch
-        attended = attended_ref[...].astype(WIDE).T.astype(LOW)
-        out_send_ref[...] = dot(attended, normed_ref[:, other]).astype(LOW)
-        out_keep_ref[...] = dot(attended, normed_ref[:, own]).astype(LOW)
 
 
 def feed_forward(
@@ -455,43 +444,32 @@
                 whole((rows, width)),
                 whole((rows, width)),
                 whole((rows, width)),
-                whole((width, units // 2)),
-                whole((width, units // 2)),
+                pl.BlockSpec((width, tile), lambda j, _: (0, jnp.minimum(j, steps // 2 - 1))),
+                pl.BlockSpec((width, tile), lambda j, _: (0, jnp.maximum(j - steps // 2, 0))),
                 down_tile,
                 down_tile,
-                whole((width, width // 2)),
-                whole((width, width // 2)),
-                whole((4, width)),
                 pl.BlockSpec((1, tile), lambda j, place: (0, turn(j, place))),
             ],
             scratch_shapes=[
-                pltpu.VMEM((rows, width), WIDE),
                 pltpu.VMEM((rows, width), LOW),
                 pltpu.VMEM((width, rows), LOW),
                 pltpu.VMEM((rows, width), WIDE),
-                pltpu.VMEM((rows, width), WIDE),
+                pltpu.VMEM((rows, width), LOW),
                 pltpu.VMEM((rows, width), LOW),
             ],
         ),
         out_shape=[
             shaped((rows, width), LOW),
             shaped((rows, width), WIDE),
-            shaped((rows, width), LOW),
+            shaped((rows, width), WIDE),
             shaped((width, units // 2), LOW),
             shaped((width, units // 2), LOW),
             shaped((units, width // 2), LOW),
             shaped((units, width // 2), LOW),
-            shaped((width, width // 2), LOW),
-            shaped((width, width // 2), LOW),
-            shaped((4, width), WIDE),
             shaped((1, units), WIDE),
         ],
         compiler_params=params(),
-        cost_estimate=pl.CostEstimate(
-            flops=12 * rows * width * units + 6 * rows * width * width,
-            bytes_accessed=8 * width * units,
-            transcendentals=2 * rows * units,
-        ),
+        cost_estimate=LONG,
         name="feed_forward",
     )(
         place,
@@ -509,6 +487,85 @@
     )
 
 
+def branch_kernel(
+    place_ref,
+    residual_ref,
+    g_normed_ref,
+    cotangent_ref,
+    attended_ref,
+    w_out_ref,
+    gain_ref,
+    *rest,
+):
+    g_residual_ref, g_attended_ref, out_send_ref, out_keep_ref, vectors_ref, total_ref = rest[-6:]
+    step, steps = pl.program_id(0), pl.num_programs(0)
+    rows, width = residual_ref.shape
+    half = width // 2
+    mine = place_ref[0]
+    alive = step * rows + lax.broadcasted_iota(jnp.int32, (rows, 1), 0) < place_ref[1]
+
+    @pl.when(step == 0)
+    def _():
+        total_ref[...] = jnp.zeros_like(total_ref)
+        vectors_ref[...] = jnp.zeros_like(vectors_ref)
+
+    unit, scale = normalize(residual_ref[...])
+    g_final = jnp.where(alive, cotangent_ref[...].astype(WIDE), 0.0)
+    g_normed = g_normed_ref[...]
+    g_residual = g_final + norm_back(g_normed, unit, scale, gain_ref[...][None])
+    g_residual_ref[...] = g_residual
+    g_branch = g_residual.astype(LOW)
+    g_attended_ref[...] = dot(g_branch, w_out_ref[...], 1, 1).astype(LOW)
+    total_ref[...] += dot(attended_ref[...], g_branch, 0, 0)
+    vectors_ref[...] += jnp.concatenate(
+        [
+            column_sums(g_branch.astype(WIDE)),
+            column_sums(g_normed * unit),
+            column_sums(g_normed),
+            column_sums(g_final),
+        ],
+        0,
+    )
+
+    @pl.when(step == steps - 1)
+    def _():
+        out_send_ref[...] = total_ref[:, half_of(1 - mine, half)].astype(LOW)
+        out_keep_ref[...] = total_ref[:, half_of(mine, half)].astype(LOW)
+
+
+def branch_back(place, residual, g_normed, cotangent, attended, w_out, gain, after):
+    rows, width = residual.shape
+    steps = 2
+    tile = pl.BlockSpec((rows // steps, width), lambda j, _: (j, 0))
+    return pl.pallas_call(
+        branch_kernel,
+        grid_spec=pltpu.PrefetchScalarGridSpec(
+            num_scalar_prefetch=1,
+            grid=(steps,),
+            in_specs=[tile, tile, tile, tile, whole((width, width)), whole((width,))]
+            + unread(after),
+            out_specs=[
+                tile,
+                tile,
+                whole((width, width // 2)),
+                whole((width, width // 2)),
+                whole((4, width)),
+            ],
+            scratch_shapes=[pltpu.VMEM((width, width), WIDE)],
+        ),
+        out_shape=[
+            shaped((rows, width), WIDE),
+            shaped((rows, width), LOW),
+            shaped((width, width // 2), LOW),
+            shaped((width, width // 2), LOW),
+            shaped((4, width), WIDE),
+        ],
+        compiler_params=params(),
+        cost_estimate=LONG,
+        name="branch_back",
+    )(place, residual, g_normed, cotangent, attended, w_out, gain, *after)
+
+
 def project_back(place_ref, normed_turned, dq_ref, own_ref, got_ref, weights, joined_ref, send_ref, keep_ref, bias_ref):
     group = dq_ref.shape[1]
     half = 3 * group // 2
@@ -517,8 +574,9 @@
     for index in range(2):
         total = own_ref[index].astype(WIDE) + got_ref[index].astype(WIDE)
         joined_ref[:, (1 + index) * group : (2 + index) * group] = total.astype(LOW)
-    send_ref[:, :half] = dot(normed_turned, joined_ref[:, half_of(1 - mine, half)]).astype(LOW)
-    keep_ref[:, :half] = dot(normed_turned, joined_ref[:, half_of(mine, half)]).astype(LOW)
+    if send_ref is not None:
+        send_ref[...] = dot(normed_turned, joined_ref[:, half_of(1 - mine, half)]).astype(LOW)
+        keep_ref[...] = dot(normed_turned, joined_ref[:, half_of(mine, half)]).astype(LOW)
     bias_ref[0:1] = column_sums(joined_ref[:, :group].astype(WIDE))
     bias_ref[1:2] = column_sums(joined_ref[:, 2 * group :].astype(WIDE))
     back = 0.0
@@ -537,14 +595,10 @@
     wq_ref,
     wk_ref,
     wv_ref,
-    after_ref,
-    send_ref,
-    keep_ref,
-    bias_ref,
-    part_ref,
-    turned_ref,
-    joined_ref,
+    *rest,
 ):
+    send_ref, keep_ref, bias_ref, part_ref, turned_ref, joined_ref = rest[-6:]
+
     @pl.when(pl.program_id(0) == 0)
     def _():
         turned_ref[...] = normed_ref[...].astype(WIDE).T.astype(LOW)
@@ -583,17 +637,10 @@
     bias_first_ref,
     vectors_ref,
     bias_up_ref,
-    send_ref,
-    keep_ref,
-    g_low_ref,
-    small_send_ref,
-    small_keep_ref,
-    turned_ref,
-    joined_ref,
-    bias_ref,
-    rows_ref,
-    owned_ref,
+    *rest,
 ):
+    send_ref, keep_ref, g_low_ref = rest[-8:-5]
+    turned_ref, joined_ref, bias_ref, rows_ref, owned_ref = rest[-5:]
     rows, width = normed_ref.shape
     half = width // 2
     mine = place_ref[0]
@@ -606,16 +653,25 @@
         got_ref,
         (wq_ref, wk_ref, wv_ref),
         joined_ref,
-        send_ref,
-        keep_ref,
+        None,
+        None,
         bias_ref,
     )
     unit, scale = normalize(embedded_ref[...])
     g_embedded = g_residual_ref[...] + norm_back(back, unit, scale, gain_ref[...][None])
     g_low_ref[...] = g_embedded.astype(LOW)
     prior = prior_ref[...].astype(WIDE).T.astype(LOW)
-    send_ref[:, half:] = dot(prior, g_low_ref[:, half_of(1 - mine, half)]).astype(LOW)
-    keep_ref[:, half:] = dot(prior, g_low_ref[:, half_of(mine, half)]).astype(LOW)
+    count = owned_ref.shape[0]
+    share = width // count
+    for out_ref, side in ((send_ref, 1 - mine), (keep_ref, mine)):
+        know = dot(prior, g_low_ref[:, half_of(side, half)]).astype(LOW)
+        project = dot(
+            turned_ref[...], joined_ref[:, half_of(side, half)]
+        ).astype(LOW)
+        for owner in range(count):
+            entry = slice(owner * share, (owner + 1) * share)
+            out_ref[owner, :share, :half] = project[entry]
+            out_ref[owner, :share, half:] = know[entry]
     expression = jnp.broadcast_to(expression_ref[...], (8, rows)).T[:, :1]
     total = column_sums(g_embedded)
     hot = lax.broadcasted_iota(jnp.int32, (groups, width), 0) == place_ref[3]
@@ -632,8 +688,6 @@
         ],
         0,
     )
-    count = owned_ref.shape[0]
-    share = width // count
     owned_ref[...] = jnp.zeros_like(owned_ref)
     for owner in range(count):
         columns = slice(owner * share, (owner + 1) * share)
@@ -647,8 +701,10 @@
             owned_ref[owner, at + part : at + part + 1, lanes] = bias_up_ref[
                 :, first : first + share
             ]
-    small_send_ref[...] = owned_ref[:, pl.ds(pl.multiple_of((1 - mine) * 16, 16), 16), :].astype(LOW)
-    small_keep_ref[...] = owned_ref[:, pl.ds(pl.multiple_of(mine * 16, 16), 16), :].astype(LOW)
+    low = up16(share)
+    for out_ref, side in ((send_ref, 1 - mine), (keep_ref, mine)):
+        rows_in = pl.ds(pl.multiple_of(side * 16, 16), 16)
+        out_ref[:, low : low + 16, :half] = owned_ref[:, rows_in, :].astype(LOW)
 
 
 def back_specs(rows, width, group, first):
@@ -676,7 +732,7 @@
         grid_spec=pltpu.PrefetchScalarGridSpec(
             num_scalar_prefetch=1,
             grid=(count,),
-            in_specs=back_specs(rows, width, group, 0) + [pl.BlockSpec(memory_space=pl.ANY)],
+            in_specs=back_specs(rows, width, group, 0) + unread(after),
             out_specs=[
                 tile,
                 tile,
@@ -697,7 +753,7 @@
         compiler_params=params(),
         cost_estimate=LONG,
         name="first_back",
-    )(place, normed, dq, own, got, w_qkv, w_qkv, w_qkv, after)
+    )(place, normed, dq, own, got, w_qkv, w_qkv, w_qkv, *after)
 
 
 def last_back(
@@ -719,10 +775,12 @@
     bias_up,
     groups,
     count,
+    after,
 ):
     rows, width = normed.shape
     half = width // 2
     first = width // group - 1
+    entry = up16(width // count) + 16
     return pl.pallas_call(
         functools.partial(last_back_kernel, groups),
         grid_spec=pltpu.PrefetchScalarGridSpec(
@@ -739,13 +797,12 @@
                 whole(bias_first.shape),
                 whole((4, width)),
                 whole(bias_up.shape),
-            ],
+            ]
+            + unread(after),
             out_specs=[
-                whole((width, width)),
-                whole((width, width)),
+                whole((count, entry, width)),
+                whole((count, entry, width)),
                 whole((rows, width)),
-                whole((count, 16, 384)),
-                whole((count, 16, 384)),
             ],
             scratch_shapes=[
                 pltpu.VMEM((width, rows), LOW),
@@ -756,11 +813,9 @@
             ],
         ),
         out_shape=[
-            shaped((width, width), LOW),
-            shaped((width, width), LOW),
+            shaped((count, entry, width), LOW),
+            shaped((count, entry, width), LOW),
             shaped((rows, width), LOW),
-            shaped((count, 16, 384), LOW),
-            shaped((count, 16, 384), LOW),
         ],
         compiler_params=params(),
         cost_estimate=LONG,
@@ -783,10 +838,12 @@
         bias_first,
         vectors,
         bias_up,
-    )
-
-
-def gene_kernel(slots_ref, ids_ref, grad_ref, after_ref, out_ref):
+        *after,
+    )
+
+
+def gene_kernel(slots_ref, ids_ref, grad_ref, *rest):
+    out_ref = rest[-1]
     slots = slots_ref[...]
     rows = grad_ref.shape[0]
     picker = jnp.where(slots == jnp.broadcast_to(ids_ref[...], (slots.shape[0], rows)), 1.0, 0.0)
@@ -804,14 +861,14 @@
             pl.BlockSpec((tile, 1), lambda j: (j, 0)),
             whole((1, rows)),
             whole((rows, width)),
-            pl.BlockSpec(memory_space=pl.ANY),
-        ],
+        ]
+        + unread(after),
         out_specs=pl.BlockSpec((tile, width), lambda j: (j, 0)),
         out_shape=shaped((count, width), LOW),
         compiler_params=params(),
         cost_estimate=LONG,
         name="gene_rows",
-    )(slots, ids, grad, after)
+    )(slots, ids, grad, *after)
 
 
 def swap_cores(array):
@@ -827,137 +884,164 @@
     return lax.dynamic_index_in_dim(array, index, position, keepdims=False)
 
 
-LANES = 384
-
-
-def up16(rows):
-    return -(-rows // 16) * 16
-
-
 class Share:
     QUAD = "quad"
 
     def __init__(self, segments, route):
         self.bits = lax.axis_size("dp").bit_length() - 1
         self.route = list(route)
-        self.rows = [arrays[0].shape[1] for arrays, _ in segments]
-        self.settle()
+        self.rows = []
+        self.sources = []
         dims = tuple(range(self.bits - 1, -1, -1))
-        self.sources = [
-            (array.reshape((2,) * self.bits + array.shape[1:]), dims, block, [(index, 0)])
-            for index, (arrays, block) in enumerate(segments)
-            for array in arrays
-        ]
+        for arrays, blocks, *rows in segments:
+            first, single = len(self.rows), len(blocks) == 1
+            rows = rows[0] if rows else [(0, arrays[0].shape[1])] * len(blocks)
+            self.rows += [size for _, size in rows]
+            parts = [
+                (first + at, rows[at][0], 0 if single else block * LANES)
+                for at, block in enumerate(blocks)
+            ]
+            columns = LANES if single else arrays[0].shape[2]
+            where, height = (0, blocks[0] if single else 0), arrays[0].shape[1]
+            start, size = rows[0]
+            if single and size % 16 == start % size == height % size == 0:
+                where, height = (start // size, where[1]), size
+                parts = [(first, 0, 0)]
+            for array in arrays:
+                shape = (2,) * self.bits + array.shape[1:]
+                self.sources.append((array.reshape(shape), dims, where, (height, columns), parts))
+        self.arriving = []
         self.fixed = ()
+        self.settle_places()
 
     def join(self, other):
         shift = len(self.rows)
+        moved = lambda sources: [
+            source[:4] + ([(index + shift, row, column) for index, row, column in source[4]],)
+            for source in sources
+        ]
         self.rows = self.rows + other.rows
-        self.sources += [
-            (array, dims, block, [(index + shift, start) for index, start in parts])
-            for array, dims, block, parts in other.sources
-        ]
-        self.settle()
+        self.sources += moved(other.sources)
+        self.arriving += moved(other.arriving)
+        self.settle_places()
         return self
 
-    def settle(self):
+    def settle_places(self):
         self.places, place = [], 0
         for rows in self.rows:
             self.places.append(place)
             place += up16(rows)
         self.height = self.places[-1] + self.rows[-1]
 
+    def parts(self):
+        return [(index, place, 0) for index, place in enumerate(self.places)]
+
     def targets(self):
-        step = self.route[0] if self.route else None
-        if step is None:
-            return [{}]
+        step = self.route[0]
         if step == self.QUAD:
             low, high = self.bits - 2, self.bits - 1
             return [{low: way & 1, high: way >> 1} for way in (1, 2, 3)]
         return [{step: 1}]
 
-    def left(self, target):
-        return [bit for bit in range(self.bits - 1, -1, -1) if bit not in self.fixed + tuple(target)]
+    def left(self, target=()):
+        gone = self.fixed + tuple(target)
+        return [bit for bit in range(self.bits - 1, -1, -1) if bit not in gone]
 
     def receive(self, targets, sent):
-        if self.route:
-            self.route.pop(0)
+        self.route.pop(0)
         for target, array in zip(targets, sent):
             mask = sum(flip << bit for bit, flip in target.items())
             dims = tuple(self.left(target))
-            parts = list(enumerate(self.places))
-            self.sources.append((bits_apart(array, mask), dims, 0, parts))
+            self.arriving.append(
+                (bits_apart(array, mask), dims, (0, 0), array.shape[-2:], self.parts())
+            )
         self.fixed += tuple(targets[0])
 
-
-def combine(place, shares, after, last=None):
+    def arrived(self):
+        self.sources, self.arriving = self.sources + self.arriving, []
+
+
+SEND, SETTLE, FINISH = range(3)
+
+
+def combine(place, shares, after, mode=SEND, last=None):
     operands, specs, plan, out_specs, out_shape = [], [], [], [], []
     steps = []
     for share in shares:
-        targets = share.targets()
+        if mode != SETTLE:
+            share.arrived()
+        targets = share.targets() if mode == SEND else [{}]
         steps.append(targets)
+        left = share.left(targets[0]) if mode != FINISH else []
+        quad = len(targets) > 1
+        used = []
+        for array, dims, block, size, parts in share.sources:
+            shape, where, picked = [], [], []
+            for bit in dims:
+                free = bit in left or (quad and bit in targets[0])
+                shape.append(2 if free else None)
+                where.append(None if free else (bit, targets[0].get(bit, 0)))
+                if quad and bit in targets[0]:
+                    picked.append(bit)
+
+            def index(_, place, where=tuple(where), block=block):
+                lead = tuple(
+                    0 if at is None else (1 - place[4 + at[0]] if at[1] else place[4 + at[0]])
+                    for at in where
+                )
+                return lead + block
+
+            specs.append(pl.BlockSpec(tuple(shape) + tuple(size), index))
+            used.append((len(operands), parts))
+            operands.append(array)
         for target in targets:
-            left = share.left(target) if last is None else []
-            used = []
-            for array, dims, block, parts in share.sources:
-                shape, where = [], []
-                for bit in dims:
-                    free = bit in left
-                    shape.append(2 if free else None)
-                    where.append(None if free else (bit, target.get(bit, 0)))
-
-                def index(_, place, where=tuple(where), block=block):
-                    lead = tuple(
-                        0 if at is None else (1 - place[4 + at[0]] if at[1] else place[4 + at[0]])
-                        for at in where
-                    )
-                    return lead + (0, block)
-
-                specs.append(pl.BlockSpec(tuple(shape) + (array.shape[-2], LANES), index))
-                used.append((len(operands), parts))
-                operands.append(array)
-            plan.append((share.rows, share.places, used))
-            if last is None:
+            plan.append((share.rows, share.places, used, target if quad else {}))
+            if mode != FINISH:
                 shape = (2,) * len(left) + (share.height, LANES)
                 out_specs.append(whole(shape))
-                out_shape.append(shaped(shape, LOW))
-    if last is not None:
-        for shape, _ in last:
-            out_specs.append(whole(shape))
-            out_shape.append(shaped(shape, WIDE))
+                out_shape.append(shaped(shape, LOW if mode == SEND else WIDE))
+    for shape, _ in last or []:
+        out_specs.append(whole(shape))
+        out_shape.append(shaped(shape, WIDE))
     count = len(operands)
 
     def kernel(*refs):
-        sources, outs = refs[1 : 1 + count], refs[1 + count + len(after) :]
-
-        def summed(item, segment):
-            rows, _, used = plan[item]
+        place_ref, sources, outs = refs[0], refs[1 : 1 + count], refs[1 + count + len(after) :]
+
+        def summed(item, block):
+            rows, _, used, target = plan[item]
             total = None
+            way = tuple(
+                1 - place_ref[4 + bit] if flip else place_ref[4 + bit]
+                for bit, flip in sorted(target.items(), reverse=True)
+            )
             for operand, parts in used:
-                for index, start in parts:
-                    if index == segment:
-                        part = sources[operand][..., start : start + rows[segment], :].astype(WIDE)
+                for index, row, column in parts:
+                    if index == block:
+                        ref = sources[operand]
+                        spot = (slice(row, row + rows[block]), slice(column, column + LANES))
+                        lead = way + (slice(None),) * (len(ref.shape) - 2 - len(way))
+                        part = ref[lead + spot].astype(WIDE)
                         total = part if total is None else total + part
             return total
 
-        if last is None:
-            for item, out in enumerate(outs):
-                for segment, start in enumerate(plan[item][1]):
-                    out[..., start : start + plan[item][0][segment], :] = summed(
-                        item, segment
-                    ).astype(LOW)
-        else:
+        if mode == FINISH:
             for (_, pieces), out in zip(last, outs):
-                for item, segment, row, column in pieces:
-                    value = summed(item, segment)
+                for item, block, row, column in pieces:
+                    value = summed(item, block)
                     out[row : row + value.shape[0], column : column + LANES] = value
+            return
+        for item, out in enumerate(outs):
+            for block, start in enumerate(plan[item][1]):
+                value = summed(item, block)
+                out[..., start : start + value.shape[-2], :] = value.astype(out.dtype)
 
     outs = pl.pallas_call(
         kernel,
         grid_spec=pltpu.PrefetchScalarGridSpec(
             num_scalar_prefetch=1,
             grid=(1,),
-            in_specs=specs + [pl.BlockSpec(memory_space=pl.ANY)] * len(after),
+            in_specs=specs + unread(after),
             out_specs=out_specs,
         ),
         out_shape=out_shape,
@@ -965,11 +1049,14 @@
         cost_estimate=LONG,
         name="combine",
     )(place, *operands, *after)
-    if last is not None:
-        return outs
     taken = 0
     for share, targets in zip(shares, steps):
-        share.receive(targets, outs[taken : taken + len(targets)])
+        if mode == SEND:
+            share.receive(targets, outs[taken : taken + len(targets)])
+        if mode == SETTLE:
+            share.sources = [
+                (outs[taken], tuple(share.left()), (0, 0), outs[taken].shape[-2:], share.parts())
+            ]
         taken += len(targets)
     return outs
 
@@ -987,11 +1074,11 @@
         if small_row is None:
             return
         group_ref, vector_refs, long_ref = outs[2], outs[3:-1], outs[-1]
-        groups, share = group_ref.shape
+        share, groups = group_ref.shape
         rows = slice(small_row, small_row + 16)
         for start in range(0, groups, 16):
             lanes = slice(start // 32 * 128, start // 32 * 128 + share)
-            group_ref[start : start + 16] = of_core(start // 16 % 2, rows, lanes)
+            group_ref[:, start : start + 16] = of_core(start // 16 % 2, rows, lanes).T
         rest = of_core(0, rows, slice(groups // 32 * 128, groups // 32 * 128 + 128))
         for index, ref in enumerate(vector_refs):
             ref[...] = rest[index, :share]
@@ -1076,15 +1163,12 @@
     attended, probs, inverse = attend(place, queries, kv_own, kv_other)
     (
         block_output,
-        g_residual,
-        g_attended,
+        residual,
+        g_normed_two,
         up_send,
         up_keep,
         down_send,
         down_keep,
-        out_send,
-        out_keep,
-        vectors,
         bias_up_grad,
     ) = feed_forward(
         place,
@@ -1100,6 +1184,16 @@
         w_down,
         bias_down,
     )
+    g_residual, g_attended, out_send, out_keep, vectors = branch_back(
+        place,
+        residual,
+        g_normed_two,
+        cotangent[0],
+        attended,
+        w_out,
+        norm2_gain,
+        [up_send, down_send],
+    )
 
     owners = lambda array: array.reshape(count, -1, array.shape[-1])
     low_bits = list(range(bits - 2))
@@ -1109,23 +1203,29 @@
     blocks = units // 2 // LANES
     out_terms = [owners(out_keep), owners(swap_cores(out_send))]
     down_terms = [owners(down_keep), owners(swap_cores(down_send))]
+    high = units // count
     early = [
-        Share([(down_terms, 0), (out_terms, 0)], low_bits + quad),
-        Share([(up_terms, block) for block in range(blocks)], turned + quad),
+        Share([(down_terms, [0]), (out_terms, [0])], low_bits + quad),
+        Share([(up_terms, list(range(blocks)))], turned + quad),
     ]
+    token = combine(place, early, [])
     dq1, own1, other1 = attend_back(
-        queries, kv_own, kv_other, attended, g_attended, probs, inverse, 0, 4, []
+        queries, kv_own, kv_other, attended, g_attended, probs, inverse, 0, 4, token
     )
     got1 = swap_cores(other1)
-    sent = combine(place, early, [dq1])
     dq2, own2, other2 = attend_back(
-        queries, kv_own, kv_other, attended, g_attended, probs, inverse, 4, 2, sent
+        queries, kv_own, kv_other, attended, g_attended, probs, inverse, 4, 2, [dq1]
     )
     got2 = swap_cores(other2)
     qkv_send, qkv_keep, bias_first, part = first_back(
-        place, normed, dq1, own1, got1, w_qkv, 256, dq2
-    )
-    tail_send, tail_keep, g_low, small_send, small_keep = last_back(
+        place, normed, dq1, own1, got1, w_qkv, 256, [dq2]
+    )
+    qkv = [owners(qkv_keep), owners(swap_cores(qkv_send))]
+    token = [part, qkv_send]
+    for _ in low_bits[1:]:
+        token = combine(place, early, token)
+    early = [early[0].join(early[1])]
+    tail_send, tail_keep, g_low = last_back(
         place,
         normed,
         dq2,
@@ -1144,35 +1244,39 @@
         bias_up_grad,
         group_table.shape[0],
         count,
+        token,
     )
     slot = jnp.arange(count * VOC_DEV, dtype=jnp.int32)[:, None]
     slot = slot + slot // VOC_DEV * VOC_DEV
-    qkv = [owners(qkv_keep), owners(swap_cores(qkv_send))]
-    gene_send = gene_rows(slot + (1 - mine) * VOC_DEV, gene_ids, g_low, qkv[1])
+    gene_send = gene_rows(slot + (1 - mine) * VOC_DEV, gene_ids, g_low, [tail_send, qkv[1]])
     gene_got = swap_cores(gene_send)
-    gene_keep = gene_rows(slot + mine * VOC_DEV, gene_ids, g_low, gene_send)
+    gene_keep = gene_rows(slot + mine * VOC_DEV, gene_ids, g_low, [gene_send])
     share = width // count
-    small = [small_keep, swap_cores(small_send)]
-    tail = [owners(tail_keep), owners(swap_cores(tail_send))]
+    tail = [tail_keep, swap_cores(tail_send)]
     gene = [owners(gene_keep), owners(gene_got)]
+    small_at = up16(share)
     late = [
-        Share([(qkv, 0), (qkv, 1), (gene, 0)], low_bits + quad),
-        Share([(tail, 0), (tail, 1), (small, 0), (gene, 1)], turned + quad),
+        Share([(qkv, [0, 1]), (gene, [0])], low_bits + quad),
+        Share(
+            [
+                (tail, [0], [(0, share)]),
+                (tail, [1], [(0, share)]),
+                (tail, [0], [(small_at, 16)]),
+                (gene, [1]),
+            ],
+            turned + quad,
+        ),
     ]
-    token = [gene_keep]
-    for _ in low_bits[1:]:
-        token = combine(place, early, token)
-    early = [early[0].join(early[1])]
-    token = combine(place, late, token)
+    token = combine(place, late, [gene_keep])
     token = combine(place, early, token)
     for _ in low_bits[1:]:
         token = combine(place, late, token)
+    token = combine(place, late, token, SETTLE)
     late = [late[0].join(late[1])]
     step = up16(share)
-    high = units // count
     layout = [(0, 0, 0, 0), (0, 1, high + blocks * step, 0)]
     layout += [(0, 2 + block, high + block * step, 0) for block in range(blocks)]
-    (own,) = combine(place, early, token, [((high + (blocks + 1) * step, LANES), layout)])
+    (own,) = combine(place, early, token, FINISH, [((high + (blocks + 1) * step, LANES), layout)])
     other = swap_cores(own)
     combine(place, late, [own])
     pieces = []
@@ -1190,7 +1294,8 @@
     own, gene_grad = combine(
         place,
         late,
-        [w_down_share],
+        [w_out_share],
+        FINISH,
         [
             ((4 * step + 16, LANES), layout),
             ((VOC_DEV, width), [(0, 2, 0, 0), (0, 6, 0, LANES)]),
@@ -1210,7 +1315,7 @@
         place,
         own,
         other,
-        [(share, 3 * width), (share, width), (group_table.shape[0], share)]
+        [(share, 3 * width), (share, width), (share, group_table.shape[0])]
         + [(share,)] * 9
         + [(units // count,)],
         pieces,
@@ -1219,7 +1324,7 @@
     return (
         block_output[None],
         gene_grad,
-        group_share,
+        group_share.T,
         w_know_share,
         extra[0],
         extra[1],

time: 222 us -> 212 us (0.955)
  Pallas kernels: 136 us -> 127 us
    pallas_call x1, Pallas kernels: 28.8 us -> 22.9 us  [feed_forward(): pl.pallas_call(ffn_kernel, grid_spec=pltpu.PrefetchScalarGridSpec(num_sca...]
    ppermute x12 -> x11, waiting for transfers between devices: 1.64 us -> 7.22 us  [swap_cores(): return lax.ppermute(array, 'blk', [(0, 1), (1, 0)])]
    ppermute x14, waiting for transfers between devices: 50.2 us -> 44.9 us  [bits_apart(): return lax.ppermute(array, 'dp', [(i, i ^ mask) for i in range(count)])]
    pallas_call x0 -> x1, Pallas kernels: none -> 3.61 us  [branch_back(): pl.pallas_call(branch_kernel, grid_spec=pltpu.PrefetchScalarGridSpec(num_...]
    pallas_call x1, Pallas kernels: 17.3 us -> 14.2 us  [attend(): pl.pallas_call(attend_kernel, grid_spec=pltpu.PrefetchScalarGridSpec(num_...]
    unnamed x45 -> x72, local copies, waits for them, and re-layouts: 7.09 us -> 5.93 us
    pallas_call x8 -> x9, Pallas kernels: 30.9 us -> 31.9 us  [combine(): pl.pallas_call(kernel, grid_spec=pltpu.PrefetchScalarGridSpec(num_scalar_...]
  transfers between devices with their start and end apart: 26 -> 25, of which waited for: 11 -> 11; matrix products, arithmetic and copies ran while one was open for 0% -> 0% of each run, Pallas kernels for 34% -> 33%
where the time goes in v3:
time: 212 us; the launch traced here: 210 us
  Pallas kernels  127 us (60%)
  waiting for transfers between devices  52.1 us (25%)
  starting transfers between devices  21.7 us (10%)
  local copies, waits for them, and re-layouts  6.54 us (3%)
  between operations  2.52 us (1%)
    ppermute x14, waiting for transfers between devices, bits_apart(): return lax.ppermute(array, 'dp', [(i, i ^ mask) for i in range(count)])  44.9 us
    pallas_call x9, Pallas kernels, combine(): pl.pallas_call(kernel, grid_spec=pltpu.PrefetchScalarGridSpec(num_scalar_...  31.9 us
    pallas_call x1, Pallas kernels, feed_forward(): pl.pallas_call(ffn_kernel, grid_spec=pltpu.PrefetchScalarGridSpec(num_sca...  22.9 us
    pallas_call x2, Pallas kernels, attend_back(): pl.pallas_call(attend_back_kernel, grid=(count,), in_specs=[near, near, f...  20.2 us
    ppermute x14, starting transfers between devices, bits_apart(): return lax.ppermute(array, 'dp', [(i, i ^ mask) for i in range(count)])  19.2 us
    pallas_call x1, Pallas kernels, attend(): pl.pallas_call(attend_kernel, grid_spec=pltpu.PrefetchScalarGridSpec(num_...  14.2 us
    pallas_call x1, Pallas kernels, embed(): pl.pallas_call(embed_kernel, grid_spec=pltpu.PrefetchScalarGridSpec(num_s...  11.5 us
    pallas_call x1, Pallas kernels, last_back(): pl.pallas_call(functools.partial(last_back_kernel, groups), grid_spec=plt...  7.29 us
  transfers between devices with their start and end apart: 25, of which 11 were waited for; matrix products, arithmetic and copies ran while one was open for 0% of the time, Pallas kernels for 33%

profile of v3, /device:TPU:0, one launch (start us, length us, event | category | flops | bytes accessed | tf_op | source)
XLA Modules:
  0.0 210.2 jit_solution(183156982795907994)
XLA Ops:
  2.0 0.6 stack.31.place_ref.refs_0_
  2.6 11.5 %embed.1 = (f32[512,768]{1,0:T(8,128)}, bf16[512,768]{1,0:T(8,128)(2,1)}, bf16[512,1536]{1,0:T(8,128)(2,1)}) custom-call(s32[8]{0:T(128)} %stack.31.place_ref.refs_0_, s32[1,512]{1,0:T(1,128)} %ids_ref.5, f32[1,512]{1,0:T(1,128)} %expression_ref.3, bf16[512,768]{1,0:T(8,128)(2,1)} %bitcast.28, bf16[2304,768]{1,0:T(8,128)(2,1)} %table_ref.1, ...), custom_call_target="tpu_custom_call" | custom-call | tf_op jit(solution)/shard_map/embed/pallas_call | solution.py:115
  14.5 1.1 copy-done.2
  15.6 0.8 queries.1.q_ref
  16.5 1.2 collective-permute-done.kr_ref.vr_ref
  17.7 14.2 %attend.1 = (bf16[512,768]{1,0:T(8,128)(2,1)S(1)}, bf16[12,1024,512]{2,1,0:T(8,128)(2,1)}, f32[6,2,512]{2,1,0:T(2,128)S(1)}) custom-call(s32[8]{0:T(128)S(1)} %copy-done.11, bf16[512,768]{1,0:T(8,128)(2,1)S(1)} %queries.1.q_ref, bf16[512,1536]{1,0:T(8,128)(2,1)S(1)} %copy-done.13, bf16[512,1536]{1,0:T(8,128)(2,1)S(1)} %copy-done.13, ...), custom_call_target="tpu_custom_call" | custom-call | flops 3221225472 | bytes 12582912 | tf_op jit(solution)/shard_map/attend/pallas_call | solution.py:218
  32.1 22.9 %feed_forward.1 = (bf16[512,768]{1,0:T(8,128)(2,1)}, f32[512,768]{1,0:T(8,128)S(1)}, f32[512,768]{1,0:T(8,128)S(1)}, bf16[768,1536]{1,0:T(8,128)(2,1)}, bf16[768...) custom-call(s32[8]{0:T(128)S(1)} %copy-done.11, ...), custom_call_target="tpu_custom_call" | custom-call | flops 999999995904 | bytes 1 | tf_op jit(solution)/shard_map/feed_forward/pallas_call | solution.py:425
  55.4 3.6 %branch_back.1 = (f32[512,768]{1,0:T(8,128)S(1)}, bf16[512,768]{1,0:T(8,128)(2,1)S(1)}, bf16[768,384]{1,0:T(8,128)(2,1)S(1)}, bf16[768,384]{1,0:T(8,128)(2,1)S(1)}, f32[4,768]{1,0:T(4,128)S(1)}) custom-call(s32[8]{0:T(128)S(1)} %copy-done.11, f32[512,768]{1,0:T(8,128)S(1)} %get-tuple-element.89.residual_ref, f32[512,768]{1,0:T(8,128)S(1)} %get-tuple-element.90.g_normed_ref, ...), custom_call_target="tpu_custom_call" | custom-call | flops 999999995904 | bytes 1 | tf_op jit(solution)/shard_map/branch_back/pallas_call | solution.py:540
  59.1 1.2 copy-done.33
  60.2 0.9 copy-done.34
  61.9 1.9 collective-permute-done.2
  63.7 1.7 copy-done.24
  65.4 4.8 %combine.9 = (bf16[2,2,2,240,384]{4,3,2,1,0:T(8,128)(2,1)}, bf16[2,2,2,192,384]{4,3,2,1,0:T(8,128)(2,1)}) custom-call(s32[8]{0:T(128)S(1)} %copy-done.11, bf16[2,2,2,2,192,384]{5,4,3,2,1,0:T(8,128)(2,1)S(1)} %bitcast.39, bf16[2,2,2,2,192,384]{5,4,3,2,1,0:T(8,128)(2,1)} %bitcast.13.refs_2_, bf16[2,2,2,2,48,384]{5,4,3,2,1,0:T(8,128)(2,1)S(1)} %bitcast.59, ...), custom_call_target="tpu_custom_call" | custom-call | flops 999999995904 | bytes 1 | tf_op jit(solution)/shard_map/combine/pallas_call | solution.py:1039
  70.3 2.8 %collective-permute-start.7 = (bf16[2,2,2,240,384]{4,3,2,1,0:T(8,128)(2,1)}, bf16[2,2,2,240,384]{4,3,2,1,0:T(8,128)(2,1)}, u32[]{:S(2)}, u32[]{:S(2)}) collective-permute-start(bf16[2,2,2,240,384]{4,3,2,1,0:T(8,128)(2,1)} %get-tuple-element.100.rest_0_), channel_id=1, source_target_pairs={{0,2},{2,0},{4,6},{6,4},{8,10},{10,8},{12,14},{14,12},{16,18},{18,... | collective-permute-start | bytes 4423688 | tf_op jit(solution)/shard_map/ppermute | solution.py:880
  73.1 1.5 collective-permute-start.8
  74.6 12.9 %attend_back.2 = (bf16[512,512]{1,0:T(8,128)(2,1)S(1)}, bf16[2,512,512]{2,1,0:T(8,128)(2,1)S(1)}, bf16[2,512,512]{2,1,0:T(8,128)(2,1)}) custom-call(bf16[512,768]{1,0:T(8,128)(2,1)S(1)} %copy-done.6, bf16[512,1536]{1,0:T(8,128)(2,1)S(1)} %copy-done.14, bf16[512,1536]{1,0:T(8,128)(2,1)S(1)} %copy-done.14, bf16[512,1536]{1,0:T(8,128)(2,1)} %copy-done.15, ...), custom_call_target="tpu_custom_call" | custom-call | flops 999999995904 | bytes 1 | tf_op jit(solution)/shard_map/attend_back/pallas_call | solution.py:301
  87.5 7.4 %attend_back.3 = (bf16[512,256]{1,0:T(8,128)(2,1)S(1)}, bf16[2,512,256]{2,1,0:T(8,128)(2,1)S(1)}, bf16[2,512,256]{2,1,0:T(8,128)(2,1)}) custom-call(bf16[512,768]{1,0:T(8,128)(2,1)S(1)} %copy-done.6, bf16[512,1536]{1,0:T(8,128)(2,1)S(1)} %copy-done.14, bf16[512,1536]{1,0:T(8,128)(2,1)S(1)} %copy-done.14, bf16[512,1536]{1,0:T(8,128)(2,1)S(1)} %copy-done.16, ...), custom_call_target="tpu_custom_call" | custom-call | flops 999999995904 | bytes 1 | tf_op jit(solution)/shard_map/attend_back/pallas_call | solution.py:301
  95.4 6.8 %first_back.1 = (bf16[768,768]{1,0:T(8,128)(2,1)}, bf16[768,768]{1,0:T(8,128)(2,1)S(1)}, f32[2,2,256]{2,1,0:T(2,128)S(1)}, f32[512,768]{1,0:T(8,128)S(1)}) custom-call(s32[8]{0:T(128)S(1)} %copy-done.11, bf16[512,768]{1,0:T(8,128)(2,1)S(1)} %copy-done.3, bf16[512,512]{1,0:T(8,128)(2,1)S(1)} %get-tuple-element.102.rest_0_.dq_ref, ...), custom_call_target="tpu_custom_call" | custom-call | flops 999999995904 | bytes 1 | tf_op jit(solution)/shard_map/first_back/pallas_call | solution.py:730
  102.3 3.8 %collective-permute-done.7.refs_5_ = bf16[2,2,2,240,384]{4,3,2,1,0:T(8,128)(2,1)} collective-permute-done((bf16[2,2,2,240,384]{4,3,2,1,0:T(8,128)(2,1)}, bf16[2,2,2,240,384]{4,3,2,1,0:T(8,128)(2,1)}, u32[]{:S(2)}, u32[]{:S(2)}) %collective-permute-start.7) | collective-permute-done | bytes 1474592 | tf_op jit(solution)/shard_map/ppermute | solution.py:880
  106.1 3.8 %combine.10 = (bf16[2,2,240,384]{3,2,1,0:T(8,128)(2,1)}, bf16[2,2,192,384]{3,2,1,0:T(8,128)(2,1)}) custom-call(s32[8]{0:T(128)S(1)} %copy-done.11, bf16[2,2,2,2,192,384]{5,4,3,2,1,0:T(8,128)(2,1)S(1)} %bitcast.40, bf16[2,2,2,2,192,384]{5,4,3,2,1,0:T(8,128)(2,1)} %bitcast.13.refs_2_, bf16[2,2,2,2,48,384]{5,4,3,2,1,0:T(8,128)(2,1)S(1)} %bitcast.60, ...), custom_call_target="tpu_custom_call" | custom-call | flops 999999995904 | bytes 1 | tf_op jit(solution)/shard_map/combine/pallas_call | solution.py:1039
  109.9 1.8 collective-permute-start.13
  111.6 1.5 collective-permute-start.14
  113.2 7.3 %last_back.1 = (bf16[16,64,768]{2,1,0:T(8,128)(2,1)}, bf16[16,64,768]{2,1,0:T(8,128)(2,1)S(1)}, bf16[512,768]{1,0:T(8,128)(2,1)S(1)}) custom-call(s32[8]{0:T(128)S(1)} %copy-done.11, bf16[512,768]{1,0:T(8,128)(2,1)S(1)} %copy-done.4, bf16[512,256]{1,0:T(8,128)(2,1)S(1)} %get-tuple-element.105.rest_0_.dq_ref, ...), custom_call_target="tpu_custom_call" | custom-call | flops 999999995904 | bytes 1 | tf_op jit(solution)/shard_map/last_back/pallas_call | solution.py:784
  120.5 2.4 %gene_rows.2.rest_0_ = bf16[1152,768]{1,0:T(8,128)(2,1)} custom-call(s32[1152,1]{1,0:T(8,128)S(1)} %broadcast_add_fusion.slots_ref, s32[1,512]{1,0:T(1,128)S(1)} %copy-done.10, bf16[512,768]{1,0:T(8,128)(2,1)S(1)} %get-tuple-element.117.grad_ref, bf16[16,64,768]{2,1,0:T(8,128)(2,1)} %get-tuple-element.118.rest_0_, bf16[16,48,768]{2,1,0:T(8,128)(2,1)} %bitcast.20.rest_1_), custom_call_target="tpu_custom_call" | custom-call | flops 999999995904 | bytes 1 | tf_op jit(solution)/shard_map/gene_rows/pallas_call | solution.py:857
  123.4 1.1 gene_rows.3.refs_13_
  124.5 2.5 %collective-permute-done.9 = bf16[1152,768]{1,0:T(8,128)(2,1)} collective-permute-done((bf16[1152,768]{1,0:T(8,128)(2,1)}, bf16[1152,768]{1,0:T(8,128)(2,1)}, u32[]{:S(2)}, u32[]{:S(2)}) %collective-permute-start.9) | collective-permute-done | bytes 1769504 | tf_op jit(solution)/shard_map/ppermute | solution.py:875
  127.0 3.9 %combine.11 = (bf16[2,2,2,168,384]{4,3,2,1,0:T(8,128)(2,1)}, bf16[2,2,2,184,384]{4,3,2,1,0:T(8,128)(2,1)}) custom-call(s32[8]{0:T(128)S(1)} %copy-done.11, bf16[2,2,2,2,48,768]{5,4,3,2,1,0:T(8,128)(2,1)S(1)} %bitcast.56, bf16[2,2,2,2,48,768]{5,4,3,2,1,0:T(8,128)(2,1)} %bitcast.19.refs_2_, bf16[2,2,2,2,72,768]{5,4,3,2,1,0:T(8,128)(2,1)S(1)} %bitcast.41, ...), custom_call_target="tpu_custom_call" | custom-call | flops 999999995904 | bytes 1 | tf_op jit(solution)/shard_map/combine/pallas_call | solution.py:1039
  131.7 4.3 %combine.12 = (bf16[432,384]{1,0:T(8,128)(2,1)}, bf16[432,384]{1,0:T(8,128)(2,1)}, bf16[432,384]{1,0:T(8,128)(2,1)}) custom-call(s32[8]{0:T(128)S(1)} %copy-done.11, bf16[2,2,2,2,192,384]{5,4,3,2,1,0:T(8,128)(2,1)} %bitcast.37, bf16[2,2,2,2,192,384]{5,4,3,2,1,0:T(8,128)(2,1)} %bitcast.13.refs_2_, bf16[2,2,2,2,48,384]{5,4,3,2,1,0:T(8,128)(2,1)S(1)} %bitcast.61, ...), custom_call_target="tpu_custom_call" | custom-call | flops 999999995904 | bytes 1 | tf_op jit(solution)/shard_map/combine/pallas_call | solution.py:1039
  136.0 1.8 collective-permute-start.17
  137.9 2.6 %collective-permute-start.18 = (bf16[432,384]{1,0:T(8,128)(2,1)}, bf16[432,384]{1,0:T(8,128)(2,1)}, u32[]{:S(2)}, u32[]{:S(2)}) collective-permute-start(bf16[432,384]{1,0:T(8,128)(2,1)} %get-tuple-element.123.refs_16_), channel_id=1, source_target_pairs={{0,16},{2,18},{4,20},{6,22},{8,24},{10,26},{12,28},{14,30},{16,0},... | collective-permute-start | bytes 995336 | tf_op jit(solution)/shard_map/ppermute | solution.py:880
  140.5 15.8 %collective-permute-done.11.refs_5_ = bf16[2,2,2,168,384]{4,3,2,1,0:T(8,128)(2,1)} collective-permute-done((bf16[2,2,2,168,384]{4,3,2,1,0:T(8,128)(2,1)}, bf16[2,2,2,168,384]{4,3,2,1,0:T(8,128)(2,1)}, u32[]{:S(2)}, u32[]{:S(2)}) %collective-permute-start.11) | collective-permute-done | bytes 1032224 | tf_op jit(solution)/shard_map/ppermute | solution.py:880
  156.3 2.4 %collective-permute-done.12.refs_14_ = bf16[2,2,2,184,384]{4,3,2,1,0:T(8,128)(2,1)} collective-permute-done((bf16[2,2,2,184,384]{4,3,2,1,0:T(8,128)(2,1)}, bf16[2,2,2,184,384]{4,3,2,1,0:T(8,128)(2,1)}, u32[]{:S(2)}, u32[]{:S(2)}) %collective-permute-start.12) | collective-permute-done | bytes 1130528 | tf_op jit(solution)/shard_map/ppermute | solution.py:880
  158.7 3.6 %combine.13 = (bf16[2,2,168,384]{3,2,1,0:T(8,128)(2,1)}, bf16[2,2,184,384]{3,2,1,0:T(8,128)(2,1)}) custom-call(s32[8]{0:T(128)S(1)} %copy-done.11, bf16[2,2,2,2,48,768]{5,4,3,2,1,0:T(8,128)(2,1)S(1)} %bitcast.57, bf16[2,2,2,2,48,768]{5,4,3,2,1,0:T(8,128)(2,1)} %bitcast.19.refs_2_, bf16[2,2,2,2,72,768]{5,4,3,2,1,0:T(8,128)(2,1)} %bitcast.43, ...), custom_call_target="tpu_custom_call" | custom-call | flops 999999995904 | bytes 1 | tf_op jit(solution)/shard_map/combine/pallas_call | solution.py:1039
  162.6 1.7 collective-permute-start.16
  164.3 2.8 %combine.14 = (f32[2,2,168,384]{3,2,1,0:T(8,128)S(1)}, f32[2,2,184,384]{3,2,1,0:T(8,128)S(1)}) custom-call(s32[8]{0:T(128)S(1)} %copy-done.11, bf16[2,2,2,2,48,768]{5,4,3,2,1,0:T(8,128)(2,1)S(1)} %bitcast.58, bf16[2,2,2,2,48,768]{5,4,3,2,1,0:T(8,128)(2,1)} %bitcast.19.refs_2_, bf16[2,2,2,2,72,768]{5,4,3,2,1,0:T(8,128)(2,1)} %bitcast.45, ...), custom_call_target="tpu_custom_call" | custom-call | flops 999999995904 | bytes 1 | tf_op jit(solution)/shard_map/combine/pallas_call | solution.py:1039
  167.1 3.4 %combine.15.refs_5_.own_ref = f32[432,384]{1,0:T(8,128)} custom-call(s32[8]{0:T(128)S(1)} %copy-done.11, bf16[2,2,2,2,192,384]{5,4,3,2,1,0:T(8,128)(2,1)} %bitcast.38, bf16[2,2,2,2,192,384]{5,4,3,2,1,0:T(8,128)(2,1)} %bitcast.13.refs_2_, bf16[2,2,2,2,48,384]{5,4,3,2,1,0:T(8,128)(2,1)S(1)} %bitcast.62, bf16[2,2,2,2,48,384]{5,4,3,2,1,0:T(8,128)(2,1)S(1)} %bitcast.35, ...), custom_call_target="tpu_custom_call" | custom-call | flops 999999995904 | bytes 1 | tf_op jit(solution)/shard_map/combine/pallas_call | solution.py:1039
  170.4 5.0 %collective-permute-done.15.refs_3_ = bf16[2,2,168,384]{3,2,1,0:T(8,128)(2,1)} collective-permute-done((bf16[2,2,168,384]{3,2,1,0:T(8,128)(2,1)}, bf16[2,2,168,384]{3,2,1,0:T(8,128)(2,1)}, u32[]{:S(2)}, u32[]{:S(2)}) %collective-permute-start.15) | collective-permute-done | bytes 516128 | tf_op jit(solution)/shard_map/ppermute | solution.py:880
  175.5 1.2 collective-permute-done.16.refs_4_
  176.7 2.8 %combine.16 = (bf16[360,384]{1,0:T(8,128)(2,1)}, bf16[360,384]{1,0:T(8,128)(2,1)}, bf16[360,384]{1,0:T(8,128)(2,1)}) custom-call(s32[8]{0:T(128)S(1)} %copy-done.11, f32[2,2,168,384]{3,2,1,0:T(8,128)S(1)} %get-tuple-element.127.refs_14_.refs_1_, f32[2,2,184,384]{3,2,1,0:T(8,128)S(1)} %get-tuple-element.128.refs_15_.refs_2_, ...), custom_call_target="tpu_custom_call" | custom-call | flops 999999995904 | bytes 1 | tf_op jit(solution)/shard_map/combine/pallas_call | solution.py:1039
  179.5 1.7 collective-permute-start.20
  181.1 2.6 %collective-permute-start.21 = (bf16[360,384]{1,0:T(8,128)(2,1)}, bf16[360,384]{1,0:T(8,128)(2,1)}, u32[]{:S(2)}, u32[]{:S(2)}) collective-permute-start(bf16[360,384]{1,0:T(8,128)(2,1)} %get-tuple-element.130), channel_id=1, source_target_pairs={{0,16},{2,18},{4,20},{6,22},{8,24},{10,26},{12,28},{14,30},{16,0},... | collective-permute-start | bytes 829448 | tf_op jit(solution)/shard_map/ppermute | solution.py:880
  183.9 2.9 %assemble.2 = (f32[192,768]{1,0:T(8,128)}, f32[48,3072]{1,0:T(8,128)}, f32[48,768]{1,0:T(8,128)}) custom-call(s32[8]{0:T(128)S(1)} %copy-done.11, f32[432,384]{1,0:T(8,128)} %combine.15.refs_5_.own_ref, f32[432,384]{1,0:T(8,128)} %collective-permute-done.23.other_ref), custom_call_target="tpu_custom_call" | custom-call | flops 999999995904 | bytes 1 | tf_op jit(solution)/shard_map/assemble/pallas_call | solution.py:1089
  186.8 3.7 %collective-permute-done.20.refs_5_ = bf16[360,384]{1,0:T(8,128)(2,1)} collective-permute-done((bf16[360,384]{1,0:T(8,128)(2,1)}, bf16[360,384]{1,0:T(8,128)(2,1)}, u32[]{:S(2)}, u32[]{:S(2)}) %collective-permute-start.20) | collective-permute-done | bytes 276512 | tf_op jit(solution)/shard_map/ppermute | solution.py:880
  190.5 13.0 %collective-permute-done.21.refs_6_ = bf16[360,384]{1,0:T(8,128)(2,1)} collective-permute-done((bf16[360,384]{1,0:T(8,128)(2,1)}, bf16[360,384]{1,0:T(8,128)(2,1)}, u32[]{:S(2)}, u32[]{:S(2)}) %collective-permute-start.21) | collective-permute-done | bytes 276512 | tf_op jit(solution)/shard_map/ppermute | solution.py:880
  203.5 0.9 copy-done.30
  204.4 2.5 %combine.17 = (f32[208,384]{1,0:T(8,128)S(1)}, f32[72,768]{1,0:T(8,128)}) custom-call(s32[8]{0:T(128)S(1)} %copy-done.11, f32[2,2,168,384]{3,2,1,0:T(8,128)S(1)} %get-tuple-element.127.refs_14_.refs_1_, f32[2,2,184,384]{3,2,1,0:T(8,128)S(1)} %get-tuple-element.128.refs_15_.refs_2_, bf16[2,2,168,384]{3,2,1,0:T(8,128)(2,1)} %collective-permute-done.15.refs_3_, ...), custom_call_target="tpu_custom_call" | custom-call | flops 999999995904 | bytes 1 | tf_op jit(solution)/shard_map/combine/pallas_call | solution.py:1039
  206.9 1.6 collective-permute-done.24.other_ref
  208.6 1.5 assemble.3
  (99 shorter events, 4.2 us)
Async XLA Ops:
  2.6 11.9 %copy-start = (bf16[768,2304]{1,0:T(8,128)(2,1)S(1)}, bf16[768,2304]{1,0:T(8,128)(2,1)}, u32[]{:S(2)}) copy-start(bf16[768,2304]{1,0:T(8,128)(2,1)} %wv_ref.3) | copy-start | bytes 10616836
  2.6 11.9 %copy-start.8 = (f32[768]{0:T(1024)S(1)}, f32[768]{0:T(1024)}, u32[]{:S(2)}) copy-start(f32[768]{0:T(1024)} %bias_ref.1) | copy-start | bytes 9220
  14.0 3.7 %collective-permute-start = (bf16[512,1536]{1,0:T(8,128)(2,1)}, bf16[512,1536]{1,0:T(8,128)(2,1)S(1)}, u32[]{:S(2)}, u32[]{:S(2)}) collective-permute-start(bf16[512,1536]{1,0:T(8,128)(2,1)} %get-tuple-element.85.ko_ref.vo_ref), channel_id=1, source_target_pairs={{0,1},{1,0},{2,3},{3,2},{4,5},{5,4},{6,7},{7,6},{8,9},{9,8},{10,11... | collective-permute-start | bytes 4718600 | tf_op jit(solution)/shard_map/ppermute | solution.py:875
  16.4 15.6 %copy-start.5 = (bf16[512,768]{1,0:T(8,128)(2,1)}, bf16[512,768]{1,0:T(8,128)(2,1)S(1)}, u32[]{:S(2)}) copy-start(bf16[512,768]{1,0:T(8,128)(2,1)S(1)} %queries.1.q_ref) | copy-start | bytes 2359300
  16.4 15.6 %copy-start.12 = (f32[512,768]{1,0:T(8,128)S(1)}, f32[512,768]{1,0:T(8,128)}, u32[]{:S(2)}) copy-start(f32[512,768]{1,0:T(8,128)} %get-tuple-element.87.embedded_ref) | copy-start | bytes 4718596
  16.4 15.6 %copy-start.17 = (bf16[768,768]{1,0:T(8,128)(2,1)S(1)}, bf16[768,768]{1,0:T(8,128)(2,1)}, u32[]{:S(2)}) copy-start(bf16[768,768]{1,0:T(8,128)(2,1)} %w_out_ref.3) | copy-start | bytes 3538948
  16.5 15.6 %copy-start.18 = (bf16[1,512,768]{2,1,0:T(8,128)(2,1)S(1)}, bf16[1,512,768]{2,1,0:T(8,128)(2,1)}, u32[]{:S(2)}) copy-start(bf16[1,512,768]{2,1,0:T(8,128)(2,1)} %param.45) | copy-start | bytes 2359300
  16.5 15.6 %copy-start.19 = (f32[3072]{0:T(1024)S(1)}, f32[3072]{0:T(1024)}, u32[]{:S(2)}) copy-start(f32[3072]{0:T(1024)} %param.42) | copy-start | bytes 36868
  16.5 15.5 %copy-start.20 = (f32[768]{0:T(1024)S(1)}, f32[768]{0:T(1024)}, u32[]{:S(2)}) copy-start(f32[768]{0:T(1024)} %bias_out_ref.1) | copy-start | bytes 9220
  16.5 15.5 %copy-start.21 = (f32[768]{0:T(1024)S(1)}, f32[768]{0:T(1024)}, u32[]{:S(2)}) copy-start(f32[768]{0:T(1024)} %offset_ref.3) | copy-start | bytes 9220
  16.5 15.5 %copy-start.22 = (f32[768]{0:T(1024)S(1)}, f32[768]{0:T(1024)}, u32[]{:S(2)}) copy-start(f32[768]{0:T(1024)} %bias_down_ref.1) | copy-start | bytes 9220
  16.5 15.5 %copy-start.23 = (f32[768]{0:T(1024)S(1)}, f32[768]{0:T(1024)}, u32[]{:S(2)}) copy-start(f32[768]{0:T(1024)} %gain_ref.6) | copy-start | bytes 9220
  17.7 14.2 %copy-start.15 = (bf16[512,1536]{1,0:T(8,128)(2,1)}, bf16[512,1536]{1,0:T(8,128)(2,1)S(1)}, u32[]{:S(2)}) copy-start(bf16[512,1536]{1,0:T(8,128)(2,1)S(1)} %collective-permute-done.kr_ref.vr_ref) | copy-start | bytes 4718596
  32.0 23.5 %copy-start.31 = (bf16[512,768]{1,0:T(8,128)(2,1)}, bf16[512,768]{1,0:T(8,128)(2,1)S(1)}, u32[]{:S(2)}) copy-start(bf16[512,768]{1,0:T(8,128)(2,1)S(1)} %get-tuple-element.86.attended_ref.a_ref) | copy-start | bytes 2359300
  54.9 8.8 %collective-permute-start.1 = (bf16[3072,384]{1,0:T(8,128)(2,1)}, bf16[3072,384]{1,0:T(8,128)(2,1)}, u32[]{:S(2)}, u32[]{:S(2)}) collective-permute-start(bf16[3072,384]{1,0:T(8,128)(2,1)} %get-tuple-element.92.rest_1_), channel_id=1, source_target_pairs={{0,1},{1,0},{2,3},{3,2},{4,5},{5,4},{6,7},{7,6},{8,9},{9,8},{10,11... | collective-permute-start | bytes 7077896 | tf_op jit(solution)/shard_map/ppermute | solution.py:875
  55.4 8.4 %collective-permute-start.3 = (bf16[768,1536]{1,0:T(8,128)(2,1)}, bf16[768,1536]{1,0:T(8,128)(2,1)}, u32[]{:S(2)}, u32[]{:S(2)}) collective-permute-start(bf16[768,1536]{1,0:T(8,128)(2,1)} %get-tuple-element.91.rest_0_), channel_id=1, source_target_pairs={{0,1},{1,0},{2,3},{3,2},{4,5},{5,4},{6,7},{7,6},{8,9},{9,8},{10,11... | collective-permute-start | bytes 7077896 | tf_op jit(solution)/shard_map/ppermute | solution.py:875
  61.1 9.1 %copy-start.27 = (bf16[768,384]{1,0:T(8,128)(2,1)}, bf16[768,384]{1,0:T(8,128)(2,1)S(1)}, u32[]{:S(2)}) copy-start(bf16[768,384]{1,0:T(8,128)(2,1)S(1)} %get-tuple-element.97) | copy-start | bytes 1769476
  61.1 2.6 %collective-permute-start.2 = (bf16[768,384]{1,0:T(8,128)(2,1)S(1)}, bf16[768,384]{1,0:T(8,128)(2,1)S(1)}, u32[]{:S(2)}, u32[]{:S(2)}) collective-permute-start(bf16[768,384]{1,0:T(8,128)(2,1)S(1)} %get-tuple-element.98), channel_id=1, source_target_pairs={{0,1},{1,0},{2,3},{3,2},{4,5},{5,4},{6,7},{7,6},{8,9},{9,8},{10,11... | collective-permute-start | bytes 1769480 | tf_op jit(solution)/shard_map/ppermute | solution.py:875
  65.4 9.2 %copy-start.6 = (bf16[512,768]{1,0:T(8,128)(2,1)S(1)}, bf16[512,768]{1,0:T(8,128)(2,1)}, u32[]{:S(2)}) copy-start(bf16[512,768]{1,0:T(8,128)(2,1)} %copy-done.5) | copy-start | bytes 2359300
  65.4 9.2 %copy-start.14 = (bf16[512,1536]{1,0:T(8,128)(2,1)S(1)}, bf16[512,1536]{1,0:T(8,128)(2,1)}, u32[]{:S(2)}) copy-start(bf16[512,1536]{1,0:T(8,128)(2,1)} %get-tuple-element.85.ko_ref.vo_ref) | copy-start | bytes 4718596
  65.4 9.2 %copy-start.32 = (bf16[512,768]{1,0:T(8,128)(2,1)S(1)}, bf16[512,768]{1,0:T(8,128)(2,1)}, u32[]{:S(2)}) copy-start(bf16[512,768]{1,0:T(8,128)(2,1)} %copy-done.31) | copy-start | bytes 2359300
  65.4 9.2 %copy-start.35 = (bf16[512,768]{1,0:T(8,128)(2,1)S(1)}, bf16[512,768]{1,0:T(8,128)(2,1)}, u32[]{:S(2)}) copy-start(bf16[512,768]{1,0:T(8,128)(2,1)} %copy-done.34) | copy-start | bytes 2359300
  70.3 35.8 %collective-permute-start.7 = (bf16[2,2,2,240,384]{4,3,2,1,0:T(8,128)(2,1)}, bf16[2,2,2,240,384]{4,3,2,1,0:T(8,128)(2,1)}, u32[]{:S(2)}, u32[]{:S(2)}) collective-permute-start(bf16[2,2,2,240,384]{4,3,2,1,0:T(8,128)(2,1)} %get-tuple-element.100.rest_0_), channel_id=1, source_target_pairs={{0,2},{2,0},{4,6},{6,4},{8,10},{10,8},{12,14},{14,12},{16,18},{18,... | collective-permute-start | bytes 4423688 | tf_op jit(solution)/shard_map/ppermute | solution.py:880
  73.1 29.2 %collective-permute-start.8 = (bf16[2,2,2,192,384]{4,3,2,1,0:T(8,128)(2,1)}, bf16[2,2,2,192,384]{4,3,2,1,0:T(8,128)(2,1)}, u32[]{:S(2)}, u32[]{:S(2)}) collective-permute-start(bf16[2,2,2,192,384]{4,3,2,1,0:T(8,128)(2,1)} %get-tuple-element.101.rest_1_), channel_id=1, source_target_pairs={{0,4},{2,6},{4,0},{6,2},{8,12},{10,14},{12,8},{14,10},{16,20},{18,... | collective-permute-start | bytes 3538952 | tf_op jit(solution)/shard_map/ppermute | solution.py:880
  74.6 12.9 %copy-start.16 = (bf16[512,1536]{1,0:T(8,128)(2,1)S(1)}, bf16[512,1536]{1,0:T(8,128)(2,1)}, u32[]{:S(2)}) copy-start(bf16[512,1536]{1,0:T(8,128)(2,1)} %copy-done.15) | copy-start | bytes 4718596
  87.5 7.9 %collective-permute-start.4 = (bf16[2,512,512]{2,1,0:T(8,128)(2,1)}, bf16[2,512,512]{2,1,0:T(8,128)(2,1)}, u32[]{:S(2)}, u32[]{:S(2)}) collective-permute-start(bf16[2,512,512]{2,1,0:T(8,128)(2,1)} %get-tuple-element.104), channel_id=1, source_target_pairs={{0,1},{1,0},{2,3},{3,2},{4,5},{5,4},{6,7},{7,6},{8,9},{9,8},{10,11... | collective-permute-start | bytes 3145736 | tf_op jit(solution)/shard_map/ppermute | solution.py:875
  87.5 7.9 %copy-start.3 = (bf16[512,768]{1,0:T(8,128)(2,1)S(1)}, bf16[512,768]{1,0:T(8,128)(2,1)}, u32[]{:S(2)}) copy-start(bf16[512,768]{1,0:T(8,128)(2,1)} %get-tuple-element.84.normed_ref) | copy-start | bytes 2359300
  94.9 18.2 %collective-permute-start.6 = (bf16[2,512,256]{2,1,0:T(8,128)(2,1)}, bf16[2,512,256]{2,1,0:T(8,128)(2,1)}, u32[]{:S(2)}, u32[]{:S(2)}) collective-permute-start(bf16[2,512,256]{2,1,0:T(8,128)(2,1)} %get-tuple-element.109), channel_id=1, source_target_pairs={{0,1},{1,0},{2,3},{3,2},{4,5},{5,4},{6,7},{7,6},{8,9},{9,8},{10,11... | collective-permute-start | bytes 1572872 | tf_op jit(solution)/shard_map/ppermute | solution.py:875
  95.4 10.6 %copy-start.25 = (bf16[3072,384]{1,0:T(8,128)(2,1)S(1)}, bf16[3072,384]{1,0:T(8,128)(2,1)}, u32[]{:S(2)}) copy-start(bf16[3072,384]{1,0:T(8,128)(2,1)} %get-tuple-element.96) | copy-start | bytes 7077892
  95.4 10.6 %copy-start.28 = (bf16[768,384]{1,0:T(8,128)(2,1)S(1)}, bf16[768,384]{1,0:T(8,128)(2,1)}, u32[]{:S(2)}) copy-start(bf16[768,384]{1,0:T(8,128)(2,1)} %copy-done.27) | copy-start | bytes 1769476
  102.2 18.3 %collective-permute-start.5 = (bf16[768,768]{1,0:T(8,128)(2,1)}, bf16[768,768]{1,0:T(8,128)(2,1)}, u32[]{:S(2)}, u32[]{:S(2)}) collective-permute-start(bf16[768,768]{1,0:T(8,128)(2,1)} %get-tuple-element.107.refs_10_), channel_id=1, source_target_pairs={{0,1},{1,0},{2,3},{3,2},{4,5},{5,4},{6,7},{7,6},{8,9},{9,8},{10,11... | collective-permute-start | bytes 3538952 | tf_op jit(solution)/shard_map/ppermute | solution.py:875
  109.9 21.8 %collective-permute-start.13 = (bf16[2,2,240,384]{3,2,1,0:T(8,128)(2,1)}, bf16[2,2,240,384]{3,2,1,0:T(8,128)(2,1)}, u32[]{:S(2)}, u32[]{:S(2)}) collective-permute-start(bf16[2,2,240,384]{3,2,1,0:T(8,128)(2,1)} %get-tuple-element.115.rest_0_), channel_id=1, source_target_pairs={{0,4},{2,6},{4,0},{6,2},{8,12},{10,14},{12,8},{14,10},{16,20},{18,... | collective-permute-start | bytes 2211848 | tf_op jit(solution)/shard_map/ppermute | solution.py:880
  111.6 20.1 %collective-permute-start.14 = (bf16[2,2,192,384]{3,2,1,0:T(8,128)(2,1)}, bf16[2,2,192,384]{3,2,1,0:T(8,128)(2,1)}, u32[]{:S(2)}, u32[]{:S(2)}) collective-permute-start(bf16[2,2,192,384]{3,2,1,0:T(8,128)(2,1)} %get-tuple-element.116.rest_1_), channel_id=1, source_target_pairs={{0,2},{2,0},{4,6},{6,4},{8,10},{10,8},{12,14},{14,12},{16,18},{18,... | collective-permute-start | bytes 1769480 | tf_op jit(solution)/shard_map/ppermute | solution.py:880
  113.2 7.3 %copy-start.10 = (s32[1,512]{1,0:T(1,128)S(1)}, s32[1,512]{1,0:T(1,128)}, u32[]{:S(2)}) copy-start(s32[1,512]{1,0:T(1,128)} %ids_ref.5) | copy-start | bytes 6148
  120.5 4.1 %collective-permute-start.10 = (bf16[16,64,768]{2,1,0:T(8,128)(2,1)}, bf16[16,64,768]{2,1,0:T(8,128)(2,1)}, u32[]{:S(2)}, u32[]{:S(2)}) collective-permute-start(bf16[16,64,768]{2,1,0:T(8,128)(2,1)} %get-tuple-element.118.rest_0_), channel_id=1, source_target_pairs={{0,1},{1,0},{2,3},{3,2},{4,5},{5,4},{6,7},{7,6},{8,9},{9,8},{10,11... | collective-permute-start | bytes 4718600 | tf_op jit(solution)/shard_map/ppermute | solution.py:875
  122.9 4.2 %collective-permute-start.9 = (bf16[1152,768]{1,0:T(8,128)(2,1)}, bf16[1152,768]{1,0:T(8,128)(2,1)}, u32[]{:S(2)}, u32[]{:S(2)}) collective-permute-start(bf16[1152,768]{1,0:T(8,128)(2,1)} %gene_rows.2.rest_0_), channel_id=1, source_target_pairs={{0,1},{1,0},{2,3},{3,2},{4,5},{5,4},{6,7},{7,6},{8,9},{9,8},{10,11... | collective-permute-start | bytes 5308424 | tf_op jit(solution)/shard_map/ppermute | solution.py:875
  130.9 25.4 %collective-permute-start.11 = (bf16[2,2,2,168,384]{4,3,2,1,0:T(8,128)(2,1)}, bf16[2,2,2,168,384]{4,3,2,1,0:T(8,128)(2,1)}, u32[]{:S(2)}, u32[]{:S(2)}) collective-permute-start(bf16[2,2,2,168,384]{4,3,2,1,0:T(8,128)(2,1)} %get-tuple-element.120.refs_11_), channel_id=1, source_target_pairs={{0,2},{2,0},{4,6},{6,4},{8,10},{10,8},{12,14},{14,12},{16,18},{18,... | collective-permute-start | bytes 3096584 | tf_op jit(solution)/shard_map/ppermute | solution.py:880
  131.4 27.2 %collective-permute-start.12 = (bf16[2,2,2,184,384]{4,3,2,1,0:T(8,128)(2,1)}, bf16[2,2,2,184,384]{4,3,2,1,0:T(8,128)(2,1)}, u32[]{:S(2)}, u32[]{:S(2)}) collective-permute-start(bf16[2,2,2,184,384]{4,3,2,1,0:T(8,128)(2,1)} %get-tuple-element.121.refs_12_), channel_id=1, source_target_pairs={{0,4},{2,6},{4,0},{6,2},{8,12},{10,14},{12,8},{14,10},{16,20},{18,... | collective-permute-start | bytes 3391496 | tf_op jit(solution)/shard_map/ppermute | solution.py:880
  136.0 31.0 %collective-permute-start.17 = (bf16[432,384]{1,0:T(8,128)(2,1)}, bf16[432,384]{1,0:T(8,128)(2,1)}, u32[]{:S(2)}, u32[]{:S(2)}) collective-permute-start(bf16[432,384]{1,0:T(8,128)(2,1)} %get-tuple-element.122.refs_15_), channel_id=1, source_target_pairs={{0,8},{2,10},{4,12},{6,14},{8,0},{10,2},{12,4},{14,6},{16,24},{18,... | collective-permute-start | bytes 995336 | tf_op jit(solution)/shard_map/ppermute | solution.py:880
  137.9 29.2 %collective-permute-start.18 = (bf16[432,384]{1,0:T(8,128)(2,1)}, bf16[432,384]{1,0:T(8,128)(2,1)}, u32[]{:S(2)}, u32[]{:S(2)}) collective-permute-start(bf16[432,384]{1,0:T(8,128)(2,1)} %get-tuple-element.123.refs_16_), channel_id=1, source_target_pairs={{0,16},{2,18},{4,20},{6,22},{8,24},{10,26},{12,28},{14,30},{16,0},... | collective-permute-start | bytes 995336 | tf_op jit(solution)/shard_map/ppermute | solution.py:880
  140.5 26.6 %collective-permute-start.19 = (bf16[432,384]{1,0:T(8,128)(2,1)}, bf16[432,384]{1,0:T(8,128)(2,1)}, u32[]{:S(2)}, u32[]{:S(2)}) collective-permute-start(bf16[432,384]{1,0:T(8,128)(2,1)} %get-tuple-element.124.refs_17_), channel_id=1, source_target_pairs={{0,24},{2,26},{4,28},{6,30},{8,16},{10,18},{12,20},{14,22},{16,8},... | collective-permute-start | bytes 995336 | tf_op jit(solution)/shard_map/ppermute | solution.py:880
  162.3 13.2 %collective-permute-start.15 = (bf16[2,2,168,384]{3,2,1,0:T(8,128)(2,1)}, bf16[2,2,168,384]{3,2,1,0:T(8,128)(2,1)}, u32[]{:S(2)}, u32[]{:S(2)}) collective-permute-start(bf16[2,2,168,384]{3,2,1,0:T(8,128)(2,1)} %get-tuple-element.125.refs_15_), channel_id=1, source_target_pairs={{0,4},{2,6},{4,0},{6,2},{8,12},{10,14},{12,8},{14,10},{16,20},{18,... | collective-permute-start | bytes 1548296 | tf_op jit(solution)/shard_map/ppermute | solution.py:880
  162.6 14.1 %collective-permute-start.16 = (bf16[2,2,184,384]{3,2,1,0:T(8,128)(2,1)}, bf16[2,2,184,384]{3,2,1,0:T(8,128)(2,1)}, u32[]{:S(2)}, u32[]{:S(2)}) collective-permute-start(bf16[2,2,184,384]{3,2,1,0:T(8,128)(2,1)} %get-tuple-element.126.refs_16_), channel_id=1, source_target_pairs={{0,2},{2,0},{4,6},{6,4},{8,10},{10,8},{12,14},{14,12},{16,18},{18,... | collective-permute-start | bytes 1695752 | tf_op jit(solution)/shard_map/ppermute | solution.py:880
  170.4 13.4 %collective-permute-start.23 = (f32[432,384]{1,0:T(8,128)}, f32[432,384]{1,0:T(8,128)}, u32[]{:S(2)}, u32[]{:S(2)}) collective-permute-start(f32[432,384]{1,0:T(8,128)} %combine.15.refs_5_.own_ref), channel_id=1, source_target_pairs={{0,1},{1,0},{2,3},{3,2},{4,5},{5,4},{6,7},{7,6},{8,9},{9,8},{10,11... | collective-permute-start | bytes 1990664 | tf_op jit(solution)/shard_map/ppermute | solution.py:875
  179.5 11.0 %collective-permute-start.20 = (bf16[360,384]{1,0:T(8,128)(2,1)}, bf16[360,384]{1,0:T(8,128)(2,1)}, u32[]{:S(2)}, u32[]{:S(2)}) collective-permute-start(bf16[360,384]{1,0:T(8,128)(2,1)} %get-tuple-element.129), channel_id=1, source_target_pairs={{0,8},{2,10},{4,12},{6,14},{8,0},{10,2},{12,4},{14,6},{16,24},{18,... | collective-permute-start | bytes 829448 | tf_op jit(solution)/shard_map/ppermute | solution.py:880
  181.1 22.3 %collective-permute-start.21 = (bf16[360,384]{1,0:T(8,128)(2,1)}, bf16[360,384]{1,0:T(8,128)(2,1)}, u32[]{:S(2)}, u32[]{:S(2)}) collective-permute-start(bf16[360,384]{1,0:T(8,128)(2,1)} %get-tuple-element.130), channel_id=1, source_target_pairs={{0,16},{2,18},{4,20},{6,22},{8,24},{10,26},{12,28},{14,30},{16,0},... | collective-permute-start | bytes 829448 | tf_op jit(solution)/shard_map/ppermute | solution.py:880
  183.7 19.7 %collective-permute-start.22 = (bf16[360,384]{1,0:T(8,128)(2,1)}, bf16[360,384]{1,0:T(8,128)(2,1)}, u32[]{:S(2)}, u32[]{:S(2)}) collective-permute-start(bf16[360,384]{1,0:T(8,128)(2,1)} %get-tuple-element.131), channel_id=1, source_target_pairs={{0,24},{2,26},{4,28},{6,30},{8,16},{10,18},{12,20},{14,22},{16,8},... | collective-permute-start | bytes 829448 | tf_op jit(solution)/shard_map/ppermute | solution.py:880
  206.9 1.6 collective-permute-start.24
  (13 other events, 49.4 us)

commit v4 on v3

--- a/solution.py
+++ b/solution.py
@@ -347,7 +347,6 @@
     down_keep_ref,
     bias_up_grad_ref,
     normed_ref,
-    turned_ref,
     total_ref,
     g_out_ref,
     g_halves_ref,
@@ -365,9 +364,7 @@
         )
         residual_ref[...] = residual
         unit, _ = normalize(residual)
-        normed = unit * gain_ref[...][None] + offset_ref[...][None]
-        normed_ref[...] = normed.astype(LOW)
-        turned_ref[...] = normed.T.astype(LOW)
+        normed_ref[...] = (unit * gain_ref[...][None] + offset_ref[...][None]).astype(LOW)
         g_out_ref[...] = jnp.where(alive, cotangent_ref[...].astype(WIDE), 0.0).astype(LOW)
         g_halves_ref[:, :half] = g_out_ref[:, half_of(1 - mine, half)]
         g_halves_ref[:, half:] = g_out_ref[:, half_of(mine, half)]
@@ -385,7 +382,7 @@
     down = dot(activated, g_halves_ref[...], 0, 0).astype(LOW)
     down_send_ref[...] = down[:, :half]
     down_keep_ref[...] = down[:, half:]
-    up = dot(turned_ref[...], g_hidden).astype(LOW)
+    up = dot(normed_ref[...], g_hidden, 0, 0).astype(LOW)
     bias_up_grad_ref[...] = column_sums(g_hidden.astype(WIDE))
 
     @pl.when(step < steps // 2)
@@ -452,7 +449,6 @@
             ],
             scratch_shapes=[
                 pltpu.VMEM((rows, width), LOW),
-                pltpu.VMEM((width, rows), LOW),
                 pltpu.VMEM((rows, width), WIDE),
                 pltpu.VMEM((rows, width), LOW),
                 pltpu.VMEM((rows, width), LOW),
@@ -967,6 +963,10 @@
 def combine(place, shares, after, mode=SEND, last=None):
     operands, specs, plan, out_specs, out_shape = [], [], [], [], []
     steps = []
+    top = shares[0].bits - 1
+    halves = mode == SETTLE or (
+        mode == SEND and not any(top in share.fixed or top in share.targets()[0] for share in shares)
+    )
     for share in shares:
         if mode != SETTLE:
             share.arrived()
@@ -979,17 +979,22 @@
             shape, where, picked = [], [], []
             for bit in dims:
                 free = bit in left or (quad and bit in targets[0])
-                shape.append(2 if free else None)
-                where.append(None if free else (bit, targets[0].get(bit, 0)))
+                stepped = halves and bit == top
+                shape.append(2 if free and not stepped else None)
+                where.append(bit if stepped else None if free else (bit, targets[0].get(bit, 0)))
                 if quad and bit in targets[0]:
                     picked.append(bit)
 
-            def index(_, place, where=tuple(where), block=block):
-                lead = tuple(
-                    0 if at is None else (1 - place[4 + at[0]] if at[1] else place[4 + at[0]])
-                    for at in where
-                )
-                return lead + block
+            def index(step, place, where=tuple(where), block=block):
+                lead = []
+                for at in where:
+                    if at is None:
+                        lead.append(0)
+                    elif at == top:
+                        lead.append(step)
+                    else:
+                        lead.append(1 - place[4 + at[0]] if at[1] else place[4 + at[0]])
+                return tuple(lead) + block
 
             specs.append(pl.BlockSpec(tuple(shape) + tuple(size), index))
             used.append((len(operands), parts))
@@ -998,7 +1003,15 @@
             plan.append((share.rows, share.places, used, target if quad else {}))
             if mode != FINISH:
                 shape = (2,) * len(left) + (share.height, LANES)
-                out_specs.append(whole(shape))
+                if halves:
+                    zeros = (0,) * (len(shape) - 1)
+                    out_specs.append(
+                        pl.BlockSpec(
+                            (None,) + shape[1:], lambda step, _, zeros=zeros: (step,) + zeros
+                        )
+                    )
+                else:
+                    out_specs.append(whole(shape))
                 out_shape.append(shaped(shape, LOW if mode == SEND else WIDE))
     for shape, _ in last or []:
         out_specs.append(whole(shape))
@@ -1040,7 +1053,7 @@
         kernel,
         grid_spec=pltpu.PrefetchScalarGridSpec(
             num_scalar_prefetch=1,
-            grid=(1,),
+            grid=(2 if halves else 1,),
             in_specs=specs + unread(after),
             out_specs=out_specs,
         ),
@@ -1072,6 +1085,7 @@
             value = of_core(core, slice(row, row + rows), slice(column, column + columns))
             outs[target][:, out_column : out_column + columns] = value
         if small_row is None:
+            outs[-1][...] = jnp.zeros_like(outs[-1])
             return
         group_ref, vector_refs, long_ref = outs[2], outs[3:-1], outs[-1]
         share, groups = group_ref.shape
@@ -1198,15 +1212,17 @@
     owners = lambda array: array.reshape(count, -1, array.shape[-1])
     low_bits = list(range(bits - 2))
     turned = low_bits[1::-1] + low_bits[2:]
-    quad = [Share.QUAD]
+    quad, high_bits = [Share.QUAD], [bits - 2, bits - 1]
     up_terms = [owners(up_keep), owners(swap_cores(up_send))]
     blocks = units // 2 // LANES
     out_terms = [owners(out_keep), owners(swap_cores(out_send))]
     down_terms = [owners(down_keep), owners(swap_cores(down_send))]
-    high = units // count
+    high, share = units // count, width // count
+    out_cut = min(share, up16(2 * share // 3))
+    out_rest = [(out_terms, [0], [(out_cut, share - out_cut)])] if out_cut < share else []
     early = [
-        Share([(down_terms, [0]), (out_terms, [0])], low_bits + quad),
-        Share([(up_terms, list(range(blocks)))], turned + quad),
+        Share([(down_terms, [0]), (out_terms, [0], [(0, out_cut)])], low_bits + quad),
+        Share([(up_terms, list(range(blocks)))] + out_rest, turned + quad),
     ]
     token = combine(place, early, [])
     dq1, own1, other1 = attend_back(
@@ -1221,9 +1237,10 @@
         place, normed, dq1, own1, got1, w_qkv, 256, [dq2]
     )
     qkv = [owners(qkv_keep), owners(swap_cores(qkv_send))]
+    project = Share([(qkv, [0, 1])], high_bits + low_bits)
     token = [part, qkv_send]
-    for _ in low_bits[1:]:
-        token = combine(place, early, token)
+    for bit in low_bits[1:]:
+        token = combine(place, early + [project] * (bit == low_bits[-1]), token)
     early = [early[0].join(early[1])]
     tail_send, tail_keep, g_low = last_back(
         place,
@@ -1248,33 +1265,29 @@
     )
     slot = jnp.arange(count * VOC_DEV, dtype=jnp.int32)[:, None]
     slot = slot + slot // VOC_DEV * VOC_DEV
-    gene_send = gene_rows(slot + (1 - mine) * VOC_DEV, gene_ids, g_low, [tail_send, qkv[1]])
+    gene_send = gene_rows(slot + (1 - mine) * VOC_DEV, gene_ids, g_low, [tail_send])
     gene_got = swap_cores(gene_send)
     gene_keep = gene_rows(slot + mine * VOC_DEV, gene_ids, g_low, [gene_send])
-    share = width // count
     tail = [tail_keep, swap_cores(tail_send)]
     gene = [owners(gene_keep), owners(gene_got)]
     small_at = up16(share)
     late = [
-        Share([(qkv, [0, 1]), (gene, [0])], low_bits + quad),
+        Share([(tail, [0], [(0, share)]), (gene, [0])], low_bits + quad),
         Share(
-            [
-                (tail, [0], [(0, share)]),
-                (tail, [1], [(0, share)]),
-                (tail, [0], [(small_at, 16)]),
-                (gene, [1]),
-            ],
-            turned + quad,
+            [(tail, [1], [(0, share)]), (tail, [0], [(small_at, 16)]), (gene, [1])], turned + quad
         ),
     ]
-    token = combine(place, late, [gene_keep])
+    token = combine(place, [project], [gene_keep])
+    token = combine(place, late, token)
     token = combine(place, early, token)
     for _ in low_bits[1:]:
-        token = combine(place, late, token)
+        token = combine(place, late + [project], token)
     token = combine(place, late, token, SETTLE)
-    late = [late[0].join(late[1])]
+    late = [late[0].join(late[1]), project]
     step = up16(share)
     layout = [(0, 0, 0, 0), (0, 1, high + blocks * step, 0)]
+    if out_rest:
+        layout.append((0, 2 + blocks, high + blocks * step + out_cut, 0))
     layout += [(0, 2 + block, high + block * step, 0) for block in range(blocks)]
     (own,) = combine(place, early, token, FINISH, [((high + (blocks + 1) * step, LANES), layout)])
     other = swap_cores(own)
@@ -1286,19 +1299,19 @@
             place_in = (core * blocks + block) * LANES
             pieces.append((core, high + block * step, share, 0, LANES, 1, place_in))
         pieces.append((core, high + blocks * step, share, 0, LANES, 2, core * LANES))
-    w_down_share, w_up_share, w_out_share = assemble(
-        place, own, other, [(high, width), (share, units), (share, width)], pieces
-    )
-    layout = [(0, 0, 0, 0), (0, 1, step, 0)]
-    layout += [(0, 3 + index, (2 + index) * step, 0) for index in range(3)]
+    w_down_share, w_up_share, w_out_share, done = assemble(
+        place, own, other, [(high, width), (share, units), (share, width), (8, 128)], pieces
+    )
+    layout = [(1, 0, 0, 0), (1, 1, step, 0), (0, 0, 2 * step, 0), (0, 2, 3 * step, 0)]
+    layout += [(0, 3, 4 * step, 0)]
     own, gene_grad = combine(
         place,
         late,
-        [w_out_share],
+        [done],
         FINISH,
         [
             ((4 * step + 16, LANES), layout),
-            ((VOC_DEV, width), [(0, 2, 0, 0), (0, 6, 0, LANES)]),
+            ((VOC_DEV, width), [(0, 1, 0, 0), (0, 4, 0, LANES)]),
         ],
     )
     other = swap_cores(own)

time: 212 us -> 206 us (0.972)
  waiting for transfers between devices: 52.1 us -> 36.2 us
  starting transfers between devices: 21.7 us -> 29.9 us
    ppermute x14 -> x18, waiting for transfers between devices: 44.9 us -> 28.2 us  [bits_apart(): return lax.ppermute(array, 'dp', [(i, i ^ mask) for i in range(count)])]
    ppermute x14 -> x18, starting transfers between devices: 19.2 us -> 27.4 us  [bits_apart(): return lax.ppermute(array, 'dp', [(i, i ^ mask) for i in range(count)])]
    pallas_call x9 -> x10, Pallas kernels: 31.9 us -> 32.7 us  [combine(): pl.pallas_call(kernel, grid_spec=pltpu.PrefetchScalarGridSpec(num_scalar_...]
    unnamed x72 -> x94, local copies, waits for them, and re-layouts: 5.93 us -> 6.56 us
  transfers between devices with their start and end apart: 25 -> 29, of which waited for: 11 -> 13; matrix products, arithmetic and copies ran while one was open for 0% -> 0% of each run, Pallas kernels for 33% -> 35%
where the time goes in v4:
time: 206 us; the launch traced here: 203 us
  Pallas kernels  127 us (62%)
  waiting for transfers between devices  36.2 us (18%)
  starting transfers between devices  29.9 us (15%)
  local copies, waits for them, and re-layouts  7.16 us (3%)
  between operations  2.67 us (1%)
    pallas_call x10, Pallas kernels, combine(): pl.pallas_call(kernel, grid_spec=pltpu.PrefetchScalarGridSpec(num_scalar_...  32.7 us
    ppermute x18, waiting for transfers between devices, bits_apart(): return lax.ppermute(array, 'dp', [(i, i ^ mask) for i in range(count)])  28.2 us
    ppermute x18, starting transfers between devices, bits_apart(): return lax.ppermute(array, 'dp', [(i, i ^ mask) for i in range(count)])  27.4 us
    pallas_call x1, Pallas kernels, feed_forward(): pl.pallas_call(ffn_kernel, grid_spec=pltpu.PrefetchScalarGridSpec(num_sca...  22.9 us
    pallas_call x2, Pallas kernels, attend_back(): pl.pallas_call(attend_back_kernel, grid=(count,), in_specs=[near, near, f...  20 us
    pallas_call x1, Pallas kernels, attend(): pl.pallas_call(attend_kernel, grid_spec=pltpu.PrefetchScalarGridSpec(num_...  14.1 us
    pallas_call x1, Pallas kernels, embed(): pl.pallas_call(embed_kernel, grid_spec=pltpu.PrefetchScalarGridSpec(num_s...  11.4 us
    ppermute x11, waiting for transfers between devices, swap_cores(): return lax.ppermute(array, 'blk', [(0, 1), (1, 0)])  8 us
  transfers between devices with their start and end apart: 29, of which 13 were waited for; matrix products, arithmetic and copies ran while one was open for 0% of the time, Pallas kernels for 35%

profile of v4, /device:TPU:0, one launch (start us, length us, event | category | flops | bytes accessed | tf_op | source)
XLA Modules:
  0.0 203.1 jit_solution(5896145481951076164)
XLA Ops:
  2.6 11.4 %embed.1 = (f32[512,768]{1,0:T(8,128)}, bf16[512,768]{1,0:T(8,128)(2,1)}, bf16[512,1536]{1,0:T(8,128)(2,1)}) custom-call(s32[8]{0:T(128)} %stack.31.place_ref.refs_0_, s32[1,512]{1,0:T(1,128)} %ids_ref.5, f32[1,512]{1,0:T(1,128)} %expression_ref.3, bf16[512,768]{1,0:T(8,128)(2,1)} %bitcast.27, bf16[2304,768]{1,0:T(8,128)(2,1)} %table_ref.1, ...), custom_call_target="tpu_custom_call" | custom-call | tf_op jit(solution)/shard_map/embed/pallas_call | solution.py:115
  14.5 1.1 copy-done.2
  16.5 1.2 collective-permute-done.kr_ref.vr_ref
  17.7 14.1 %attend.1 = (bf16[512,768]{1,0:T(8,128)(2,1)S(1)}, bf16[12,1024,512]{2,1,0:T(8,128)(2,1)}, f32[6,2,512]{2,1,0:T(2,128)S(1)}) custom-call(s32[8]{0:T(128)S(1)} %copy-done.11, bf16[512,768]{1,0:T(8,128)(2,1)S(1)} %queries.1.q_ref, bf16[512,1536]{1,0:T(8,128)(2,1)S(1)} %copy-done.14, bf16[512,1536]{1,0:T(8,128)(2,1)S(1)} %copy-done.14, ...), custom_call_target="tpu_custom_call" | custom-call | flops 3221225472 | bytes 12582912 | tf_op jit(solution)/shard_map/attend/pallas_call | solution.py:218
  31.9 22.9 %feed_forward.1 = (bf16[512,768]{1,0:T(8,128)(2,1)}, f32[512,768]{1,0:T(8,128)S(1)}, f32[512,768]{1,0:T(8,128)S(1)}, bf16[768,1536]{1,0:T(8,128)(2,1)}, bf16[768...) custom-call(s32[8]{0:T(128)S(1)} %copy-done.11, ...), custom_call_target="tpu_custom_call" | custom-call | flops 999999995904 | bytes 1 | tf_op jit(solution)/shard_map/feed_forward/pallas_call | solution.py:422
  55.3 3.6 %branch_back.1 = (f32[512,768]{1,0:T(8,128)S(1)}, bf16[512,768]{1,0:T(8,128)(2,1)S(1)}, bf16[768,384]{1,0:T(8,128)(2,1)S(1)}, bf16[768,384]{1,0:T(8,128)(2,1)S(1)}, f32[4,768]{1,0:T(4,128)S(1)}) custom-call(s32[8]{0:T(128)S(1)} %copy-done.11, f32[512,768]{1,0:T(8,128)S(1)} %get-tuple-element.93.residual_ref, f32[512,768]{1,0:T(8,128)S(1)} %get-tuple-element.94.g_normed_ref, ...), custom_call_target="tpu_custom_call" | custom-call | flops 999999995904 | bytes 1 | tf_op jit(solution)/shard_map/branch_back/pallas_call | solution.py:536
  58.9 1.2 copy-done.36
  60.4 3.1 %collective-permute-done.2 = bf16[768,384]{1,0:T(8,128)(2,1)S(1)} collective-permute-done((bf16[768,384]{1,0:T(8,128)(2,1)S(1)}, bf16[768,384]{1,0:T(8,128)(2,1)S(1)}, u32[]{:S(2)}, u32[]{:S(2)}) %collective-permute-start.2) | collective-permute-done | bytes 589856 | tf_op jit(solution)/shard_map/ppermute | solution.py:871
  63.5 4.1 %combine.10 = (bf16[2,2,2,224,384]{4,3,2,1,0:T(8,128)(2,1)}, bf16[2,2,2,208,384]{4,3,2,1,0:T(8,128)(2,1)}) custom-call(s32[8]{0:T(128)S(1)} %copy-done.11, bf16[2,2,2,2,192,384]{5,4,3,2,1,0:T(8,128)(2,1)S(1)} %bitcast.47, bf16[2,2,2,2,192,384]{5,4,3,2,1,0:T(8,128)(2,1)} %bitcast.13.refs_2_, bf16[2,2,2,2,48,384]{5,4,3,2,1,0:T(8,128)(2,1)S(1)} %bitcast.69, ...), custom_call_target="tpu_custom_call" | custom-call | flops 999999995904 | bytes 1 | tf_op jit(solution)/shard_map/combine/pallas_call | solution.py:1052
  67.7 2.9 %collective-permute-start.6 = (bf16[2,2,2,224,384]{4,3,2,1,0:T(8,128)(2,1)}, bf16[2,2,2,224,384]{4,3,2,1,0:T(8,128)(2,1)}, u32[]{:S(2)}, u32[]{:S(2)}) collective-permute-start(bf16[2,2,2,224,384]{4,3,2,1,0:T(8,128)(2,1)} %get-tuple-element.104.rest_0_), channel_id=1, source_target_pairs={{0,2},{2,0},{4,6},{6,4},{8,10},{10,8},{12,14},{14,12},{16,18},{18,... | collective-permute-start | bytes 4128776 | tf_op jit(solution)/shard_map/ppermute | solution.py:876
  70.6 1.5 collective-permute-start.7
  72.1 12.6 %attend_back.2 = (bf16[512,512]{1,0:T(8,128)(2,1)S(1)}, bf16[2,512,512]{2,1,0:T(8,128)(2,1)S(1)}, bf16[2,512,512]{2,1,0:T(8,128)(2,1)}) custom-call(bf16[512,768]{1,0:T(8,128)(2,1)S(1)} %copy-done.6, bf16[512,1536]{1,0:T(8,128)(2,1)S(1)} %copy-done.15, bf16[512,1536]{1,0:T(8,128)(2,1)S(1)} %copy-done.15, bf16[512,1536]{1,0:T(8,128)(2,1)} %copy-done.16, ...), custom_call_target="tpu_custom_call" | custom-call | flops 999999995904 | bytes 1 | tf_op jit(solution)/shard_map/attend_back/pallas_call | solution.py:301
  84.8 7.4 %attend_back.3 = (bf16[512,256]{1,0:T(8,128)(2,1)S(1)}, bf16[2,512,256]{2,1,0:T(8,128)(2,1)S(1)}, bf16[2,512,256]{2,1,0:T(8,128)(2,1)}) custom-call(bf16[512,768]{1,0:T(8,128)(2,1)S(1)} %copy-done.6, bf16[512,1536]{1,0:T(8,128)(2,1)S(1)} %copy-done.15, bf16[512,1536]{1,0:T(8,128)(2,1)S(1)} %copy-done.15, bf16[512,1536]{1,0:T(8,128)(2,1)S(1)} %copy-done.17, ...), custom_call_target="tpu_custom_call" | custom-call | flops 999999995904 | bytes 1 | tf_op jit(solution)/shard_map/attend_back/pallas_call | solution.py:301
  92.2 6.4 %first_back.1 = (bf16[768,768]{1,0:T(8,128)(2,1)S(1)}, bf16[768,768]{1,0:T(8,128)(2,1)S(1)}, f32[2,2,256]{2,1,0:T(2,128)S(1)}, f32[512,768]{1,0:T(8,128)S(1)}) custom-call(s32[8]{0:T(128)S(1)} %copy-done.11, bf16[512,768]{1,0:T(8,128)(2,1)S(1)} %copy-done.3, bf16[512,512]{1,0:T(8,128)(2,1)S(1)} %get-tuple-element.106.rest_0_.dq_ref, ...), custom_call_target="tpu_custom_call" | custom-call | flops 999999995904 | bytes 1 | tf_op jit(solution)/shard_map/first_back/pallas_call | solution.py:726
  99.6 1.2 copy-done.37
  102.3 2.1 %collective-permute-done.8 = bf16[768,768]{1,0:T(8,128)(2,1)S(1)} collective-permute-done((bf16[768,768]{1,0:T(8,128)(2,1)S(1)}, bf16[768,768]{1,0:T(8,128)(2,1)S(1)}, u32[]{:S(2)}, u32[]{:S(2)}) %collective-permute-start.8) | collective-permute-done | bytes 1179680 | tf_op jit(solution)/shard_map/ppermute | solution.py:871
  104.4 1.3 copy-done.32
  105.7 4.1 %combine.11 = (bf16[2,2,224,384]{3,2,1,0:T(8,128)(2,1)}, bf16[2,2,208,384]{3,2,1,0:T(8,128)(2,1)}, bf16[2,2,2,96,384]{4,3,2,1,0:T(8,128)(2,1)}) custom-call(s32[8]{0:T(128)S(1)} %copy-done.12, bf16[2,2,2,2,192,384]{5,4,3,2,1,0:T(8,128)(2,1)} %bitcast.45, bf16[2,2,2,2,192,384]{5,4,3,2,1,0:T(8,128)(2,1)} %bitcast.13.refs_2_, ...), custom_call_target="tpu_custom_call" | custom-call | flops 999999995904 | bytes 1 | tf_op jit(solution)/shard_map/combine/pallas_call | solution.py:1052
  109.9 1.6 collective-permute-start.11
  112.6 7.3 %last_back.1 = (bf16[16,64,768]{2,1,0:T(8,128)(2,1)}, bf16[16,64,768]{2,1,0:T(8,128)(2,1)S(1)}, bf16[512,768]{1,0:T(8,128)(2,1)S(1)}) custom-call(s32[8]{0:T(128)S(1)} %copy-done.12, bf16[512,768]{1,0:T(8,128)(2,1)S(1)} %copy-done.4, bf16[512,256]{1,0:T(8,128)(2,1)S(1)} %copy-done.42, bf16[2,512,256]{2,1,0:T(8,128)(2,1)S(1)} %copy-done.40, ...), custom_call_target="tpu_custom_call" | custom-call | flops 999999995904 | bytes 1 | tf_op jit(solution)/shard_map/last_back/pallas_call | solution.py:780
  119.9 2.4 %gene_rows.2.rest_0_ = bf16[1152,768]{1,0:T(8,128)(2,1)} custom-call(s32[1152,1]{1,0:T(8,128)S(1)} %broadcast_add_fusion.slots_ref, s32[1,512]{1,0:T(1,128)S(1)} %copy-done.10, bf16[512,768]{1,0:T(8,128)(2,1)S(1)} %get-tuple-element.124.grad_ref, bf16[16,64,768]{2,1,0:T(8,128)(2,1)} %get-tuple-element.123.rest_0_), custom_call_target="tpu_custom_call" | custom-call | flops 999999995904 | bytes 1 | tf_op jit(solution)/shard_map/gene_rows/pallas_call | solution.py:853
  122.8 1.1 gene_rows.3.refs_4_
  123.9 1.8 collective-permute-done.11.refs_3_.refs_15_.refs_7_.refs_10_
  125.8 2.3 %combine.12.refs_11_ = bf16[2,2,96,384]{3,2,1,0:T(8,128)(2,1)} custom-call(s32[8]{0:T(128)S(1)} %copy-done.12, bf16[2,2,2,2,48,768]{5,4,3,2,1,0:T(8,128)(2,1)S(1)} %bitcast.65, bf16[2,2,2,2,48,768]{5,4,3,2,1,0:T(8,128)(2,1)S(1)} %bitcast.30, bf16[2,2,2,96,384]{4,3,2,1,0:T(8,128)(2,1)} %collective-permute-done.11.refs_3_.refs_15_.refs_7_.refs_10_, ...), custom_call_target="tpu_custom_call" | custom-call | flops 999999995904 | bytes 1 | tf_op jit(solution)/shard_map/combine/pallas_call | solution.py:1052
  128.1 2.6 %collective-permute-start.14 = (bf16[2,2,96,384]{3,2,1,0:T(8,128)(2,1)}, bf16[2,2,96,384]{3,2,1,0:T(8,128)(2,1)}, u32[]{:S(2)}, u32[]{:S(2)}) collective-permute-start(bf16[2,2,96,384]{3,2,1,0:T(8,128)(2,1)} %combine.12.refs_11_), channel_id=1, source_target_pairs={{0,16},{2,18},{4,20},{6,22},{8,24},{10,26},{12,28},{14,30},{16,0},... | collective-permute-start | bytes 884744 | tf_op jit(solution)/shard_map/ppermute | solution.py:876
  130.7 3.5 %combine.13 = (bf16[2,2,2,120,384]{4,3,2,1,0:T(8,128)(2,1)}, bf16[2,2,2,136,384]{4,3,2,1,0:T(8,128)(2,1)}) custom-call(s32[8]{0:T(128)S(1)} %copy-done.12, bf16[2,2,2,2,64,768]{5,4,3,2,1,0:T(8,128)(2,1)S(1)} %bitcast.55, bf16[2,2,2,2,64,768]{5,4,3,2,1,0:T(8,128)(2,1)} %bitcast.21.refs_2_.refs_6_.refs_8_.refs_7_.refs_9_, ...), custom_call_target="tpu_custom_call" | custom-call | flops 999999995904 | bytes 1 | tf_op jit(solution)/shard_map/combine/pallas_call | solution.py:1052
  135.5 4.1 %combine.14 = (bf16[432,384]{1,0:T(8,128)(2,1)}, bf16[432,384]{1,0:T(8,128)(2,1)}, bf16[432,384]{1,0:T(8,128)(2,1)}) custom-call(s32[8]{0:T(128)S(1)} %copy-done.12, bf16[2,2,2,2,192,384]{5,4,3,2,1,0:T(8,128)(2,1)S(1)} %bitcast.48, bf16[2,2,2,2,192,384]{5,4,3,2,1,0:T(8,128)(2,1)} %bitcast.13.refs_2_, bf16[2,2,2,2,48,384]{5,4,3,2,1,0:T(8,128)(2,1)S(1)} %bitcast.73, ...), custom_call_target="tpu_custom_call" | custom-call | flops 999999995904 | bytes 1 | tf_op jit(solution)/shard_map/combine/pallas_call | solution.py:1052
  139.6 1.3 collective-permute-start.20
  141.3 3.7 %collective-permute-done.14.refs_16_.refs_8_.refs_11_ = bf16[2,2,96,384]{3,2,1,0:T(8,128)(2,1)} collective-permute-done((bf16[2,2,96,384]{3,2,1,0:T(8,128)(2,1)}, bf16[2,2,96,384]{3,2,1,0:T(8,128)(2,1)}, u32[]{:S(2)}, u32[]{:S(2)}) %collective-permute-start.14) | collective-permute-done | bytes 294944 | tf_op jit(solution)/shard_map/ppermute | solution.py:876
  145.1 2.7 %collective-permute-start.22 = (bf16[432,384]{1,0:T(8,128)(2,1)}, bf16[432,384]{1,0:T(8,128)(2,1)}, u32[]{:S(2)}, u32[]{:S(2)}) collective-permute-start(bf16[432,384]{1,0:T(8,128)(2,1)} %get-tuple-element.129.refs_19_), channel_id=1, source_target_pairs={{0,24},{2,26},{4,28},{6,30},{8,16},{10,18},{12,20},{14,22},{16,8},... | collective-permute-start | bytes 995336 | tf_op jit(solution)/shard_map/ppermute | solution.py:876
  147.8 4.6 %collective-permute-done.12.refs_5_ = bf16[2,2,2,120,384]{4,3,2,1,0:T(8,128)(2,1)} collective-permute-done((bf16[2,2,2,120,384]{4,3,2,1,0:T(8,128)(2,1)}, bf16[2,2,2,120,384]{4,3,2,1,0:T(8,128)(2,1)}, u32[]{:S(2)}, u32[]{:S(2)}) %collective-permute-start.12) | collective-permute-done | bytes 737312 | tf_op jit(solution)/shard_map/ppermute | solution.py:876
  152.4 1.9 collective-permute-done.13.refs_12_
  154.3 3.4 %combine.15 = (bf16[2,2,120,384]{3,2,1,0:T(8,128)(2,1)}, bf16[2,2,136,384]{3,2,1,0:T(8,128)(2,1)}, bf16[2,96,384]{2,1,0:T(8,128)(2,1)}) custom-call(s32[8]{0:T(128)S(1)} %copy-done.12, bf16[2,2,2,2,64,768]{5,4,3,2,1,0:T(8,128)(2,1)S(1)} %bitcast.58, bf16[2,2,2,2,64,768]{5,4,3,2,1,0:T(8,128)(2,1)} %bitcast.21.refs_2_.refs_6_.refs_8_.refs_7_.refs_9_, ...), custom_call_target="tpu_custom_call" | custom-call | flops 999999995904 | bytes 1 | tf_op jit(solution)/shard_map/combine/pallas_call | solution.py:1052
  158.2 1.2 collective-permute-start.17
  159.4 2.4 %combine.16 = (f32[2,2,120,384]{3,2,1,0:T(8,128)S(1)}, f32[2,2,136,384]{3,2,1,0:T(8,128)S(1)}) custom-call(s32[8]{0:T(128)S(1)} %copy-done.12, bf16[2,2,2,2,64,768]{5,4,3,2,1,0:T(8,128)(2,1)S(1)} %bitcast.61, bf16[2,2,2,2,64,768]{5,4,3,2,1,0:T(8,128)(2,1)} %bitcast.21.refs_2_.refs_6_.refs_8_.refs_7_.refs_9_, bf16[2,2,2,2,72,768]{5,4,3,2,1,0:T(8,128)(2,1)S(1)} %bitcast.53, ...), custom_call_target="tpu_custom_call" | custom-call | flops 999999995904 | bytes 1 | tf_op jit(solution)/shard_map/combine/pallas_call | solution.py:1052
  162.7 4.4 %collective-permute-done.21.refs_14_ = bf16[432,384]{1,0:T(8,128)(2,1)} collective-permute-done((bf16[432,384]{1,0:T(8,128)(2,1)}, bf16[432,384]{1,0:T(8,128)(2,1)}, u32[]{:S(2)}, u32[]{:S(2)}) %collective-permute-start.21) | collective-permute-done | bytes 331808 | tf_op jit(solution)/shard_map/ppermute | solution.py:876
  167.1 3.4 %combine.17.refs_10_.own_ref = f32[432,384]{1,0:T(8,128)} custom-call(s32[8]{0:T(128)S(1)} %copy-done.12, bf16[2,2,2,2,192,384]{5,4,3,2,1,0:T(8,128)(2,1)} %bitcast.46, bf16[2,2,2,2,192,384]{5,4,3,2,1,0:T(8,128)(2,1)} %bitcast.13.refs_2_, bf16[2,2,2,2,48,384]{5,4,3,2,1,0:T(8,128)(2,1)S(1)} %bitcast.75, bf16[2,2,2,2,48,384]{5,4,3,2,1,0:T(8,128)(2,1)S(1)} %bitcast.42, ...), custom_call_target="tpu_custom_call" | custom-call | flops 999999995904 | bytes 1 | tf_op jit(solution)/shard_map/combine/pallas_call | solution.py:1052
  171.1 2.6 %combine.18 = (bf16[264,384]{1,0:T(8,128)(2,1)}, bf16[264,384]{1,0:T(8,128)(2,1)}, bf16[264,384]{1,0:T(8,128)(2,1)}, bf16[96,384]{1,0:T(8,128)(2,1)}) custom-call(s32[8]{0:T(128)S(1)} %copy-done.12, f32[2,2,120,384]{3,2,1,0:T(8,128)S(1)} %get-tuple-element.133.refs_16_.refs_1_, f32[2,2,136,384]{3,2,1,0:T(8,128)S(1)} %get-tuple-element.134.refs_17_.refs_2_, ...), custom_call_target="tpu_custom_call" | custom-call | flops 999999995904 | bytes 1 | tf_op jit(solution)/shard_map/combine/pallas_call | solution.py:1052
  173.8 5.6 %collective-permute-start.23 = (bf16[264,384]{1,0:T(8,128)(2,1)}, bf16[264,384]{1,0:T(8,128)(2,1)}, u32[]{:S(2)}, u32[]{:S(2)}) collective-permute-start(bf16[264,384]{1,0:T(8,128)(2,1)} %get-tuple-element.135), channel_id=1, source_target_pairs={{0,8},{2,10},{4,12},{6,14},{8,0},{10,2},{12,4},{14,6},{16,24},{18,... | collective-permute-start | bytes 608264 | tf_op jit(solution)/shard_map/ppermute | solution.py:876
  179.3 1.9 collective-permute-start.24
  181.3 1.4 collective-permute-start.25
  183.2 2.9 %assemble.2 = (f32[192,768]{1,0:T(8,128)}, f32[48,3072]{1,0:T(8,128)}, f32[48,768]{1,0:T(8,128)}, f32[8,128]{1,0:T(8,128)S(1)}) custom-call(s32[8]{0:T(128)S(1)} %copy-done.12, f32[432,384]{1,0:T(8,128)} %combine.17.refs_10_.own_ref, f32[432,384]{1,0:T(8,128)} %collective-permute-done.27.other_ref), custom_call_target="tpu_custom_call" | custom-call | flops 999999995904 | bytes 1 | tf_op jit(solution)/shard_map/assemble/pallas_call | solution.py:1103
  186.2 1.2 collective-permute-done.26.refs_13_
  187.4 2.3 %collective-permute-done.23.refs_5_ = bf16[264,384]{1,0:T(8,128)(2,1)} collective-permute-done((bf16[264,384]{1,0:T(8,128)(2,1)}, bf16[264,384]{1,0:T(8,128)(2,1)}, u32[]{:S(2)}, u32[]{:S(2)}) %collective-permute-start.23) | collective-permute-done | bytes 202784 | tf_op jit(solution)/shard_map/ppermute | solution.py:876
  189.7 7.5 %collective-permute-done.25.refs_7_ = bf16[264,384]{1,0:T(8,128)(2,1)} collective-permute-done((bf16[264,384]{1,0:T(8,128)(2,1)}, bf16[264,384]{1,0:T(8,128)(2,1)}, u32[]{:S(2)}, u32[]{:S(2)}) %collective-permute-start.25) | collective-permute-done | bytes 202784 | tf_op jit(solution)/shard_map/ppermute | solution.py:876
  197.2 2.6 %combine.19 = (f32[208,384]{1,0:T(8,128)S(1)}, f32[72,768]{1,0:T(8,128)}) custom-call(s32[8]{0:T(128)S(1)} %copy-done.12, f32[2,2,120,384]{3,2,1,0:T(8,128)S(1)} %get-tuple-element.133.refs_16_.refs_1_, f32[2,2,136,384]{3,2,1,0:T(8,128)S(1)} %get-tuple-element.134.refs_17_.refs_2_, bf16[2,2,120,384]{3,2,1,0:T(8,128)(2,1)} %collective-permute-done.17.refs_3_, ...), custom_call_target="tpu_custom_call" | custom-call | flops 999999995904 | bytes 1 | tf_op jit(solution)/shard_map/combine/pallas_call | solution.py:1052
  199.8 1.6 collective-permute-done.28.other_ref
  201.4 1.5 assemble.3
  (130 shorter events, 11.1 us)
Async XLA Ops:
  2.6 11.9 %copy-start = (bf16[768,2304]{1,0:T(8,128)(2,1)S(1)}, bf16[768,2304]{1,0:T(8,128)(2,1)}, u32[]{:S(2)}) copy-start(bf16[768,2304]{1,0:T(8,128)(2,1)} %wv_ref.3) | copy-start | bytes 10616836
  2.6 11.9 %copy-start.8 = (f32[768]{0:T(1024)S(1)}, f32[768]{0:T(1024)}, u32[]{:S(2)}) copy-start(f32[768]{0:T(1024)} %bias_ref.1) | copy-start | bytes 9220
  14.0 3.7 %collective-permute-start = (bf16[512,1536]{1,0:T(8,128)(2,1)}, bf16[512,1536]{1,0:T(8,128)(2,1)S(1)}, u32[]{:S(2)}, u32[]{:S(2)}) collective-permute-start(bf16[512,1536]{1,0:T(8,128)(2,1)} %get-tuple-element.89.ko_ref.vo_ref), channel_id=1, source_target_pairs={{0,1},{1,0},{2,3},{3,2},{4,5},{5,4},{6,7},{7,6},{8,9},{9,8},{10,11... | collective-permute-start | bytes 4718600 | tf_op jit(solution)/shard_map/ppermute | solution.py:871
  16.4 15.4 %copy-start.5 = (bf16[512,768]{1,0:T(8,128)(2,1)}, bf16[512,768]{1,0:T(8,128)(2,1)S(1)}, u32[]{:S(2)}) copy-start(bf16[512,768]{1,0:T(8,128)(2,1)S(1)} %queries.1.q_ref) | copy-start | bytes 2359300
  16.4 15.4 %copy-start.13 = (f32[512,768]{1,0:T(8,128)S(1)}, f32[512,768]{1,0:T(8,128)}, u32[]{:S(2)}) copy-start(f32[512,768]{1,0:T(8,128)} %get-tuple-element.91.embedded_ref) | copy-start | bytes 4718596
  16.4 15.4 %copy-start.18 = (bf16[768,768]{1,0:T(8,128)(2,1)S(1)}, bf16[768,768]{1,0:T(8,128)(2,1)}, u32[]{:S(2)}) copy-start(bf16[768,768]{1,0:T(8,128)(2,1)} %w_out_ref.3) | copy-start | bytes 3538948
  16.4 15.4 %copy-start.19 = (bf16[1,512,768]{2,1,0:T(8,128)(2,1)S(1)}, bf16[1,512,768]{2,1,0:T(8,128)(2,1)}, u32[]{:S(2)}) copy-start(bf16[1,512,768]{2,1,0:T(8,128)(2,1)} %param.45) | copy-start | bytes 2359300
  16.4 15.4 %copy-start.22 = (f32[3072]{0:T(1024)S(1)}, f32[3072]{0:T(1024)}, u32[]{:S(2)}) copy-start(f32[3072]{0:T(1024)} %param.42) | copy-start | bytes 36868
  16.5 15.4 %copy-start.23 = (f32[768]{0:T(1024)S(1)}, f32[768]{0:T(1024)}, u32[]{:S(2)}) copy-start(f32[768]{0:T(1024)} %bias_out_ref.1) | copy-start | bytes 9220
  16.5 15.4 %copy-start.24 = (f32[768]{0:T(1024)S(1)}, f32[768]{0:T(1024)}, u32[]{:S(2)}) copy-start(f32[768]{0:T(1024)} %offset_ref.3) | copy-start | bytes 9220
  16.5 15.4 %copy-start.25 = (f32[768]{0:T(1024)S(1)}, f32[768]{0:T(1024)}, u32[]{:S(2)}) copy-start(f32[768]{0:T(1024)} %bias_down_ref.1) | copy-start | bytes 9220
  16.5 15.4 %copy-start.26 = (f32[768]{0:T(1024)S(1)}, f32[768]{0:T(1024)}, u32[]{:S(2)}) copy-start(f32[768]{0:T(1024)} %gain_ref.6) | copy-start | bytes 9220
  17.7 14.1 %copy-start.16 = (bf16[512,1536]{1,0:T(8,128)(2,1)}, bf16[512,1536]{1,0:T(8,128)(2,1)S(1)}, u32[]{:S(2)}) copy-start(bf16[512,1536]{1,0:T(8,128)(2,1)S(1)} %collective-permute-done.kr_ref.vr_ref) | copy-start | bytes 4718596
  54.7 8.8 %collective-permute-start.1 = (bf16[3072,384]{1,0:T(8,128)(2,1)}, bf16[3072,384]{1,0:T(8,128)(2,1)}, u32[]{:S(2)}, u32[]{:S(2)}) collective-permute-start(bf16[3072,384]{1,0:T(8,128)(2,1)} %get-tuple-element.96.rest_1_), channel_id=1, source_target_pairs={{0,1},{1,0},{2,3},{3,2},{4,5},{5,4},{6,7},{7,6},{8,9},{9,8},{10,11... | collective-permute-start | bytes 7077896 | tf_op jit(solution)/shard_map/ppermute | solution.py:871
  55.1 8.4 %collective-permute-start.3 = (bf16[768,1536]{1,0:T(8,128)(2,1)}, bf16[768,1536]{1,0:T(8,128)(2,1)}, u32[]{:S(2)}, u32[]{:S(2)}) collective-permute-start(bf16[768,1536]{1,0:T(8,128)(2,1)} %get-tuple-element.95.rest_0_), channel_id=1, source_target_pairs={{0,1},{1,0},{2,3},{3,2},{4,5},{5,4},{6,7},{7,6},{8,9},{9,8},{10,11... | collective-permute-start | bytes 7077896 | tf_op jit(solution)/shard_map/ppermute | solution.py:871
  55.3 8.3 %copy-start.27 = (bf16[3072,384]{1,0:T(8,128)(2,1)S(1)}, bf16[3072,384]{1,0:T(8,128)(2,1)}, u32[]{:S(2)}) copy-start(bf16[3072,384]{1,0:T(8,128)(2,1)} %get-tuple-element.100) | copy-start | bytes 7077892
  60.0 3.5 %collective-permute-start.2 = (bf16[768,384]{1,0:T(8,128)(2,1)S(1)}, bf16[768,384]{1,0:T(8,128)(2,1)S(1)}, u32[]{:S(2)}, u32[]{:S(2)}) collective-permute-start(bf16[768,384]{1,0:T(8,128)(2,1)S(1)} %get-tuple-element.102), channel_id=1, source_target_pairs={{0,1},{1,0},{2,3},{3,2},{4,5},{5,4},{6,7},{7,6},{8,9},{9,8},{10,11... | collective-permute-start | bytes 1769480 | tf_op jit(solution)/shard_map/ppermute | solution.py:871
  63.5 8.6 %copy-start.6 = (bf16[512,768]{1,0:T(8,128)(2,1)S(1)}, bf16[512,768]{1,0:T(8,128)(2,1)}, u32[]{:S(2)}) copy-start(bf16[512,768]{1,0:T(8,128)(2,1)} %copy-done.5) | copy-start | bytes 2359300
  63.5 8.6 %copy-start.15 = (bf16[512,1536]{1,0:T(8,128)(2,1)S(1)}, bf16[512,1536]{1,0:T(8,128)(2,1)}, u32[]{:S(2)}) copy-start(bf16[512,1536]{1,0:T(8,128)(2,1)} %get-tuple-element.89.ko_ref.vo_ref) | copy-start | bytes 4718596
  67.7 34.6 %collective-permute-start.6 = (bf16[2,2,2,224,384]{4,3,2,1,0:T(8,128)(2,1)}, bf16[2,2,2,224,384]{4,3,2,1,0:T(8,128)(2,1)}, u32[]{:S(2)}, u32[]{:S(2)}) collective-permute-start(bf16[2,2,2,224,384]{4,3,2,1,0:T(8,128)(2,1)} %get-tuple-element.104.rest_0_), channel_id=1, source_target_pairs={{0,2},{2,0},{4,6},{6,4},{8,10},{10,8},{12,14},{14,12},{16,18},{18,... | collective-permute-start | bytes 4128776 | tf_op jit(solution)/shard_map/ppermute | solution.py:876
  70.6 31.6 %collective-permute-start.7 = (bf16[2,2,2,208,384]{4,3,2,1,0:T(8,128)(2,1)}, bf16[2,2,2,208,384]{4,3,2,1,0:T(8,128)(2,1)}, u32[]{:S(2)}, u32[]{:S(2)}) collective-permute-start(bf16[2,2,2,208,384]{4,3,2,1,0:T(8,128)(2,1)} %get-tuple-element.105.rest_1_), channel_id=1, source_target_pairs={{0,4},{2,6},{4,0},{6,2},{8,12},{10,14},{12,8},{14,10},{16,20},{18,... | collective-permute-start | bytes 3833864 | tf_op jit(solution)/shard_map/ppermute | solution.py:876
  72.1 12.6 %copy-start.17 = (bf16[512,1536]{1,0:T(8,128)(2,1)S(1)}, bf16[512,1536]{1,0:T(8,128)(2,1)}, u32[]{:S(2)}) copy-start(bf16[512,1536]{1,0:T(8,128)(2,1)} %copy-done.16) | copy-start | bytes 4718596
  84.8 7.4 %collective-permute-start.5 = (bf16[2,512,512]{2,1,0:T(8,128)(2,1)}, bf16[2,512,512]{2,1,0:T(8,128)(2,1)}, u32[]{:S(2)}, u32[]{:S(2)}) collective-permute-start(bf16[2,512,512]{2,1,0:T(8,128)(2,1)} %get-tuple-element.111), channel_id=1, source_target_pairs={{0,1},{1,0},{2,3},{3,2},{4,5},{5,4},{6,7},{7,6},{8,9},{9,8},{10,11... | collective-permute-start | bytes 3145736 | tf_op jit(solution)/shard_map/ppermute | solution.py:871
  92.2 12.2 %copy-start.12 = (s32[8]{0:T(128)S(1)}, s32[8]{0:T(128)}, u32[]{:S(2)}) copy-start(s32[8]{0:T(128)} %stack.31.place_ref.refs_0_) | copy-start | bytes 100
  92.2 12.2 %copy-start.21 = (bf16[768,384]{1,0:T(8,128)(2,1)S(1)}, bf16[768,384]{1,0:T(8,128)(2,1)}, u32[]{:S(2)}) copy-start(bf16[768,384]{1,0:T(8,128)(2,1)} %copy-done.20) | copy-start | bytes 1769476
  92.2 12.2 %copy-start.35 = (bf16[768,384]{1,0:T(8,128)(2,1)S(1)}, bf16[768,384]{1,0:T(8,128)(2,1)}, u32[]{:S(2)}) copy-start(bf16[768,384]{1,0:T(8,128)(2,1)} %copy-done.34) | copy-start | bytes 1769476
  101.4 3.0 %collective-permute-start.8 = (bf16[768,768]{1,0:T(8,128)(2,1)S(1)}, bf16[768,768]{1,0:T(8,128)(2,1)S(1)}, u32[]{:S(2)}, u32[]{:S(2)}) collective-permute-start(bf16[768,768]{1,0:T(8,128)(2,1)S(1)} %get-tuple-element.118.refs_14_), channel_id=1, source_target_pairs={{0,1},{1,0},{2,3},{3,2},{4,5},{5,4},{6,7},{7,6},{8,9},{9,8},{10,11... | collective-permute-start | bytes 3538952 | tf_op jit(solution)/shard_map/ppermute | solution.py:871
  102.2 10.3 %collective-permute-start.4 = (bf16[2,512,256]{2,1,0:T(8,128)(2,1)}, bf16[2,512,256]{2,1,0:T(8,128)(2,1)}, u32[]{:S(2)}, u32[]{:S(2)}) collective-permute-start(bf16[2,512,256]{2,1,0:T(8,128)(2,1)} %get-tuple-element.109), channel_id=1, source_target_pairs={{0,1},{1,0},{2,3},{3,2},{4,5},{5,4},{6,7},{7,6},{8,9},{9,8},{10,11... | collective-permute-start | bytes 1572872 | tf_op jit(solution)/shard_map/ppermute | solution.py:871
  109.9 15.9 %collective-permute-start.11 = (bf16[2,2,2,96,384]{4,3,2,1,0:T(8,128)(2,1)}, bf16[2,2,2,96,384]{4,3,2,1,0:T(8,128)(2,1)}, u32[]{:S(2)}, u32[]{:S(2)}) collective-permute-start(bf16[2,2,2,96,384]{4,3,2,1,0:T(8,128)(2,1)} %get-tuple-element.121.rest_2_), channel_id=1, source_target_pairs={{0,8},{2,10},{4,12},{6,14},{8,0},{10,2},{12,4},{14,6},{16,24},{18,... | collective-permute-start | bytes 1769480 | tf_op jit(solution)/shard_map/ppermute | solution.py:876
  111.4 24.1 %collective-permute-start.15 = (bf16[2,2,224,384]{3,2,1,0:T(8,128)(2,1)}, bf16[2,2,224,384]{3,2,1,0:T(8,128)(2,1)}, u32[]{:S(2)}, u32[]{:S(2)}) collective-permute-start(bf16[2,2,224,384]{3,2,1,0:T(8,128)(2,1)} %get-tuple-element.119.rest_0_), channel_id=1, source_target_pairs={{0,4},{2,6},{4,0},{6,2},{8,12},{10,14},{12,8},{14,10},{16,20},{18,... | collective-permute-start | bytes 2064392 | tf_op jit(solution)/shard_map/ppermute | solution.py:876
  112.0 23.5 %collective-permute-start.16 = (bf16[2,2,208,384]{3,2,1,0:T(8,128)(2,1)}, bf16[2,2,208,384]{3,2,1,0:T(8,128)(2,1)}, u32[]{:S(2)}, u32[]{:S(2)}) collective-permute-start(bf16[2,2,208,384]{3,2,1,0:T(8,128)(2,1)} %get-tuple-element.120.rest_1_), channel_id=1, source_target_pairs={{0,2},{2,0},{4,6},{6,4},{8,10},{10,8},{12,14},{14,12},{16,18},{18,... | collective-permute-start | bytes 1916936 | tf_op jit(solution)/shard_map/ppermute | solution.py:876
  119.9 10.8 %collective-permute-start.9 = (bf16[16,64,768]{2,1,0:T(8,128)(2,1)}, bf16[16,64,768]{2,1,0:T(8,128)(2,1)}, u32[]{:S(2)}, u32[]{:S(2)}) collective-permute-start(bf16[16,64,768]{2,1,0:T(8,128)(2,1)} %get-tuple-element.123.rest_0_), channel_id=1, source_target_pairs={{0,1},{1,0},{2,3},{3,2},{4,5},{5,4},{6,7},{7,6},{8,9},{9,8},{10,11... | collective-permute-start | bytes 4718600 | tf_op jit(solution)/shard_map/ppermute | solution.py:871
  122.3 8.4 %collective-permute-start.10 = (bf16[1152,768]{1,0:T(8,128)(2,1)}, bf16[1152,768]{1,0:T(8,128)(2,1)}, u32[]{:S(2)}, u32[]{:S(2)}) collective-permute-start(bf16[1152,768]{1,0:T(8,128)(2,1)} %gene_rows.2.rest_0_), channel_id=1, source_target_pairs={{0,1},{1,0},{2,3},{3,2},{4,5},{5,4},{6,7},{7,6},{8,9},{9,8},{10,11... | collective-permute-start | bytes 5308424 | tf_op jit(solution)/shard_map/ppermute | solution.py:871
  128.1 16.9 %collective-permute-start.14 = (bf16[2,2,96,384]{3,2,1,0:T(8,128)(2,1)}, bf16[2,2,96,384]{3,2,1,0:T(8,128)(2,1)}, u32[]{:S(2)}, u32[]{:S(2)}) collective-permute-start(bf16[2,2,96,384]{3,2,1,0:T(8,128)(2,1)} %combine.12.refs_11_), channel_id=1, source_target_pairs={{0,16},{2,18},{4,20},{6,22},{8,24},{10,26},{12,28},{14,30},{16,0},... | collective-permute-start | bytes 884744 | tf_op jit(solution)/shard_map/ppermute | solution.py:876
  134.2 20.1 %collective-permute-start.13 = (bf16[2,2,2,136,384]{4,3,2,1,0:T(8,128)(2,1)}, bf16[2,2,2,136,384]{4,3,2,1,0:T(8,128)(2,1)}, u32[]{:S(2)}, u32[]{:S(2)}) collective-permute-start(bf16[2,2,2,136,384]{4,3,2,1,0:T(8,128)(2,1)} %get-tuple-element.126.refs_14_), channel_id=1, source_target_pairs={{0,4},{2,6},{4,0},{6,2},{8,12},{10,14},{12,8},{14,10},{16,20},{18,... | collective-permute-start | bytes 2506760 | tf_op jit(solution)/shard_map/ppermute | solution.py:876
  134.7 17.7 %collective-permute-start.12 = (bf16[2,2,2,120,384]{4,3,2,1,0:T(8,128)(2,1)}, bf16[2,2,2,120,384]{4,3,2,1,0:T(8,128)(2,1)}, u32[]{:S(2)}, u32[]{:S(2)}) collective-permute-start(bf16[2,2,2,120,384]{4,3,2,1,0:T(8,128)(2,1)} %get-tuple-element.125.refs_13_), channel_id=1, source_target_pairs={{0,2},{2,0},{4,6},{6,4},{8,10},{10,8},{12,14},{14,12},{16,18},{18,... | collective-permute-start | bytes 2211848 | tf_op jit(solution)/shard_map/ppermute | solution.py:876
  139.6 22.2 %collective-permute-start.20 = (bf16[432,384]{1,0:T(8,128)(2,1)}, bf16[432,384]{1,0:T(8,128)(2,1)}, u32[]{:S(2)}, u32[]{:S(2)}) collective-permute-start(bf16[432,384]{1,0:T(8,128)(2,1)} %get-tuple-element.127.refs_17_), channel_id=1, source_target_pairs={{0,8},{2,10},{4,12},{6,14},{8,0},{10,2},{12,4},{14,6},{16,24},{18,... | collective-permute-start | bytes 995336 | tf_op jit(solution)/shard_map/ppermute | solution.py:876
  141.0 26.2 %collective-permute-start.21 = (bf16[432,384]{1,0:T(8,128)(2,1)}, bf16[432,384]{1,0:T(8,128)(2,1)}, u32[]{:S(2)}, u32[]{:S(2)}) collective-permute-start(bf16[432,384]{1,0:T(8,128)(2,1)} %get-tuple-element.128.refs_18_), channel_id=1, source_target_pairs={{0,16},{2,18},{4,20},{6,22},{8,24},{10,26},{12,28},{14,30},{16,0},... | collective-permute-start | bytes 995336 | tf_op jit(solution)/shard_map/ppermute | solution.py:876
  145.1 22.1 %collective-permute-start.22 = (bf16[432,384]{1,0:T(8,128)(2,1)}, bf16[432,384]{1,0:T(8,128)(2,1)}, u32[]{:S(2)}, u32[]{:S(2)}) collective-permute-start(bf16[432,384]{1,0:T(8,128)(2,1)} %get-tuple-element.129.refs_19_), channel_id=1, source_target_pairs={{0,24},{2,26},{4,28},{6,30},{8,16},{10,18},{12,20},{14,22},{16,8},... | collective-permute-start | bytes 995336 | tf_op jit(solution)/shard_map/ppermute | solution.py:876
  157.7 13.4 %collective-permute-start.18 = (bf16[2,2,136,384]{3,2,1,0:T(8,128)(2,1)}, bf16[2,2,136,384]{3,2,1,0:T(8,128)(2,1)}, u32[]{:S(2)}, u32[]{:S(2)}) collective-permute-start(bf16[2,2,136,384]{3,2,1,0:T(8,128)(2,1)} %get-tuple-element.131.refs_14_), channel_id=1, source_target_pairs={{0,2},{2,0},{4,6},{6,4},{8,10},{10,8},{12,14},{14,12},{16,18},{18,... | collective-permute-start | bytes 1253384 | tf_op jit(solution)/shard_map/ppermute | solution.py:876
  158.2 12.9 %collective-permute-start.17 = (bf16[2,2,120,384]{3,2,1,0:T(8,128)(2,1)}, bf16[2,2,120,384]{3,2,1,0:T(8,128)(2,1)}, u32[]{:S(2)}, u32[]{:S(2)}) collective-permute-start(bf16[2,2,120,384]{3,2,1,0:T(8,128)(2,1)} %get-tuple-element.130.refs_13_), channel_id=1, source_target_pairs={{0,4},{2,6},{4,0},{6,2},{8,12},{10,14},{12,8},{14,10},{16,20},{18,... | collective-permute-start | bytes 1105928 | tf_op jit(solution)/shard_map/ppermute | solution.py:876
  161.9 9.2 %collective-permute-start.19 = (bf16[2,96,384]{2,1,0:T(8,128)(2,1)}, bf16[2,96,384]{2,1,0:T(8,128)(2,1)}, u32[]{:S(2)}, u32[]{:S(2)}) collective-permute-start(bf16[2,96,384]{2,1,0:T(8,128)(2,1)} %get-tuple-element.132.refs_15_), channel_id=1, source_target_pairs={{0,2},{2,0},{4,6},{6,4},{8,10},{10,8},{12,14},{14,12},{16,18},{18,... | collective-permute-start | bytes 442376 | tf_op jit(solution)/shard_map/ppermute | solution.py:876
  170.5 12.7 %collective-permute-start.27 = (f32[432,384]{1,0:T(8,128)}, f32[432,384]{1,0:T(8,128)}, u32[]{:S(2)}, u32[]{:S(2)}) collective-permute-start(f32[432,384]{1,0:T(8,128)} %combine.17.refs_10_.own_ref), channel_id=1, source_target_pairs={{0,1},{1,0},{2,3},{3,2},{4,5},{5,4},{6,7},{7,6},{8,9},{9,8},{10,11... | collective-permute-start | bytes 1990664 | tf_op jit(solution)/shard_map/ppermute | solution.py:871
  173.8 15.9 %collective-permute-start.23 = (bf16[264,384]{1,0:T(8,128)(2,1)}, bf16[264,384]{1,0:T(8,128)(2,1)}, u32[]{:S(2)}, u32[]{:S(2)}) collective-permute-start(bf16[264,384]{1,0:T(8,128)(2,1)} %get-tuple-element.135), channel_id=1, source_target_pairs={{0,8},{2,10},{4,12},{6,14},{8,0},{10,2},{12,4},{14,6},{16,24},{18,... | collective-permute-start | bytes 608264 | tf_op jit(solution)/shard_map/ppermute | solution.py:876
  179.3 10.4 %collective-permute-start.24 = (bf16[264,384]{1,0:T(8,128)(2,1)}, bf16[264,384]{1,0:T(8,128)(2,1)}, u32[]{:S(2)}, u32[]{:S(2)}) collective-permute-start(bf16[264,384]{1,0:T(8,128)(2,1)} %get-tuple-element.136), channel_id=1, source_target_pairs={{0,16},{2,18},{4,20},{6,22},{8,24},{10,26},{12,28},{14,30},{16,0},... | collective-permute-start | bytes 608264 | tf_op jit(solution)/shard_map/ppermute | solution.py:876
  181.3 16.0 %collective-permute-start.25 = (bf16[264,384]{1,0:T(8,128)(2,1)}, bf16[264,384]{1,0:T(8,128)(2,1)}, u32[]{:S(2)}, u32[]{:S(2)}) collective-permute-start(bf16[264,384]{1,0:T(8,128)(2,1)} %get-tuple-element.137), channel_id=1, source_target_pairs={{0,24},{2,26},{4,28},{6,30},{8,16},{10,18},{12,20},{14,22},{16,8},... | collective-permute-start | bytes 608264 | tf_op jit(solution)/shard_map/ppermute | solution.py:876
  182.7 4.7 %collective-permute-start.26 = (bf16[96,384]{1,0:T(8,128)(2,1)}, bf16[96,384]{1,0:T(8,128)(2,1)}, u32[]{:S(2)}, u32[]{:S(2)}) collective-permute-start(bf16[96,384]{1,0:T(8,128)(2,1)} %get-tuple-element.138), channel_id=1, source_target_pairs={{0,4},{2,6},{4,0},{6,2},{8,12},{10,14},{12,8},{14,10},{16,20},{18,... | collective-permute-start | bytes 221192 | tf_op jit(solution)/shard_map/ppermute | solution.py:876
  199.8 1.6 collective-permute-start.28
  (28 other events, 139.1 us)

commit v5 on v4

--- a/solution.py
+++ b/solution.py
@@ -1061,7 +1061,7 @@
         compiler_params=params(),
         cost_estimate=LONG,
         name="combine",
-    )(place, *operands, *after)
+    )(place, *[pltpu.with_memory_space_constraint(x, pltpu.HBM) for x in operands], *after)
     taken = 0
     for share, targets in zip(shares, steps):
         if mode == SEND:

time: 206 us -> 205 us (level)
  waiting for transfers between devices: 36.2 us -> 32.9 us
  Pallas kernels: 127 us -> 130 us
    pallas_call x10, Pallas kernels: 32.7 us -> 35.7 us  [combine(): pl.pallas_call(kernel, grid_spec=pltpu.PrefetchScalarGridSpec(num_scalar_...]
    unnamed x94 -> x74, local copies, waits for them, and re-layouts: 6.56 us -> 5.1 us
  transfers between devices with their start and end apart: 29 -> 29, of which waited for: 13 -> 15; matrix products, arithmetic and copies ran while one was open for 0% -> 0% of each run, Pallas kernels for 35% -> 36%
where the time goes in v5:
time: 205 us; the launch traced here: 203 us
  Pallas kernels  130 us (63%)
  waiting for transfers between devices  32.9 us (16%)
  starting transfers between devices  30.9 us (15%)
  local copies, waits for them, and re-layouts  5.71 us (3%)
  between operations  2.54 us (1%)
    pallas_call x10, Pallas kernels, combine(): pl.pallas_call(kernel, grid_spec=pltpu.PrefetchScalarGridSpec(num_scalar_...  35.7 us
    ppermute x18, starting transfers between devices, bits_apart(): return lax.ppermute(array, 'dp', [(i, i ^ mask) for i in range(count)])  28.4 us
    ppermute x18, waiting for transfers between devices, bits_apart(): return lax.ppermute(array, 'dp', [(i, i ^ mask) for i in range(count)])  26.5 us
    pallas_call x1, Pallas kernels, feed_forward(): pl.pallas_call(ffn_kernel, grid_spec=pltpu.PrefetchScalarGridSpec(num_sca...  22.8 us
    pallas_call x2, Pallas kernels, attend_back(): pl.pallas_call(attend_back_kernel, grid=(count,), in_specs=[near, near, f...  20.2 us
    pallas_call x1, Pallas kernels, attend(): pl.pallas_call(attend_kernel, grid_spec=pltpu.PrefetchScalarGridSpec(num_...  14.1 us
    pallas_call x1, Pallas kernels, embed(): pl.pallas_call(embed_kernel, grid_spec=pltpu.PrefetchScalarGridSpec(num_s...  11.4 us
    pallas_call x1, Pallas kernels, last_back(): pl.pallas_call(functools.partial(last_back_kernel, groups), grid_spec=plt...  7.37 us
  transfers between devices with their start and end apart: 29, of which 15 were waited for; matrix products, arithmetic and copies ran while one was open for 0% of the time, Pallas kernels for 36%

profile of v5, /device:TPU:0, one launch (start us, length us, event | category | flops | bytes accessed | tf_op | source)
XLA Modules:
  0.0 202.6 jit_solution(16498030957971866876)
XLA Ops:
  2.6 11.4 %embed.1 = (f32[512,768]{1,0:T(8,128)}, bf16[512,768]{1,0:T(8,128)(2,1)}, bf16[512,1536]{1,0:T(8,128)(2,1)}) custom-call(s32[8]{0:T(128)} %stack.31.place_ref.refs_0_, s32[1,512]{1,0:T(1,128)} %ids_ref.5, f32[1,512]{1,0:T(1,128)} %expression_ref.3, bf16[512,768]{1,0:T(8,128)(2,1)} %bitcast.27, bf16[2304,768]{1,0:T(8,128)(2,1)} %table_ref.1, ...), custom_call_target="tpu_custom_call" | custom-call | tf_op jit(solution)/shard_map/embed/pallas_call | solution.py:115
  14.4 1.1 copy-done.2
  16.5 1.2 collective-permute-done.kr_ref.vr_ref
  17.7 14.1 %attend.1 = (bf16[512,768]{1,0:T(8,128)(2,1)S(1)}, bf16[12,1024,512]{2,1,0:T(8,128)(2,1)}, f32[6,2,512]{2,1,0:T(2,128)S(1)}) custom-call(s32[8]{0:T(128)S(1)} %copy-done.11, bf16[512,768]{1,0:T(8,128)(2,1)S(1)} %queries.1.q_ref, bf16[512,1536]{1,0:T(8,128)(2,1)S(1)} %copy-done.14, bf16[512,1536]{1,0:T(8,128)(2,1)S(1)} %copy-done.14, ...), custom_call_target="tpu_custom_call" | custom-call | flops 3221225472 | bytes 12582912 | tf_op jit(solution)/shard_map/attend/pallas_call | solution.py:218
  31.9 22.8 %feed_forward.1 = (bf16[512,768]{1,0:T(8,128)(2,1)}, f32[512,768]{1,0:T(8,128)S(1)}, f32[512,768]{1,0:T(8,128)S(1)}, bf16[768,1536]{1,0:T(8,128)(2,1)}, bf16[768...) custom-call(s32[8]{0:T(128)S(1)} %copy-done.11, ...), custom_call_target="tpu_custom_call" | custom-call | flops 999999995904 | bytes 1 | tf_op jit(solution)/shard_map/feed_forward/pallas_call | solution.py:422
  55.2 3.6 %branch_back.1 = (f32[512,768]{1,0:T(8,128)S(1)}, bf16[512,768]{1,0:T(8,128)(2,1)S(1)}, bf16[768,384]{1,0:T(8,128)(2,1)S(1)}, bf16[768,384]{1,0:T(8,128)(2,1)S(1)}, f32[4,768]{1,0:T(4,128)S(1)}) custom-call(s32[8]{0:T(128)S(1)} %copy-done.11, f32[512,768]{1,0:T(8,128)S(1)} %get-tuple-element.93.residual_ref, f32[512,768]{1,0:T(8,128)S(1)} %get-tuple-element.94.g_normed_ref, ...), custom_call_target="tpu_custom_call" | custom-call | flops 999999995904 | bytes 1 | tf_op jit(solution)/shard_map/branch_back/pallas_call | solution.py:536
  59.6 1.2 copy-done.31
  61.2 2.2 %collective-permute-done.2 = bf16[768,384]{1,0:T(8,128)(2,1)S(1)} collective-permute-done((bf16[768,384]{1,0:T(8,128)(2,1)S(1)}, bf16[768,384]{1,0:T(8,128)(2,1)S(1)}, u32[]{:S(2)}, u32[]{:S(2)}) %collective-permute-start.2) | collective-permute-done | bytes 589856 | tf_op jit(solution)/shard_map/ppermute | solution.py:871
  64.3 4.7 %combine.10 = (bf16[2,2,2,224,384]{4,3,2,1,0:T(8,128)(2,1)}, bf16[2,2,2,208,384]{4,3,2,1,0:T(8,128)(2,1)}) custom-call(s32[8]{0:T(128)S(1)} %copy-done.11, bf16[2,2,2,2,192,384]{5,4,3,2,1,0:T(8,128)(2,1)} %bitcast.72, bf16[2,2,2,2,192,384]{5,4,3,2,1,0:T(8,128)(2,1)} %bitcast.13.refs_2_, bf16[2,2,2,2,48,384]{5,4,3,2,1,0:T(8,128)(2,1)} %bitcast.52, ...), custom_call_target="tpu_custom_call" | custom-call | flops 999999995904 | bytes 1 | tf_op jit(solution)/shard_map/combine/pallas_call | solution.py:1052
  69.0 2.8 %collective-permute-start.6 = (bf16[2,2,2,224,384]{4,3,2,1,0:T(8,128)(2,1)}, bf16[2,2,2,224,384]{4,3,2,1,0:T(8,128)(2,1)}, u32[]{:S(2)}, u32[]{:S(2)}) collective-permute-start(bf16[2,2,2,224,384]{4,3,2,1,0:T(8,128)(2,1)} %get-tuple-element.104.rest_0_), channel_id=1, source_target_pairs={{0,2},{2,0},{4,6},{6,4},{8,10},{10,8},{12,14},{14,12},{16,18},{18,... | collective-permute-start | bytes 4128776 | tf_op jit(solution)/shard_map/ppermute | solution.py:876
  71.8 1.5 collective-permute-start.7
  73.3 12.6 %attend_back.2 = (bf16[512,512]{1,0:T(8,128)(2,1)S(1)}, bf16[2,512,512]{2,1,0:T(8,128)(2,1)S(1)}, bf16[2,512,512]{2,1,0:T(8,128)(2,1)}) custom-call(bf16[512,768]{1,0:T(8,128)(2,1)S(1)} %copy-done.6, bf16[512,1536]{1,0:T(8,128)(2,1)S(1)} %copy-done.15, bf16[512,1536]{1,0:T(8,128)(2,1)S(1)} %copy-done.15, bf16[512,1536]{1,0:T(8,128)(2,1)} %copy-done.16, ...), custom_call_target="tpu_custom_call" | custom-call | flops 999999995904 | bytes 1 | tf_op jit(solution)/shard_map/attend_back/pallas_call | solution.py:301
  86.0 7.5 %attend_back.3 = (bf16[512,256]{1,0:T(8,128)(2,1)S(1)}, bf16[2,512,256]{2,1,0:T(8,128)(2,1)S(1)}, bf16[2,512,256]{2,1,0:T(8,128)(2,1)}) custom-call(bf16[512,768]{1,0:T(8,128)(2,1)S(1)} %copy-done.6, bf16[512,1536]{1,0:T(8,128)(2,1)S(1)} %copy-done.15, bf16[512,1536]{1,0:T(8,128)(2,1)S(1)} %copy-done.15, bf16[512,1536]{1,0:T(8,128)(2,1)S(1)} %copy-done.17, ...), custom_call_target="tpu_custom_call" | custom-call | flops 999999995904 | bytes 1 | tf_op jit(solution)/shard_map/attend_back/pallas_call | solution.py:301
  93.5 6.4 %first_back.1 = (bf16[768,768]{1,0:T(8,128)(2,1)S(1)}, bf16[768,768]{1,0:T(8,128)(2,1)S(1)}, f32[2,2,256]{2,1,0:T(2,128)S(1)}, f32[512,768]{1,0:T(8,128)S(1)}) custom-call(s32[8]{0:T(128)S(1)} %copy-done.11, bf16[512,768]{1,0:T(8,128)(2,1)S(1)} %copy-done.3, bf16[512,512]{1,0:T(8,128)(2,1)S(1)} %get-tuple-element.106.rest_0_.dq_ref, ...), custom_call_target="tpu_custom_call" | custom-call | flops 999999995904 | bytes 1 | tf_op jit(solution)/shard_map/first_back/pallas_call | solution.py:726
  99.9 1.0 copy-done.27
  102.6 1.3 collective-permute-done.8
  104.0 4.4 %combine.11 = (bf16[2,2,224,384]{3,2,1,0:T(8,128)(2,1)}, bf16[2,2,208,384]{3,2,1,0:T(8,128)(2,1)}, bf16[2,2,2,96,384]{4,3,2,1,0:T(8,128)(2,1)}) custom-call(s32[8]{0:T(128)S(1)} %copy-done.12, bf16[2,2,2,2,192,384]{5,4,3,2,1,0:T(8,128)(2,1)} %bitcast.73, bf16[2,2,2,2,192,384]{5,4,3,2,1,0:T(8,128)(2,1)} %bitcast.13.refs_2_, ...), custom_call_target="tpu_custom_call" | custom-call | flops 999999995904 | bytes 1 | tf_op jit(solution)/shard_map/combine/pallas_call | solution.py:1052
  108.4 1.6 collective-permute-start.11
  110.5 1.5 collective-permute-start.16
  112.0 7.4 %last_back.1 = (bf16[16,64,768]{2,1,0:T(8,128)(2,1)}, bf16[16,64,768]{2,1,0:T(8,128)(2,1)S(1)}, bf16[512,768]{1,0:T(8,128)(2,1)S(1)}) custom-call(s32[8]{0:T(128)S(1)} %copy-done.12, bf16[512,768]{1,0:T(8,128)(2,1)S(1)} %copy-done.4, bf16[512,256]{1,0:T(8,128)(2,1)S(1)} %copy-done.35, bf16[2,512,256]{2,1,0:T(8,128)(2,1)S(1)} %get-tuple-element.108.own_ref, ...), custom_call_target="tpu_custom_call" | custom-call | flops 999999995904 | bytes 1 | tf_op jit(solution)/shard_map/last_back/pallas_call | solution.py:780
  119.4 2.3 %gene_rows.2.rest_0_ = bf16[1152,768]{1,0:T(8,128)(2,1)} custom-call(s32[1152,1]{1,0:T(8,128)S(1)} %broadcast_add_fusion.slots_ref, s32[1,512]{1,0:T(1,128)S(1)} %copy-done.10, bf16[512,768]{1,0:T(8,128)(2,1)S(1)} %get-tuple-element.124.grad_ref, bf16[16,64,768]{2,1,0:T(8,128)(2,1)} %get-tuple-element.123.rest_0_), custom_call_target="tpu_custom_call" | custom-call | flops 999999995904 | bytes 1 | tf_op jit(solution)/shard_map/gene_rows/pallas_call | solution.py:853
  122.3 1.1 gene_rows.3.refs_4_
  123.4 0.9 collective-permute-done.11.refs_3_.refs_15_.refs_7_.refs_10_
  124.3 2.5 %combine.12.refs_11_ = bf16[2,2,96,384]{3,2,1,0:T(8,128)(2,1)} custom-call(s32[8]{0:T(128)S(1)} %copy-done.12, bf16[2,2,2,2,48,768]{5,4,3,2,1,0:T(8,128)(2,1)} %bitcast.48, bf16[2,2,2,2,48,768]{5,4,3,2,1,0:T(8,128)(2,1)} %bitcast.19.refs_12_.refs_2_.refs_14_.refs_6_.refs_9_, ...), custom_call_target="tpu_custom_call" | custom-call | flops 999999995904 | bytes 1 | tf_op jit(solution)/shard_map/combine/pallas_call | solution.py:1052
  126.8 2.6 %collective-permute-start.14 = (bf16[2,2,96,384]{3,2,1,0:T(8,128)(2,1)}, bf16[2,2,96,384]{3,2,1,0:T(8,128)(2,1)}, u32[]{:S(2)}, u32[]{:S(2)}) collective-permute-start(bf16[2,2,96,384]{3,2,1,0:T(8,128)(2,1)} %combine.12.refs_11_), channel_id=1, source_target_pairs={{0,16},{2,18},{4,20},{6,22},{8,24},{10,26},{12,28},{14,30},{16,0},... | collective-permute-start | bytes 884744 | tf_op jit(solution)/shard_map/ppermute | solution.py:876
  129.4 4.0 %combine.13 = (bf16[2,2,2,120,384]{4,3,2,1,0:T(8,128)(2,1)}, bf16[2,2,2,136,384]{4,3,2,1,0:T(8,128)(2,1)}) custom-call(s32[8]{0:T(128)S(1)} %copy-done.12, bf16[2,2,2,2,64,768]{5,4,3,2,1,0:T(8,128)(2,1)} %bitcast.38, bf16[2,2,2,2,64,768]{5,4,3,2,1,0:T(8,128)(2,1)} %bitcast.21.refs_2_.refs_6_.refs_8_.refs_7_.refs_9_, ...), custom_call_target="tpu_custom_call" | custom-call | flops 999999995904 | bytes 1 | tf_op jit(solution)/shard_map/combine/pallas_call | solution.py:1052
  134.8 4.4 %combine.14 = (bf16[432,384]{1,0:T(8,128)(2,1)}, bf16[432,384]{1,0:T(8,128)(2,1)}, bf16[432,384]{1,0:T(8,128)(2,1)}) custom-call(s32[8]{0:T(128)S(1)} %copy-done.12, bf16[2,2,2,2,192,384]{5,4,3,2,1,0:T(8,128)(2,1)} %bitcast.74, bf16[2,2,2,2,192,384]{5,4,3,2,1,0:T(8,128)(2,1)} %bitcast.13.refs_2_, bf16[2,2,2,2,48,384]{5,4,3,2,1,0:T(8,128)(2,1)} %bitcast.56, ...), custom_call_target="tpu_custom_call" | custom-call | flops 999999995904 | bytes 1 | tf_op jit(solution)/shard_map/combine/pallas_call | solution.py:1052
  139.1 1.4 collective-permute-start.20
  140.8 2.2 %collective-permute-done.14.refs_16_.refs_8_.refs_11_ = bf16[2,2,96,384]{3,2,1,0:T(8,128)(2,1)} collective-permute-done((bf16[2,2,96,384]{3,2,1,0:T(8,128)(2,1)}, bf16[2,2,96,384]{3,2,1,0:T(8,128)(2,1)}, u32[]{:S(2)}, u32[]{:S(2)}) %collective-permute-start.14) | collective-permute-done | bytes 294944 | tf_op jit(solution)/shard_map/ppermute | solution.py:876
  143.1 3.4 %collective-permute-start.22 = (bf16[432,384]{1,0:T(8,128)(2,1)}, bf16[432,384]{1,0:T(8,128)(2,1)}, u32[]{:S(2)}, u32[]{:S(2)}) collective-permute-start(bf16[432,384]{1,0:T(8,128)(2,1)} %get-tuple-element.129.refs_19_), channel_id=1, source_target_pairs={{0,24},{2,26},{4,28},{6,30},{8,16},{10,18},{12,20},{14,22},{16,8},... | collective-permute-start | bytes 995336 | tf_op jit(solution)/shard_map/ppermute | solution.py:876
  146.4 5.2 %collective-permute-done.12.refs_5_ = bf16[2,2,2,120,384]{4,3,2,1,0:T(8,128)(2,1)} collective-permute-done((bf16[2,2,2,120,384]{4,3,2,1,0:T(8,128)(2,1)}, bf16[2,2,2,120,384]{4,3,2,1,0:T(8,128)(2,1)}, u32[]{:S(2)}, u32[]{:S(2)}) %collective-permute-start.12) | collective-permute-done | bytes 737312 | tf_op jit(solution)/shard_map/ppermute | solution.py:876
  151.7 1.9 collective-permute-done.13.refs_12_
  153.5 3.6 %combine.15 = (bf16[2,2,120,384]{3,2,1,0:T(8,128)(2,1)}, bf16[2,2,136,384]{3,2,1,0:T(8,128)(2,1)}, bf16[2,96,384]{2,1,0:T(8,128)(2,1)}) custom-call(s32[8]{0:T(128)S(1)} %copy-done.12, bf16[2,2,2,2,64,768]{5,4,3,2,1,0:T(8,128)(2,1)} %bitcast.41, bf16[2,2,2,2,64,768]{5,4,3,2,1,0:T(8,128)(2,1)} %bitcast.21.refs_2_.refs_6_.refs_8_.refs_7_.refs_9_, ...), custom_call_target="tpu_custom_call" | custom-call | flops 999999995904 | bytes 1 | tf_op jit(solution)/shard_map/combine/pallas_call | solution.py:1052
  157.7 1.2 collective-permute-start.17
  158.9 2.7 %combine.16 = (f32[2,2,120,384]{3,2,1,0:T(8,128)S(1)}, f32[2,2,136,384]{3,2,1,0:T(8,128)S(1)}) custom-call(s32[8]{0:T(128)S(1)} %copy-done.12, bf16[2,2,2,2,64,768]{5,4,3,2,1,0:T(8,128)(2,1)} %bitcast.44, bf16[2,2,2,2,64,768]{5,4,3,2,1,0:T(8,128)(2,1)} %bitcast.21.refs_2_.refs_6_.refs_8_.refs_7_.refs_9_, bf16[2,2,2,2,72,768]{5,4,3,2,1,0:T(8,128)(2,1)} %bitcast.36, ...), custom_call_target="tpu_custom_call" | custom-call | flops 999999995904 | bytes 1 | tf_op jit(solution)/shard_map/combine/pallas_call | solution.py:1052
  162.5 4.1 %collective-permute-done.21.refs_14_ = bf16[432,384]{1,0:T(8,128)(2,1)} collective-permute-done((bf16[432,384]{1,0:T(8,128)(2,1)}, bf16[432,384]{1,0:T(8,128)(2,1)}, u32[]{:S(2)}, u32[]{:S(2)}) %collective-permute-start.21) | collective-permute-done | bytes 331808 | tf_op jit(solution)/shard_map/ppermute | solution.py:876
  166.6 3.4 %combine.17.refs_10_.own_ref = f32[432,384]{1,0:T(8,128)} custom-call(s32[8]{0:T(128)S(1)} %copy-done.12, bf16[2,2,2,2,192,384]{5,4,3,2,1,0:T(8,128)(2,1)} %bitcast.75, bf16[2,2,2,2,192,384]{5,4,3,2,1,0:T(8,128)(2,1)} %bitcast.13.refs_2_, bf16[2,2,2,2,48,384]{5,4,3,2,1,0:T(8,128)(2,1)} %bitcast.58, bf16[2,2,2,2,48,384]{5,4,3,2,1,0:T(8,128)(2,1)} %bitcast.66, ...), custom_call_target="tpu_custom_call" | custom-call | flops 999999995904 | bytes 1 | tf_op jit(solution)/shard_map/combine/pallas_call | solution.py:1052
  170.5 3.2 %combine.18 = (bf16[264,384]{1,0:T(8,128)(2,1)}, bf16[264,384]{1,0:T(8,128)(2,1)}, bf16[264,384]{1,0:T(8,128)(2,1)}, bf16[96,384]{1,0:T(8,128)(2,1)}) custom-call(s32[8]{0:T(128)S(1)} %copy-done.12, f32[2,2,120,384]{3,2,1,0:T(8,128)} %copy-done.33, f32[2,2,136,384]{3,2,1,0:T(8,128)} %copy-done.32, bf16[2,2,120,384]{3,2,1,0:T(8,128)(2,1)} %collective-permute-done.17.refs_3_, ...), custom_call_target="tpu_custom_call" | custom-call | flops 999999995904 | bytes 1 | tf_op jit(solution)/shard_map/combine/pallas_call | solution.py:1052
  173.7 5.0 %collective-permute-start.23 = (bf16[264,384]{1,0:T(8,128)(2,1)}, bf16[264,384]{1,0:T(8,128)(2,1)}, u32[]{:S(2)}, u32[]{:S(2)}) collective-permute-start(bf16[264,384]{1,0:T(8,128)(2,1)} %get-tuple-element.135), channel_id=1, source_target_pairs={{0,8},{2,10},{4,12},{6,14},{8,0},{10,2},{12,4},{14,6},{16,24},{18,... | collective-permute-start | bytes 608264 | tf_op jit(solution)/shard_map/ppermute | solution.py:876
  178.6 2.0 collective-permute-start.24
  180.6 1.4 collective-permute-start.25
  182.5 2.9 %assemble.2 = (f32[192,768]{1,0:T(8,128)}, f32[48,3072]{1,0:T(8,128)}, f32[48,768]{1,0:T(8,128)}, f32[8,128]{1,0:T(8,128)S(1)}) custom-call(s32[8]{0:T(128)S(1)} %copy-done.12, f32[432,384]{1,0:T(8,128)} %combine.17.refs_10_.own_ref, f32[432,384]{1,0:T(8,128)} %collective-permute-done.27.other_ref), custom_call_target="tpu_custom_call" | custom-call | flops 999999995904 | bytes 1 | tf_op jit(solution)/shard_map/assemble/pallas_call | solution.py:1103
  185.4 1.2 collective-permute-done.26.refs_13_
  186.7 2.3 %collective-permute-done.23.refs_5_ = bf16[264,384]{1,0:T(8,128)(2,1)} collective-permute-done((bf16[264,384]{1,0:T(8,128)(2,1)}, bf16[264,384]{1,0:T(8,128)(2,1)}, u32[]{:S(2)}, u32[]{:S(2)}) %collective-permute-start.23) | collective-permute-done | bytes 202784 | tf_op jit(solution)/shard_map/ppermute | solution.py:876
  189.0 7.6 %collective-permute-done.25.refs_7_ = bf16[264,384]{1,0:T(8,128)(2,1)} collective-permute-done((bf16[264,384]{1,0:T(8,128)(2,1)}, bf16[264,384]{1,0:T(8,128)(2,1)}, u32[]{:S(2)}, u32[]{:S(2)}) %collective-permute-start.25) | collective-permute-done | bytes 202784 | tf_op jit(solution)/shard_map/ppermute | solution.py:876
  196.5 2.8 %combine.19 = (f32[208,384]{1,0:T(8,128)S(1)}, f32[72,768]{1,0:T(8,128)}) custom-call(s32[8]{0:T(128)S(1)} %copy-done.12, f32[2,2,120,384]{3,2,1,0:T(8,128)} %copy-done.33, f32[2,2,136,384]{3,2,1,0:T(8,128)} %copy-done.32, bf16[2,2,120,384]{3,2,1,0:T(8,128)(2,1)} %collective-permute-done.17.refs_3_, ...), custom_call_target="tpu_custom_call" | custom-call | flops 999999995904 | bytes 1 | tf_op jit(solution)/shard_map/combine/pallas_call | solution.py:1052
  199.3 1.6 collective-permute-done.28.other_ref
  200.9 1.5 assemble.3
  (110 shorter events, 11.2 us)
Async XLA Ops:
  2.6 11.9 %copy-start = (bf16[768,2304]{1,0:T(8,128)(2,1)S(1)}, bf16[768,2304]{1,0:T(8,128)(2,1)}, u32[]{:S(2)}) copy-start(bf16[768,2304]{1,0:T(8,128)(2,1)} %wv_ref.3) | copy-start | bytes 10616836
  2.6 11.9 %copy-start.8 = (f32[768]{0:T(1024)S(1)}, f32[768]{0:T(1024)}, u32[]{:S(2)}) copy-start(f32[768]{0:T(1024)} %bias_ref.1) | copy-start | bytes 9220
  14.0 3.7 %collective-permute-start = (bf16[512,1536]{1,0:T(8,128)(2,1)}, bf16[512,1536]{1,0:T(8,128)(2,1)S(1)}, u32[]{:S(2)}, u32[]{:S(2)}) collective-permute-start(bf16[512,1536]{1,0:T(8,128)(2,1)} %get-tuple-element.89.ko_ref.vo_ref), channel_id=1, source_target_pairs={{0,1},{1,0},{2,3},{3,2},{4,5},{5,4},{6,7},{7,6},{8,9},{9,8},{10,11... | collective-permute-start | bytes 4718600 | tf_op jit(solution)/shard_map/ppermute | solution.py:871
  16.4 15.4 %copy-start.5 = (bf16[512,768]{1,0:T(8,128)(2,1)}, bf16[512,768]{1,0:T(8,128)(2,1)S(1)}, u32[]{:S(2)}) copy-start(bf16[512,768]{1,0:T(8,128)(2,1)S(1)} %queries.1.q_ref) | copy-start | bytes 2359300
  16.4 15.4 %copy-start.13 = (f32[512,768]{1,0:T(8,128)S(1)}, f32[512,768]{1,0:T(8,128)}, u32[]{:S(2)}) copy-start(f32[512,768]{1,0:T(8,128)} %get-tuple-element.91.embedded_ref) | copy-start | bytes 4718596
  16.4 15.4 %copy-start.18 = (bf16[768,768]{1,0:T(8,128)(2,1)S(1)}, bf16[768,768]{1,0:T(8,128)(2,1)}, u32[]{:S(2)}) copy-start(bf16[768,768]{1,0:T(8,128)(2,1)} %w_out_ref.3) | copy-start | bytes 3538948
  16.4 15.4 %copy-start.19 = (bf16[1,512,768]{2,1,0:T(8,128)(2,1)S(1)}, bf16[1,512,768]{2,1,0:T(8,128)(2,1)}, u32[]{:S(2)}) copy-start(bf16[1,512,768]{2,1,0:T(8,128)(2,1)} %param.45) | copy-start | bytes 2359300
  16.4 15.4 %copy-start.20 = (f32[3072]{0:T(1024)S(1)}, f32[3072]{0:T(1024)}, u32[]{:S(2)}) copy-start(f32[3072]{0:T(1024)} %param.42) | copy-start | bytes 36868
  16.4 15.4 %copy-start.21 = (f32[768]{0:T(1024)S(1)}, f32[768]{0:T(1024)}, u32[]{:S(2)}) copy-start(f32[768]{0:T(1024)} %bias_out_ref.1) | copy-start | bytes 9220
  16.4 15.4 %copy-start.22 = (f32[768]{0:T(1024)S(1)}, f32[768]{0:T(1024)}, u32[]{:S(2)}) copy-start(f32[768]{0:T(1024)} %offset_ref.3) | copy-start | bytes 9220
  16.5 15.4 %copy-start.23 = (f32[768]{0:T(1024)S(1)}, f32[768]{0:T(1024)}, u32[]{:S(2)}) copy-start(f32[768]{0:T(1024)} %bias_down_ref.1) | copy-start | bytes 9220
  16.5 15.4 %copy-start.24 = (f32[768]{0:T(1024)S(1)}, f32[768]{0:T(1024)}, u32[]{:S(2)}) copy-start(f32[768]{0:T(1024)} %gain_ref.6) | copy-start | bytes 9220
  17.7 14.1 %copy-start.16 = (bf16[512,1536]{1,0:T(8,128)(2,1)}, bf16[512,1536]{1,0:T(8,128)(2,1)S(1)}, u32[]{:S(2)}) copy-start(bf16[512,1536]{1,0:T(8,128)(2,1)S(1)} %collective-permute-done.kr_ref.vr_ref) | copy-start | bytes 4718596
  31.8 23.4 %copy-start.29 = (bf16[512,768]{1,0:T(8,128)(2,1)}, bf16[512,768]{1,0:T(8,128)(2,1)S(1)}, u32[]{:S(2)}) copy-start(bf16[512,768]{1,0:T(8,128)(2,1)S(1)} %get-tuple-element.90.attended_ref.a_ref) | copy-start | bytes 2359300
  54.7 8.8 %collective-permute-start.1 = (bf16[3072,384]{1,0:T(8,128)(2,1)}, bf16[3072,384]{1,0:T(8,128)(2,1)}, u32[]{:S(2)}, u32[]{:S(2)}) collective-permute-start(bf16[3072,384]{1,0:T(8,128)(2,1)} %get-tuple-element.96.rest_1_), channel_id=1, source_target_pairs={{0,1},{1,0},{2,3},{3,2},{4,5},{5,4},{6,7},{7,6},{8,9},{9,8},{10,11... | collective-permute-start | bytes 7077896 | tf_op jit(solution)/shard_map/ppermute | solution.py:871
  55.1 8.4 %collective-permute-start.3 = (bf16[768,1536]{1,0:T(8,128)(2,1)}, bf16[768,1536]{1,0:T(8,128)(2,1)}, u32[]{:S(2)}, u32[]{:S(2)}) collective-permute-start(bf16[768,1536]{1,0:T(8,128)(2,1)} %get-tuple-element.95.rest_0_), channel_id=1, source_target_pairs={{0,1},{1,0},{2,3},{3,2},{4,5},{5,4},{6,7},{7,6},{8,9},{9,8},{10,11... | collective-permute-start | bytes 7077896 | tf_op jit(solution)/shard_map/ppermute | solution.py:871
  60.8 2.7 %collective-permute-start.2 = (bf16[768,384]{1,0:T(8,128)(2,1)S(1)}, bf16[768,384]{1,0:T(8,128)(2,1)S(1)}, u32[]{:S(2)}, u32[]{:S(2)}) collective-permute-start(bf16[768,384]{1,0:T(8,128)(2,1)S(1)} %get-tuple-element.102), channel_id=1, source_target_pairs={{0,1},{1,0},{2,3},{3,2},{4,5},{5,4},{6,7},{7,6},{8,9},{9,8},{10,11... | collective-permute-start | bytes 1769480 | tf_op jit(solution)/shard_map/ppermute | solution.py:871
  64.3 9.0 %copy-start.6 = (bf16[512,768]{1,0:T(8,128)(2,1)S(1)}, bf16[512,768]{1,0:T(8,128)(2,1)}, u32[]{:S(2)}) copy-start(bf16[512,768]{1,0:T(8,128)(2,1)} %copy-done.5) | copy-start | bytes 2359300
  64.3 9.0 %copy-start.15 = (bf16[512,1536]{1,0:T(8,128)(2,1)S(1)}, bf16[512,1536]{1,0:T(8,128)(2,1)}, u32[]{:S(2)}) copy-start(bf16[512,1536]{1,0:T(8,128)(2,1)} %get-tuple-element.89.ko_ref.vo_ref) | copy-start | bytes 4718596
  64.3 9.0 %copy-start.30 = (bf16[512,768]{1,0:T(8,128)(2,1)S(1)}, bf16[512,768]{1,0:T(8,128)(2,1)}, u32[]{:S(2)}) copy-start(bf16[512,768]{1,0:T(8,128)(2,1)} %copy-done.29) | copy-start | bytes 2359300
  69.0 33.6 %collective-permute-start.6 = (bf16[2,2,2,224,384]{4,3,2,1,0:T(8,128)(2,1)}, bf16[2,2,2,224,384]{4,3,2,1,0:T(8,128)(2,1)}, u32[]{:S(2)}, u32[]{:S(2)}) collective-permute-start(bf16[2,2,2,224,384]{4,3,2,1,0:T(8,128)(2,1)} %get-tuple-element.104.rest_0_), channel_id=1, source_target_pairs={{0,2},{2,0},{4,6},{6,4},{8,10},{10,8},{12,14},{14,12},{16,18},{18,... | collective-permute-start | bytes 4128776 | tf_op jit(solution)/shard_map/ppermute | solution.py:876
  71.8 30.2 %collective-permute-start.7 = (bf16[2,2,2,208,384]{4,3,2,1,0:T(8,128)(2,1)}, bf16[2,2,2,208,384]{4,3,2,1,0:T(8,128)(2,1)}, u32[]{:S(2)}, u32[]{:S(2)}) collective-permute-start(bf16[2,2,2,208,384]{4,3,2,1,0:T(8,128)(2,1)} %get-tuple-element.105.rest_1_), channel_id=1, source_target_pairs={{0,4},{2,6},{4,0},{6,2},{8,12},{10,14},{12,8},{14,10},{16,20},{18,... | collective-permute-start | bytes 3833864 | tf_op jit(solution)/shard_map/ppermute | solution.py:876
  73.3 12.6 %copy-start.17 = (bf16[512,1536]{1,0:T(8,128)(2,1)S(1)}, bf16[512,1536]{1,0:T(8,128)(2,1)}, u32[]{:S(2)}) copy-start(bf16[512,1536]{1,0:T(8,128)(2,1)} %copy-done.16) | copy-start | bytes 4718596
  85.9 7.6 %collective-permute-start.5 = (bf16[2,512,512]{2,1,0:T(8,128)(2,1)}, bf16[2,512,512]{2,1,0:T(8,128)(2,1)}, u32[]{:S(2)}, u32[]{:S(2)}) collective-permute-start(bf16[2,512,512]{2,1,0:T(8,128)(2,1)} %get-tuple-element.111), channel_id=1, source_target_pairs={{0,1},{1,0},{2,3},{3,2},{4,5},{5,4},{6,7},{7,6},{8,9},{9,8},{10,11... | collective-permute-start | bytes 3145736 | tf_op jit(solution)/shard_map/ppermute | solution.py:871
  93.5 10.4 %copy-start.12 = (s32[8]{0:T(128)S(1)}, s32[8]{0:T(128)}, u32[]{:S(2)}) copy-start(s32[8]{0:T(128)} %stack.31.place_ref.refs_0_) | copy-start | bytes 100
  100.9 3.0 %collective-permute-start.8 = (bf16[768,768]{1,0:T(8,128)(2,1)S(1)}, bf16[768,768]{1,0:T(8,128)(2,1)}, u32[]{:S(2)}, u32[]{:S(2)}) collective-permute-start(bf16[768,768]{1,0:T(8,128)(2,1)S(1)} %get-tuple-element.118.refs_14_), channel_id=1, source_target_pairs={{0,1},{1,0},{2,3},{3,2},{4,5},{5,4},{6,7},{7,6},{8,9},{9,8},{10,11... | collective-permute-start | bytes 3538952 | tf_op jit(solution)/shard_map/ppermute | solution.py:871
  101.5 10.5 %collective-permute-start.4 = (bf16[2,512,256]{2,1,0:T(8,128)(2,1)}, bf16[2,512,256]{2,1,0:T(8,128)(2,1)}, u32[]{:S(2)}, u32[]{:S(2)}) collective-permute-start(bf16[2,512,256]{2,1,0:T(8,128)(2,1)} %get-tuple-element.109), channel_id=1, source_target_pairs={{0,1},{1,0},{2,3},{3,2},{4,5},{5,4},{6,7},{7,6},{8,9},{9,8},{10,11... | collective-permute-start | bytes 1572872 | tf_op jit(solution)/shard_map/ppermute | solution.py:871
  108.4 15.9 %collective-permute-start.11 = (bf16[2,2,2,96,384]{4,3,2,1,0:T(8,128)(2,1)}, bf16[2,2,2,96,384]{4,3,2,1,0:T(8,128)(2,1)}, u32[]{:S(2)}, u32[]{:S(2)}) collective-permute-start(bf16[2,2,2,96,384]{4,3,2,1,0:T(8,128)(2,1)} %get-tuple-element.121.rest_2_), channel_id=1, source_target_pairs={{0,8},{2,10},{4,12},{6,14},{8,0},{10,2},{12,4},{14,6},{16,24},{18,... | collective-permute-start | bytes 1769480 | tf_op jit(solution)/shard_map/ppermute | solution.py:876
  110.0 24.7 %collective-permute-start.15 = (bf16[2,2,224,384]{3,2,1,0:T(8,128)(2,1)}, bf16[2,2,224,384]{3,2,1,0:T(8,128)(2,1)}, u32[]{:S(2)}, u32[]{:S(2)}) collective-permute-start(bf16[2,2,224,384]{3,2,1,0:T(8,128)(2,1)} %get-tuple-element.119.rest_0_), channel_id=1, source_target_pairs={{0,4},{2,6},{4,0},{6,2},{8,12},{10,14},{12,8},{14,10},{16,20},{18,... | collective-permute-start | bytes 2064392 | tf_op jit(solution)/shard_map/ppermute | solution.py:876
  110.5 24.2 %collective-permute-start.16 = (bf16[2,2,208,384]{3,2,1,0:T(8,128)(2,1)}, bf16[2,2,208,384]{3,2,1,0:T(8,128)(2,1)}, u32[]{:S(2)}, u32[]{:S(2)}) collective-permute-start(bf16[2,2,208,384]{3,2,1,0:T(8,128)(2,1)} %get-tuple-element.120.rest_1_), channel_id=1, source_target_pairs={{0,2},{2,0},{4,6},{6,4},{8,10},{10,8},{12,14},{14,12},{16,18},{18,... | collective-permute-start | bytes 1916936 | tf_op jit(solution)/shard_map/ppermute | solution.py:876
  119.4 10.0 %collective-permute-start.9 = (bf16[16,64,768]{2,1,0:T(8,128)(2,1)}, bf16[16,64,768]{2,1,0:T(8,128)(2,1)}, u32[]{:S(2)}, u32[]{:S(2)}) collective-permute-start(bf16[16,64,768]{2,1,0:T(8,128)(2,1)} %get-tuple-element.123.rest_0_), channel_id=1, source_target_pairs={{0,1},{1,0},{2,3},{3,2},{4,5},{5,4},{6,7},{7,6},{8,9},{9,8},{10,11... | collective-permute-start | bytes 4718600 | tf_op jit(solution)/shard_map/ppermute | solution.py:871
  121.8 7.6 %collective-permute-start.10 = (bf16[1152,768]{1,0:T(8,128)(2,1)}, bf16[1152,768]{1,0:T(8,128)(2,1)}, u32[]{:S(2)}, u32[]{:S(2)}) collective-permute-start(bf16[1152,768]{1,0:T(8,128)(2,1)} %gene_rows.2.rest_0_), channel_id=1, source_target_pairs={{0,1},{1,0},{2,3},{3,2},{4,5},{5,4},{6,7},{7,6},{8,9},{9,8},{10,11... | collective-permute-start | bytes 5308424 | tf_op jit(solution)/shard_map/ppermute | solution.py:871
  126.8 16.2 %collective-permute-start.14 = (bf16[2,2,96,384]{3,2,1,0:T(8,128)(2,1)}, bf16[2,2,96,384]{3,2,1,0:T(8,128)(2,1)}, u32[]{:S(2)}, u32[]{:S(2)}) collective-permute-start(bf16[2,2,96,384]{3,2,1,0:T(8,128)(2,1)} %combine.12.refs_11_), channel_id=1, source_target_pairs={{0,16},{2,18},{4,20},{6,22},{8,24},{10,26},{12,28},{14,30},{16,0},... | collective-permute-start | bytes 884744 | tf_op jit(solution)/shard_map/ppermute | solution.py:876
  133.4 20.1 %collective-permute-start.13 = (bf16[2,2,2,136,384]{4,3,2,1,0:T(8,128)(2,1)}, bf16[2,2,2,136,384]{4,3,2,1,0:T(8,128)(2,1)}, u32[]{:S(2)}, u32[]{:S(2)}) collective-permute-start(bf16[2,2,2,136,384]{4,3,2,1,0:T(8,128)(2,1)} %get-tuple-element.126.refs_14_), channel_id=1, source_target_pairs={{0,4},{2,6},{4,0},{6,2},{8,12},{10,14},{12,8},{14,10},{16,20},{18,... | collective-permute-start | bytes 2506760 | tf_op jit(solution)/shard_map/ppermute | solution.py:876
  134.0 17.7 %collective-permute-start.12 = (bf16[2,2,2,120,384]{4,3,2,1,0:T(8,128)(2,1)}, bf16[2,2,2,120,384]{4,3,2,1,0:T(8,128)(2,1)}, u32[]{:S(2)}, u32[]{:S(2)}) collective-permute-start(bf16[2,2,2,120,384]{4,3,2,1,0:T(8,128)(2,1)} %get-tuple-element.125.refs_13_), channel_id=1, source_target_pairs={{0,2},{2,0},{4,6},{6,4},{8,10},{10,8},{12,14},{14,12},{16,18},{18,... | collective-permute-start | bytes 2211848 | tf_op jit(solution)/shard_map/ppermute | solution.py:876
  139.1 22.5 %collective-permute-start.20 = (bf16[432,384]{1,0:T(8,128)(2,1)}, bf16[432,384]{1,0:T(8,128)(2,1)}, u32[]{:S(2)}, u32[]{:S(2)}) collective-permute-start(bf16[432,384]{1,0:T(8,128)(2,1)} %get-tuple-element.127.refs_17_), channel_id=1, source_target_pairs={{0,8},{2,10},{4,12},{6,14},{8,0},{10,2},{12,4},{14,6},{16,24},{18,... | collective-permute-start | bytes 995336 | tf_op jit(solution)/shard_map/ppermute | solution.py:876
  140.5 26.2 %collective-permute-start.21 = (bf16[432,384]{1,0:T(8,128)(2,1)}, bf16[432,384]{1,0:T(8,128)(2,1)}, u32[]{:S(2)}, u32[]{:S(2)}) collective-permute-start(bf16[432,384]{1,0:T(8,128)(2,1)} %get-tuple-element.128.refs_18_), channel_id=1, source_target_pairs={{0,16},{2,18},{4,20},{6,22},{8,24},{10,26},{12,28},{14,30},{16,0},... | collective-permute-start | bytes 995336 | tf_op jit(solution)/shard_map/ppermute | solution.py:876
  143.1 23.6 %collective-permute-start.22 = (bf16[432,384]{1,0:T(8,128)(2,1)}, bf16[432,384]{1,0:T(8,128)(2,1)}, u32[]{:S(2)}, u32[]{:S(2)}) collective-permute-start(bf16[432,384]{1,0:T(8,128)(2,1)} %get-tuple-element.129.refs_19_), channel_id=1, source_target_pairs={{0,24},{2,26},{4,28},{6,30},{8,16},{10,18},{12,20},{14,22},{16,8},... | collective-permute-start | bytes 995336 | tf_op jit(solution)/shard_map/ppermute | solution.py:876
  157.1 13.3 %collective-permute-start.18 = (bf16[2,2,136,384]{3,2,1,0:T(8,128)(2,1)}, bf16[2,2,136,384]{3,2,1,0:T(8,128)(2,1)}, u32[]{:S(2)}, u32[]{:S(2)}) collective-permute-start(bf16[2,2,136,384]{3,2,1,0:T(8,128)(2,1)} %get-tuple-element.131.refs_14_), channel_id=1, source_target_pairs={{0,2},{2,0},{4,6},{6,4},{8,10},{10,8},{12,14},{14,12},{16,18},{18,... | collective-permute-start | bytes 1253384 | tf_op jit(solution)/shard_map/ppermute | solution.py:876
  157.7 12.8 %collective-permute-start.17 = (bf16[2,2,120,384]{3,2,1,0:T(8,128)(2,1)}, bf16[2,2,120,384]{3,2,1,0:T(8,128)(2,1)}, u32[]{:S(2)}, u32[]{:S(2)}) collective-permute-start(bf16[2,2,120,384]{3,2,1,0:T(8,128)(2,1)} %get-tuple-element.130.refs_13_), channel_id=1, source_target_pairs={{0,4},{2,6},{4,0},{6,2},{8,12},{10,14},{12,8},{14,10},{16,20},{18,... | collective-permute-start | bytes 1105928 | tf_op jit(solution)/shard_map/ppermute | solution.py:876
  161.6 8.4 %copy-start.32 = (f32[2,2,136,384]{3,2,1,0:T(8,128)}, f32[2,2,136,384]{3,2,1,0:T(8,128)S(1)}, u32[]{:S(2)}) copy-start(f32[2,2,136,384]{3,2,1,0:T(8,128)S(1)} %get-tuple-element.134.refs_17_.refs_2_) | copy-start | bytes 2506756
  161.7 8.8 %collective-permute-start.19 = (bf16[2,96,384]{2,1,0:T(8,128)(2,1)}, bf16[2,96,384]{2,1,0:T(8,128)(2,1)}, u32[]{:S(2)}, u32[]{:S(2)}) collective-permute-start(bf16[2,96,384]{2,1,0:T(8,128)(2,1)} %get-tuple-element.132.refs_15_), channel_id=1, source_target_pairs={{0,2},{2,0},{4,6},{6,4},{8,10},{10,8},{12,14},{14,12},{16,18},{18,... | collective-permute-start | bytes 442376 | tf_op jit(solution)/shard_map/ppermute | solution.py:876
  170.1 12.5 %collective-permute-start.27 = (f32[432,384]{1,0:T(8,128)}, f32[432,384]{1,0:T(8,128)}, u32[]{:S(2)}, u32[]{:S(2)}) collective-permute-start(f32[432,384]{1,0:T(8,128)} %combine.17.refs_10_.own_ref), channel_id=1, source_target_pairs={{0,1},{1,0},{2,3},{3,2},{4,5},{5,4},{6,7},{7,6},{8,9},{9,8},{10,11... | collective-permute-start | bytes 1990664 | tf_op jit(solution)/shard_map/ppermute | solution.py:871
  173.7 15.3 %collective-permute-start.23 = (bf16[264,384]{1,0:T(8,128)(2,1)}, bf16[264,384]{1,0:T(8,128)(2,1)}, u32[]{:S(2)}, u32[]{:S(2)}) collective-permute-start(bf16[264,384]{1,0:T(8,128)(2,1)} %get-tuple-element.135), channel_id=1, source_target_pairs={{0,8},{2,10},{4,12},{6,14},{8,0},{10,2},{12,4},{14,6},{16,24},{18,... | collective-permute-start | bytes 608264 | tf_op jit(solution)/shard_map/ppermute | solution.py:876
  178.6 10.3 %collective-permute-start.24 = (bf16[264,384]{1,0:T(8,128)(2,1)}, bf16[264,384]{1,0:T(8,128)(2,1)}, u32[]{:S(2)}, u32[]{:S(2)}) collective-permute-start(bf16[264,384]{1,0:T(8,128)(2,1)} %get-tuple-element.136), channel_id=1, source_target_pairs={{0,16},{2,18},{4,20},{6,22},{8,24},{10,26},{12,28},{14,30},{16,0},... | collective-permute-start | bytes 608264 | tf_op jit(solution)/shard_map/ppermute | solution.py:876
  180.6 15.9 %collective-permute-start.25 = (bf16[264,384]{1,0:T(8,128)(2,1)}, bf16[264,384]{1,0:T(8,128)(2,1)}, u32[]{:S(2)}, u32[]{:S(2)}) collective-permute-start(bf16[264,384]{1,0:T(8,128)(2,1)} %get-tuple-element.137), channel_id=1, source_target_pairs={{0,24},{2,26},{4,28},{6,30},{8,16},{10,18},{12,20},{14,22},{16,8},... | collective-permute-start | bytes 608264 | tf_op jit(solution)/shard_map/ppermute | solution.py:876
  182.0 4.7 %collective-permute-start.26 = (bf16[96,384]{1,0:T(8,128)(2,1)}, bf16[96,384]{1,0:T(8,128)(2,1)}, u32[]{:S(2)}, u32[]{:S(2)}) collective-permute-start(bf16[96,384]{1,0:T(8,128)(2,1)} %get-tuple-element.138), channel_id=1, source_target_pairs={{0,4},{2,6},{4,0},{6,2},{8,12},{10,14},{12,8},{14,10},{16,20},{18,... | collective-permute-start | bytes 221192 | tf_op jit(solution)/shard_map/ppermute | solution.py:876
  199.3 1.6 collective-permute-start.28
  (18 other events, 85.1 us)

commit v6 on v5

--- a/solution.py
+++ b/solution.py
@@ -415,7 +415,7 @@
 ):
     rows, width = attended.shape
     units = w_up.shape[1]
-    tile = 768
+    tile = 512
     steps = units // tile
     turn = lambda j, place: lax.rem(j + (1 - place[0]) * (steps // 2), steps)
     down_tile = pl.BlockSpec((tile, width // 2), lambda j, place: (turn(j, place), 0))

time: 205 us -> 205 us (level)
  no operation moved by 1% of the time
where the time goes in v6:
time: 205 us; the launch traced here: 203 us
  Pallas kernels  130 us (63%)
  waiting for transfers between devices  33 us (16%)
  starting transfers between devices  30.9 us (15%)
  local copies, waits for them, and re-layouts  5.71 us (3%)
  between operations  2.54 us (1%)
    pallas_call x10, Pallas kernels, combine(): pl.pallas_call(kernel, grid_spec=pltpu.PrefetchScalarGridSpec(num_scalar_...  35.7 us
    ppermute x18, starting transfers between devices, bits_apart(): return lax.ppermute(array, 'dp', [(i, i ^ mask) for i in range(count)])  28.4 us
    ppermute x18, waiting for transfers between devices, bits_apart(): return lax.ppermute(array, 'dp', [(i, i ^ mask) for i in range(count)])  26.5 us
    pallas_call x1, Pallas kernels, feed_forward(): pl.pallas_call(ffn_kernel, grid_spec=pltpu.PrefetchScalarGridSpec(num_sca...  22.7 us
    pallas_call x2, Pallas kernels, attend_back(): pl.pallas_call(attend_back_kernel, grid=(count,), in_specs=[near, near, f...  20.2 us
    pallas_call x1, Pallas kernels, attend(): pl.pallas_call(attend_kernel, grid_spec=pltpu.PrefetchScalarGridSpec(num_...  14.1 us
    pallas_call x1, Pallas kernels, embed(): pl.pallas_call(embed_kernel, grid_spec=pltpu.PrefetchScalarGridSpec(num_s...  11.4 us
    pallas_call x1, Pallas kernels, last_back(): pl.pallas_call(functools.partial(last_back_kernel, groups), grid_spec=plt...  7.37 us
  transfers between devices with their start and end apart: 29, of which 15 were waited for; matrix products, arithmetic and copies ran while one was open for 0% of the time, Pallas kernels for 36%

profile of v6, /device:TPU:0, one launch (start us, length us, event | category | flops | bytes accessed | tf_op | source)
XLA Modules:
  0.0 202.5 jit_solution(4000481993280901503)
XLA Ops:
  2.6 11.4 %embed.1 = (f32[512,768]{1,0:T(8,128)}, bf16[512,768]{1,0:T(8,128)(2,1)}, bf16[512,1536]{1,0:T(8,128)(2,1)}) custom-call(s32[8]{0:T(128)} %stack.31.place_ref.refs_0_, s32[1,512]{1,0:T(1,128)} %ids_ref.5, f32[1,512]{1,0:T(1,128)} %expression_ref.3, bf16[512,768]{1,0:T(8,128)(2,1)} %bitcast.27, bf16[2304,768]{1,0:T(8,128)(2,1)} %table_ref.1, ...), custom_call_target="tpu_custom_call" | custom-call | tf_op jit(solution)/shard_map/embed/pallas_call | solution.py:115
  14.4 1.1 copy-done.2
  16.5 1.2 collective-permute-done.kr_ref.vr_ref
  17.7 14.1 %attend.1 = (bf16[512,768]{1,0:T(8,128)(2,1)S(1)}, bf16[12,1024,512]{2,1,0:T(8,128)(2,1)}, f32[6,2,512]{2,1,0:T(2,128)S(1)}) custom-call(s32[8]{0:T(128)S(1)} %copy-done.11, bf16[512,768]{1,0:T(8,128)(2,1)S(1)} %queries.1.q_ref, bf16[512,1536]{1,0:T(8,128)(2,1)S(1)} %copy-done.14, bf16[512,1536]{1,0:T(8,128)(2,1)S(1)} %copy-done.14, ...), custom_call_target="tpu_custom_call" | custom-call | flops 3221225472 | bytes 12582912 | tf_op jit(solution)/shard_map/attend/pallas_call | solution.py:218
  31.9 22.7 %feed_forward.1 = (bf16[512,768]{1,0:T(8,128)(2,1)}, f32[512,768]{1,0:T(8,128)S(1)}, f32[512,768]{1,0:T(8,128)S(1)}, bf16[768,1536]{1,0:T(8,128)(2,1)}, bf16[768...) custom-call(s32[8]{0:T(128)S(1)} %copy-done.11, ...), custom_call_target="tpu_custom_call" | custom-call | flops 999999995904 | bytes 1 | tf_op jit(solution)/shard_map/feed_forward/pallas_call | solution.py:422
  55.1 3.6 %branch_back.1 = (f32[512,768]{1,0:T(8,128)S(1)}, bf16[512,768]{1,0:T(8,128)(2,1)S(1)}, bf16[768,384]{1,0:T(8,128)(2,1)S(1)}, bf16[768,384]{1,0:T(8,128)(2,1)S(1)}, f32[4,768]{1,0:T(4,128)S(1)}) custom-call(s32[8]{0:T(128)S(1)} %copy-done.11, f32[512,768]{1,0:T(8,128)S(1)} %get-tuple-element.93.residual_ref, f32[512,768]{1,0:T(8,128)S(1)} %get-tuple-element.94.g_normed_ref, ...), custom_call_target="tpu_custom_call" | custom-call | flops 999999995904 | bytes 1 | tf_op jit(solution)/shard_map/branch_back/pallas_call | solution.py:536
  59.5 1.2 copy-done.31
  61.1 2.2 %collective-permute-done.2 = bf16[768,384]{1,0:T(8,128)(2,1)S(1)} collective-permute-done((bf16[768,384]{1,0:T(8,128)(2,1)S(1)}, bf16[768,384]{1,0:T(8,128)(2,1)S(1)}, u32[]{:S(2)}, u32[]{:S(2)}) %collective-permute-start.2) | collective-permute-done | bytes 589856 | tf_op jit(solution)/shard_map/ppermute | solution.py:871
  64.2 4.7 %combine.10 = (bf16[2,2,2,224,384]{4,3,2,1,0:T(8,128)(2,1)}, bf16[2,2,2,208,384]{4,3,2,1,0:T(8,128)(2,1)}) custom-call(s32[8]{0:T(128)S(1)} %copy-done.11, bf16[2,2,2,2,192,384]{5,4,3,2,1,0:T(8,128)(2,1)} %bitcast.72, bf16[2,2,2,2,192,384]{5,4,3,2,1,0:T(8,128)(2,1)} %bitcast.13.refs_2_, bf16[2,2,2,2,48,384]{5,4,3,2,1,0:T(8,128)(2,1)} %bitcast.52, ...), custom_call_target="tpu_custom_call" | custom-call | flops 999999995904 | bytes 1 | tf_op jit(solution)/shard_map/combine/pallas_call | solution.py:1052
  68.9 2.9 %collective-permute-start.6 = (bf16[2,2,2,224,384]{4,3,2,1,0:T(8,128)(2,1)}, bf16[2,2,2,224,384]{4,3,2,1,0:T(8,128)(2,1)}, u32[]{:S(2)}, u32[]{:S(2)}) collective-permute-start(bf16[2,2,2,224,384]{4,3,2,1,0:T(8,128)(2,1)} %get-tuple-element.104.rest_0_), channel_id=1, source_target_pairs={{0,2},{2,0},{4,6},{6,4},{8,10},{10,8},{12,14},{14,12},{16,18},{18,... | collective-permute-start | bytes 4128776 | tf_op jit(solution)/shard_map/ppermute | solution.py:876
  71.7 1.5 collective-permute-start.7
  73.3 12.6 %attend_back.2 = (bf16[512,512]{1,0:T(8,128)(2,1)S(1)}, bf16[2,512,512]{2,1,0:T(8,128)(2,1)S(1)}, bf16[2,512,512]{2,1,0:T(8,128)(2,1)}) custom-call(bf16[512,768]{1,0:T(8,128)(2,1)S(1)} %copy-done.6, bf16[512,1536]{1,0:T(8,128)(2,1)S(1)} %copy-done.15, bf16[512,1536]{1,0:T(8,128)(2,1)S(1)} %copy-done.15, bf16[512,1536]{1,0:T(8,128)(2,1)} %copy-done.16, ...), custom_call_target="tpu_custom_call" | custom-call | flops 999999995904 | bytes 1 | tf_op jit(solution)/shard_map/attend_back/pallas_call | solution.py:301
  85.9 7.5 %attend_back.3 = (bf16[512,256]{1,0:T(8,128)(2,1)S(1)}, bf16[2,512,256]{2,1,0:T(8,128)(2,1)S(1)}, bf16[2,512,256]{2,1,0:T(8,128)(2,1)}) custom-call(bf16[512,768]{1,0:T(8,128)(2,1)S(1)} %copy-done.6, bf16[512,1536]{1,0:T(8,128)(2,1)S(1)} %copy-done.15, bf16[512,1536]{1,0:T(8,128)(2,1)S(1)} %copy-done.15, bf16[512,1536]{1,0:T(8,128)(2,1)S(1)} %copy-done.17, ...), custom_call_target="tpu_custom_call" | custom-call | flops 999999995904 | bytes 1 | tf_op jit(solution)/shard_map/attend_back/pallas_call | solution.py:301
  93.5 6.4 %first_back.1 = (bf16[768,768]{1,0:T(8,128)(2,1)S(1)}, bf16[768,768]{1,0:T(8,128)(2,1)S(1)}, f32[2,2,256]{2,1,0:T(2,128)S(1)}, f32[512,768]{1,0:T(8,128)S(1)}) custom-call(s32[8]{0:T(128)S(1)} %copy-done.11, bf16[512,768]{1,0:T(8,128)(2,1)S(1)} %copy-done.3, bf16[512,512]{1,0:T(8,128)(2,1)S(1)} %get-tuple-element.106.rest_0_.dq_ref, ...), custom_call_target="tpu_custom_call" | custom-call | flops 999999995904 | bytes 1 | tf_op jit(solution)/shard_map/first_back/pallas_call | solution.py:726
  99.9 1.0 copy-done.27
  102.5 1.3 collective-permute-done.8
  103.9 4.4 %combine.11 = (bf16[2,2,224,384]{3,2,1,0:T(8,128)(2,1)}, bf16[2,2,208,384]{3,2,1,0:T(8,128)(2,1)}, bf16[2,2,2,96,384]{4,3,2,1,0:T(8,128)(2,1)}) custom-call(s32[8]{0:T(128)S(1)} %copy-done.12, bf16[2,2,2,2,192,384]{5,4,3,2,1,0:T(8,128)(2,1)} %bitcast.73, bf16[2,2,2,2,192,384]{5,4,3,2,1,0:T(8,128)(2,1)} %bitcast.13.refs_2_, ...), custom_call_target="tpu_custom_call" | custom-call | flops 999999995904 | bytes 1 | tf_op jit(solution)/shard_map/combine/pallas_call | solution.py:1052
  108.3 1.6 collective-permute-start.11
  110.5 1.4 collective-permute-start.16
  112.0 7.4 %last_back.1 = (bf16[16,64,768]{2,1,0:T(8,128)(2,1)}, bf16[16,64,768]{2,1,0:T(8,128)(2,1)S(1)}, bf16[512,768]{1,0:T(8,128)(2,1)S(1)}) custom-call(s32[8]{0:T(128)S(1)} %copy-done.12, bf16[512,768]{1,0:T(8,128)(2,1)S(1)} %copy-done.4, bf16[512,256]{1,0:T(8,128)(2,1)S(1)} %copy-done.35, bf16[2,512,256]{2,1,0:T(8,128)(2,1)S(1)} %get-tuple-element.108.own_ref, ...), custom_call_target="tpu_custom_call" | custom-call | flops 999999995904 | bytes 1 | tf_op jit(solution)/shard_map/last_back/pallas_call | solution.py:780
  119.3 2.3 %gene_rows.2.rest_0_ = bf16[1152,768]{1,0:T(8,128)(2,1)} custom-call(s32[1152,1]{1,0:T(8,128)S(1)} %broadcast_add_fusion.slots_ref, s32[1,512]{1,0:T(1,128)S(1)} %copy-done.10, bf16[512,768]{1,0:T(8,128)(2,1)S(1)} %get-tuple-element.124.grad_ref, bf16[16,64,768]{2,1,0:T(8,128)(2,1)} %get-tuple-element.123.rest_0_), custom_call_target="tpu_custom_call" | custom-call | flops 999999995904 | bytes 1 | tf_op jit(solution)/shard_map/gene_rows/pallas_call | solution.py:853
  122.2 1.1 gene_rows.3.refs_4_
  123.3 0.9 collective-permute-done.11.refs_3_.refs_15_.refs_7_.refs_10_
  124.2 2.5 %combine.12.refs_11_ = bf16[2,2,96,384]{3,2,1,0:T(8,128)(2,1)} custom-call(s32[8]{0:T(128)S(1)} %copy-done.12, bf16[2,2,2,2,48,768]{5,4,3,2,1,0:T(8,128)(2,1)} %bitcast.48, bf16[2,2,2,2,48,768]{5,4,3,2,1,0:T(8,128)(2,1)} %bitcast.19.refs_12_.refs_2_.refs_14_.refs_6_.refs_9_, ...), custom_call_target="tpu_custom_call" | custom-call | flops 999999995904 | bytes 1 | tf_op jit(solution)/shard_map/combine/pallas_call | solution.py:1052
  126.8 2.6 %collective-permute-start.14 = (bf16[2,2,96,384]{3,2,1,0:T(8,128)(2,1)}, bf16[2,2,96,384]{3,2,1,0:T(8,128)(2,1)}, u32[]{:S(2)}, u32[]{:S(2)}) collective-permute-start(bf16[2,2,96,384]{3,2,1,0:T(8,128)(2,1)} %combine.12.refs_11_), channel_id=1, source_target_pairs={{0,16},{2,18},{4,20},{6,22},{8,24},{10,26},{12,28},{14,30},{16,0},... | collective-permute-start | bytes 884744 | tf_op jit(solution)/shard_map/ppermute | solution.py:876
  129.3 4.0 %combine.13 = (bf16[2,2,2,120,384]{4,3,2,1,0:T(8,128)(2,1)}, bf16[2,2,2,136,384]{4,3,2,1,0:T(8,128)(2,1)}) custom-call(s32[8]{0:T(128)S(1)} %copy-done.12, bf16[2,2,2,2,64,768]{5,4,3,2,1,0:T(8,128)(2,1)} %bitcast.38, bf16[2,2,2,2,64,768]{5,4,3,2,1,0:T(8,128)(2,1)} %bitcast.21.refs_2_.refs_6_.refs_8_.refs_7_.refs_9_, ...), custom_call_target="tpu_custom_call" | custom-call | flops 999999995904 | bytes 1 | tf_op jit(solution)/shard_map/combine/pallas_call | solution.py:1052
  134.7 4.4 %combine.14 = (bf16[432,384]{1,0:T(8,128)(2,1)}, bf16[432,384]{1,0:T(8,128)(2,1)}, bf16[432,384]{1,0:T(8,128)(2,1)}) custom-call(s32[8]{0:T(128)S(1)} %copy-done.12, bf16[2,2,2,2,192,384]{5,4,3,2,1,0:T(8,128)(2,1)} %bitcast.74, bf16[2,2,2,2,192,384]{5,4,3,2,1,0:T(8,128)(2,1)} %bitcast.13.refs_2_, bf16[2,2,2,2,48,384]{5,4,3,2,1,0:T(8,128)(2,1)} %bitcast.56, ...), custom_call_target="tpu_custom_call" | custom-call | flops 999999995904 | bytes 1 | tf_op jit(solution)/shard_map/combine/pallas_call | solution.py:1052
  139.1 1.4 collective-permute-start.20
  140.8 2.2 %collective-permute-done.14.refs_16_.refs_8_.refs_11_ = bf16[2,2,96,384]{3,2,1,0:T(8,128)(2,1)} collective-permute-done((bf16[2,2,96,384]{3,2,1,0:T(8,128)(2,1)}, bf16[2,2,96,384]{3,2,1,0:T(8,128)(2,1)}, u32[]{:S(2)}, u32[]{:S(2)}) %collective-permute-start.14) | collective-permute-done | bytes 294944 | tf_op jit(solution)/shard_map/ppermute | solution.py:876
  143.0 3.4 %collective-permute-start.22 = (bf16[432,384]{1,0:T(8,128)(2,1)}, bf16[432,384]{1,0:T(8,128)(2,1)}, u32[]{:S(2)}, u32[]{:S(2)}) collective-permute-start(bf16[432,384]{1,0:T(8,128)(2,1)} %get-tuple-element.129.refs_19_), channel_id=1, source_target_pairs={{0,24},{2,26},{4,28},{6,30},{8,16},{10,18},{12,20},{14,22},{16,8},... | collective-permute-start | bytes 995336 | tf_op jit(solution)/shard_map/ppermute | solution.py:876
  146.4 5.2 %collective-permute-done.12.refs_5_ = bf16[2,2,2,120,384]{4,3,2,1,0:T(8,128)(2,1)} collective-permute-done((bf16[2,2,2,120,384]{4,3,2,1,0:T(8,128)(2,1)}, bf16[2,2,2,120,384]{4,3,2,1,0:T(8,128)(2,1)}, u32[]{:S(2)}, u32[]{:S(2)}) %collective-permute-start.12) | collective-permute-done | bytes 737312 | tf_op jit(solution)/shard_map/ppermute | solution.py:876
  151.6 1.9 collective-permute-done.13.refs_12_
  153.5 3.6 %combine.15 = (bf16[2,2,120,384]{3,2,1,0:T(8,128)(2,1)}, bf16[2,2,136,384]{3,2,1,0:T(8,128)(2,1)}, bf16[2,96,384]{2,1,0:T(8,128)(2,1)}) custom-call(s32[8]{0:T(128)S(1)} %copy-done.12, bf16[2,2,2,2,64,768]{5,4,3,2,1,0:T(8,128)(2,1)} %bitcast.41, bf16[2,2,2,2,64,768]{5,4,3,2,1,0:T(8,128)(2,1)} %bitcast.21.refs_2_.refs_6_.refs_8_.refs_7_.refs_9_, ...), custom_call_target="tpu_custom_call" | custom-call | flops 999999995904 | bytes 1 | tf_op jit(solution)/shard_map/combine/pallas_call | solution.py:1052
  157.6 1.2 collective-permute-start.17
  158.9 2.7 %combine.16 = (f32[2,2,120,384]{3,2,1,0:T(8,128)S(1)}, f32[2,2,136,384]{3,2,1,0:T(8,128)S(1)}) custom-call(s32[8]{0:T(128)S(1)} %copy-done.12, bf16[2,2,2,2,64,768]{5,4,3,2,1,0:T(8,128)(2,1)} %bitcast.44, bf16[2,2,2,2,64,768]{5,4,3,2,1,0:T(8,128)(2,1)} %bitcast.21.refs_2_.refs_6_.refs_8_.refs_7_.refs_9_, bf16[2,2,2,2,72,768]{5,4,3,2,1,0:T(8,128)(2,1)} %bitcast.36, ...), custom_call_target="tpu_custom_call" | custom-call | flops 999999995904 | bytes 1 | tf_op jit(solution)/shard_map/combine/pallas_call | solution.py:1052
  162.5 4.1 %collective-permute-done.21.refs_14_ = bf16[432,384]{1,0:T(8,128)(2,1)} collective-permute-done((bf16[432,384]{1,0:T(8,128)(2,1)}, bf16[432,384]{1,0:T(8,128)(2,1)}, u32[]{:S(2)}, u32[]{:S(2)}) %collective-permute-start.21) | collective-permute-done | bytes 331808 | tf_op jit(solution)/shard_map/ppermute | solution.py:876
  166.6 3.4 %combine.17.refs_10_.own_ref = f32[432,384]{1,0:T(8,128)} custom-call(s32[8]{0:T(128)S(1)} %copy-done.12, bf16[2,2,2,2,192,384]{5,4,3,2,1,0:T(8,128)(2,1)} %bitcast.75, bf16[2,2,2,2,192,384]{5,4,3,2,1,0:T(8,128)(2,1)} %bitcast.13.refs_2_, bf16[2,2,2,2,48,384]{5,4,3,2,1,0:T(8,128)(2,1)} %bitcast.58, bf16[2,2,2,2,48,384]{5,4,3,2,1,0:T(8,128)(2,1)} %bitcast.66, ...), custom_call_target="tpu_custom_call" | custom-call | flops 999999995904 | bytes 1 | tf_op jit(solution)/shard_map/combine/pallas_call | solution.py:1052
  170.4 3.2 %combine.18 = (bf16[264,384]{1,0:T(8,128)(2,1)}, bf16[264,384]{1,0:T(8,128)(2,1)}, bf16[264,384]{1,0:T(8,128)(2,1)}, bf16[96,384]{1,0:T(8,128)(2,1)}) custom-call(s32[8]{0:T(128)S(1)} %copy-done.12, f32[2,2,120,384]{3,2,1,0:T(8,128)} %copy-done.33, f32[2,2,136,384]{3,2,1,0:T(8,128)} %copy-done.32, bf16[2,2,120,384]{3,2,1,0:T(8,128)(2,1)} %collective-permute-done.17.refs_3_, ...), custom_call_target="tpu_custom_call" | custom-call | flops 999999995904 | bytes 1 | tf_op jit(solution)/shard_map/combine/pallas_call | solution.py:1052
  173.6 5.0 %collective-permute-start.23 = (bf16[264,384]{1,0:T(8,128)(2,1)}, bf16[264,384]{1,0:T(8,128)(2,1)}, u32[]{:S(2)}, u32[]{:S(2)}) collective-permute-start(bf16[264,384]{1,0:T(8,128)(2,1)} %get-tuple-element.135), channel_id=1, source_target_pairs={{0,8},{2,10},{4,12},{6,14},{8,0},{10,2},{12,4},{14,6},{16,24},{18,... | collective-permute-start | bytes 608264 | tf_op jit(solution)/shard_map/ppermute | solution.py:876
  178.6 2.0 collective-permute-start.24
  180.5 1.4 collective-permute-start.25
  182.5 2.9 %assemble.2 = (f32[192,768]{1,0:T(8,128)}, f32[48,3072]{1,0:T(8,128)}, f32[48,768]{1,0:T(8,128)}, f32[8,128]{1,0:T(8,128)S(1)}) custom-call(s32[8]{0:T(128)S(1)} %copy-done.12, f32[432,384]{1,0:T(8,128)} %combine.17.refs_10_.own_ref, f32[432,384]{1,0:T(8,128)} %collective-permute-done.27.other_ref), custom_call_target="tpu_custom_call" | custom-call | flops 999999995904 | bytes 1 | tf_op jit(solution)/shard_map/assemble/pallas_call | solution.py:1103
  185.4 1.2 collective-permute-done.26.refs_13_
  186.6 2.3 %collective-permute-done.23.refs_5_ = bf16[264,384]{1,0:T(8,128)(2,1)} collective-permute-done((bf16[264,384]{1,0:T(8,128)(2,1)}, bf16[264,384]{1,0:T(8,128)(2,1)}, u32[]{:S(2)}, u32[]{:S(2)}) %collective-permute-start.23) | collective-permute-done | bytes 202784 | tf_op jit(solution)/shard_map/ppermute | solution.py:876
  188.9 7.6 %collective-permute-done.25.refs_7_ = bf16[264,384]{1,0:T(8,128)(2,1)} collective-permute-done((bf16[264,384]{1,0:T(8,128)(2,1)}, bf16[264,384]{1,0:T(8,128)(2,1)}, u32[]{:S(2)}, u32[]{:S(2)}) %collective-permute-start.25) | collective-permute-done | bytes 202784 | tf_op jit(solution)/shard_map/ppermute | solution.py:876
  196.5 2.8 %combine.19 = (f32[208,384]{1,0:T(8,128)S(1)}, f32[72,768]{1,0:T(8,128)}) custom-call(s32[8]{0:T(128)S(1)} %copy-done.12, f32[2,2,120,384]{3,2,1,0:T(8,128)} %copy-done.33, f32[2,2,136,384]{3,2,1,0:T(8,128)} %copy-done.32, bf16[2,2,120,384]{3,2,1,0:T(8,128)(2,1)} %collective-permute-done.17.refs_3_, ...), custom_call_target="tpu_custom_call" | custom-call | flops 999999995904 | bytes 1 | tf_op jit(solution)/shard_map/combine/pallas_call | solution.py:1052
  199.2 1.6 collective-permute-done.28.other_ref
  200.8 1.5 assemble.3
  (110 shorter events, 11.1 us)
Async XLA Ops:
  2.6 11.9 %copy-start = (bf16[768,2304]{1,0:T(8,128)(2,1)S(1)}, bf16[768,2304]{1,0:T(8,128)(2,1)}, u32[]{:S(2)}) copy-start(bf16[768,2304]{1,0:T(8,128)(2,1)} %wv_ref.3) | copy-start | bytes 10616836
  2.6 11.9 %copy-start.8 = (f32[768]{0:T(1024)S(1)}, f32[768]{0:T(1024)}, u32[]{:S(2)}) copy-start(f32[768]{0:T(1024)} %bias_ref.1) | copy-start | bytes 9220
  14.0 3.7 %collective-permute-start = (bf16[512,1536]{1,0:T(8,128)(2,1)}, bf16[512,1536]{1,0:T(8,128)(2,1)S(1)}, u32[]{:S(2)}, u32[]{:S(2)}) collective-permute-start(bf16[512,1536]{1,0:T(8,128)(2,1)} %get-tuple-element.89.ko_ref.vo_ref), channel_id=1, source_target_pairs={{0,1},{1,0},{2,3},{3,2},{4,5},{5,4},{6,7},{7,6},{8,9},{9,8},{10,11... | collective-permute-start | bytes 4718600 | tf_op jit(solution)/shard_map/ppermute | solution.py:871
  16.4 15.4 %copy-start.5 = (bf16[512,768]{1,0:T(8,128)(2,1)}, bf16[512,768]{1,0:T(8,128)(2,1)S(1)}, u32[]{:S(2)}) copy-start(bf16[512,768]{1,0:T(8,128)(2,1)S(1)} %queries.1.q_ref) | copy-start | bytes 2359300
  16.4 15.4 %copy-start.13 = (f32[512,768]{1,0:T(8,128)S(1)}, f32[512,768]{1,0:T(8,128)}, u32[]{:S(2)}) copy-start(f32[512,768]{1,0:T(8,128)} %get-tuple-element.91.embedded_ref) | copy-start | bytes 4718596
  16.4 15.4 %copy-start.18 = (bf16[768,768]{1,0:T(8,128)(2,1)S(1)}, bf16[768,768]{1,0:T(8,128)(2,1)}, u32[]{:S(2)}) copy-start(bf16[768,768]{1,0:T(8,128)(2,1)} %w_out_ref.3) | copy-start | bytes 3538948
  16.4 15.4 %copy-start.19 = (bf16[1,512,768]{2,1,0:T(8,128)(2,1)S(1)}, bf16[1,512,768]{2,1,0:T(8,128)(2,1)}, u32[]{:S(2)}) copy-start(bf16[1,512,768]{2,1,0:T(8,128)(2,1)} %param.45) | copy-start | bytes 2359300
  16.4 15.4 %copy-start.20 = (f32[3072]{0:T(1024)S(1)}, f32[3072]{0:T(1024)}, u32[]{:S(2)}) copy-start(f32[3072]{0:T(1024)} %param.42) | copy-start | bytes 36868
  16.4 15.4 %copy-start.21 = (f32[768]{0:T(1024)S(1)}, f32[768]{0:T(1024)}, u32[]{:S(2)}) copy-start(f32[768]{0:T(1024)} %bias_out_ref.1) | copy-start | bytes 9220
  16.4 15.4 %copy-start.22 = (f32[768]{0:T(1024)S(1)}, f32[768]{0:T(1024)}, u32[]{:S(2)}) copy-start(f32[768]{0:T(1024)} %offset_ref.3) | copy-start | bytes 9220
  16.5 15.4 %copy-start.23 = (f32[768]{0:T(1024)S(1)}, f32[768]{0:T(1024)}, u32[]{:S(2)}) copy-start(f32[768]{0:T(1024)} %bias_down_ref.1) | copy-start | bytes 9220
  16.5 15.4 %copy-start.24 = (f32[768]{0:T(1024)S(1)}, f32[768]{0:T(1024)}, u32[]{:S(2)}) copy-start(f32[768]{0:T(1024)} %gain_ref.6) | copy-start | bytes 9220
  17.7 14.1 %copy-start.16 = (bf16[512,1536]{1,0:T(8,128)(2,1)}, bf16[512,1536]{1,0:T(8,128)(2,1)S(1)}, u32[]{:S(2)}) copy-start(bf16[512,1536]{1,0:T(8,128)(2,1)S(1)} %collective-permute-done.kr_ref.vr_ref) | copy-start | bytes 4718596
  31.8 23.3 %copy-start.29 = (bf16[512,768]{1,0:T(8,128)(2,1)}, bf16[512,768]{1,0:T(8,128)(2,1)S(1)}, u32[]{:S(2)}) copy-start(bf16[512,768]{1,0:T(8,128)(2,1)S(1)} %get-tuple-element.90.attended_ref.a_ref) | copy-start | bytes 2359300
  54.6 8.8 %collective-permute-start.1 = (bf16[3072,384]{1,0:T(8,128)(2,1)}, bf16[3072,384]{1,0:T(8,128)(2,1)}, u32[]{:S(2)}, u32[]{:S(2)}) collective-permute-start(bf16[3072,384]{1,0:T(8,128)(2,1)} %get-tuple-element.96.rest_1_), channel_id=1, source_target_pairs={{0,1},{1,0},{2,3},{3,2},{4,5},{5,4},{6,7},{7,6},{8,9},{9,8},{10,11... | collective-permute-start | bytes 7077896 | tf_op jit(solution)/shard_map/ppermute | solution.py:871
  55.0 8.4 %collective-permute-start.3 = (bf16[768,1536]{1,0:T(8,128)(2,1)}, bf16[768,1536]{1,0:T(8,128)(2,1)}, u32[]{:S(2)}, u32[]{:S(2)}) collective-permute-start(bf16[768,1536]{1,0:T(8,128)(2,1)} %get-tuple-element.95.rest_0_), channel_id=1, source_target_pairs={{0,1},{1,0},{2,3},{3,2},{4,5},{5,4},{6,7},{7,6},{8,9},{9,8},{10,11... | collective-permute-start | bytes 7077896 | tf_op jit(solution)/shard_map/ppermute | solution.py:871
  60.7 2.6 %collective-permute-start.2 = (bf16[768,384]{1,0:T(8,128)(2,1)S(1)}, bf16[768,384]{1,0:T(8,128)(2,1)S(1)}, u32[]{:S(2)}, u32[]{:S(2)}) collective-permute-start(bf16[768,384]{1,0:T(8,128)(2,1)S(1)} %get-tuple-element.102), channel_id=1, source_target_pairs={{0,1},{1,0},{2,3},{3,2},{4,5},{5,4},{6,7},{7,6},{8,9},{9,8},{10,11... | collective-permute-start | bytes 1769480 | tf_op jit(solution)/shard_map/ppermute | solution.py:871
  64.2 9.1 %copy-start.6 = (bf16[512,768]{1,0:T(8,128)(2,1)S(1)}, bf16[512,768]{1,0:T(8,128)(2,1)}, u32[]{:S(2)}) copy-start(bf16[512,768]{1,0:T(8,128)(2,1)} %copy-done.5) | copy-start | bytes 2359300
  64.2 9.1 %copy-start.15 = (bf16[512,1536]{1,0:T(8,128)(2,1)S(1)}, bf16[512,1536]{1,0:T(8,128)(2,1)}, u32[]{:S(2)}) copy-start(bf16[512,1536]{1,0:T(8,128)(2,1)} %get-tuple-element.89.ko_ref.vo_ref) | copy-start | bytes 4718596
  64.2 9.1 %copy-start.30 = (bf16[512,768]{1,0:T(8,128)(2,1)S(1)}, bf16[512,768]{1,0:T(8,128)(2,1)}, u32[]{:S(2)}) copy-start(bf16[512,768]{1,0:T(8,128)(2,1)} %copy-done.29) | copy-start | bytes 2359300
  68.9 33.6 %collective-permute-start.6 = (bf16[2,2,2,224,384]{4,3,2,1,0:T(8,128)(2,1)}, bf16[2,2,2,224,384]{4,3,2,1,0:T(8,128)(2,1)}, u32[]{:S(2)}, u32[]{:S(2)}) collective-permute-start(bf16[2,2,2,224,384]{4,3,2,1,0:T(8,128)(2,1)} %get-tuple-element.104.rest_0_), channel_id=1, source_target_pairs={{0,2},{2,0},{4,6},{6,4},{8,10},{10,8},{12,14},{14,12},{16,18},{18,... | collective-permute-start | bytes 4128776 | tf_op jit(solution)/shard_map/ppermute | solution.py:876
  71.7 30.2 %collective-permute-start.7 = (bf16[2,2,2,208,384]{4,3,2,1,0:T(8,128)(2,1)}, bf16[2,2,2,208,384]{4,3,2,1,0:T(8,128)(2,1)}, u32[]{:S(2)}, u32[]{:S(2)}) collective-permute-start(bf16[2,2,2,208,384]{4,3,2,1,0:T(8,128)(2,1)} %get-tuple-element.105.rest_1_), channel_id=1, source_target_pairs={{0,4},{2,6},{4,0},{6,2},{8,12},{10,14},{12,8},{14,10},{16,20},{18,... | collective-permute-start | bytes 3833864 | tf_op jit(solution)/shard_map/ppermute | solution.py:876
  73.2 12.6 %copy-start.17 = (bf16[512,1536]{1,0:T(8,128)(2,1)S(1)}, bf16[512,1536]{1,0:T(8,128)(2,1)}, u32[]{:S(2)}) copy-start(bf16[512,1536]{1,0:T(8,128)(2,1)} %copy-done.16) | copy-start | bytes 4718596
  85.9 7.6 %collective-permute-start.5 = (bf16[2,512,512]{2,1,0:T(8,128)(2,1)}, bf16[2,512,512]{2,1,0:T(8,128)(2,1)}, u32[]{:S(2)}, u32[]{:S(2)}) collective-permute-start(bf16[2,512,512]{2,1,0:T(8,128)(2,1)} %get-tuple-element.111), channel_id=1, source_target_pairs={{0,1},{1,0},{2,3},{3,2},{4,5},{5,4},{6,7},{7,6},{8,9},{9,8},{10,11... | collective-permute-start | bytes 3145736 | tf_op jit(solution)/shard_map/ppermute | solution.py:871
  93.5 10.4 %copy-start.12 = (s32[8]{0:T(128)S(1)}, s32[8]{0:T(128)}, u32[]{:S(2)}) copy-start(s32[8]{0:T(128)} %stack.31.place_ref.refs_0_) | copy-start | bytes 100
  100.9 3.0 %collective-permute-start.8 = (bf16[768,768]{1,0:T(8,128)(2,1)S(1)}, bf16[768,768]{1,0:T(8,128)(2,1)}, u32[]{:S(2)}, u32[]{:S(2)}) collective-permute-start(bf16[768,768]{1,0:T(8,128)(2,1)S(1)} %get-tuple-element.118.refs_14_), channel_id=1, source_target_pairs={{0,1},{1,0},{2,3},{3,2},{4,5},{5,4},{6,7},{7,6},{8,9},{9,8},{10,11... | collective-permute-start | bytes 3538952 | tf_op jit(solution)/shard_map/ppermute | solution.py:871
  101.5 10.4 %collective-permute-start.4 = (bf16[2,512,256]{2,1,0:T(8,128)(2,1)}, bf16[2,512,256]{2,1,0:T(8,128)(2,1)}, u32[]{:S(2)}, u32[]{:S(2)}) collective-permute-start(bf16[2,512,256]{2,1,0:T(8,128)(2,1)} %get-tuple-element.109), channel_id=1, source_target_pairs={{0,1},{1,0},{2,3},{3,2},{4,5},{5,4},{6,7},{7,6},{8,9},{9,8},{10,11... | collective-permute-start | bytes 1572872 | tf_op jit(solution)/shard_map/ppermute | solution.py:871
  108.3 15.9 %collective-permute-start.11 = (bf16[2,2,2,96,384]{4,3,2,1,0:T(8,128)(2,1)}, bf16[2,2,2,96,384]{4,3,2,1,0:T(8,128)(2,1)}, u32[]{:S(2)}, u32[]{:S(2)}) collective-permute-start(bf16[2,2,2,96,384]{4,3,2,1,0:T(8,128)(2,1)} %get-tuple-element.121.rest_2_), channel_id=1, source_target_pairs={{0,8},{2,10},{4,12},{6,14},{8,0},{10,2},{12,4},{14,6},{16,24},{18,... | collective-permute-start | bytes 1769480 | tf_op jit(solution)/shard_map/ppermute | solution.py:876
  110.0 24.7 %collective-permute-start.15 = (bf16[2,2,224,384]{3,2,1,0:T(8,128)(2,1)}, bf16[2,2,224,384]{3,2,1,0:T(8,128)(2,1)}, u32[]{:S(2)}, u32[]{:S(2)}) collective-permute-start(bf16[2,2,224,384]{3,2,1,0:T(8,128)(2,1)} %get-tuple-element.119.rest_0_), channel_id=1, source_target_pairs={{0,4},{2,6},{4,0},{6,2},{8,12},{10,14},{12,8},{14,10},{16,20},{18,... | collective-permute-start | bytes 2064392 | tf_op jit(solution)/shard_map/ppermute | solution.py:876
  110.5 24.2 %collective-permute-start.16 = (bf16[2,2,208,384]{3,2,1,0:T(8,128)(2,1)}, bf16[2,2,208,384]{3,2,1,0:T(8,128)(2,1)}, u32[]{:S(2)}, u32[]{:S(2)}) collective-permute-start(bf16[2,2,208,384]{3,2,1,0:T(8,128)(2,1)} %get-tuple-element.120.rest_1_), channel_id=1, source_target_pairs={{0,2},{2,0},{4,6},{6,4},{8,10},{10,8},{12,14},{14,12},{16,18},{18,... | collective-permute-start | bytes 1916936 | tf_op jit(solution)/shard_map/ppermute | solution.py:876
  119.3 10.0 %collective-permute-start.9 = (bf16[16,64,768]{2,1,0:T(8,128)(2,1)}, bf16[16,64,768]{2,1,0:T(8,128)(2,1)}, u32[]{:S(2)}, u32[]{:S(2)}) collective-permute-start(bf16[16,64,768]{2,1,0:T(8,128)(2,1)} %get-tuple-element.123.rest_0_), channel_id=1, source_target_pairs={{0,1},{1,0},{2,3},{3,2},{4,5},{5,4},{6,7},{7,6},{8,9},{9,8},{10,11... | collective-permute-start | bytes 4718600 | tf_op jit(solution)/shard_map/ppermute | solution.py:871
  121.7 7.7 %collective-permute-start.10 = (bf16[1152,768]{1,0:T(8,128)(2,1)}, bf16[1152,768]{1,0:T(8,128)(2,1)}, u32[]{:S(2)}, u32[]{:S(2)}) collective-permute-start(bf16[1152,768]{1,0:T(8,128)(2,1)} %gene_rows.2.rest_0_), channel_id=1, source_target_pairs={{0,1},{1,0},{2,3},{3,2},{4,5},{5,4},{6,7},{7,6},{8,9},{9,8},{10,11... | collective-permute-start | bytes 5308424 | tf_op jit(solution)/shard_map/ppermute | solution.py:871
  126.8 16.2 %collective-permute-start.14 = (bf16[2,2,96,384]{3,2,1,0:T(8,128)(2,1)}, bf16[2,2,96,384]{3,2,1,0:T(8,128)(2,1)}, u32[]{:S(2)}, u32[]{:S(2)}) collective-permute-start(bf16[2,2,96,384]{3,2,1,0:T(8,128)(2,1)} %combine.12.refs_11_), channel_id=1, source_target_pairs={{0,16},{2,18},{4,20},{6,22},{8,24},{10,26},{12,28},{14,30},{16,0},... | collective-permute-start | bytes 884744 | tf_op jit(solution)/shard_map/ppermute | solution.py:876
  133.4 20.1 %collective-permute-start.13 = (bf16[2,2,2,136,384]{4,3,2,1,0:T(8,128)(2,1)}, bf16[2,2,2,136,384]{4,3,2,1,0:T(8,128)(2,1)}, u32[]{:S(2)}, u32[]{:S(2)}) collective-permute-start(bf16[2,2,2,136,384]{4,3,2,1,0:T(8,128)(2,1)} %get-tuple-element.126.refs_14_), channel_id=1, source_target_pairs={{0,4},{2,6},{4,0},{6,2},{8,12},{10,14},{12,8},{14,10},{16,20},{18,... | collective-permute-start | bytes 2506760 | tf_op jit(solution)/shard_map/ppermute | solution.py:876
  133.9 17.7 %collective-permute-start.12 = (bf16[2,2,2,120,384]{4,3,2,1,0:T(8,128)(2,1)}, bf16[2,2,2,120,384]{4,3,2,1,0:T(8,128)(2,1)}, u32[]{:S(2)}, u32[]{:S(2)}) collective-permute-start(bf16[2,2,2,120,384]{4,3,2,1,0:T(8,128)(2,1)} %get-tuple-element.125.refs_13_), channel_id=1, source_target_pairs={{0,2},{2,0},{4,6},{6,4},{8,10},{10,8},{12,14},{14,12},{16,18},{18,... | collective-permute-start | bytes 2211848 | tf_op jit(solution)/shard_map/ppermute | solution.py:876
  139.1 22.5 %collective-permute-start.20 = (bf16[432,384]{1,0:T(8,128)(2,1)}, bf16[432,384]{1,0:T(8,128)(2,1)}, u32[]{:S(2)}, u32[]{:S(2)}) collective-permute-start(bf16[432,384]{1,0:T(8,128)(2,1)} %get-tuple-element.127.refs_17_), channel_id=1, source_target_pairs={{0,8},{2,10},{4,12},{6,14},{8,0},{10,2},{12,4},{14,6},{16,24},{18,... | collective-permute-start | bytes 995336 | tf_op jit(solution)/shard_map/ppermute | solution.py:876
  140.4 26.2 %collective-permute-start.21 = (bf16[432,384]{1,0:T(8,128)(2,1)}, bf16[432,384]{1,0:T(8,128)(2,1)}, u32[]{:S(2)}, u32[]{:S(2)}) collective-permute-start(bf16[432,384]{1,0:T(8,128)(2,1)} %get-tuple-element.128.refs_18_), channel_id=1, source_target_pairs={{0,16},{2,18},{4,20},{6,22},{8,24},{10,26},{12,28},{14,30},{16,0},... | collective-permute-start | bytes 995336 | tf_op jit(solution)/shard_map/ppermute | solution.py:876
  143.0 23.6 %collective-permute-start.22 = (bf16[432,384]{1,0:T(8,128)(2,1)}, bf16[432,384]{1,0:T(8,128)(2,1)}, u32[]{:S(2)}, u32[]{:S(2)}) collective-permute-start(bf16[432,384]{1,0:T(8,128)(2,1)} %get-tuple-element.129.refs_19_), channel_id=1, source_target_pairs={{0,24},{2,26},{4,28},{6,30},{8,16},{10,18},{12,20},{14,22},{16,8},... | collective-permute-start | bytes 995336 | tf_op jit(solution)/shard_map/ppermute | solution.py:876
  157.1 13.3 %collective-permute-start.18 = (bf16[2,2,136,384]{3,2,1,0:T(8,128)(2,1)}, bf16[2,2,136,384]{3,2,1,0:T(8,128)(2,1)}, u32[]{:S(2)}, u32[]{:S(2)}) collective-permute-start(bf16[2,2,136,384]{3,2,1,0:T(8,128)(2,1)} %get-tuple-element.131.refs_14_), channel_id=1, source_target_pairs={{0,2},{2,0},{4,6},{6,4},{8,10},{10,8},{12,14},{14,12},{16,18},{18,... | collective-permute-start | bytes 1253384 | tf_op jit(solution)/shard_map/ppermute | solution.py:876
  157.6 12.8 %collective-permute-start.17 = (bf16[2,2,120,384]{3,2,1,0:T(8,128)(2,1)}, bf16[2,2,120,384]{3,2,1,0:T(8,128)(2,1)}, u32[]{:S(2)}, u32[]{:S(2)}) collective-permute-start(bf16[2,2,120,384]{3,2,1,0:T(8,128)(2,1)} %get-tuple-element.130.refs_13_), channel_id=1, source_target_pairs={{0,4},{2,6},{4,0},{6,2},{8,12},{10,14},{12,8},{14,10},{16,20},{18,... | collective-permute-start | bytes 1105928 | tf_op jit(solution)/shard_map/ppermute | solution.py:876
  161.6 8.4 %copy-start.32 = (f32[2,2,136,384]{3,2,1,0:T(8,128)}, f32[2,2,136,384]{3,2,1,0:T(8,128)S(1)}, u32[]{:S(2)}) copy-start(f32[2,2,136,384]{3,2,1,0:T(8,128)S(1)} %get-tuple-element.134.refs_17_.refs_2_) | copy-start | bytes 2506756
  161.6 8.8 %collective-permute-start.19 = (bf16[2,96,384]{2,1,0:T(8,128)(2,1)}, bf16[2,96,384]{2,1,0:T(8,128)(2,1)}, u32[]{:S(2)}, u32[]{:S(2)}) collective-permute-start(bf16[2,96,384]{2,1,0:T(8,128)(2,1)} %get-tuple-element.132.refs_15_), channel_id=1, source_target_pairs={{0,2},{2,0},{4,6},{6,4},{8,10},{10,8},{12,14},{14,12},{16,18},{18,... | collective-permute-start | bytes 442376 | tf_op jit(solution)/shard_map/ppermute | solution.py:876
  170.0 12.5 %collective-permute-start.27 = (f32[432,384]{1,0:T(8,128)}, f32[432,384]{1,0:T(8,128)}, u32[]{:S(2)}, u32[]{:S(2)}) collective-permute-start(f32[432,384]{1,0:T(8,128)} %combine.17.refs_10_.own_ref), channel_id=1, source_target_pairs={{0,1},{1,0},{2,3},{3,2},{4,5},{5,4},{6,7},{7,6},{8,9},{9,8},{10,11... | collective-permute-start | bytes 1990664 | tf_op jit(solution)/shard_map/ppermute | solution.py:871
  173.6 15.3 %collective-permute-start.23 = (bf16[264,384]{1,0:T(8,128)(2,1)}, bf16[264,384]{1,0:T(8,128)(2,1)}, u32[]{:S(2)}, u32[]{:S(2)}) collective-permute-start(bf16[264,384]{1,0:T(8,128)(2,1)} %get-tuple-element.135), channel_id=1, source_target_pairs={{0,8},{2,10},{4,12},{6,14},{8,0},{10,2},{12,4},{14,6},{16,24},{18,... | collective-permute-start | bytes 608264 | tf_op jit(solution)/shard_map/ppermute | solution.py:876
  178.6 10.3 %collective-permute-start.24 = (bf16[264,384]{1,0:T(8,128)(2,1)}, bf16[264,384]{1,0:T(8,128)(2,1)}, u32[]{:S(2)}, u32[]{:S(2)}) collective-permute-start(bf16[264,384]{1,0:T(8,128)(2,1)} %get-tuple-element.136), channel_id=1, source_target_pairs={{0,16},{2,18},{4,20},{6,22},{8,24},{10,26},{12,28},{14,30},{16,0},... | collective-permute-start | bytes 608264 | tf_op jit(solution)/shard_map/ppermute | solution.py:876
  180.5 15.9 %collective-permute-start.25 = (bf16[264,384]{1,0:T(8,128)(2,1)}, bf16[264,384]{1,0:T(8,128)(2,1)}, u32[]{:S(2)}, u32[]{:S(2)}) collective-permute-start(bf16[264,384]{1,0:T(8,128)(2,1)} %get-tuple-element.137), channel_id=1, source_target_pairs={{0,24},{2,26},{4,28},{6,30},{8,16},{10,18},{12,20},{14,22},{16,8},... | collective-permute-start | bytes 608264 | tf_op jit(solution)/shard_map/ppermute | solution.py:876
  182.0 4.7 %collective-permute-start.26 = (bf16[96,384]{1,0:T(8,128)(2,1)}, bf16[96,384]{1,0:T(8,128)(2,1)}, u32[]{:S(2)}, u32[]{:S(2)}) collective-permute-start(bf16[96,384]{1,0:T(8,128)(2,1)} %get-tuple-element.138), channel_id=1, source_target_pairs={{0,4},{2,6},{4,0},{6,2},{8,12},{10,14},{12,8},{14,10},{16,20},{18,... | collective-permute-start | bytes 221192 | tf_op jit(solution)/shard_map/ppermute | solution.py:876
  199.2 1.6 collective-permute-start.28
  (18 other events, 85.0 us)
